TPU v7x, 32 devices: a whole 2x2x4 slice. The times are simulated.
32 devices in a mesh: band: 4 (over y, x), slab: 8 (over z, core).
Axes of the slice: x: 2, y: 2, z: 4, core: 2. Of those that a mesh axis runs over, the one named last changes fastest.
Arguments:
- psi: bfloat16 [32, 524288], P(('band', 'slab')), may hold values from -6 to 6
- beta: bfloat16 [8, 512, 1152], P('slab', 'band'), may hold values from -0.75 to 0.75
- pair_atom: int32 [8, 512], P('slab'), may hold values from 0 to 128, as said below
- pair_block: int32 [8, 512], P('slab'), may hold values from 0 to 1023
- proj_count: int32 [128], replicated, may hold values from 4 to 18, as said below
- strength: float32 [128, 18, 18], replicated, may hold values from -0.6 to 0.6
Outputs:
- applied: bfloat16 [32, 524288], P(('band', 'slab'))
Inputs may be any that keep to these rules, and one draw needn't show every extreme that they name: `pair_atom`: in each slab's 512 slots the used ones come first and the empty ones hold 128; some slab uses all its slots. `proj_count`: each atom has 4, 8, 13 or 18 projectors; some atom has 18.
All inputs are finite; a program needn't handle non-finite values.
Results may differ from a plain program's by a relative error of at most 0.0049.
Values may be sent and summed in bfloat16 or wider, within the bound.
No kernel may reach another device: no remote copies, remote signals or barrier semaphores. Data moves between devices by JAX's collectives and lax.ppermute only.
A program may use at most 192 MiB of HBM per device.

v0:
```python
import jax
import jax.numpy as jnp
from jax import lax
from jax.sharding import PartitionSpec as P


def project(grid_blocks, tables, atom_ids, block_ids, atom_total):
    picked = jnp.take(grid_blocks, block_ids, axis=1)
    products = jnp.einsum("bkg,kpg->kpb", picked, tables, preferred_element_type=jnp.float32)
    slot_total = products.shape[0]
    onehot = (atom_ids[None, :] == jnp.arange(atom_total, dtype=jnp.int32)[:, None]).astype(
        jnp.float32
    )
    summed = jnp.dot(onehot, products.reshape(slot_total, -1), precision=lax.Precision.HIGHEST)
    return summed.reshape(atom_total, products.shape[1], products.shape[2])


def apply_strength(coef_total, strength, proj_valid):
    masked = coef_total * proj_valid[:, :, None]
    coupled = jnp.einsum("apq,aqb->apb", strength, masked, precision=lax.Precision.HIGHEST)
    return (coupled * proj_valid[:, :, None]).astype(jnp.bfloat16)


def back_project(scaled, tables, atom_ids, block_ids, block_total):
    padded = jnp.concatenate([scaled, jnp.zeros((1,) + scaled.shape[1:], jnp.bfloat16)], axis=0)
    picked = jnp.take(padded, atom_ids, axis=0)
    products = jnp.einsum("kpg,kpb->kbg", tables, picked, preferred_element_type=jnp.float32)
    summed = jax.ops.segment_sum(products, block_ids, num_segments=block_total)
    band_rows = summed.shape[1]
    return summed.transpose(1, 0, 2).reshape(band_rows, -1).astype(jnp.bfloat16)


def body(psi, beta, pair_atom, pair_block, proj_count, strength):
    atom_total = strength.shape[0]
    proj_total = strength.shape[1]
    block_size = beta.shape[2] // proj_total
    proj_valid = (jnp.arange(proj_total, dtype=jnp.int32)[None, :] < proj_count[:, None]).astype(
        jnp.float32
    )
    slab_tables = lax.all_gather(beta, "band", axis=1, tiled=True)
    slot_count = slab_tables.shape[1]
    slab_rows = lax.all_to_all(psi, "slab", split_axis=1, concat_axis=0, tiled=True)
    group_rows = slab_rows.shape[0]
    block_local = slab_rows.shape[1] // block_size
    grid_blocks = slab_rows.reshape(group_rows, block_local, block_size)
    tables = slab_tables.reshape(slot_count, proj_total, block_size)
    atom_ids = pair_atom.reshape(slot_count)
    block_ids = pair_block.reshape(slot_count)
    coef_part = project(grid_blocks, tables, atom_ids, block_ids, atom_total)
    coef_total = lax.psum(coef_part, "slab")
    scaled = apply_strength(coef_total, strength, proj_valid)
    slab_applied = back_project(scaled, tables, atom_ids, block_ids, block_local)
    return lax.all_to_all(slab_applied, "slab", split_axis=0, concat_axis=1, tiled=True)


def solution(mesh):
    placed = (
        P(("band", "slab"), None),
        P("slab", "band", None),
        P("slab", None),
        P("slab", None),
        P(),
        P(),
    )
    return jax.shard_map(
        body, mesh=mesh, in_specs=placed, out_specs=P(("band", "slab"), None), check_vma=False
    )
```

profile of v0, /device:TPU:0, one launch (start us, length us, event | category | flops | bytes accessed | tf_op | source)
XLA Modules:
  0.0 267.1 jit_solution(5069158315128048152)
XLA Ops:
  6.5 0.5 broadcast.85
  7.1 8.4 %reduce.2 = bf16[8,65536]{1,0:T(8,128)(2,1)S(1)} reduce(bf16[8,1,65536]{2,1,0:T(2,128)(2,1)} %bitcast.35, bf16[]{:T(256)} %broadcast.85), dimensions={1}, to_apply=%bitcast.28.reduce_sub_computation | reduce | bytes 2097154
  15.4 0.0 copy-start.1
  15.4 0.0 copy-start.4
  15.4 0.0 copy-start.3
  15.4 0.0 copy-start.5
  15.5 1.9 reshape.167
  17.3 6.3 %all-to-all-start = ((bf16[8,2,32768]{2,1,0:T(2,128)(2,1)}), bf16[8,2,32768]{2,1,0:T(2,128)(2,1)}, u32[]{:S(2)}, u32[]{:S(2)}) async-start(bf16[8,2,32768]{2,1,0:T(2,128)(2,1)} %reshape.167), calls=%async_computation | async-start | bytes 2097152 | tf_op jit(solution)/shard_map/all_to_all | solution.py:42
  23.6 0.0 all-gather.2.cloned.1.call-start
  23.7 0.0 copy-done.1
  23.7 0.9 copy.14
  24.6 0.0 all-gather.2.cloned.1.call-update
  24.6 0.2 all-reduce.3.cloned.1.call-start
  24.8 0.0 copy-done.4
  24.9 0.0 copy-done.3
  24.9 0.0 copy-done.5
  24.9 30.4 %all-gather.2.cloned.1.call-done = bf16[1,512,1152]{1,2,0:T(8,128)(2,1)} async-done(((bf16[1,128,1152]{1,2,0:T(8,128)(2,1)}), bf16[1,512,1152]{1,2,0:T(8,128)(2,1)}) %all-gather.2.cloned.1.call-update) | async-done | bytes 1179664 | tf_op jit(solution)/shard_map/all_gather | solution.py:40
  55.4 3.8 %copy.15 = bf16[512,18,64]{2,1,0:T(8,128)(2,1)S(1)} copy(bf16[512,18,64]{0,2,1:T(8,128)(2,1)} %bitcast.36) | data formatting | bytes 2359296 | tf_op jit(solution)/shard_map/reshape | solution.py:46
  59.1 0.0 all-to-all-done
  59.2 5.8 %reshape.168 = bf16[8,1,65536]{2,1,0:T(2,128)(2,1)} reshape(bf16[8,2,32768]{2,1,0:T(2,128)(2,1)} %all-to-all-done) | data formatting | bytes 2097152
  64.9 8.6 %bitcast_reduce_fusion = bf16[8,65536]{1,0:T(8,128)(2,1)} fusion(bf16[8,1,65536]{2,1,0:T(2,128)(2,1)} %reshape.168), kind=kLoop, calls=%fused_computation.34 | loop fusion | bytes 2097152 | tf_op jit(solution)/shard_map/all_to_all | solution.py:42
  73.5 4.5 %reshape.136 = bf16[8,1024,64]{2,1,0:T(8,128)(2,1)} reshape(bf16[8,65536]{1,0:T(8,128)(2,1)} %bitcast_reduce_fusion) | data formatting | bytes 2097152 | tf_op jit(solution)/shard_map/reshape | solution.py:45
  78.0 4.3 %copy.13 = bf16[8,1024,64]{2,0,1:T(8,128)(2,1)} copy(bf16[8,1024,64]{2,1,0:T(8,128)(2,1)} %reshape.136) | data formatting | bytes 2097152 | tf_op jit(solution)/shard_map/reshape | solution.py:45
  82.3 3.6 %gather_fusion = bf16[512,8,64]{2,1,0:T(8,128)(2,1)} fusion(bf16[8,1024,64]{2,0,1:T(8,128)(2,1)} %copy.13, s32[1024]{0:T(1024)S(1)} %pad_clamp_fusion.1), kind=kCustom, calls=%fused_computation | custom fusion | bytes 1050624 | tf_op jit(solution)/shard_map/jit(_take)/gather | solution.py:8
  85.9 3.6 %convolution_bitcast_fusion = f32[18,8,512]{0,1,2:T(8,128)S(1)} fusion(bf16[512,18,64]{2,1,0:T(8,128)(2,1)S(1)} %copy.15, bf16[512,8,64]{2,1,0:T(8,128)(2,1)} %gather_fusion, pred[512]{0:T(512)(128)(4,1)S(1)} %compare_and_fusion), kind=kOutput, calls=%fused_computation.6 | convolution fusion | flops 9699328 | bytes 1999360 | tf_op jit(solution)/shard_map/bkg,kpg->kpb/dot_general | solution.py:9
  89.6 0.0 copy-start.2
  89.6 2.4 fusion
  92.0 0.0 all-reduce.3.cloned.1.call-update
  92.0 0.1 copy.20
  92.2 0.0 copy-done.2
  92.2 1.7 copy.19
  93.8 50.0 %all-reduce.3.cloned.1.call-done = f32[128,18,8]{0,1,2:T(8,128)} async-done(((f32[128,18,8]{0,1,2:T(8,128)}), f32[128,18,8]{0,1,2:T(8,128)}) %all-reduce.3.cloned.1.call-update) | async-done | bytes 73744 | tf_op jit(solution)/shard_map/psum | solution.py:50
  143.8 0.9 broadcast_multiply_fusion
  144.7 1.0 copy.18
  145.7 4.1 %fusion.3 = bf16[128,18,8]{1,2,0:T(8,128)(2,1)S(1)} fusion(f32[128,18,8]{1,2,0:T(8,128)} %copy.18, f32[128,18,18]{2,1,0:T(8,128)} %copy.19, f32[128,18]{1,0:T(8,128)S(1)} %copy.20), kind=kOutput, calls=%fused_computation.9 | convolution fusion | flops 4018176 | bytes 285696 | tf_op jit(solution)/shard_map/apq,aqb->apb/dot_general | solution.py:20
  149.9 0.1 concatenate.3
  149.9 2.4 gather_fusion.1
  152.3 3.7 %fusion.6 = f32[512,8,64]{2,1,0:T(8,128)} fusion(bf16[512,18,64]{2,1,0:T(8,128)(2,1)S(1)} %copy.15, bf16[512,18,8]{1,2,0:T(8,128)(2,1)} %gather_fusion.1, pred[512]{0:T(512)(128)(4,1)S(1)} %compare_and_fusion.1), kind=kOutput, calls=%fused_computation.12 | convolution fusion | flops 9510912 | bytes 2376192 | tf_op jit(solution)/shard_map/kpg,kpb->kbg/dot_general | solution.py:27
  156.0 2.2 broadcast_in_dim.29
  158.2 0.2 copy-done
  158.4 49.8 %scatter_fusion = f32[1024,8,64]{2,1,0:T(8,128)} fusion(f32[1024,8,64]{2,1,0:T(8,128)} %broadcast_in_dim.29, s32[512]{0:T(512)S(1)} %bitcast.40, f32[512,8,64]{2,1,0:T(8,128)S(1)} %copy-done), kind=kCustom, calls=%fused_computation.2 | custom fusion | flops 262144 | bytes 3147776 | tf_op jit(solution)/shard_map/scatter-add | solution.py:28
  208.3 2.4 convert_bitcast_fusion
  210.7 1.7 copy.22
  212.3 5.1 %convert_element_type.36 = bf16[8,1,65536]{2,1,0:T(2,128)(2,1)S(1)} reshape(bf16[8,1024,64]{2,1,0:T(8,128)(2,1)} %copy.22) | data formatting | bytes 2097152 | tf_op jit(solution)/shard_map/convert_element_type | solution.py:30
  217.4 7.0 %reduce.3 = bf16[8,65536]{1,0:T(8,128)(2,1)S(1)} reduce(bf16[8,1,65536]{2,1,0:T(2,128)(2,1)S(1)} %convert_element_type.36, bf16[]{:T(256)} %broadcast.85), dimensions={1}, to_apply=%convert_element_type.36.reduce_sub_computation | reduce | bytes 2097154 | tf_op jit(solution)/shard_map/convert_element_type | solution.py:30
  224.4 0.9 reshape.169
  225.3 31.6 %all_to_all.26 = bf16[8,2,32768]{2,1,0:T(2,128)(2,1)S(1)} all-to-all(bf16[8,2,32768]{2,1,0:T(2,128)(2,1)S(1)} %reshape.169), channel_id=1, replica_groups=mesh['band'=4,'slab'=8] {'slab'}, dimensions={0} | all-to-all | bytes 2097152 | tf_op jit(solution)/shard_map/all_to_all | solution.py:53
  256.9 3.4 %reshape.170 = bf16[8,1,65536]{2,1,0:T(2,128)(2,1)} reshape(bf16[8,2,32768]{2,1,0:T(2,128)(2,1)S(1)} %all_to_all.26) | data formatting | bytes 2097152
  (8 shorter events, 0.0 us)
Async XLA Ops:
  15.4 8.3 %copy-start.1 = (bf16[1,128,1152]{2,1,0:T(8,128)(2,1)S(1)}, bf16[1,128,1152]{2,1,0:T(8,128)(2,1)}, u32[]{:S(2)}) copy-start(bf16[1,128,1152]{2,1,0:T(8,128)(2,1)} %param.7) | copy-start | bytes 884740
  15.4 9.4 %copy-start.4 = (s32[1,512]{1,0:T(1,128)S(1)}, s32[1,512]{1,0:T(1,128)}, u32[]{:S(2)}) copy-start(s32[1,512]{1,0:T(1,128)} %param.9) | copy-start | bytes 6148
  15.4 9.4 %copy-start.3 = (s32[1,512]{1,0:T(1,128)S(1)}, s32[1,512]{1,0:T(1,128)}, u32[]{:S(2)}) copy-start(s32[1,512]{1,0:T(1,128)} %param.8) | copy-start | bytes 6148
  15.4 9.5 %copy-start.5 = (s32[128]{0:T(128)S(1)}, s32[128]{0:T(128)}, u32[]{:S(2)}) copy-start(s32[128]{0:T(128)} %param.10) | copy-start | bytes 1540
  17.3 41.8 %all-to-all-start = ((bf16[8,2,32768]{2,1,0:T(2,128)(2,1)}), bf16[8,2,32768]{2,1,0:T(2,128)(2,1)}, u32[]{:S(2)}, u32[]{:S(2)}) async-start(bf16[8,2,32768]{2,1,0:T(2,128)(2,1)} %reshape.167), calls=%async_computation | async-start | bytes 2097152 | tf_op jit(solution)/shard_map/all_to_all | solution.py:42
  23.6 31.7 %all-gather.2.cloned.1.call-start = ((), (), s32[]{:S(2)}) async-start(), calls=%async_computation.2 | async-start | bytes 1474560 | tf_op jit(solution)/shard_map/all_gather | solution.py:40
  24.6 119.2 %all-reduce.3.cloned.1.call-start = ((), (), s32[]{:S(2)}) async-start(), calls=%async_computation.3 | async-start | bytes 196608 | tf_op jit(solution)/shard_map/psum | solution.py:50
  89.6 2.6 copy-start.2
  156.0 2.4 copy-start
Sparse Core Ops, SparseCore 0:
  26.3 29.0 all-gather.1
  92.2 51.6 all-reduce.2
where the time goes:
time: 269 us; the launch traced here: 267 us
  waiting for transfers between devices  80.5 us (30%)
  other arithmetic  68.5 us (25%)
  local copies, waits for them, and re-layouts  52.5 us (20%)
  blocking collectives  31.6 us (12%)
  matrix products  13.9 us (5%)
  between operations  13.6 us (5%)
  starting transfers between devices  6.58 us (2%)
    psum x1, waiting for transfers between devices, body(): coef_total = lax.psum(coef_part, 'slab')  50 us
    scatter-add x1, other arithmetic, back_project(): summed = jax.ops.segment_sum(products, block_ids, num_segments=block_total)  49.8 us
    all_to_all x1, blocking collectives, body(): lax.all_to_all(slab_applied, 'slab', split_axis=0, concat_axis=1, tiled=T...  31.6 us
    all_gather x1, waiting for transfers between devices, body(): slab_tables = lax.all_gather(beta, 'band', axis=1, tiled=True)  30.4 us
    unnamed x19, local copies, waits for them, and re-layouts  15.3 us
    convert_element_type x2, other arithmetic, back_project(): return summed.transpose(1, 0, 2).reshape(band_rows, -1).astype(jnp.bfloat16)  9.4 us
    reshape x2, local copies, waits for them, and re-layouts, body(): grid_blocks = slab_rows.reshape(group_rows, block_local, block_size)  8.77 us
    all_to_all x1, local copies, waits for them, and re-layouts, body(): lax.all_to_all(psi, 'slab', split_axis=1, concat_axis=0, tiled=True)  8.6 us
  transfers between devices with their start and end apart: 3, of which 2 were waited for; matrix products, arithmetic and copies ran while one was open for 2% of the time, Pallas kernels for 0%

commit v1 on v0

v1 whole, which is shorter than its diff:
```python
import functools

import jax
import jax.numpy as jnp
from jax import lax
from jax.experimental import pallas as pl
from jax.experimental.pallas import tpu as pltpu
from jax.sharding import PartitionSpec as P

CORES = 2
LANES = 128
GROUP = 16
F32 = jnp.float32
BF16 = jnp.bfloat16
VMEM_SPEC = pl.BlockSpec(memory_space=pltpu.VMEM)
SMEM_SPEC = pl.BlockSpec(memory_space=pltpu.SMEM)
PARAMS = pltpu.CompilerParams(vmem_limit_bytes=40 * 1024 * 1024)


def dot(a, b, contract=((1,), (0,))):
    return lax.dot_general(a, b, (contract, ((), ())), preferred_element_type=F32)


def two_terms(x):
    high = x.astype(BF16)
    return high, (x - high.astype(F32)).astype(BF16)


def iota(shape, axis):
    return lax.broadcasted_iota(jnp.int32, shape, axis)


def column(row):
    return jnp.transpose(jnp.broadcast_to(row, (LANES, LANES)))


def rows_kernel(place_ref, psi_ref, *out_refs):
    step = pl.program_id(0)
    for index, out_ref in enumerate(out_refs):

        @pl.when(step == index)
        def _(out_ref=out_ref):
            def move(i, carry):
                part = psi_ref[0:1, pl.ds(pl.multiple_of(i * 2048, 2048), 2048)]
                out_ref[pl.ds(pl.multiple_of(i * 16, 16), 16), :] = part.reshape(16, LANES)
                return carry

            lax.fori_loop(0, out_ref.shape[0] // 16, move, 0, unroll=8)


def to_rows(psi, chip, chips):
    points = psi.shape[1] // chips
    rows = points // LANES
    return pl.pallas_call(
        rows_kernel,
        grid_spec=pltpu.PrefetchScalarGridSpec(
            num_scalar_prefetch=1,
            grid=(chips,),
            in_specs=[pl.BlockSpec((1, points), lambda i, chip: (0, lax.rem(chip[0] + i, chips)))],
            out_specs=[pl.BlockSpec((rows, LANES), lambda i, chip: (0, 0))] * chips,
        ),
        out_shape=[jax.ShapeDtypeStruct((rows, LANES), BF16)] * chips,
        compiler_params=PARAMS,
    )(chip.reshape(1), psi)


def project_kernel(bands, projectors, padded, core_ref, atom_refs, block_refs, beta_refs, psi_refs, coef_ref, prods):
    slots = atom_refs[0].shape[1]
    slab_rows = psi_refs[0].shape[0] // CORES
    pair_count = projectors // 2
    wide = 2 * bands * GROUP
    lane = iota((LANES, LANES), 1)
    low = lane < LANES // 2
    source = iota((pair_count * wide, bands * padded), 0) // GROUP
    target = iota((pair_count * wide, bands * padded), 1)
    gather_lanes = (target == lax.rem(source, bands) * padded + source // bands).astype(BF16)
    diagonal = lax.rem(iota((GROUP, wide), 0), GROUP) == lax.rem(iota((GROUP, wide), 1), GROUP)
    coef_ref[...] = jnp.zeros_like(coef_ref)
    for slab in range(CORES):
        place = core_ref[0] if slab == 0 else CORES - 1 - core_ref[0]
        first_row = pl.multiple_of(place * slab_rows, slab_rows)

        def chunk(i, carry, slab=slab, first_row=first_row):
            at = pl.ds(pl.multiple_of(i * LANES, LANES), LANES)
            atoms = atom_refs[slab][0:1, at]
            blocks = column(block_refs[slab][0:1, at])
            wanted = jnp.right_shift(blocks, 1)
            odd = jnp.bitwise_and(blocks, 1) == 1
            hits = jnp.concatenate(
                [(wanted - t * LANES == lane).astype(BF16) for t in range(slab_rows // LANES)], axis=1
            )
            lows, highs = [], []
            for psi_ref in psi_refs:
                picked = dot(hits, psi_ref[pl.ds(first_row, slab_rows), :])
                turned = pltpu.roll(picked, LANES // 2, 1)
                both = jnp.where(low == odd, turned, picked)
                lows.append(jnp.where(low, both, 0.0).astype(BF16))
                highs.append(jnp.where(low, 0.0, both).astype(BF16))
            for group in range(LANES // GROUP):
                own = slice(group * GROUP, (group + 1) * GROUP)
                rows = pl.ds(pl.multiple_of(i * LANES + group * GROUP, GROUP), GROUP)
                values = jnp.concatenate([part[own] for part in lows + highs], axis=0)
                tables = jnp.concatenate(
                    [beta_refs[slab][rows, t * LANES : (t + 1) * LANES] for t in range(pair_count)], axis=0
                )
                crossed = dot(tables, values, ((1,), (1,)))
                for t in range(pair_count):
                    kept = jnp.where(diagonal, crossed[t * GROUP : (t + 1) * GROUP], 0.0)
                    prods[own, t * wide : (t + 1) * wide] = kept
            high, rest = two_terms(prods[...])
            slot_coef = dot(high, gather_lanes) + dot(rest, gather_lanes)
            high, rest = two_terms(slot_coef)
            of_atom = (column(atoms) == lane).astype(BF16)
            summed = dot(high, of_atom, ((0,), (0,))) + dot(rest, of_atom, ((0,), (0,)))
            coef_ref[...] += summed
            return carry

        lax.fori_loop(0, slots // LANES, chunk, 0)


def project(core, atoms, blocks, tables, values, projectors, padded, atom_total):
    bands = len(values)
    pair_count = projectors // 2

    def kernel(core_ref, a0, a1, k0, k1, b0, b1, *rest):
        project_kernel(
            bands, projectors, padded, core_ref, (a0, a1), (k0, k1), (b0, b1), rest[:bands], rest[bands], rest[bands + 1]
        )

    return pl.pallas_call(
        kernel,
        in_specs=[SMEM_SPEC] + [VMEM_SPEC] * (6 + bands),
        out_specs=VMEM_SPEC,
        out_shape=jax.ShapeDtypeStruct((bands * padded, atom_total), F32),
        scratch_shapes=[pltpu.VMEM((LANES, pair_count * 2 * bands * GROUP), F32)],
        compiler_params=PARAMS,
    )(core.reshape(1), *atoms, *blocks, *tables, *values)


def apply_kernel(bands, projectors, padded, atom_refs, beta_refs, count_ref, strength_ref, coef_refs, out_refs, wide_refs):
    slots = atom_refs[0].shape[1]
    pair_count = projectors // 2
    width = projectors * LANES // 2
    atom_total = strength_ref.shape[2]
    lane = iota((LANES, LANES), 1)
    low = iota((LANES // 2, LANES), 1) < LANES // 2
    valid = (iota((projectors, atom_total), 0) < count_ref[...]).astype(F32)
    spread = (iota((projectors, width), 0) == iota((projectors, width), 1) // (LANES // 2)).astype(BF16)
    for band in range(bands):
        total = coef_refs[0][band * padded : band * padded + projectors, :]
        for away in range(1, bands):
            first = (band - away) % bands * padded
            total = total + coef_refs[away][first : first + projectors, :]
        total = total * valid
        coupled = strength_ref[:, 0, :] * total[0:1]
        for q in range(1, projectors):
            coupled = coupled + strength_ref[:, q, :] * total[q : q + 1]
        scaled = (coupled * valid).astype(BF16)
        wide_refs[band][...] = dot(scaled, spread, ((0,), (0,))).astype(BF16)
    for slab in range(CORES):

        def chunk(i, carry, slab=slab):
            at = pl.ds(pl.multiple_of(i * LANES, LANES), LANES)
            of_atom = (column(atom_refs[slab][0:1, at]) == lane).astype(BF16)
            for band in range(bands):
                total = None
                for t in range(pair_count):
                    tile = slice(t * LANES, (t + 1) * LANES)
                    term = dot(of_atom, wide_refs[band][:, tile]) * beta_refs[slab][at, tile].astype(F32)
                    total = term if total is None else total + term
                total = total + pltpu.roll(total, LANES // 2, 1)
                packed = jnp.where(low, total[: LANES // 2], total[LANES // 2 :])
                first = slab * slots // 2 + i * (LANES // 2)
                out_refs[band][pl.ds(pl.multiple_of(first, LANES // 2), LANES // 2), :] = packed.astype(BF16)
            return carry

        lax.fori_loop(0, slots // LANES, chunk, 0)


def back_project(atoms, tables, count, strength, coefs, projectors, padded):
    bands = len(coefs)
    slots = atoms[0].shape[1]
    atom_total = strength.shape[2]

    def kernel(a0, a1, b0, b1, count_ref, strength_ref, *rest):
        apply_kernel(
            bands, projectors, padded, (a0, a1), (b0, b1), count_ref, strength_ref,
            rest[:bands], rest[bands : 2 * bands], rest[2 * bands :],
        )

    return pl.pallas_call(
        kernel,
        in_specs=[VMEM_SPEC] * (6 + bands),
        out_specs=[VMEM_SPEC] * bands,
        out_shape=[jax.ShapeDtypeStruct((slots, LANES), BF16)] * bands,
        scratch_shapes=[pltpu.VMEM((atom_total, projectors * LANES // 2), BF16)] * bands,
        compiler_params=PARAMS,
    )(*atoms, *tables, count, strength, *coefs)


def place_kernel(chips, place_ref, *refs):
    block_refs, value_refs, out_ref, total = refs[: CORES * chips], refs[CORES * chips : -2], refs[-2], refs[-1]
    step = pl.program_id(0)
    slots = block_refs[0].shape[1]
    rows = out_ref.shape[1] // LANES // CORES
    low = iota((LANES // 2, LANES), 1) < LANES // 2
    for chip in range(chips):

        @pl.when(step == chip)
        def _(chip=chip):
            for slab in range(CORES):
                place = place_ref[1] if slab == 0 else CORES - 1 - place_ref[1]
                block_ref = block_refs[chip * CORES + slab]
                parts = []
                for i in range(slots // LANES):
                    odd = jnp.bitwise_and(column(block_ref[0:1, i * LANES : (i + 1) * LANES]), 1) == 1
                    first = slab * slots // 2 + i * (LANES // 2)
                    value = value_refs[chip][first : first + LANES // 2, :].astype(F32)
                    turned = pltpu.roll(value, LANES // 2, 1)
                    odd_a, odd_b = odd[: LANES // 2], odd[LANES // 2 :]
                    part_a = jnp.where(odd_a, turned, value)
                    part_b = jnp.where(odd_b, value, turned)
                    parts.append(jnp.where(low != odd_a, part_a, 0.0).astype(BF16))
                    parts.append(jnp.where(low != odd_b, part_b, 0.0).astype(BF16))
                values = jnp.concatenate(parts, axis=0)
                wanted = jnp.right_shift(block_ref[...], 1)
                for t in range(rows // LANES):
                    hits = (iota((LANES, slots), 0) + t * LANES == wanted).astype(BF16)
                    total[t * LANES : (t + 1) * LANES, :] = dot(hits, values).astype(BF16)
                start = place * rows * LANES

                def move(i, carry):
                    part = total[pl.ds(pl.multiple_of(i * 16, 16), 16), :]
                    out_ref[0:1, pl.ds(pl.multiple_of(start + i * 2048, 2048), 2048)] = part.reshape(1, 2048)
                    return carry

                lax.fori_loop(0, rows // 16, move, 0, unroll=8)


def place_rows(place, blocks, values, points):
    chips = len(values)
    share = points // chips
    whole = lambda i, place: (0, 0)
    return pl.pallas_call(
        functools.partial(place_kernel, chips),
        grid_spec=pltpu.PrefetchScalarGridSpec(
            num_scalar_prefetch=1,
            grid=(chips,),
            in_specs=[pl.BlockSpec(x.shape, whole) for x in (*blocks, *values)],
            out_specs=pl.BlockSpec((1, share), lambda i, place: (0, lax.rem(place[0] + i, chips))),
            scratch_shapes=[pltpu.VMEM((share // LANES // CORES, LANES), BF16)],
        ),
        out_shape=jax.ShapeDtypeStruct((1, points), BF16),
        compiler_params=PARAMS,
    )(place, *blocks, *values)


def body(slabs, psi, beta, pair_atom, pair_block, proj_count, strength):
    chips = slabs // CORES
    atom_total, projectors = strength.shape[:2]
    padded = -(-projectors // 8) * 8
    position = lax.axis_index("slab").astype(jnp.int32)
    chip, core = position // CORES, lax.rem(position, CORES)

    def turn(x, chips_on):
        return lax.ppermute(x, "slab", [(i, (i + CORES * chips_on) % slabs) for i in range(slabs)])

    def swap(x):
        return lax.ppermute(x, "slab", [(i, i ^ 1) for i in range(slabs)])

    rows = to_rows(psi, chip, chips)
    values = [rows[0]] + [turn(rows[away], away) for away in range(1, chips)]
    own_tables = lax.all_gather(beta[0], "band", axis=0, tiled=True)
    ids = swap(jnp.concatenate([pair_atom, pair_block], axis=0))
    atoms = (pair_atom, ids[0:1])
    blocks = (pair_block, ids[1:2])
    tables = (own_tables, swap(own_tables))
    coef = project(core, atoms, blocks, tables, values, projectors, padded, atom_total)
    coefs = [coef] + [turn(coef, away) for away in range(1, chips)]
    results = back_project(
        atoms, tables, proj_count.reshape(1, atom_total), strength.transpose(1, 2, 0), coefs, projectors, padded
    )
    results = [results[0]] + [turn(results[away], -away) for away in range(1, chips)]
    both = jnp.concatenate(blocks, axis=0)
    taken = [both] + [turn(both, -away) for away in range(1, chips)]
    block_rows = [x[s : s + 1] for x in taken for s in range(CORES)]
    return place_rows(jnp.stack([chip, core]), block_rows, results, psi.shape[1])


def solution(mesh):
    placed = (
        P(("band", "slab"), None),
        P("slab", "band", None),
        P("slab", None),
        P("slab", None),
        P(),
        P(),
    )
    return jax.shard_map(
        functools.partial(body, mesh.shape["slab"]),
        mesh=mesh,
        in_specs=placed,
        out_specs=P(("band", "slab"), None),
        check_vma=False,
    )
```

time: 269 us -> 120 us (0.45)
  other arithmetic: 68.5 us -> 0.89 us
  local copies, waits for them, and re-layouts: 52.5 us -> 1.63 us
  blocking collectives: 31.6 us -> 0 us
  Pallas kernels: 0 us -> 22.3 us
  waiting for transfers between devices: 80.5 us -> 62.3 us
  matrix products: 13.9 us -> 0 us
  starting transfers between devices: 6.58 us -> 19.2 us
    psum x1 -> x0, waiting for transfers between devices: 50 us -> none  [body(): coef_total = lax.psum(coef_part, 'slab')]
    scatter-add x1 -> x0, other arithmetic: 49.8 us -> none  [back_project(): summed = jax.ops.segment_sum(products, block_ids, num_segments=block_total)]
    all_to_all x1 -> x0, blocking collectives: 31.6 us -> none  [body(): lax.all_to_all(slab_applied, 'slab', split_axis=0, concat_axis=1, tiled=T...]
    ppermute x0 -> x14, waiting for transfers between devices: none -> 29.2 us  [the longest x12 29.2 us: turn(): lax.ppermute(x, 'slab', [(i, (i + CORES * chips_on) % slabs) for i in ran...]
    pallas_call x0 -> x4, Pallas kernels: none -> 22.3 us  [the longest x1 9.43 us: project(): pl.pallas_call(kernel, in_specs=[SMEM_SPEC] + [VMEM_SPEC] * (6 + bands),...]
    ppermute x0 -> x14, starting transfers between devices: none -> 19.2 us  [the longest x12 18.8 us: turn(): lax.ppermute(x, 'slab', [(i, (i + CORES * chips_on) % slabs) for i in ran...]
    dot_general x4 -> x0, matrix products: 13.9 us -> none  [the longest x1 4.12 us: apply_strength(): jnp.einsum('apq,aqb->apb', strength, masked, precision=lax.Precision.HIGH...]
    unnamed x19 -> x12, local copies, waits for them, and re-layouts: 15.3 us -> 1.61 us
  transfers between devices with their start and end apart: 3 -> 15, of which waited for: 2 -> 7; matrix products, arithmetic and copies ran while one was open for 2% -> 1% of each run, Pallas kernels for 0% -> 13%
where the time goes in v1:
time: 120 us
  waiting for transfers between devices  62.3 us (52%)
  Pallas kernels  22.3 us (19%)
  starting transfers between devices  19.2 us (16%)
  between operations  13.5 us (11%)
  local copies, waits for them, and re-layouts  1.63 us (1%)
    all_gather x1, waiting for transfers between devices, body(): own_tables = lax.all_gather(beta[0], 'band', axis=0, tiled=True)  32.4 us
    ppermute x12, waiting for transfers between devices, turn(): lax.ppermute(x, 'slab', [(i, (i + CORES * chips_on) % slabs) for i in ran...  29.2 us
    ppermute x12, starting transfers between devices, turn(): lax.ppermute(x, 'slab', [(i, (i + CORES * chips_on) % slabs) for i in ran...  18.8 us
    pallas_call x1, Pallas kernels, project(): pl.pallas_call(kernel, in_specs=[SMEM_SPEC] + [VMEM_SPEC] * (6 + bands),...  9.43 us
    pallas_call x1, Pallas kernels, place_rows(): pl.pallas_call(functools.partial(place_kernel, chips), grid_spec=pltpu.Pr...  6.45 us
    pallas_call x1, Pallas kernels, back_project(): pl.pallas_call(kernel, in_specs=[VMEM_SPEC] * (6 + bands), out_specs=[VME...  5.67 us
  transfers between devices with their start and end apart: 15, of which 7 were waited for; matrix products, arithmetic and copies ran while one was open for 1% of the time, Pallas kernels for 13%

profile of v1, /device:TPU:0, one launch (start us, length us, event | category | flops | bytes accessed | tf_op | source)
XLA Modules:
  0.0 119.9 jit_solution(4554223660804193657)
XLA Ops:
  6.5 0.0 copy-start.4
  6.5 0.0 copy-start.3
  6.5 0.0 all-gather.3.cloned.1.call-start
  6.5 0.7 all-gather.3.cloned.1.call-update
  7.3 32.4 %all-gather.3.cloned.1.call-done = bf16[1,512,1152]{2,1,0:T(8,128)(2,1)} async-done(((bf16[1,128,1152]{2,1,0:T(8,128)(2,1)}), bf16[1,512,1152]{2,1,0:T(8,128)(2,1)}) %all-gather.3.cloned.1.call-update) | async-done | bytes 1179664 | tf_op jit(solution)/shard_map/all_gather | solution.py:273
  39.7 0.0 copy-start
  39.7 0.0 collective-permute-start.4
  39.7 0.8 pad_add_fusion
  40.5 0.4 collective-permute-start
  40.9 1.6 %copy-done.1 = bf16[1,524288]{1,0:T(2,128)(2,1)S(1)} copy-done((bf16[1,524288]{1,0:T(2,128)(2,1)S(1)}, bf16[1,524288]{1,0:T(2,128)(2,1)}, u32[]{:S(2)}) %copy-start.1) | copy-done | bytes 1048600
  42.5 0.7 shard_map.64
  43.2 0.0 copy-start.2
  43.2 0.0 copy-start.5
  43.2 1.5 %collective-permute-start.5 = (bf16[1024,128]{1,0:T(8,128)(2,1)S(1)}, bf16[1024,128]{1,0:T(8,128)(2,1)S(1)}, u32[]{:S(2)}, u32[]{:S(2)}) collective-permute-start(bf16[1024,128]{1,0:T(8,128)(2,1)S(1)} %get-tuple-element.14), channel_id=1, source_target_pairs={{0,2},{1,3},{2,4},{3,5},{4,6},{5,7},{6,0},{7,1},{8,10},{9,11},{10,... | collective-permute-start | bytes 786440 | tf_op jit(solution)/shard_map/ppermute | solution.py:266
  44.8 2.4 %collective-permute-start.6 = (bf16[1024,128]{1,0:T(8,128)(2,1)S(1)}, bf16[1024,128]{1,0:T(8,128)(2,1)S(1)}, u32[]{:S(2)}, u32[]{:S(2)}) collective-permute-start(bf16[1024,128]{1,0:T(8,128)(2,1)S(1)} %get-tuple-element.15), channel_id=1, source_target_pairs={{0,4},{1,5},{2,6},{3,7},{4,0},{5,1},{6,2},{7,3},{8,12},{9,13},{10,... | collective-permute-start | bytes 786440 | tf_op jit(solution)/shard_map/ppermute | solution.py:266
  47.2 1.4 %collective-permute-start.7 = (bf16[1024,128]{1,0:T(8,128)(2,1)S(1)}, bf16[1024,128]{1,0:T(8,128)(2,1)S(1)}, u32[]{:S(2)}, u32[]{:S(2)}) collective-permute-start(bf16[1024,128]{1,0:T(8,128)(2,1)S(1)} %get-tuple-element.16), channel_id=1, source_target_pairs={{0,6},{1,7},{2,0},{3,1},{4,2},{5,3},{6,4},{7,5},{8,14},{9,15},{10,... | collective-permute-start | bytes 786440 | tf_op jit(solution)/shard_map/ppermute | solution.py:266
  48.6 0.0 collective-permute-done
  48.6 0.0 copy-done.3
  48.7 0.6 collective-permute-start.3
  49.3 0.1 pad_add_fusion.2.place_ref
  49.4 15.5 %collective-permute-done.3 = s32[2,512]{1,0:T(2,128)S(1)} collective-permute-done((s32[2,512]{1,0:T(2,128)S(1)}, s32[2,512]{1,0:T(2,128)S(1)}, u32[]{:S(2)}, u32[]{:S(2)}) %collective-permute-start.3) | collective-permute-done | bytes 4128 | tf_op jit(solution)/shard_map/ppermute | solution.py:266
  64.9 6.1 %collective-permute-start.2 = (s32[2,512]{1,0:T(2,128)S(1)}, s32[2,512]{1,0:T(2,128)S(1)}, u32[]{:S(2)}, u32[]{:S(2)}) collective-permute-start(s32[2,512]{1,0:T(2,128)S(1)} %pad_add_fusion.1), channel_id=1, source_target_pairs={{0,4},{1,5},{2,6},{3,7},{4,0},{5,1},{6,2},{7,3},{8,12},{9,13},{10,... | collective-permute-start | bytes 12296 | tf_op jit(solution)/shard_map/ppermute | solution.py:266
  71.0 0.0 collective-permute-done.5.rest_1_
  71.0 0.5 collective-permute-start.1
  71.5 0.0 collective-permute-done.6.rest_2_
  71.5 0.0 collective-permute-done.7.rest_3_
  71.5 0.0 collective-permute-done.4.b1
  71.5 0.0 copy-done.4
  71.5 0.0 copy-done
  71.5 9.4 %shard_map.65.rest_0_ = f32[96,128]{1,0:T(8,128)S(1)} custom-call(s32[1]{0:T(128)} %bitcast.1.core_ref, s32[1,512]{1,0:T(1,128)S(1)} %copy-done.4, s32[1,512]{1,0:T(1,128)S(1)} %get-tuple-element.21.a1, s32[1,512]{1,0:T(1,128)S(1)} %copy-done.3, s32[1,512]{1,0:T(1,128)S(1)} %get-tuple-element.22.k1.refs_1_, bf16[512,1152]{1,0:T(8,128)(2,1)S(1)} %bitcast.6, ...), custom_call_target="tpu_custom_call" | custom-call | tf_op jit(solution)/shard_map/pallas_call | solution.py:130
  81.0 1.1 collective-permute-start.10
  82.1 1.0 collective-permute-start.8
  83.1 1.0 collective-permute-start.9
  84.1 0.0 collective-permute-done.2
  84.1 1.8 %collective-permute-done.10.rest_3_ = f32[96,128]{1,0:T(8,128)S(1)} collective-permute-done((f32[96,128]{1,0:T(8,128)S(1)}, f32[96,128]{1,0:T(8,128)S(1)}, u32[]{:S(2)}, u32[]{:S(2)}) %collective-permute-start.10) | collective-permute-done | bytes 49184 | tf_op jit(solution)/shard_map/ppermute | solution.py:266
  85.9 2.1 %collective-permute-done.8.rest_1_ = f32[96,128]{1,0:T(8,128)S(1)} collective-permute-done((f32[96,128]{1,0:T(8,128)S(1)}, f32[96,128]{1,0:T(8,128)S(1)}, u32[]{:S(2)}, u32[]{:S(2)}) %collective-permute-start.8) | collective-permute-done | bytes 49184 | tf_op jit(solution)/shard_map/ppermute | solution.py:266
  88.0 0.5 collective-permute-done.9.rest_2_
  88.5 0.0 copy-done.2
  88.5 0.0 copy-done.5
  88.5 5.7 %shard_map.66 = (bf16[512,128]{1,0:T(8,128)(2,1)S(1)}, bf16[512,128]{1,0:T(8,128)(2,1)S(1)}, bf16[512,128]{1,0:T(8,128)(2,1)S(1)}, bf16[512,128]{1,0:T(8,128)(2,1)S(1)}) custom-call(s32[1,512]{1,0:T(1,128)S(1)} %copy-done.4, s32[1,512]{1,0:T(1,128)S(1)} %get-tuple-element.21.a1, bf16[512,1152]{1,0:T(8,128)(2,1)S(1)} %bitcast.7, ...), custom_call_target="tpu_custom_call" | custom-call | tf_op jit(solution)/shard_map/pallas_call | solution.py:191
  94.2 2.4 %collective-permute-start.11 = (bf16[512,128]{1,0:T(8,128)(2,1)S(1)}, bf16[512,128]{1,0:T(8,128)(2,1)S(1)}, u32[]{:S(2)}, u32[]{:S(2)}) collective-permute-start(bf16[512,128]{1,0:T(8,128)(2,1)S(1)} %get-tuple-element.18), channel_id=1, source_target_pairs={{0,6},{1,7},{2,0},{3,1},{4,2},{5,3},{6,4},{7,5},{8,14},{9,15},{10,... | collective-permute-start | bytes 393224 | tf_op jit(solution)/shard_map/ppermute | solution.py:266
  96.6 0.2 collective-permute-start.12
  96.8 0.4 collective-permute-start.13
  97.2 0.0 collective-permute-done.1
  97.2 4.1 %collective-permute-done.11.refs_9_ = bf16[512,128]{1,0:T(8,128)(2,1)S(1)} collective-permute-done((bf16[512,128]{1,0:T(8,128)(2,1)S(1)}, bf16[512,128]{1,0:T(8,128)(2,1)S(1)}, u32[]{:S(2)}, u32[]{:S(2)}) %collective-permute-start.11) | collective-permute-done | bytes 131104 | tf_op jit(solution)/shard_map/ppermute | solution.py:266
  101.3 5.2 %collective-permute-done.12.refs_10_ = bf16[512,128]{1,0:T(8,128)(2,1)S(1)} collective-permute-done((bf16[512,128]{1,0:T(8,128)(2,1)S(1)}, bf16[512,128]{1,0:T(8,128)(2,1)S(1)}, u32[]{:S(2)}, u32[]{:S(2)}) %collective-permute-start.12) | collective-permute-done | bytes 131104 | tf_op jit(solution)/shard_map/ppermute | solution.py:266
  106.6 0.0 collective-permute-done.13.refs_11_
  106.6 6.5 %shard_map.67 = bf16[1,524288]{1,0:T(2,128)(2,1)} custom-call(s32[2]{0:T(128)S(1)} %pad_add_fusion.2.place_ref, s32[1,512]{1,0:T(1,128)S(1)} %copy-done.3, s32[1,512]{1,0:T(1,128)S(1)} %get-tuple-element.22.k1.refs_1_, s32[1,512]{1,0:T(1,128)S(1)} %get-tuple-element.28.refs_2_, s32[1,512]{1,0:T(1,128)S(1)} %get-tuple-element.27.refs_3_, ...), custom_call_target="tpu_custom_call" | custom-call | tf_op jit(solution)/shard_map/pallas_call | solution.py:244
  (6 shorter events, 0.0 us)
Async XLA Ops:
  6.5 65.0 %copy-start.4 = (s32[1,512]{1,0:T(1,128)S(1)}, s32[1,512]{1,0:T(1,128)}, u32[]{:S(2)}) copy-start(s32[1,512]{1,0:T(1,128)} %a0.3) | copy-start | bytes 6148
  6.5 42.1 %copy-start.3 = (s32[1,512]{1,0:T(1,128)S(1)}, s32[1,512]{1,0:T(1,128)}, u32[]{:S(2)}) copy-start(s32[1,512]{1,0:T(1,128)} %refs_0_.1) | copy-start | bytes 6148
  6.5 33.1 %all-gather.3.cloned.1.call-start = ((), (), s32[]{:S(2)}) async-start(), calls=%async_computation | async-start | bytes 1474560 | tf_op jit(solution)/shard_map/all_gather | solution.py:273
  39.7 31.9 %copy-start = (bf16[1,512,1152]{2,1,0:T(8,128)(2,1)S(1)}, bf16[1,512,1152]{2,1,0:T(8,128)(2,1)}, u32[]{:S(2)}) copy-start(bf16[1,512,1152]{2,1,0:T(8,128)(2,1)} %all-gather.3.cloned.1.call-done) | copy-start | bytes 3538948
  39.7 31.9 %collective-permute-start.4 = (bf16[512,1152]{1,0:T(8,128)(2,1)}, bf16[512,1152]{1,0:T(8,128)(2,1)S(1)}, u32[]{:S(2)}, u32[]{:S(2)}) collective-permute-start(bf16[512,1152]{1,0:T(8,128)(2,1)} %bitcast.5), channel_id=1, source_target_pairs={{0,1},{1,0},{2,3},{3,2},{4,5},{5,4},{6,7},{7,6},{8,9},{9,8},{10,11... | collective-permute-start | bytes 3538952 | tf_op jit(solution)/shard_map/ppermute | solution.py:269
  40.5 8.2 %collective-permute-start = (s32[2,512]{1,0:T(2,128)S(1)}, s32[2,512]{1,0:T(2,128)S(1)}, u32[]{:S(2)}, u32[]{:S(2)}) collective-permute-start(s32[2,512]{1,0:T(2,128)S(1)} %pad_add_fusion), channel_id=1, source_target_pairs={{0,1},{1,0},{2,3},{3,2},{4,5},{5,4},{6,7},{7,6},{8,9},{9,8},{10,11... | collective-permute-start | bytes 12296 | tf_op jit(solution)/shard_map/ppermute | solution.py:269
  40.9 1.6 %copy-start.1 = (bf16[1,524288]{1,0:T(2,128)(2,1)S(1)}, bf16[1,524288]{1,0:T(2,128)(2,1)}, u32[]{:S(2)}) copy-start(bf16[1,524288]{1,0:T(2,128)(2,1)} %psi_ref.1) | copy-start | bytes 3145732
  43.2 45.3 %copy-start.2 = (f32[128,18,18]{0,2,1:T(8,128)S(1)}, f32[128,18,18]{0,2,1:T(8,128)}, u32[]{:S(2)}) copy-start(f32[128,18,18]{0,2,1:T(8,128)} %param.11) | copy-start | bytes 497668
  43.2 45.2 %copy-start.5 = (s32[128]{0:T(128)S(1)}, s32[128]{0:T(128)}, u32[]{:S(2)}) copy-start(s32[128]{0:T(128)} %param.10) | copy-start | bytes 1540
  43.2 27.8 %collective-permute-start.5 = (bf16[1024,128]{1,0:T(8,128)(2,1)S(1)}, bf16[1024,128]{1,0:T(8,128)(2,1)S(1)}, u32[]{:S(2)}, u32[]{:S(2)}) collective-permute-start(bf16[1024,128]{1,0:T(8,128)(2,1)S(1)} %get-tuple-element.14), channel_id=1, source_target_pairs={{0,2},{1,3},{2,4},{3,5},{4,6},{5,7},{6,0},{7,1},{8,10},{9,11},{10,... | collective-permute-start | bytes 786440 | tf_op jit(solution)/shard_map/ppermute | solution.py:266
  44.8 26.7 %collective-permute-start.6 = (bf16[1024,128]{1,0:T(8,128)(2,1)S(1)}, bf16[1024,128]{1,0:T(8,128)(2,1)S(1)}, u32[]{:S(2)}, u32[]{:S(2)}) collective-permute-start(bf16[1024,128]{1,0:T(8,128)(2,1)S(1)} %get-tuple-element.15), channel_id=1, source_target_pairs={{0,4},{1,5},{2,6},{3,7},{4,0},{5,1},{6,2},{7,3},{8,12},{9,13},{10,... | collective-permute-start | bytes 786440 | tf_op jit(solution)/shard_map/ppermute | solution.py:266
  47.2 24.3 %collective-permute-start.7 = (bf16[1024,128]{1,0:T(8,128)(2,1)S(1)}, bf16[1024,128]{1,0:T(8,128)(2,1)S(1)}, u32[]{:S(2)}, u32[]{:S(2)}) collective-permute-start(bf16[1024,128]{1,0:T(8,128)(2,1)S(1)} %get-tuple-element.16), channel_id=1, source_target_pairs={{0,6},{1,7},{2,0},{3,1},{4,2},{5,3},{6,4},{7,5},{8,14},{9,15},{10,... | collective-permute-start | bytes 786440 | tf_op jit(solution)/shard_map/ppermute | solution.py:266
  48.7 16.2 %collective-permute-start.3 = (s32[2,512]{1,0:T(2,128)S(1)}, s32[2,512]{1,0:T(2,128)S(1)}, u32[]{:S(2)}, u32[]{:S(2)}) collective-permute-start(s32[2,512]{1,0:T(2,128)S(1)} %pad_add_fusion.1), channel_id=1, source_target_pairs={{0,2},{1,3},{2,4},{3,5},{4,6},{5,7},{6,0},{7,1},{8,10},{9,11},{10,... | collective-permute-start | bytes 12296 | tf_op jit(solution)/shard_map/ppermute | solution.py:266
  64.9 19.2 %collective-permute-start.2 = (s32[2,512]{1,0:T(2,128)S(1)}, s32[2,512]{1,0:T(2,128)S(1)}, u32[]{:S(2)}, u32[]{:S(2)}) collective-permute-start(s32[2,512]{1,0:T(2,128)S(1)} %pad_add_fusion.1), channel_id=1, source_target_pairs={{0,4},{1,5},{2,6},{3,7},{4,0},{5,1},{6,2},{7,3},{8,12},{9,13},{10,... | collective-permute-start | bytes 12296 | tf_op jit(solution)/shard_map/ppermute | solution.py:266
  71.0 26.2 %collective-permute-start.1 = (s32[2,512]{1,0:T(2,128)S(1)}, s32[2,512]{1,0:T(2,128)S(1)}, u32[]{:S(2)}, u32[]{:S(2)}) collective-permute-start(s32[2,512]{1,0:T(2,128)S(1)} %pad_add_fusion.1), channel_id=1, source_target_pairs={{0,6},{1,7},{2,0},{3,1},{4,2},{5,3},{6,4},{7,5},{8,14},{9,15},{10,... | collective-permute-start | bytes 12296 | tf_op jit(solution)/shard_map/ppermute | solution.py:266
  81.0 4.9 %collective-permute-start.10 = (f32[96,128]{1,0:T(8,128)S(1)}, f32[96,128]{1,0:T(8,128)S(1)}, u32[]{:S(2)}, u32[]{:S(2)}) collective-permute-start(f32[96,128]{1,0:T(8,128)S(1)} %shard_map.65.rest_0_), channel_id=1, source_target_pairs={{0,6},{1,7},{2,0},{3,1},{4,2},{5,3},{6,4},{7,5},{8,14},{9,15},{10,... | collective-permute-start | bytes 147464 | tf_op jit(solution)/shard_map/ppermute | solution.py:266
  82.1 5.9 %collective-permute-start.8 = (f32[96,128]{1,0:T(8,128)S(1)}, f32[96,128]{1,0:T(8,128)S(1)}, u32[]{:S(2)}, u32[]{:S(2)}) collective-permute-start(f32[96,128]{1,0:T(8,128)S(1)} %shard_map.65.rest_0_), channel_id=1, source_target_pairs={{0,2},{1,3},{2,4},{3,5},{4,6},{5,7},{6,0},{7,1},{8,10},{9,11},{10,... | collective-permute-start | bytes 147464 | tf_op jit(solution)/shard_map/ppermute | solution.py:266
  83.1 5.4 %collective-permute-start.9 = (f32[96,128]{1,0:T(8,128)S(1)}, f32[96,128]{1,0:T(8,128)S(1)}, u32[]{:S(2)}, u32[]{:S(2)}) collective-permute-start(f32[96,128]{1,0:T(8,128)S(1)} %shard_map.65.rest_0_), channel_id=1, source_target_pairs={{0,4},{1,5},{2,6},{3,7},{4,0},{5,1},{6,2},{7,3},{8,12},{9,13},{10,... | collective-permute-start | bytes 147464 | tf_op jit(solution)/shard_map/ppermute | solution.py:266
  94.2 7.2 %collective-permute-start.11 = (bf16[512,128]{1,0:T(8,128)(2,1)S(1)}, bf16[512,128]{1,0:T(8,128)(2,1)S(1)}, u32[]{:S(2)}, u32[]{:S(2)}) collective-permute-start(bf16[512,128]{1,0:T(8,128)(2,1)S(1)} %get-tuple-element.18), channel_id=1, source_target_pairs={{0,6},{1,7},{2,0},{3,1},{4,2},{5,3},{6,4},{7,5},{8,14},{9,15},{10,... | collective-permute-start | bytes 393224 | tf_op jit(solution)/shard_map/ppermute | solution.py:266
  96.6 10.0 %collective-permute-start.12 = (bf16[512,128]{1,0:T(8,128)(2,1)S(1)}, bf16[512,128]{1,0:T(8,128)(2,1)S(1)}, u32[]{:S(2)}, u32[]{:S(2)}) collective-permute-start(bf16[512,128]{1,0:T(8,128)(2,1)S(1)} %get-tuple-element.19), channel_id=1, source_target_pairs={{0,4},{1,5},{2,6},{3,7},{4,0},{5,1},{6,2},{7,3},{8,12},{9,13},{10,... | collective-permute-start | bytes 393224 | tf_op jit(solution)/shard_map/ppermute | solution.py:266
  96.8 9.7 %collective-permute-start.13 = (bf16[512,128]{1,0:T(8,128)(2,1)S(1)}, bf16[512,128]{1,0:T(8,128)(2,1)S(1)}, u32[]{:S(2)}, u32[]{:S(2)}) collective-permute-start(bf16[512,128]{1,0:T(8,128)(2,1)S(1)} %get-tuple-element.20), channel_id=1, source_target_pairs={{0,2},{1,3},{2,4},{3,5},{4,6},{5,7},{6,0},{7,1},{8,10},{9,11},{10,... | collective-permute-start | bytes 393224 | tf_op jit(solution)/shard_map/ppermute | solution.py:266
Sparse Core Ops, SparseCore 0:
  9.2 30.4 all-gather.2

commit v2 on v1

v2 whole, which is shorter than its diff:
```python
import functools

import jax
import jax.numpy as jnp
from jax import lax
from jax.experimental import pallas as pl
from jax.experimental.pallas import tpu as pltpu
from jax.sharding import PartitionSpec as P

CORES = 2
LANES = 128
GROUP = 16
F32 = jnp.float32
BF16 = jnp.bfloat16
VMEM_SPEC = pl.BlockSpec(memory_space=pltpu.VMEM)
SMEM_SPEC = pl.BlockSpec(memory_space=pltpu.SMEM)
PARAMS = pltpu.CompilerParams(vmem_limit_bytes=40 * 1024 * 1024)


def dot(a, b, contract=((1,), (0,))):
    return lax.dot_general(a, b, (contract, ((), ())), preferred_element_type=F32)


def two_terms(x):
    high = x.astype(BF16)
    return high, (x - high.astype(F32)).astype(BF16)


def iota(shape, axis):
    return lax.broadcasted_iota(jnp.int32, shape, axis)


def ids_row(ref, place_ref, piece, share):
    if share == ref.shape[1]:
        return ref[...]
    first = jnp.bitwise_xor(place_ref[1], piece) * share
    return ref[0:1, pl.ds(pl.multiple_of(first, share), share)]


def ids_column(ref, place_ref, piece, share):
    row = ids_row(ref, place_ref, piece, share)
    parts = [
        jnp.transpose(jnp.broadcast_to(row[:, i * LANES : (i + 1) * LANES], (LANES, LANES)))
        for i in range(share // LANES)
    ]
    return jnp.concatenate(parts, axis=0)


def rows_kernel(place_ref, psi_ref, *out_refs):
    step = pl.program_id(0)
    for index, out_ref in enumerate(out_refs):

        @pl.when(step == index)
        def _(out_ref=out_ref):
            def move(i, carry):
                part = psi_ref[0:1, pl.ds(pl.multiple_of(i * 2048, 2048), 2048)]
                out_ref[pl.ds(pl.multiple_of(i * 16, 16), 16), :] = part.reshape(16, LANES)
                return carry

            lax.fori_loop(0, out_ref.shape[0] // 16, move, 0, unroll=8)


def to_rows(psi, chip, chips):
    points = psi.shape[1] // chips
    rows = points // LANES
    return pl.pallas_call(
        rows_kernel,
        grid_spec=pltpu.PrefetchScalarGridSpec(
            num_scalar_prefetch=1,
            grid=(chips,),
            in_specs=[pl.BlockSpec((1, points), lambda i, chip: (0, lax.rem(chip[0] + i, chips)))],
            out_specs=[pl.BlockSpec((rows, LANES), lambda i, chip: (0, 0))] * chips,
        ),
        out_shape=[jax.ShapeDtypeStruct((rows, LANES), BF16)] * chips,
        compiler_params=PARAMS,
    )(chip.reshape(1), psi)


def project_kernel(bands, projectors, padded, pieces, place_ref, atom_refs, block_refs, beta_refs, psi_refs, coef_ref, picks, highs, rests):
    slots = atom_refs[0].shape[1]
    share = slots // pieces
    slab_rows = psi_refs[0].shape[0] // CORES
    pair_count = projectors // 2
    wide = 2 * bands * GROUP
    lane = iota((share, LANES), 1)
    low = lane < LANES // 2
    source = iota((pair_count * wide, bands * padded), 0) // GROUP
    target = iota((pair_count * wide, bands * padded), 1)
    gather_lanes = (target == lax.rem(source, bands) * padded + source // bands).astype(BF16)
    diagonal = lax.rem(iota((GROUP, wide), 0), GROUP) == lax.rem(iota((GROUP, wide), 1), GROUP)
    for slab in range(CORES):
        place = place_ref[0] if slab == 0 else CORES - 1 - place_ref[0]
        first_row = pl.multiple_of(place * slab_rows, slab_rows)
        hits, odds, of_atom = [], [], []
        for piece in range(pieces):
            blocks = ids_column(block_refs[slab], place_ref, piece, share)
            wanted = jnp.right_shift(blocks, 1)
            odds.append(jnp.bitwise_and(blocks, 1) == 1)
            hits.append(
                jnp.concatenate([(wanted - t * LANES == lane).astype(BF16) for t in range(slab_rows // LANES)], axis=1)
            )
            of_atom.append((ids_column(atom_refs[slab], place_ref, piece, share) == lane).astype(BF16))
        hits = jnp.concatenate(hits, axis=0)
        for band, psi_ref in enumerate(psi_refs):
            picked = dot(hits, psi_ref[pl.ds(first_row, slab_rows), :])
            for piece in range(pieces):
                rows = slice(piece * share, (piece + 1) * share)
                straight = picked[rows]
                turned = pltpu.roll(straight, LANES // 2, 1)
                both = jnp.where(low == odds[piece], turned, straight)
                picks[band, rows, :] = jnp.where(low, both, 0.0).astype(BF16)
                picks[bands + band, rows, :] = jnp.where(low, 0.0, both).astype(BF16)
        for piece in range(pieces):
            table_ref = beta_refs[slab * pieces + piece]
            for group in range(share // GROUP):
                own = slice(group * GROUP, (group + 1) * GROUP)
                rows = slice(piece * share + group * GROUP, piece * share + (group + 1) * GROUP)
                values = jnp.concatenate([picks[part, rows, :] for part in range(2 * bands)], axis=0)
                tables = jnp.concatenate([table_ref[own, t * LANES : (t + 1) * LANES] for t in range(pair_count)], axis=0)
                crossed = dot(tables, values, ((1,), (1,)))
                for t in range(pair_count):
                    kept = jnp.where(diagonal, crossed[t * GROUP : (t + 1) * GROUP], 0.0)
                    highs[rows, t * wide : (t + 1) * wide], rests[rows, t * wide : (t + 1) * wide] = two_terms(kept)
        slot_coef = dot(highs[...], gather_lanes) + dot(rests[...], gather_lanes)
        high, rest = two_terms(slot_coef)
        of_atom = jnp.concatenate(of_atom, axis=0)
        summed = dot(high, of_atom, ((0,), (0,))) + dot(rest, of_atom, ((0,), (0,)))
        if slab == 0:
            coef_ref[...] = summed
        else:
            coef_ref[...] += summed


def project(place, atoms, blocks, tables, values, projectors, padded, atom_total):
    bands = len(values)
    pieces = len(tables) // CORES
    slots = atoms[0].shape[1]
    width = projectors * bands * GROUP

    def kernel(place_ref, a0, a1, k0, k1, *rest):
        refs = [rest[: len(tables)], rest[len(tables) : len(tables) + bands], rest[len(tables) + bands :]]
        project_kernel(bands, projectors, padded, pieces, place_ref, (a0, a1), (k0, k1), refs[0], refs[1], *refs[2])

    return pl.pallas_call(
        kernel,
        in_specs=[SMEM_SPEC] + [VMEM_SPEC] * (4 + len(tables) + bands),
        out_specs=VMEM_SPEC,
        out_shape=jax.ShapeDtypeStruct((bands * padded, atom_total), F32),
        scratch_shapes=[pltpu.VMEM((2 * bands, slots, LANES), BF16)] + [pltpu.VMEM((slots, width), BF16)] * 2,
        compiler_params=PARAMS,
    )(place, *atoms, *blocks, *tables, *values)


def apply_kernel(bands, projectors, padded, pieces, place_ref, atom_refs, beta_refs, count_ref, strength_ref, coef_refs, out_refs, wide_refs):
    slots = atom_refs[0].shape[1]
    share = slots // pieces
    pair_count = projectors // 2
    width = projectors * LANES // 2
    atom_total = strength_ref.shape[2]
    lane = iota((share, LANES), 1)
    low = iota((LANES // 2, LANES), 1) < LANES // 2
    valid = (iota((projectors, atom_total), 0) < count_ref[...]).astype(F32)
    spread = (iota((projectors, width), 0) == iota((projectors, width), 1) // (LANES // 2)).astype(BF16)
    for band in range(bands):
        total = coef_refs[0][band * padded : band * padded + projectors, :]
        for away in range(1, bands):
            first = (band - away) % bands * padded
            total = total + coef_refs[away][first : first + projectors, :]
        total = total * valid
        coupled = strength_ref[:, 0, :] * total[0:1]
        for q in range(1, projectors):
            coupled = coupled + strength_ref[:, q, :] * total[q : q + 1]
        scaled = (coupled * valid).astype(BF16)
        wide_refs[band][...] = dot(scaled, spread, ((0,), (0,))).astype(BF16)
    for slab in range(CORES):
        of_atom = [
            (ids_column(atom_refs[slab], place_ref, piece, share) == lane).astype(BF16) for piece in range(pieces)
        ]
        for band in range(bands):
            for piece in range(pieces):
                total = None
                for t in range(pair_count):
                    tile = slice(t * LANES, (t + 1) * LANES)
                    term = dot(of_atom[piece], wide_refs[band][:, tile]) * beta_refs[slab * pieces + piece][:, tile].astype(F32)
                    total = term if total is None else total + term
                total = total + pltpu.roll(total, LANES // 2, 1)
                for i in range(share // LANES):
                    part = total[i * LANES : (i + 1) * LANES]
                    packed = jnp.where(low, part[: LANES // 2], part[LANES // 2 :])
                    first = (slab * slots + piece * share + i * LANES) // 2
                    out_refs[band][first : first + LANES // 2, :] = packed.astype(BF16)


def back_project(place, atoms, tables, count, strength, coefs, projectors, padded):
    bands = len(coefs)
    pieces = len(tables) // CORES
    slots = atoms[0].shape[1]
    atom_total = strength.shape[2]

    def kernel(place_ref, a0, a1, count_ref, strength_ref, *rest):
        ends = [len(tables), len(tables) + bands, len(tables) + 2 * bands]
        apply_kernel(
            bands, projectors, padded, pieces, place_ref, (a0, a1), rest[: ends[0]], count_ref, strength_ref,
            rest[ends[0] : ends[1]], rest[ends[1] : ends[2]], rest[ends[2] :],
        )

    return pl.pallas_call(
        kernel,
        in_specs=[SMEM_SPEC] + [VMEM_SPEC] * (4 + len(tables) + bands),
        out_specs=[VMEM_SPEC] * bands,
        out_shape=[jax.ShapeDtypeStruct((slots, LANES), BF16)] * bands,
        scratch_shapes=[pltpu.VMEM((atom_total, projectors * LANES // 2), BF16)] * bands,
        compiler_params=PARAMS,
    )(place, *atoms, count, strength, *tables, *coefs)


def place_kernel(chips, pieces, place_ref, *refs):
    block_refs, value_refs, out_ref = refs[: CORES * chips], refs[CORES * chips : -1], refs[-1]
    step = pl.program_id(0)
    slots = block_refs[0].shape[1]
    share = slots // pieces
    rows = out_ref.shape[1] // LANES // CORES
    low = iota((LANES // 2, LANES), 1) < LANES // 2
    for chip in range(chips):

        @pl.when(step == chip)
        def _(chip=chip):
            for slab in range(CORES):
                place = place_ref[0] if slab == 0 else CORES - 1 - place_ref[0]
                block_ref = block_refs[chip * CORES + slab]
                parts, wanted = [], []
                for piece in range(pieces):
                    blocks = ids_column(block_ref, place_ref, piece, share)
                    wanted.append(jnp.right_shift(ids_row(block_ref, place_ref, piece, share), 1))
                    for i in range(share // LANES):
                        odd = jnp.bitwise_and(blocks[i * LANES : (i + 1) * LANES], 1) == 1
                        first = (slab * slots + piece * share + i * LANES) // 2
                        value = value_refs[chip][first : first + LANES // 2, :].astype(F32)
                        turned = pltpu.roll(value, LANES // 2, 1)
                        odd_a, odd_b = odd[: LANES // 2], odd[LANES // 2 :]
                        part_a = jnp.where(odd_a, turned, value)
                        part_b = jnp.where(odd_b, value, turned)
                        parts.append(jnp.where(low != odd_a, part_a, 0.0).astype(BF16))
                        parts.append(jnp.where(low != odd_b, part_b, 0.0).astype(BF16))
                values = jnp.concatenate(parts, axis=0)
                wanted = jnp.concatenate(wanted, axis=1)
                start = place * rows * LANES
                for t in range(rows // LANES):
                    hits = (iota((LANES, slots), 0) + t * LANES == wanted).astype(BF16)
                    total = dot(hits, values).astype(BF16)
                    for i in range(LANES // 16):
                        at = pl.multiple_of(start + t * LANES * LANES + i * 2048, 2048)
                        out_ref[0:1, pl.ds(at, 2048)] = total[i * 16 : (i + 1) * 16].reshape(1, 2048)


def place_rows(place, blocks, values, points, pieces):
    chips = len(values)
    share = points // chips
    whole = lambda i, place: (0, 0)
    return pl.pallas_call(
        functools.partial(place_kernel, chips, pieces),
        grid_spec=pltpu.PrefetchScalarGridSpec(
            num_scalar_prefetch=1,
            grid=(chips,),
            in_specs=[pl.BlockSpec(x.shape, whole) for x in (*blocks, *values)],
            out_specs=pl.BlockSpec((1, share), lambda i, place: (0, lax.rem(place[2] + i, chips))),
        ),
        out_shape=jax.ShapeDtypeStruct((1, points), BF16),
        compiler_params=PARAMS,
    )(place, *blocks, *values)


def body(bands, slabs, psi, beta, pair_atom, pair_block, proj_count, strength):
    chips = slabs // CORES
    atom_total, projectors = strength.shape[:2]
    padded = -(-projectors // 8) * 8
    position = lax.axis_index("slab").astype(jnp.int32)
    chip, core = position // CORES, lax.rem(position, CORES)
    place = jnp.stack([core, lax.axis_index("band").astype(jnp.int32), chip])

    def turn(x, chips_on):
        return lax.ppermute(x, "slab", [(i, (i + CORES * chips_on) % slabs) for i in range(slabs)])

    def swap(x):
        return lax.ppermute(x, "slab", [(i, i ^ 1) for i in range(slabs)])

    def across(x, bit):
        return lax.ppermute(x, "band", [(i, i ^ bit) for i in range(bands)])

    if beta.shape[1] % LANES == 0 and bands & (bands - 1) == 0:
        tables = [beta[0]] + [across(beta[0], bit) for bit in range(1, bands)]
    else:
        tables = [lax.all_gather(beta[0], "band", axis=0, tiled=True)]
    tables = tables + [swap(x) for x in tables]
    rows = to_rows(psi, chip, chips)
    values = [rows[0]] + [turn(rows[away], away) for away in range(1, chips)]
    ids = swap(jnp.concatenate([pair_atom, pair_block], axis=0))
    atoms = (pair_atom, ids[0:1])
    blocks = (pair_block, ids[1:2])
    coef = project(place, atoms, blocks, tables, values, projectors, padded, atom_total)
    coefs = [coef] + [turn(coef, away) for away in range(1, chips)]
    results = back_project(
        place, atoms, tables, proj_count.reshape(1, atom_total), strength.transpose(1, 2, 0), coefs, projectors, padded
    )
    results = [results[0]] + [turn(results[away], -away) for away in range(1, chips)]
    both = jnp.concatenate(blocks, axis=0)
    taken = [both] + [turn(both, -away) for away in range(1, chips)]
    block_rows = [x[s : s + 1] for x in taken for s in range(CORES)]
    return place_rows(place, block_rows, results, psi.shape[1], len(tables) // CORES)


def solution(mesh):
    placed = (
        P(("band", "slab"), None),
        P("slab", "band", None),
        P("slab", None),
        P("slab", None),
        P(),
        P(),
    )
    return jax.shard_map(
        functools.partial(body, mesh.shape["band"], mesh.shape["slab"]),
        mesh=mesh,
        in_specs=placed,
        out_specs=P(("band", "slab"), None),
        check_vma=False,
    )
```

time: 120 us -> 75.4 us (0.63)
  waiting for transfers between devices: 62.3 us -> 29.8 us
  between operations: 13.5 us -> 0.11 us
  starting transfers between devices: 19.2 us -> 28.3 us
  Pallas kernels: 22.3 us -> 14.5 us
    all_gather x1 -> x0, waiting for transfers between devices: 32.4 us -> none  [body(): own_tables = lax.all_gather(beta[0], 'band', axis=0, tiled=True)]
    pallas_call x3, Pallas kernels: 21.5 us -> 13.7 us  [the longest x1 5.47 us: project(): pl.pallas_call(kernel, in_specs=[SMEM_SPEC] + [VMEM_SPEC] * (4 + len(tabl...]
    ppermute x0 -> x3, starting transfers between devices: none -> 4.17 us  [across(): return lax.ppermute(x, 'band', [(i, i ^ bit) for i in range(bands)])]
    ppermute x12, starting transfers between devices: 18.8 us -> 22.7 us  [turn(): lax.ppermute(x, 'slab', [(i, (i + CORES * chips_on) % slabs) for i in ran...]
  transfers between devices with their start and end apart: 15 -> 20, of which waited for: 7 -> 6; matrix products, arithmetic and copies ran while one was open for 1% -> 0% of each run, Pallas kernels for 13% -> 14%
where the time goes in v2:
time: 75.4 us; the launch traced here: 75.2 us
  waiting for transfers between devices  29.8 us (40%)
  starting transfers between devices  28.3 us (38%)
  Pallas kernels  14.5 us (19%)
  local copies, waits for them, and re-layouts  1.63 us (2%)
  other arithmetic  0.85 us (1%)
    ppermute x12, waiting for transfers between devices, turn(): lax.ppermute(x, 'slab', [(i, (i + CORES * chips_on) % slabs) for i in ran...  29.8 us
    ppermute x12, starting transfers between devices, turn(): lax.ppermute(x, 'slab', [(i, (i + CORES * chips_on) % slabs) for i in ran...  22.7 us
    pallas_call x1, Pallas kernels, project(): pl.pallas_call(kernel, in_specs=[SMEM_SPEC] + [VMEM_SPEC] * (4 + len(tabl...  5.47 us
    pallas_call x1, Pallas kernels, place_rows(): pl.pallas_call(functools.partial(place_kernel, chips, pieces), grid_spec=...  4.28 us
    ppermute x3, starting transfers between devices, across(): return lax.ppermute(x, 'band', [(i, i ^ bit) for i in range(bands)])  4.17 us
    pallas_call x1, Pallas kernels, back_project(): pl.pallas_call(kernel, in_specs=[SMEM_SPEC] + [VMEM_SPEC] * (4 + len(tabl...  3.97 us
    unnamed x12, local copies, waits for them, and re-layouts  1.61 us
  transfers between devices with their start and end apart: 20, of which 6 were waited for; matrix products, arithmetic and copies ran while one was open for 0% of the time, Pallas kernels for 14%

profile of v2, /device:TPU:0, one launch (start us, length us, event | category | flops | bytes accessed | tf_op | source)
XLA Modules:
  0.0 75.2 jit_solution(9623331882396919875)
XLA Ops:
  0.0 0.8 %pad_add_fusion = s32[2,512]{1,0:T(2,128)S(1)} fusion(s32[1,512]{1,0:T(1,128)} %refs_0_.1, s32[1,512]{1,0:T(1,128)} %a0.3), kind=kLoop, calls=%fused_computation | loop fusion | flops 1024 | bytes 8192 | tf_op jit(solution)/shard_map/concatenate | solution.py:297
  0.8 0.5 collective-permute-start
  1.2 3.5 %collective-permute-start.6 = (bf16[128,1152]{1,0:T(8,128)(2,1)}, bf16[128,1152]{1,0:T(8,128)(2,1)S(1)}, u32[]{:S(2)}, u32[]{:S(2)}) collective-permute-start(bf16[128,1152]{1,0:T(8,128)(2,1)} %bitcast.6), channel_id=1, source_target_pairs={{0,24},{8,16},{16,8},{24,0},{1,25},{9,17},{17,9},{25,1},{2,26},{10... | collective-permute-start | bytes 884744 | tf_op jit(solution)/shard_map/ppermute | solution.py:288
  4.7 0.5 collective-permute-start.4
  5.3 0.1 collective-permute-start.5
  5.4 1.6 %copy-done = bf16[1,524288]{1,0:T(2,128)(2,1)S(1)} copy-done((bf16[1,524288]{1,0:T(2,128)(2,1)S(1)}, bf16[1,524288]{1,0:T(2,128)(2,1)}, u32[]{:S(2)}) %copy-start) | copy-done | bytes 1048600
  7.0 0.7 shard_map.64
  7.7 0.0 copy-start.2
  7.7 0.0 copy-start.5
  7.8 2.0 %collective-permute-start.11 = (bf16[1024,128]{1,0:T(8,128)(2,1)S(1)}, bf16[1024,128]{1,0:T(8,128)(2,1)S(1)}, u32[]{:S(2)}, u32[]{:S(2)}) collective-permute-start(bf16[1024,128]{1,0:T(8,128)(2,1)S(1)} %get-tuple-element.14), channel_id=1, source_target_pairs={{0,2},{1,3},{2,4},{3,5},{4,6},{5,7},{6,0},{7,1},{8,10},{9,11},{10,... | collective-permute-start | bytes 786440 | tf_op jit(solution)/shard_map/ppermute | solution.py:282
  9.8 0.0 collective-permute-done
  9.8 1.6 %collective-permute-start.3 = (s32[2,512]{1,0:T(2,128)S(1)}, s32[2,512]{1,0:T(2,128)S(1)}, u32[]{:S(2)}, u32[]{:S(2)}) collective-permute-start(s32[2,512]{1,0:T(2,128)S(1)} %pad_add_fusion.1), channel_id=1, source_target_pairs={{0,2},{1,3},{2,4},{3,5},{4,6},{5,7},{6,0},{7,1},{8,10},{9,11},{10,... | collective-permute-start | bytes 12296 | tf_op jit(solution)/shard_map/ppermute | solution.py:282
  11.4 6.5 %collective-permute-done.3 = s32[2,512]{1,0:T(2,128)S(1)} collective-permute-done((s32[2,512]{1,0:T(2,128)S(1)}, s32[2,512]{1,0:T(2,128)S(1)}, u32[]{:S(2)}, u32[]{:S(2)}) %collective-permute-start.3) | collective-permute-done | bytes 4128 | tf_op jit(solution)/shard_map/ppermute | solution.py:282
  18.0 0.7 collective-permute-start.12
  18.7 0.0 collective-permute-done.11.rest_9_
  18.7 1.3 %collective-permute-start.13 = (bf16[1024,128]{1,0:T(8,128)(2,1)S(1)}, bf16[1024,128]{1,0:T(8,128)(2,1)S(1)}, u32[]{:S(2)}, u32[]{:S(2)}) collective-permute-start(bf16[1024,128]{1,0:T(8,128)(2,1)S(1)} %get-tuple-element.16), channel_id=1, source_target_pairs={{0,6},{1,7},{2,0},{3,1},{4,2},{5,3},{6,4},{7,5},{8,14},{9,15},{10,... | collective-permute-start | bytes 786440 | tf_op jit(solution)/shard_map/ppermute | solution.py:282
  20.0 10.6 %collective-permute-done.12.rest_10_ = bf16[1024,128]{1,0:T(8,128)(2,1)S(1)} collective-permute-done((bf16[1024,128]{1,0:T(8,128)(2,1)S(1)}, bf16[1024,128]{1,0:T(8,128)(2,1)S(1)}, u32[]{:S(2)}, u32[]{:S(2)}) %collective-permute-start.12) | collective-permute-done | bytes 262176 | tf_op jit(solution)/shard_map/ppermute | solution.py:282
  30.7 0.0 collective-permute-start.7
  30.7 0.0 collective-permute-done.6.rest_3_
  30.7 0.5 collective-permute-start.10
  31.2 0.0 collective-permute-done.4.rest_1_
  31.2 0.1 collective-permute-start.8
  31.3 0.0 collective-permute-done.5.rest_2_
  31.3 0.4 collective-permute-start.9
  31.7 0.1 pad_add_fusion.2.place_ref
  31.8 0.0 collective-permute-done.13.rest_11_
  31.8 4.0 %collective-permute-start.2 = (s32[2,512]{1,0:T(2,128)S(1)}, s32[2,512]{1,0:T(2,128)S(1)}, u32[]{:S(2)}, u32[]{:S(2)}) collective-permute-start(s32[2,512]{1,0:T(2,128)S(1)} %pad_add_fusion.1), channel_id=1, source_target_pairs={{0,4},{1,5},{2,6},{3,7},{4,0},{5,1},{6,2},{7,3},{8,12},{9,13},{10,... | collective-permute-start | bytes 12296 | tf_op jit(solution)/shard_map/ppermute | solution.py:282
  35.7 0.0 collective-permute-done.7.rest_4_
  35.7 4.5 %collective-permute-start.1 = (s32[2,512]{1,0:T(2,128)S(1)}, s32[2,512]{1,0:T(2,128)S(1)}, u32[]{:S(2)}, u32[]{:S(2)}) collective-permute-start(s32[2,512]{1,0:T(2,128)S(1)} %pad_add_fusion.1), channel_id=1, source_target_pairs={{0,6},{1,7},{2,0},{3,1},{4,2},{5,3},{6,4},{7,5},{8,14},{9,15},{10,... | collective-permute-start | bytes 12296 | tf_op jit(solution)/shard_map/ppermute | solution.py:282
  40.2 0.0 collective-permute-done.10.rest_7_
  40.2 0.0 collective-permute-done.8.rest_5_
  40.2 0.0 collective-permute-done.9.rest_6_
  40.2 5.5 %shard_map.65.rest_8_ = f32[96,128]{1,0:T(8,128)S(1)} custom-call(s32[3]{0:T(128)S(1)} %pad_add_fusion.2.place_ref, s32[1,512]{1,0:T(1,128)S(1)} %copy-done.4, s32[1,512]{1,0:T(1,128)S(1)} %get-tuple-element.21.a1, s32[1,512]{1,0:T(1,128)S(1)} %copy-done.3, s32[1,512]{1,0:T(1,128)S(1)} %get-tuple-element.22.k1.refs_1_, bf16[128,1152]{1,0:T(8,128)(2,1)S(1)} %bitcast.10, ...), custom_call_target="tpu_custom_call" | custom-call | tf_op jit(solution)/shard_map/pallas_call | solution.py:144
  45.7 0.2 collective-permute-start.14
  46.0 1.6 %collective-permute-start.15 = (f32[96,128]{1,0:T(8,128)S(1)}, f32[96,128]{1,0:T(8,128)S(1)}, u32[]{:S(2)}, u32[]{:S(2)}) collective-permute-start(f32[96,128]{1,0:T(8,128)S(1)} %shard_map.65.rest_8_), channel_id=1, source_target_pairs={{0,4},{1,5},{2,6},{3,7},{4,0},{5,1},{6,2},{7,3},{8,12},{9,13},{10,... | collective-permute-start | bytes 147464 | tf_op jit(solution)/shard_map/ppermute | solution.py:282
  47.6 2.8 %collective-permute-start.16 = (f32[96,128]{1,0:T(8,128)S(1)}, f32[96,128]{1,0:T(8,128)S(1)}, u32[]{:S(2)}, u32[]{:S(2)}) collective-permute-start(f32[96,128]{1,0:T(8,128)S(1)} %shard_map.65.rest_8_), channel_id=1, source_target_pairs={{0,6},{1,7},{2,0},{3,1},{4,2},{5,3},{6,4},{7,5},{8,14},{9,15},{10,... | collective-permute-start | bytes 147464 | tf_op jit(solution)/shard_map/ppermute | solution.py:282
  50.3 1.8 %collective-permute-done.14.rest_9_ = f32[96,128]{1,0:T(8,128)S(1)} collective-permute-done((f32[96,128]{1,0:T(8,128)S(1)}, f32[96,128]{1,0:T(8,128)S(1)}, u32[]{:S(2)}, u32[]{:S(2)}) %collective-permute-start.14) | collective-permute-done | bytes 49184 | tf_op jit(solution)/shard_map/ppermute | solution.py:282
  52.1 0.8 %collective-permute-done.15.rest_10_ = f32[96,128]{1,0:T(8,128)S(1)} collective-permute-done((f32[96,128]{1,0:T(8,128)S(1)}, f32[96,128]{1,0:T(8,128)S(1)}, u32[]{:S(2)}, u32[]{:S(2)}) %collective-permute-start.15) | collective-permute-done | bytes 49184 | tf_op jit(solution)/shard_map/ppermute | solution.py:282
  52.9 0.0 collective-permute-done.16.rest_11_
  52.9 4.0 %shard_map.66 = (bf16[512,128]{1,0:T(8,128)(2,1)S(1)}, bf16[512,128]{1,0:T(8,128)(2,1)S(1)}, bf16[512,128]{1,0:T(8,128)(2,1)S(1)}, bf16[512,128]{1,0:T(8,128)(2,1)S(1)}) custom-call(s32[3]{0:T(128)S(1)} %pad_add_fusion.2.place_ref, s32[1,512]{1,0:T(1,128)S(1)} %copy-done.4, s32[1,512]{1,0:T(1,128)S(1)} %get-tuple-element.21.a1, s32[1,128]{1,0:T(1,128)S(1)} %bitcast.13, ...), custom_call_target="tpu_custom_call" | custom-call | tf_op jit(solution)/shard_map/pallas_call | solution.py:207
  56.9 3.3 %collective-permute-start.17 = (bf16[512,128]{1,0:T(8,128)(2,1)S(1)}, bf16[512,128]{1,0:T(8,128)(2,1)S(1)}, u32[]{:S(2)}, u32[]{:S(2)}) collective-permute-start(bf16[512,128]{1,0:T(8,128)(2,1)S(1)} %get-tuple-element.18), channel_id=1, source_target_pairs={{0,6},{1,7},{2,0},{3,1},{4,2},{5,3},{6,4},{7,5},{8,14},{9,15},{10,... | collective-permute-start | bytes 393224 | tf_op jit(solution)/shard_map/ppermute | solution.py:282
  60.2 0.0 collective-permute-start.18
  60.2 0.6 collective-permute-start.19
  60.9 0.0 collective-permute-done.1
  60.9 3.3 %collective-permute-done.17.refs_9_ = bf16[512,128]{1,0:T(8,128)(2,1)S(1)} collective-permute-done((bf16[512,128]{1,0:T(8,128)(2,1)S(1)}, bf16[512,128]{1,0:T(8,128)(2,1)S(1)}, u32[]{:S(2)}, u32[]{:S(2)}) %collective-permute-start.17) | collective-permute-done | bytes 131104 | tf_op jit(solution)/shard_map/ppermute | solution.py:282
  64.2 6.8 %collective-permute-done.18.refs_10_ = bf16[512,128]{1,0:T(8,128)(2,1)S(1)} collective-permute-done((bf16[512,128]{1,0:T(8,128)(2,1)S(1)}, bf16[512,128]{1,0:T(8,128)(2,1)S(1)}, u32[]{:S(2)}, u32[]{:S(2)}) %collective-permute-start.18) | collective-permute-done | bytes 131104 | tf_op jit(solution)/shard_map/ppermute | solution.py:282
  70.9 0.0 collective-permute-done.19.refs_11_
  70.9 4.3 %shard_map.67 = bf16[1,524288]{1,0:T(2,128)(2,1)} custom-call(s32[3]{0:T(128)S(1)} %pad_add_fusion.2.place_ref, s32[1,512]{1,0:T(1,128)S(1)} %copy-done.3, s32[1,512]{1,0:T(1,128)S(1)} %get-tuple-element.22.k1.refs_1_, s32[1,512]{1,0:T(1,128)S(1)} %get-tuple-element.28.refs_2_, s32[1,512]{1,0:T(1,128)S(1)} %get-tuple-element.27.refs_3_, ...), custom_call_target="tpu_custom_call" | custom-call | tf_op jit(solution)/shard_map/pallas_call | solution.py:260
  (15 shorter events, 0.0 us)
Async XLA Ops:
  0.0 40.2 %copy-start.4 = (s32[1,512]{1,0:T(1,128)S(1)}, s32[1,512]{1,0:T(1,128)}, u32[]{:S(2)}) copy-start(s32[1,512]{1,0:T(1,128)} %a0.3) | copy-start | bytes 6148
  0.0 9.8 %copy-start.3 = (s32[1,512]{1,0:T(1,128)S(1)}, s32[1,512]{1,0:T(1,128)}, u32[]{:S(2)}) copy-start(s32[1,512]{1,0:T(1,128)} %refs_0_.1) | copy-start | bytes 6148
  0.8 9.0 %collective-permute-start = (s32[2,512]{1,0:T(2,128)S(1)}, s32[2,512]{1,0:T(2,128)S(1)}, u32[]{:S(2)}, u32[]{:S(2)}) collective-permute-start(s32[2,512]{1,0:T(2,128)S(1)} %pad_add_fusion), channel_id=1, source_target_pairs={{0,1},{1,0},{2,3},{3,2},{4,5},{5,4},{6,7},{7,6},{8,9},{9,8},{10,11... | collective-permute-start | bytes 12296 | tf_op jit(solution)/shard_map/ppermute | solution.py:285
  1.2 29.4 %collective-permute-start.6 = (bf16[128,1152]{1,0:T(8,128)(2,1)}, bf16[128,1152]{1,0:T(8,128)(2,1)S(1)}, u32[]{:S(2)}, u32[]{:S(2)}) collective-permute-start(bf16[128,1152]{1,0:T(8,128)(2,1)} %bitcast.6), channel_id=1, source_target_pairs={{0,24},{8,16},{16,8},{24,0},{1,25},{9,17},{17,9},{25,1},{2,26},{10... | collective-permute-start | bytes 884744 | tf_op jit(solution)/shard_map/ppermute | solution.py:288
  4.7 26.4 %collective-permute-start.4 = (bf16[128,1152]{1,0:T(8,128)(2,1)}, bf16[128,1152]{1,0:T(8,128)(2,1)S(1)}, u32[]{:S(2)}, u32[]{:S(2)}) collective-permute-start(bf16[128,1152]{1,0:T(8,128)(2,1)} %bitcast.7), channel_id=1, source_target_pairs={{0,8},{8,0},{16,24},{24,16},{1,9},{9,1},{17,25},{25,17},{2,10},{10... | collective-permute-start | bytes 884744 | tf_op jit(solution)/shard_map/ppermute | solution.py:288
  5.3 26.0 %collective-permute-start.5 = (bf16[128,1152]{1,0:T(8,128)(2,1)}, bf16[128,1152]{1,0:T(8,128)(2,1)S(1)}, u32[]{:S(2)}, u32[]{:S(2)}) collective-permute-start(bf16[128,1152]{1,0:T(8,128)(2,1)} %bitcast.8), channel_id=1, source_target_pairs={{0,16},{8,24},{16,0},{24,8},{1,17},{9,25},{17,1},{25,9},{2,18},{10... | collective-permute-start | bytes 884744 | tf_op jit(solution)/shard_map/ppermute | solution.py:288
  5.4 1.6 %copy-start = (bf16[1,524288]{1,0:T(2,128)(2,1)S(1)}, bf16[1,524288]{1,0:T(2,128)(2,1)}, u32[]{:S(2)}) copy-start(bf16[1,524288]{1,0:T(2,128)(2,1)} %psi_ref.1) | copy-start | bytes 3145732
  7.0 23.7 %copy-start.1 = (bf16[1,128,1152]{2,1,0:T(8,128)(2,1)S(1)}, bf16[1,128,1152]{2,1,0:T(8,128)(2,1)}, u32[]{:S(2)}) copy-start(bf16[1,128,1152]{2,1,0:T(8,128)(2,1)} %param.7) | copy-start | bytes 884740
  7.7 45.2 %copy-start.2 = (f32[128,18,18]{0,2,1:T(8,128)S(1)}, f32[128,18,18]{0,2,1:T(8,128)}, u32[]{:S(2)}) copy-start(f32[128,18,18]{0,2,1:T(8,128)} %param.11) | copy-start | bytes 497668
  7.7 45.2 %copy-start.5 = (s32[128]{0:T(128)S(1)}, s32[128]{0:T(128)}, u32[]{:S(2)}) copy-start(s32[128]{0:T(128)} %param.10) | copy-start | bytes 1540
  7.8 10.9 %collective-permute-start.11 = (bf16[1024,128]{1,0:T(8,128)(2,1)S(1)}, bf16[1024,128]{1,0:T(8,128)(2,1)S(1)}, u32[]{:S(2)}, u32[]{:S(2)}) collective-permute-start(bf16[1024,128]{1,0:T(8,128)(2,1)S(1)} %get-tuple-element.14), channel_id=1, source_target_pairs={{0,2},{1,3},{2,4},{3,5},{4,6},{5,7},{6,0},{7,1},{8,10},{9,11},{10,... | collective-permute-start | bytes 786440 | tf_op jit(solution)/shard_map/ppermute | solution.py:282
  9.8 8.1 %collective-permute-start.3 = (s32[2,512]{1,0:T(2,128)S(1)}, s32[2,512]{1,0:T(2,128)S(1)}, u32[]{:S(2)}, u32[]{:S(2)}) collective-permute-start(s32[2,512]{1,0:T(2,128)S(1)} %pad_add_fusion.1), channel_id=1, source_target_pairs={{0,2},{1,3},{2,4},{3,5},{4,6},{5,7},{6,0},{7,1},{8,10},{9,11},{10,... | collective-permute-start | bytes 12296 | tf_op jit(solution)/shard_map/ppermute | solution.py:282
  18.0 12.7 %collective-permute-start.12 = (bf16[1024,128]{1,0:T(8,128)(2,1)S(1)}, bf16[1024,128]{1,0:T(8,128)(2,1)S(1)}, u32[]{:S(2)}, u32[]{:S(2)}) collective-permute-start(bf16[1024,128]{1,0:T(8,128)(2,1)S(1)} %get-tuple-element.15), channel_id=1, source_target_pairs={{0,4},{1,5},{2,6},{3,7},{4,0},{5,1},{6,2},{7,3},{8,12},{9,13},{10,... | collective-permute-start | bytes 786440 | tf_op jit(solution)/shard_map/ppermute | solution.py:282
  18.7 13.1 %collective-permute-start.13 = (bf16[1024,128]{1,0:T(8,128)(2,1)S(1)}, bf16[1024,128]{1,0:T(8,128)(2,1)S(1)}, u32[]{:S(2)}, u32[]{:S(2)}) collective-permute-start(bf16[1024,128]{1,0:T(8,128)(2,1)S(1)} %get-tuple-element.16), channel_id=1, source_target_pairs={{0,6},{1,7},{2,0},{3,1},{4,2},{5,3},{6,4},{7,5},{8,14},{9,15},{10,... | collective-permute-start | bytes 786440 | tf_op jit(solution)/shard_map/ppermute | solution.py:282
  30.7 5.1 %collective-permute-start.7 = (bf16[128,1152]{1,0:T(8,128)(2,1)S(1)}, bf16[128,1152]{1,0:T(8,128)(2,1)S(1)}, u32[]{:S(2)}, u32[]{:S(2)}) collective-permute-start(bf16[128,1152]{1,0:T(8,128)(2,1)S(1)} %bitcast.9), channel_id=1, source_target_pairs={{0,1},{1,0},{2,3},{3,2},{4,5},{5,4},{6,7},{7,6},{8,9},{9,8},{10,11... | collective-permute-start | bytes 884744 | tf_op jit(solution)/shard_map/ppermute | solution.py:285
  30.7 9.5 %collective-permute-start.10 = (bf16[128,1152]{1,0:T(8,128)(2,1)S(1)}, bf16[128,1152]{1,0:T(8,128)(2,1)S(1)}, u32[]{:S(2)}, u32[]{:S(2)}) collective-permute-start(bf16[128,1152]{1,0:T(8,128)(2,1)S(1)} %collective-permute-done.6.rest_3_), channel_id=1, source_target_pairs={{0,1},{1,0},{2,3},{3,2},{4,5},{5,4},{6,7},{7,6},{8,9},{9,8},{10,11... | collective-permute-start | bytes 884744 | tf_op jit(solution)/shard_map/ppermute | solution.py:285
  31.2 9.0 %collective-permute-start.8 = (bf16[128,1152]{1,0:T(8,128)(2,1)S(1)}, bf16[128,1152]{1,0:T(8,128)(2,1)S(1)}, u32[]{:S(2)}, u32[]{:S(2)}) collective-permute-start(bf16[128,1152]{1,0:T(8,128)(2,1)S(1)} %collective-permute-done.4.rest_1_), channel_id=1, source_target_pairs={{0,1},{1,0},{2,3},{3,2},{4,5},{5,4},{6,7},{7,6},{8,9},{9,8},{10,11... | collective-permute-start | bytes 884744 | tf_op jit(solution)/shard_map/ppermute | solution.py:285
  31.3 9.0 %collective-permute-start.9 = (bf16[128,1152]{1,0:T(8,128)(2,1)S(1)}, bf16[128,1152]{1,0:T(8,128)(2,1)S(1)}, u32[]{:S(2)}, u32[]{:S(2)}) collective-permute-start(bf16[128,1152]{1,0:T(8,128)(2,1)S(1)} %collective-permute-done.5.rest_2_), channel_id=1, source_target_pairs={{0,1},{1,0},{2,3},{3,2},{4,5},{5,4},{6,7},{7,6},{8,9},{9,8},{10,11... | collective-permute-start | bytes 884744 | tf_op jit(solution)/shard_map/ppermute | solution.py:285
  31.8 18.5 %collective-permute-start.2 = (s32[2,512]{1,0:T(2,128)S(1)}, s32[2,512]{1,0:T(2,128)S(1)}, u32[]{:S(2)}, u32[]{:S(2)}) collective-permute-start(s32[2,512]{1,0:T(2,128)S(1)} %pad_add_fusion.1), channel_id=1, source_target_pairs={{0,4},{1,5},{2,6},{3,7},{4,0},{5,1},{6,2},{7,3},{8,12},{9,13},{10,... | collective-permute-start | bytes 12296 | tf_op jit(solution)/shard_map/ppermute | solution.py:282
  35.7 25.1 %collective-permute-start.1 = (s32[2,512]{1,0:T(2,128)S(1)}, s32[2,512]{1,0:T(2,128)S(1)}, u32[]{:S(2)}, u32[]{:S(2)}) collective-permute-start(s32[2,512]{1,0:T(2,128)S(1)} %pad_add_fusion.1), channel_id=1, source_target_pairs={{0,6},{1,7},{2,0},{3,1},{4,2},{5,3},{6,4},{7,5},{8,14},{9,15},{10,... | collective-permute-start | bytes 12296 | tf_op jit(solution)/shard_map/ppermute | solution.py:282
  45.7 6.4 %collective-permute-start.14 = (f32[96,128]{1,0:T(8,128)S(1)}, f32[96,128]{1,0:T(8,128)S(1)}, u32[]{:S(2)}, u32[]{:S(2)}) collective-permute-start(f32[96,128]{1,0:T(8,128)S(1)} %shard_map.65.rest_8_), channel_id=1, source_target_pairs={{0,2},{1,3},{2,4},{3,5},{4,6},{5,7},{6,0},{7,1},{8,10},{9,11},{10,... | collective-permute-start | bytes 147464 | tf_op jit(solution)/shard_map/ppermute | solution.py:282
  46.0 7.0 %collective-permute-start.15 = (f32[96,128]{1,0:T(8,128)S(1)}, f32[96,128]{1,0:T(8,128)S(1)}, u32[]{:S(2)}, u32[]{:S(2)}) collective-permute-start(f32[96,128]{1,0:T(8,128)S(1)} %shard_map.65.rest_8_), channel_id=1, source_target_pairs={{0,4},{1,5},{2,6},{3,7},{4,0},{5,1},{6,2},{7,3},{8,12},{9,13},{10,... | collective-permute-start | bytes 147464 | tf_op jit(solution)/shard_map/ppermute | solution.py:282
  47.6 5.4 %collective-permute-start.16 = (f32[96,128]{1,0:T(8,128)S(1)}, f32[96,128]{1,0:T(8,128)S(1)}, u32[]{:S(2)}, u32[]{:S(2)}) collective-permute-start(f32[96,128]{1,0:T(8,128)S(1)} %shard_map.65.rest_8_), channel_id=1, source_target_pairs={{0,6},{1,7},{2,0},{3,1},{4,2},{5,3},{6,4},{7,5},{8,14},{9,15},{10,... | collective-permute-start | bytes 147464 | tf_op jit(solution)/shard_map/ppermute | solution.py:282
  56.9 7.3 %collective-permute-start.17 = (bf16[512,128]{1,0:T(8,128)(2,1)S(1)}, bf16[512,128]{1,0:T(8,128)(2,1)S(1)}, u32[]{:S(2)}, u32[]{:S(2)}) collective-permute-start(bf16[512,128]{1,0:T(8,128)(2,1)S(1)} %get-tuple-element.18), channel_id=1, source_target_pairs={{0,6},{1,7},{2,0},{3,1},{4,2},{5,3},{6,4},{7,5},{8,14},{9,15},{10,... | collective-permute-start | bytes 393224 | tf_op jit(solution)/shard_map/ppermute | solution.py:282
  60.2 10.7 %collective-permute-start.18 = (bf16[512,128]{1,0:T(8,128)(2,1)S(1)}, bf16[512,128]{1,0:T(8,128)(2,1)S(1)}, u32[]{:S(2)}, u32[]{:S(2)}) collective-permute-start(bf16[512,128]{1,0:T(8,128)(2,1)S(1)} %get-tuple-element.19), channel_id=1, source_target_pairs={{0,4},{1,5},{2,6},{3,7},{4,0},{5,1},{6,2},{7,3},{8,12},{9,13},{10,... | collective-permute-start | bytes 393224 | tf_op jit(solution)/shard_map/ppermute | solution.py:282
  60.2 10.7 %collective-permute-start.19 = (bf16[512,128]{1,0:T(8,128)(2,1)S(1)}, bf16[512,128]{1,0:T(8,128)(2,1)S(1)}, u32[]{:S(2)}, u32[]{:S(2)}) collective-permute-start(bf16[512,128]{1,0:T(8,128)(2,1)S(1)} %get-tuple-element.20), channel_id=1, source_target_pairs={{0,2},{1,3},{2,4},{3,5},{4,6},{5,7},{6,0},{7,1},{8,10},{9,11},{10,... | collective-permute-start | bytes 393224 | tf_op jit(solution)/shard_map/ppermute | solution.py:282

commit v3 on v1

v3 whole, which is shorter than its diff:
```python
import functools

import jax
import jax.numpy as jnp
from jax import lax
from jax.experimental import pallas as pl
from jax.experimental.pallas import tpu as pltpu
from jax.sharding import PartitionSpec as P

CORES = 2
LANES = 128
GROUP = 16
GATHER_BYTES = 10_000_000
F32 = jnp.float32
BF16 = jnp.bfloat16
VMEM_SPEC = pl.BlockSpec(memory_space=pltpu.VMEM)
SMEM_SPEC = pl.BlockSpec(memory_space=pltpu.SMEM)
PARAMS = pltpu.CompilerParams(vmem_limit_bytes=40 * 1024 * 1024)


def dot(a, b, contract=((1,), (0,))):
    return lax.dot_general(a, b, (contract, ((), ())), preferred_element_type=F32)


def two_terms(x):
    high = x.astype(BF16)
    return high, (x - high.astype(F32)).astype(BF16)


def after(x, *others):
    return lax.optimization_barrier((x, *others))[0]


def iota(shape, axis):
    return lax.broadcasted_iota(jnp.int32, shape, axis)


def slab_index(place_ref, chips, away, slab):
    core = place_ref[0] if slab == 0 else CORES - 1 - place_ref[0]
    return lax.rem(place_ref[2] + away, chips) * CORES + core


def slot_ids(ids_ref, place_ref, index, pieces, kind):
    slot_rows = ids_ref.shape[1] // 2
    share = slot_rows // pieces
    for piece in range(pieces):
        first = 0 if pieces == 1 else jnp.bitwise_xor(place_ref[1], piece) * share
        for i in range(share):
            yield ids_ref[index, pl.ds(kind * slot_rows + first + i, 1), :]


def down(ids):
    return jnp.transpose(jnp.broadcast_to(ids, (LANES, LANES)))


def rows_kernel(psi_ref, out_ref):
    def move(i, carry):
        part = psi_ref[0:1, pl.ds(pl.multiple_of(i * 2048, 2048), 2048)]
        out_ref[pl.ds(pl.multiple_of(i * 16, 16), 16), :] = part.reshape(16, LANES)
        return carry

    lax.fori_loop(0, out_ref.shape[0] // 16, move, 0, unroll=8)


def to_rows(psi):
    rows = psi.shape[1] // LANES
    return pl.pallas_call(
        rows_kernel,
        in_specs=[VMEM_SPEC],
        out_specs=VMEM_SPEC,
        out_shape=jax.ShapeDtypeStruct((rows, LANES), BF16),
        compiler_params=PARAMS,
    )(psi)


def gather_kernel(pieces, place_ref, ids_ref, rows_ref, out_refs):
    slots = ids_ref.shape[1] // 2 * LANES
    chips = len(out_refs)
    slab_rows = rows_ref.shape[0] // (CORES * chips)
    lane = iota((LANES, LANES), 1)
    low = iota((LANES // 2, LANES), 1) < LANES // 2
    for away, out_ref in enumerate(out_refs):
        for slab in range(CORES):
            index = slab_index(place_ref, chips, away, slab)
            odds, hits = [], []
            for ids in slot_ids(ids_ref, place_ref, index, pieces, 0):
                blocks = down(ids)
                wanted = jnp.right_shift(blocks, 1)
                odds.append(jnp.bitwise_and(blocks, 1) == 1)
                hits.append(
                    jnp.concatenate([(wanted - t * LANES == lane).astype(BF16) for t in range(slab_rows // LANES)], axis=1)
                )
            first_row = pl.multiple_of(index * slab_rows, slab_rows)
            picked = dot(jnp.concatenate(hits, axis=0), rows_ref[pl.ds(first_row, slab_rows), :])
            for i, odd in enumerate(odds):
                straight = picked[i * LANES : (i + 1) * LANES]
                turned = pltpu.roll(straight, LANES // 2, 1)
                lower = jnp.where(odd, turned, straight)[: LANES // 2]
                upper = jnp.where(odd, straight, turned)[LANES // 2 :]
                first = (slab * slots + i * LANES) // 2
                out_ref[first : first + LANES // 2, :] = jnp.where(low, lower, upper).astype(BF16)


def gather(place, ids, rows, pieces, chips):
    slots = ids.shape[1] // 2 * LANES

    def kernel(place_ref, ids_ref, rows_ref, *out_refs):
        gather_kernel(pieces, place_ref, ids_ref, rows_ref, out_refs)

    return pl.pallas_call(
        kernel,
        in_specs=[SMEM_SPEC] + [VMEM_SPEC] * 2,
        out_specs=[VMEM_SPEC] * chips,
        out_shape=[jax.ShapeDtypeStruct((slots, LANES), BF16)] * chips,
        cost_estimate=pl.CostEstimate(flops=0, bytes_accessed=GATHER_BYTES, transcendentals=0),
        compiler_params=PARAMS,
    )(place, ids, rows)


def project_kernel(projectors, padded, pieces, place_ref, ids_ref, table_refs, packed_refs, coef_ref, picks_of, highs, rests):
    bands = len(packed_refs)
    slots = table_refs[0].shape[0]
    pair_count = projectors // 2
    wide = 2 * bands * GROUP
    lane = iota((LANES, LANES), 1)
    low = iota((bands * GROUP, LANES), 1) < LANES // 2
    source = iota((pair_count * wide, bands * padded), 0) // GROUP
    target = iota((pair_count * wide, bands * padded), 1)
    gather_lanes = (target == lax.rem(source, bands) * padded + source // bands).astype(BF16)
    diagonal = lax.rem(iota((GROUP, wide), 0), GROUP) == lax.rem(iota((GROUP, wide), 1), GROUP)
    none = jnp.zeros((bands * GROUP, LANES), BF16)
    half = LANES // 2
    left = iota((half, LANES), 1) < half
    for band, packed_ref in enumerate(packed_refs):
        for i in range(CORES * slots // LANES):
            straight = packed_ref[i * half : (i + 1) * half, :].astype(F32)
            turned = pltpu.roll(straight, half, 1)
            picks_of[band, i * LANES : i * LANES + half, :] = jnp.where(left, straight, turned).astype(BF16)
            picks_of[band, i * LANES + half : (i + 1) * LANES, :] = jnp.where(left, turned, straight).astype(BF16)
    for slab, table_ref in enumerate(table_refs):
        index = slab_index(place_ref, ids_ref.shape[0] // CORES, 0, slab)
        atoms = slot_ids(ids_ref, place_ref, index, pieces, 1)
        of_atom = jnp.concatenate([(down(ids) == lane).astype(BF16) for ids in atoms], axis=0)
        for group in range(slots // GROUP):
            rows = slice(group * GROUP, (group + 1) * GROUP)
            picked = slice(slab * slots + group * GROUP, slab * slots + (group + 1) * GROUP)
            picks = jnp.concatenate([picks_of[band, picked, :] for band in range(bands)], axis=0)
            values = jnp.concatenate([jnp.where(low, picks, none), jnp.where(low, none, picks)], axis=0)
            tables = jnp.concatenate([table_ref[rows, t * LANES : (t + 1) * LANES] for t in range(pair_count)], axis=0)
            crossed = dot(tables, values, ((1,), (1,)))
            for t in range(pair_count):
                kept = jnp.where(diagonal, crossed[t * GROUP : (t + 1) * GROUP], 0.0)
                highs[rows, t * wide : (t + 1) * wide], rests[rows, t * wide : (t + 1) * wide] = two_terms(kept)
        slot_coef = dot(highs[...], gather_lanes) + dot(rests[...], gather_lanes)
        high, rest = two_terms(slot_coef)
        summed = dot(high, of_atom, ((0,), (0,))) + dot(rest, of_atom, ((0,), (0,)))
        coef_ref[...] = summed if slab == 0 else coef_ref[...] + summed


def project(place, ids, tables, picks, projectors, padded, pieces):
    bands = len(picks)
    slots = tables[0].shape[0]
    width = projectors * bands * GROUP

    def kernel(place_ref, ids_ref, own_ref, other_ref, *rest):
        project_kernel(projectors, padded, pieces, place_ref, ids_ref, (own_ref, other_ref), rest[:bands], *rest[bands:])

    return pl.pallas_call(
        kernel,
        in_specs=[SMEM_SPEC] + [VMEM_SPEC] * (3 + bands),
        out_specs=VMEM_SPEC,
        out_shape=jax.ShapeDtypeStruct((bands * padded, LANES), F32),
        scratch_shapes=[pltpu.VMEM((bands, CORES * slots, LANES), BF16)] + [pltpu.VMEM((slots, width), BF16)] * 2,
        compiler_params=PARAMS,
    )(place, ids, *tables, *picks)


def apply_kernel(bands, projectors, padded, pieces, place_ref, ids_ref, table_refs, count_ref, strength_ref, coef_refs, out_refs, wide_refs):
    slots = table_refs[0].shape[0]
    pair_count = projectors // 2
    width = projectors * LANES // 2
    atom_total = strength_ref.shape[2]
    lane = iota((LANES, LANES), 1)
    low = iota((LANES // 2, LANES), 1) < LANES // 2
    valid = (iota((projectors, atom_total), 0) < count_ref[...]).astype(F32)
    spread = (iota((projectors, width), 0) == iota((projectors, width), 1) // (LANES // 2)).astype(BF16)
    for band in range(bands):
        total = coef_refs[0][band * padded : band * padded + projectors, :]
        for away in range(1, bands):
            first = (band - away) % bands * padded
            total = total + coef_refs[away][first : first + projectors, :]
        total = total * valid
        coupled = strength_ref[:, 0, :] * total[0:1]
        for q in range(1, projectors):
            coupled = coupled + strength_ref[:, q, :] * total[q : q + 1]
        scaled = (coupled * valid).astype(BF16)
        wide_refs[band][...] = dot(scaled, spread, ((0,), (0,))).astype(BF16)
    for slab, table_ref in enumerate(table_refs):
        index = slab_index(place_ref, ids_ref.shape[0] // CORES, 0, slab)
        for i, atoms in enumerate(slot_ids(ids_ref, place_ref, index, pieces, 1)):
            of_atom = (down(atoms) == lane).astype(BF16)
            rows = slice(i * LANES, (i + 1) * LANES)
            first = (slab * slots + i * LANES) // 2
            for band in range(bands):
                total = None
                for t in range(pair_count):
                    tile = slice(t * LANES, (t + 1) * LANES)
                    term = dot(of_atom, wide_refs[band][:, tile]) * table_ref[rows, tile].astype(F32)
                    total = term if total is None else total + term
                total = total + pltpu.roll(total, LANES // 2, 1)
                packed = jnp.where(low, total[: LANES // 2], total[LANES // 2 :])
                out_refs[band][first : first + LANES // 2, :] = packed.astype(BF16)


def back_project(place, ids, tables, count, strength, coefs, projectors, padded, pieces):
    bands = len(coefs)
    slots = tables[0].shape[0]
    atom_total = strength.shape[2]

    def kernel(place_ref, ids_ref, own_ref, other_ref, count_ref, strength_ref, *rest):
        apply_kernel(
            bands, projectors, padded, pieces, place_ref, ids_ref, (own_ref, other_ref), count_ref, strength_ref,
            rest[:bands], rest[bands : 2 * bands], rest[2 * bands :],
        )

    return pl.pallas_call(
        kernel,
        in_specs=[SMEM_SPEC] + [VMEM_SPEC] * (5 + bands),
        out_specs=[VMEM_SPEC] * bands,
        out_shape=[jax.ShapeDtypeStruct((slots, LANES), BF16)] * bands,
        scratch_shapes=[pltpu.VMEM((atom_total, projectors * LANES // 2), BF16)] * bands,
        compiler_params=PARAMS,
    )(place, ids, *tables, count, strength, *coefs)


def place_kernel(chips, pieces, place_ref, *refs):
    ids_ref, value_refs, out_ref = refs[0], refs[1:-1], refs[-1]
    step = pl.program_id(0)
    slots = ids_ref.shape[1] // 2 * LANES
    rows = out_ref.shape[1] // LANES // CORES
    low = iota((LANES // 2, LANES), 1) < LANES // 2
    for chip in range(chips):

        @pl.when(step == chip)
        def _(chip=chip):
            for slab in range(CORES):
                place = place_ref[0] if slab == 0 else CORES - 1 - place_ref[0]
                index = slab_index(place_ref, chips, chip, slab)
                parts, wanted = [], []
                for i, blocks in enumerate(slot_ids(ids_ref, place_ref, index, pieces, 0)):
                    wanted.append(jnp.right_shift(blocks, 1))
                    odd = jnp.bitwise_and(down(blocks), 1) == 1
                    first = (slab * slots + i * LANES) // 2
                    value = value_refs[chip][first : first + LANES // 2, :].astype(F32)
                    turned = pltpu.roll(value, LANES // 2, 1)
                    odd_a, odd_b = odd[: LANES // 2], odd[LANES // 2 :]
                    part_a = jnp.where(odd_a, turned, value)
                    part_b = jnp.where(odd_b, value, turned)
                    parts.append(jnp.where(low != odd_a, part_a, 0.0).astype(BF16))
                    parts.append(jnp.where(low != odd_b, part_b, 0.0).astype(BF16))
                values = jnp.concatenate(parts, axis=0)
                wanted = jnp.concatenate(wanted, axis=1)
                start = place * rows * LANES
                for t in range(rows // LANES):
                    hits = (iota((LANES, slots), 0) + t * LANES == wanted).astype(BF16)
                    total = dot(hits, values).astype(BF16)
                    for i in range(LANES // 16):
                        at = pl.multiple_of(start + t * LANES * LANES + i * 2048, 2048)
                        out_ref[0:1, pl.ds(at, 2048)] = total[i * 16 : (i + 1) * 16].reshape(1, 2048)


def place_rows(place, ids, values, points, pieces):
    chips = len(values)
    share = points // chips
    return pl.pallas_call(
        functools.partial(place_kernel, chips, pieces),
        grid_spec=pltpu.PrefetchScalarGridSpec(
            num_scalar_prefetch=1,
            grid=(chips,),
            in_specs=[pl.BlockSpec(x.shape, lambda i, place, rank=x.ndim: (0,) * rank) for x in (ids, *values)],
            out_specs=pl.BlockSpec((1, share), lambda i, place: (0, lax.rem(place[2] + i, chips))),
        ),
        out_shape=jax.ShapeDtypeStruct((1, points), BF16),
        compiler_params=PARAMS,
    )(place, ids, *values)


def body(bands, slabs, psi, beta, pair_atom, pair_block, proj_count, strength):
    chips = slabs // CORES
    atom_total, projectors = strength.shape[:2]
    padded = -(-projectors // 8) * 8
    position = lax.axis_index("slab").astype(jnp.int32)
    chip, core = position // CORES, lax.rem(position, CORES)
    place = jnp.stack([core, lax.axis_index("band").astype(jnp.int32), chip])

    def turn(x, chips_on):
        return lax.ppermute(x, "slab", [(i, (i + CORES * chips_on) % slabs) for i in range(slabs)])

    def swap(x):
        return lax.ppermute(x, "slab", [(i, i ^ 1) for i in range(slabs)])

    def across(x, bit):
        return lax.ppermute(x, "band", [(i, i ^ bit) for i in range(bands)])

    ids = jnp.concatenate([pair_block, pair_atom], axis=0).reshape(1, -1, LANES)
    ids = lax.all_to_all(jnp.broadcast_to(ids, (slabs, *ids.shape[1:])), "slab", 0, 0, tiled=True)
    rows = to_rows(psi)
    pieces = bands if beta.shape[1] % LANES == 0 and bands & (bands - 1) == 0 else 1
    if pieces > 1:
        tables = [beta[0]] + [across(beta[0], bit) for bit in range(1, bands)]
    else:
        tables = [lax.all_gather(beta[0], "band", axis=0, tiled=True)]
    picks = gather(place, ids, rows, pieces, chips)
    tables = jnp.concatenate([after(table, picks[0]) for table in tables], axis=0)
    tables = (tables, swap(tables))
    picks = [picks[0]] + [turn(picks[away], away) for away in range(1, chips)]
    coef = project(place, ids, tables, picks, projectors, padded, pieces)
    coefs = [coef] + [turn(coef, away) for away in range(1, chips)]
    count, strength = proj_count.reshape(1, atom_total), strength.transpose(1, 2, 0)
    results = back_project(place, ids, tables, count, strength, coefs, projectors, padded, pieces)
    results = [results[0]] + [turn(results[away], -away) for away in range(1, chips)]
    return place_rows(place, ids, results, psi.shape[1], pieces)


def solution(mesh):
    placed = (
        P(("band", "slab"), None),
        P("slab", "band", None),
        P("slab", None),
        P("slab", None),
        P(),
        P(),
    )
    return jax.shard_map(
        functools.partial(body, mesh.shape["band"], mesh.shape["slab"]),
        mesh=mesh,
        in_specs=placed,
        out_specs=P(("band", "slab"), None),
        check_vma=False,
    )
```

time: 120 us -> 67 us (0.56)
  waiting for transfers between devices: 62.3 us -> 25.7 us
  between operations: 13.5 us -> 0.14 us
  Pallas kernels: 22.3 us -> 14.7 us
  starting transfers between devices: 19.2 us -> 23 us
    all_gather x1 -> x0, waiting for transfers between devices: 32.4 us -> none  [body(): own_tables = lax.all_gather(beta[0], 'band', axis=0, tiled=True)]
    pallas_call x4 -> x5, Pallas kernels: 22.3 us -> 14.7 us  [the longest x1 4.28 us: place_rows(): pl.pallas_call(functools.partial(place_kernel, chips, pieces), grid_spec=...]
    ppermute x12 -> x9, waiting for transfers between devices: 29.2 us -> 22.3 us  [turn(): lax.ppermute(x, 'slab', [(i, (i + CORES * chips_on) % slabs) for i in ran...]
    ppermute x12 -> x9, starting transfers between devices: 18.8 us -> 13.1 us  [turn(): lax.ppermute(x, 'slab', [(i, (i + CORES * chips_on) % slabs) for i in ran...]
    all_to_all x0 -> x1, starting transfers between devices: none -> 5.35 us  [body(): lax.all_to_all(jnp.broadcast_to(ids, (slabs, *ids.shape[1:])), 'slab', 0,...]
    ppermute x0 -> x3, starting transfers between devices: none -> 4.46 us  [across(): return lax.ppermute(x, 'band', [(i, i ^ bit) for i in range(bands)])]
    all_to_all x0 -> x1, waiting for transfers between devices: none -> 3.41 us  [body(): lax.all_to_all(jnp.broadcast_to(ids, (slabs, *ids.shape[1:])), 'slab', 0,...]
  transfers between devices with their start and end apart: 15 -> 14, of which waited for: 7 -> 7; matrix products, arithmetic and copies ran while one was open for 1% -> 2% of each run, Pallas kernels for 13% -> 4%
where the time goes in v3:
time: 67 us; the launch traced here: 66.7 us
  waiting for transfers between devices  25.7 us (38%)
  starting transfers between devices  23 us (34%)
  Pallas kernels  14.7 us (22%)
  local copies, waits for them, and re-layouts  2.35 us (4%)
  other arithmetic  0.79 us (1%)
    ppermute x9, waiting for transfers between devices, turn(): lax.ppermute(x, 'slab', [(i, (i + CORES * chips_on) % slabs) for i in ran...  22.3 us
    ppermute x9, starting transfers between devices, turn(): lax.ppermute(x, 'slab', [(i, (i + CORES * chips_on) % slabs) for i in ran...  13.1 us
    all_to_all x1, starting transfers between devices, body(): lax.all_to_all(jnp.broadcast_to(ids, (slabs, *ids.shape[1:])), 'slab', 0,...  5.35 us
    ppermute x3, starting transfers between devices, across(): return lax.ppermute(x, 'band', [(i, i ^ bit) for i in range(bands)])  4.46 us
    pallas_call x1, Pallas kernels, place_rows(): pl.pallas_call(functools.partial(place_kernel, chips, pieces), grid_spec=...  4.28 us
    pallas_call x1, Pallas kernels, project(): pl.pallas_call(kernel, in_specs=[SMEM_SPEC] + [VMEM_SPEC] * (3 + bands),...  3.88 us
    pallas_call x1, Pallas kernels, back_project(): pl.pallas_call(kernel, in_specs=[SMEM_SPEC] + [VMEM_SPEC] * (5 + bands),...  3.84 us
    all_to_all x1, waiting for transfers between devices, body(): lax.all_to_all(jnp.broadcast_to(ids, (slabs, *ids.shape[1:])), 'slab', 0,...  3.41 us
  transfers between devices with their start and end apart: 14, of which 7 were waited for; matrix products, arithmetic and copies ran while one was open for 2% of the time, Pallas kernels for 4%

profile of v3, /device:TPU:0, one launch (start us, length us, event | category | flops | bytes accessed | tf_op | source)
XLA Modules:
  0.0 66.7 jit_solution(13690222845872840743)
XLA Ops:
  0.0 2.9 %collective-permute-start = (bf16[128,1152]{1,0:T(8,128)(2,1)}, bf16[128,1152]{1,0:T(8,128)(2,1)S(1)}, u32[]{:S(2)}, u32[]{:S(2)}) collective-permute-start(bf16[128,1152]{1,0:T(8,128)(2,1)} %bitcast.8), channel_id=1, source_target_pairs={{0,8},{8,0},{16,24},{24,16},{1,9},{9,1},{17,25},{25,17},{2,10},{10... | collective-permute-start | bytes 884744 | tf_op jit(solution)/shard_map/ppermute | solution.py:303
  2.9 1.5 %collective-permute-start.1 = (bf16[128,1152]{1,0:T(8,128)(2,1)}, bf16[128,1152]{1,0:T(8,128)(2,1)S(1)}, u32[]{:S(2)}, u32[]{:S(2)}) collective-permute-start(bf16[128,1152]{1,0:T(8,128)(2,1)} %bitcast.9), channel_id=1, source_target_pairs={{0,16},{8,24},{16,0},{24,8},{1,17},{9,25},{17,1},{25,9},{2,18},{10... | collective-permute-start | bytes 884744 | tf_op jit(solution)/shard_map/ppermute | solution.py:303
  4.5 0.0 collective-permute-start.2
  4.5 0.7 %pad_add_fusion = s32[2,512]{1,0:T(2,128)S(1)} fusion(s32[1,512]{1,0:T(1,128)} %param.8, s32[1,512]{1,0:T(1,128)} %param.9), kind=kLoop, calls=%fused_computation.4 | loop fusion | flops 1024 | bytes 8192 | tf_op jit(solution)/shard_map/concatenate | solution.py:305
  5.2 0.6 broadcast_in_dim.8
  5.8 5.4 %all-to-all-start = ((s32[8,8,128]{2,1,0:T(8,128)}), s32[8,8,128]{2,1,0:T(8,128)S(1)}, u32[]{:S(2)}, u32[]{:S(2)}) async-start(s32[8,8,128]{2,1,0:T(8,128)} %broadcast_in_dim.8), calls=%async_computation | async-start | bytes 65536 | tf_op jit(solution)/shard_map/all_to_all | solution.py:306
  11.2 0.0 copy-start
  11.2 1.6 %copy-done = bf16[1,524288]{1,0:T(2,128)(2,1)S(1)} copy-done((bf16[1,524288]{1,0:T(2,128)(2,1)S(1)}, bf16[1,524288]{1,0:T(2,128)(2,1)}, u32[]{:S(2)}) %copy-start) | copy-done | bytes 1048600
  12.7 0.6 shard_map.64.rows_ref
  13.4 0.0 copy-start.3
  13.4 0.1 pad_add_fusion.1.place_ref
  13.5 3.4 %all-to-all-done.ids_ref.refs_0_ = s32[8,8,128]{2,1,0:T(8,128)S(1)} async-done(((s32[8,8,128]{2,1,0:T(8,128)}), s32[8,8,128]{2,1,0:T(8,128)S(1)}, u32[]{:S(2)}, u32[]{:S(2)}) %all-to-all-start) | async-done | bytes 32800 | tf_op jit(solution)/shard_map/all_to_all | solution.py:306
  16.9 2.1 %shard_map.65 = (bf16[512,128]{1,0:T(8,128)(2,1)S(1)}, bf16[512,128]{1,0:T(8,128)(2,1)S(1)}, bf16[512,128]{1,0:T(8,128)(2,1)S(1)}, bf16[512,128]{1,0:T(8,128)(2,1)S(1)}) custom-call(s32[3]{0:T(128)S(1)} %pad_add_fusion.1.place_ref, s32[8,8,128]{2,1,0:T(8,128)S(1)} %all-to-all-done.ids_ref.refs_0_, bf16[4096,128]{1,0:T(8,128)(2,1)S(1)} %shard_map.64.rows_ref), custom_call_target="tpu_custom_call" | custom-call | bytes 10000000 | tf_op jit(solution)/shard_map/pallas_call | solution.py:110
  19.0 0.0 copy-done.3
  19.0 0.0 collective-permute-done
  19.0 0.0 collective-permute-done.1
  19.0 0.0 collective-permute-done.2
  19.1 0.1 collective-permute-start.3
  19.2 0.7 %collective-permute-start.4 = (bf16[512,128]{1,0:T(8,128)(2,1)S(1)}, bf16[512,128]{1,0:T(8,128)(2,1)S(1)}, u32[]{:S(2)}, u32[]{:S(2)}) collective-permute-start(bf16[512,128]{1,0:T(8,128)(2,1)S(1)} %get-tuple-element.22), channel_id=1, source_target_pairs={{0,2},{1,3},{2,4},{3,5},{4,6},{5,7},{6,0},{7,1},{8,10},{9,11},{10,... | collective-permute-start | bytes 393224 | tf_op jit(solution)/shard_map/ppermute | solution.py:297
  19.9 2.4 %collective-permute-start.5 = (bf16[512,128]{1,0:T(8,128)(2,1)S(1)}, bf16[512,128]{1,0:T(8,128)(2,1)S(1)}, u32[]{:S(2)}, u32[]{:S(2)}) collective-permute-start(bf16[512,128]{1,0:T(8,128)(2,1)S(1)} %get-tuple-element.23), channel_id=1, source_target_pairs={{0,4},{1,5},{2,6},{3,7},{4,0},{5,1},{6,2},{7,3},{8,12},{9,13},{10,... | collective-permute-start | bytes 393224 | tf_op jit(solution)/shard_map/ppermute | solution.py:297
  22.4 0.0 copy-start.1
  22.4 0.0 copy-start.2
  22.4 1.3 %collective-permute-start.6 = (bf16[512,128]{1,0:T(8,128)(2,1)S(1)}, bf16[512,128]{1,0:T(8,128)(2,1)S(1)}, u32[]{:S(2)}, u32[]{:S(2)}) collective-permute-start(bf16[512,128]{1,0:T(8,128)(2,1)S(1)} %get-tuple-element.24), channel_id=1, source_target_pairs={{0,6},{1,7},{2,0},{3,1},{4,2},{5,3},{6,4},{7,5},{8,14},{9,15},{10,... | collective-permute-start | bytes 393224 | tf_op jit(solution)/shard_map/ppermute | solution.py:297
  23.7 3.8 %collective-permute-done.4.rest_1_ = bf16[512,128]{1,0:T(8,128)(2,1)S(1)} collective-permute-done((bf16[512,128]{1,0:T(8,128)(2,1)S(1)}, bf16[512,128]{1,0:T(8,128)(2,1)S(1)}, u32[]{:S(2)}, u32[]{:S(2)}) %collective-permute-start.4) | collective-permute-done | bytes 131104 | tf_op jit(solution)/shard_map/ppermute | solution.py:297
  27.5 5.1 %collective-permute-done.5.rest_2_ = bf16[512,128]{1,0:T(8,128)(2,1)S(1)} collective-permute-done((bf16[512,128]{1,0:T(8,128)(2,1)S(1)}, bf16[512,128]{1,0:T(8,128)(2,1)S(1)}, u32[]{:S(2)}, u32[]{:S(2)}) %collective-permute-start.5) | collective-permute-done | bytes 131104 | tf_op jit(solution)/shard_map/ppermute | solution.py:297
  32.6 0.0 collective-permute-done.6.rest_3_
  32.6 0.0 collective-permute-done.3.other_ref
  32.6 3.9 %shard_map.66.rest_0_ = f32[96,128]{1,0:T(8,128)S(1)} custom-call(s32[3]{0:T(128)S(1)} %pad_add_fusion.1.place_ref, s32[8,8,128]{2,1,0:T(8,128)S(1)} %all-to-all-done.ids_ref.refs_0_, bf16[512,1152]{1,0:T(8,128)(2,1)S(1)} %constant_dynamic-update-slice_fusion.own_ref, bf16[512,1152]{1,0:T(8,128)(2,1)S(1)} %collective-permute-done.3.other_ref, ...), custom_call_target="tpu_custom_call" | custom-call | tf_op jit(solution)/shard_map/pallas_call | solution.py:168
  36.5 2.8 %collective-permute-start.7 = (f32[96,128]{1,0:T(8,128)S(1)}, f32[96,128]{1,0:T(8,128)S(1)}, u32[]{:S(2)}, u32[]{:S(2)}) collective-permute-start(f32[96,128]{1,0:T(8,128)S(1)} %shard_map.66.rest_0_), channel_id=1, source_target_pairs={{0,2},{1,3},{2,4},{3,5},{4,6},{5,7},{6,0},{7,1},{8,10},{9,11},{10,... | collective-permute-start | bytes 147464 | tf_op jit(solution)/shard_map/ppermute | solution.py:297
  39.4 1.1 %collective-permute-start.8 = (f32[96,128]{1,0:T(8,128)S(1)}, f32[96,128]{1,0:T(8,128)S(1)}, u32[]{:S(2)}, u32[]{:S(2)}) collective-permute-start(f32[96,128]{1,0:T(8,128)S(1)} %shard_map.66.rest_0_), channel_id=1, source_target_pairs={{0,4},{1,5},{2,6},{3,7},{4,0},{5,1},{6,2},{7,3},{8,12},{9,13},{10,... | collective-permute-start | bytes 147464 | tf_op jit(solution)/shard_map/ppermute | solution.py:297
  40.5 1.3 %collective-permute-start.9 = (f32[96,128]{1,0:T(8,128)S(1)}, f32[96,128]{1,0:T(8,128)S(1)}, u32[]{:S(2)}, u32[]{:S(2)}) collective-permute-start(f32[96,128]{1,0:T(8,128)S(1)} %shard_map.66.rest_0_), channel_id=1, source_target_pairs={{0,6},{1,7},{2,0},{3,1},{4,2},{5,3},{6,4},{7,5},{8,14},{9,15},{10,... | collective-permute-start | bytes 147464 | tf_op jit(solution)/shard_map/ppermute | solution.py:297
  41.8 1.2 %collective-permute-done.7.rest_1_ = f32[96,128]{1,0:T(8,128)S(1)} collective-permute-done((f32[96,128]{1,0:T(8,128)S(1)}, f32[96,128]{1,0:T(8,128)S(1)}, u32[]{:S(2)}, u32[]{:S(2)}) %collective-permute-start.7) | collective-permute-done | bytes 49184 | tf_op jit(solution)/shard_map/ppermute | solution.py:297
  43.0 2.0 %collective-permute-done.8.rest_2_ = f32[96,128]{1,0:T(8,128)S(1)} collective-permute-done((f32[96,128]{1,0:T(8,128)S(1)}, f32[96,128]{1,0:T(8,128)S(1)}, u32[]{:S(2)}, u32[]{:S(2)}) %collective-permute-start.8) | collective-permute-done | bytes 49184 | tf_op jit(solution)/shard_map/ppermute | solution.py:297
  45.1 0.0 collective-permute-done.9.rest_3_
  45.1 0.0 copy-done.1
  45.1 0.0 copy-done.2
  45.1 3.8 %shard_map.67 = (bf16[512,128]{1,0:T(8,128)(2,1)S(1)}, bf16[512,128]{1,0:T(8,128)(2,1)S(1)}, bf16[512,128]{1,0:T(8,128)(2,1)S(1)}, bf16[512,128]{1,0:T(8,128)(2,1)S(1)}) custom-call(s32[3]{0:T(128)S(1)} %pad_add_fusion.1.place_ref, s32[8,8,128]{2,1,0:T(8,128)S(1)} %all-to-all-done.ids_ref.refs_0_, ...), custom_call_target="tpu_custom_call" | custom-call | tf_op jit(solution)/shard_map/pallas_call | solution.py:226
  48.9 2.7 %collective-permute-start.10 = (bf16[512,128]{1,0:T(8,128)(2,1)S(1)}, bf16[512,128]{1,0:T(8,128)(2,1)S(1)}, u32[]{:S(2)}, u32[]{:S(2)}) collective-permute-start(bf16[512,128]{1,0:T(8,128)(2,1)S(1)} %get-tuple-element.26), channel_id=1, source_target_pairs={{0,6},{1,7},{2,0},{3,1},{4,2},{5,3},{6,4},{7,5},{8,14},{9,15},{10,... | collective-permute-start | bytes 393224 | tf_op jit(solution)/shard_map/ppermute | solution.py:297
  51.6 0.0 collective-permute-start.11
  51.6 0.7 %collective-permute-start.12 = (bf16[512,128]{1,0:T(8,128)(2,1)S(1)}, bf16[512,128]{1,0:T(8,128)(2,1)S(1)}, u32[]{:S(2)}, u32[]{:S(2)}) collective-permute-start(bf16[512,128]{1,0:T(8,128)(2,1)S(1)} %get-tuple-element.28), channel_id=1, source_target_pairs={{0,2},{1,3},{2,4},{3,5},{4,6},{5,7},{6,0},{7,1},{8,10},{9,11},{10,... | collective-permute-start | bytes 393224 | tf_op jit(solution)/shard_map/ppermute | solution.py:297
  52.3 3.2 %collective-permute-done.10.refs_2_ = bf16[512,128]{1,0:T(8,128)(2,1)S(1)} collective-permute-done((bf16[512,128]{1,0:T(8,128)(2,1)S(1)}, bf16[512,128]{1,0:T(8,128)(2,1)S(1)}, u32[]{:S(2)}, u32[]{:S(2)}) %collective-permute-start.10) | collective-permute-done | bytes 131104 | tf_op jit(solution)/shard_map/ppermute | solution.py:297
  55.6 6.9 %collective-permute-done.11.refs_3_ = bf16[512,128]{1,0:T(8,128)(2,1)S(1)} collective-permute-done((bf16[512,128]{1,0:T(8,128)(2,1)S(1)}, bf16[512,128]{1,0:T(8,128)(2,1)S(1)}, u32[]{:S(2)}, u32[]{:S(2)}) %collective-permute-start.11) | collective-permute-done | bytes 131104 | tf_op jit(solution)/shard_map/ppermute | solution.py:297
  62.4 0.0 collective-permute-done.12.refs_4_
  62.4 4.3 %shard_map.68 = bf16[1,524288]{1,0:T(2,128)(2,1)} custom-call(s32[3]{0:T(128)S(1)} %pad_add_fusion.1.place_ref, s32[8,8,128]{2,1,0:T(8,128)S(1)} %all-to-all-done.ids_ref.refs_0_, bf16[512,128]{1,0:T(8,128)(2,1)S(1)} %get-tuple-element.25.refs_1_, bf16[512,128]{1,0:T(8,128)(2,1)S(1)} %collective-permute-done.10.refs_2_, ...), custom_call_target="tpu_custom_call" | custom-call | tf_op jit(solution)/shard_map/pallas_call | solution.py:275
  (5 shorter events, 0.1 us)
Async XLA Ops:
  0.0 19.0 %collective-permute-start = (bf16[128,1152]{1,0:T(8,128)(2,1)}, bf16[128,1152]{1,0:T(8,128)(2,1)S(1)}, u32[]{:S(2)}, u32[]{:S(2)}) collective-permute-start(bf16[128,1152]{1,0:T(8,128)(2,1)} %bitcast.8), channel_id=1, source_target_pairs={{0,8},{8,0},{16,24},{24,16},{1,9},{9,1},{17,25},{25,17},{2,10},{10... | collective-permute-start | bytes 884744 | tf_op jit(solution)/shard_map/ppermute | solution.py:303
  2.9 16.1 %collective-permute-start.1 = (bf16[128,1152]{1,0:T(8,128)(2,1)}, bf16[128,1152]{1,0:T(8,128)(2,1)S(1)}, u32[]{:S(2)}, u32[]{:S(2)}) collective-permute-start(bf16[128,1152]{1,0:T(8,128)(2,1)} %bitcast.9), channel_id=1, source_target_pairs={{0,16},{8,24},{16,0},{24,8},{1,17},{9,25},{17,1},{25,9},{2,18},{10... | collective-permute-start | bytes 884744 | tf_op jit(solution)/shard_map/ppermute | solution.py:303
  4.5 14.6 %collective-permute-start.2 = (bf16[128,1152]{1,0:T(8,128)(2,1)}, bf16[128,1152]{1,0:T(8,128)(2,1)S(1)}, u32[]{:S(2)}, u32[]{:S(2)}) collective-permute-start(bf16[128,1152]{1,0:T(8,128)(2,1)} %bitcast.10), channel_id=1, source_target_pairs={{0,24},{8,16},{16,8},{24,0},{1,25},{9,17},{17,9},{25,1},{2,26},{10... | collective-permute-start | bytes 884744 | tf_op jit(solution)/shard_map/ppermute | solution.py:303
  5.8 11.1 %all-to-all-start = ((s32[8,8,128]{2,1,0:T(8,128)}), s32[8,8,128]{2,1,0:T(8,128)S(1)}, u32[]{:S(2)}, u32[]{:S(2)}) async-start(s32[8,8,128]{2,1,0:T(8,128)} %broadcast_in_dim.8), calls=%async_computation | async-start | bytes 65536 | tf_op jit(solution)/shard_map/all_to_all | solution.py:306
  11.2 1.6 %copy-start = (bf16[1,524288]{1,0:T(2,128)(2,1)S(1)}, bf16[1,524288]{1,0:T(2,128)(2,1)}, u32[]{:S(2)}) copy-start(bf16[1,524288]{1,0:T(2,128)(2,1)} %psi_ref.1) | copy-start | bytes 3145732
  13.4 5.6 %copy-start.3 = (bf16[1,128,1152]{2,1,0:T(8,128)(2,1)S(1)}, bf16[1,128,1152]{2,1,0:T(8,128)(2,1)}, u32[]{:S(2)}) copy-start(bf16[1,128,1152]{2,1,0:T(8,128)(2,1)} %param.7) | copy-start | bytes 884740
  19.1 13.5 %collective-permute-start.3 = (bf16[512,1152]{1,0:T(8,128)(2,1)S(1)}, bf16[512,1152]{1,0:T(8,128)(2,1)S(1)}, u32[]{:S(2)}, u32[]{:S(2)}) collective-permute-start(bf16[512,1152]{1,0:T(8,128)(2,1)S(1)} %constant_dynamic-update-slice_fusion.own_ref), channel_id=1, source_target_pairs={{0,1},{1,0},{2,3},{3,2},{4,5},{5,4},{6,7},{7,6},{8,9},{9,8},{10,11... | collective-permute-start | bytes 3538952 | tf_op jit(solution)/shard_map/ppermute | solution.py:300
  19.2 8.3 %collective-permute-start.4 = (bf16[512,128]{1,0:T(8,128)(2,1)S(1)}, bf16[512,128]{1,0:T(8,128)(2,1)S(1)}, u32[]{:S(2)}, u32[]{:S(2)}) collective-permute-start(bf16[512,128]{1,0:T(8,128)(2,1)S(1)} %get-tuple-element.22), channel_id=1, source_target_pairs={{0,2},{1,3},{2,4},{3,5},{4,6},{5,7},{6,0},{7,1},{8,10},{9,11},{10,... | collective-permute-start | bytes 393224 | tf_op jit(solution)/shard_map/ppermute | solution.py:297
  19.9 12.7 %collective-permute-start.5 = (bf16[512,128]{1,0:T(8,128)(2,1)S(1)}, bf16[512,128]{1,0:T(8,128)(2,1)S(1)}, u32[]{:S(2)}, u32[]{:S(2)}) collective-permute-start(bf16[512,128]{1,0:T(8,128)(2,1)S(1)} %get-tuple-element.23), channel_id=1, source_target_pairs={{0,4},{1,5},{2,6},{3,7},{4,0},{5,1},{6,2},{7,3},{8,12},{9,13},{10,... | collective-permute-start | bytes 393224 | tf_op jit(solution)/shard_map/ppermute | solution.py:297
  22.4 22.7 %copy-start.1 = (f32[128,18,18]{0,2,1:T(8,128)S(1)}, f32[128,18,18]{0,2,1:T(8,128)}, u32[]{:S(2)}) copy-start(f32[128,18,18]{0,2,1:T(8,128)} %param.11) | copy-start | bytes 497668
  22.4 22.7 %copy-start.2 = (s32[128]{0:T(128)S(1)}, s32[128]{0:T(128)}, u32[]{:S(2)}) copy-start(s32[128]{0:T(128)} %param.10) | copy-start | bytes 1540
  22.4 10.3 %collective-permute-start.6 = (bf16[512,128]{1,0:T(8,128)(2,1)S(1)}, bf16[512,128]{1,0:T(8,128)(2,1)S(1)}, u32[]{:S(2)}, u32[]{:S(2)}) collective-permute-start(bf16[512,128]{1,0:T(8,128)(2,1)S(1)} %get-tuple-element.24), channel_id=1, source_target_pairs={{0,6},{1,7},{2,0},{3,1},{4,2},{5,3},{6,4},{7,5},{8,14},{9,15},{10,... | collective-permute-start | bytes 393224 | tf_op jit(solution)/shard_map/ppermute | solution.py:297
  36.5 6.5 %collective-permute-start.7 = (f32[96,128]{1,0:T(8,128)S(1)}, f32[96,128]{1,0:T(8,128)S(1)}, u32[]{:S(2)}, u32[]{:S(2)}) collective-permute-start(f32[96,128]{1,0:T(8,128)S(1)} %shard_map.66.rest_0_), channel_id=1, source_target_pairs={{0,2},{1,3},{2,4},{3,5},{4,6},{5,7},{6,0},{7,1},{8,10},{9,11},{10,... | collective-permute-start | bytes 147464 | tf_op jit(solution)/shard_map/ppermute | solution.py:297
  39.4 5.7 %collective-permute-start.8 = (f32[96,128]{1,0:T(8,128)S(1)}, f32[96,128]{1,0:T(8,128)S(1)}, u32[]{:S(2)}, u32[]{:S(2)}) collective-permute-start(f32[96,128]{1,0:T(8,128)S(1)} %shard_map.66.rest_0_), channel_id=1, source_target_pairs={{0,4},{1,5},{2,6},{3,7},{4,0},{5,1},{6,2},{7,3},{8,12},{9,13},{10,... | collective-permute-start | bytes 147464 | tf_op jit(solution)/shard_map/ppermute | solution.py:297
  40.5 4.6 %collective-permute-start.9 = (f32[96,128]{1,0:T(8,128)S(1)}, f32[96,128]{1,0:T(8,128)S(1)}, u32[]{:S(2)}, u32[]{:S(2)}) collective-permute-start(f32[96,128]{1,0:T(8,128)S(1)} %shard_map.66.rest_0_), channel_id=1, source_target_pairs={{0,6},{1,7},{2,0},{3,1},{4,2},{5,3},{6,4},{7,5},{8,14},{9,15},{10,... | collective-permute-start | bytes 147464 | tf_op jit(solution)/shard_map/ppermute | solution.py:297
  48.9 6.6 %collective-permute-start.10 = (bf16[512,128]{1,0:T(8,128)(2,1)S(1)}, bf16[512,128]{1,0:T(8,128)(2,1)S(1)}, u32[]{:S(2)}, u32[]{:S(2)}) collective-permute-start(bf16[512,128]{1,0:T(8,128)(2,1)S(1)} %get-tuple-element.26), channel_id=1, source_target_pairs={{0,6},{1,7},{2,0},{3,1},{4,2},{5,3},{6,4},{7,5},{8,14},{9,15},{10,... | collective-permute-start | bytes 393224 | tf_op jit(solution)/shard_map/ppermute | solution.py:297
  51.6 10.8 %collective-permute-start.11 = (bf16[512,128]{1,0:T(8,128)(2,1)S(1)}, bf16[512,128]{1,0:T(8,128)(2,1)S(1)}, u32[]{:S(2)}, u32[]{:S(2)}) collective-permute-start(bf16[512,128]{1,0:T(8,128)(2,1)S(1)} %get-tuple-element.27), channel_id=1, source_target_pairs={{0,4},{1,5},{2,6},{3,7},{4,0},{5,1},{6,2},{7,3},{8,12},{9,13},{10,... | collective-permute-start | bytes 393224 | tf_op jit(solution)/shard_map/ppermute | solution.py:297
  51.6 10.8 %collective-permute-start.12 = (bf16[512,128]{1,0:T(8,128)(2,1)S(1)}, bf16[512,128]{1,0:T(8,128)(2,1)S(1)}, u32[]{:S(2)}, u32[]{:S(2)}) collective-permute-start(bf16[512,128]{1,0:T(8,128)(2,1)S(1)} %get-tuple-element.28), channel_id=1, source_target_pairs={{0,2},{1,3},{2,4},{3,5},{4,6},{5,7},{6,0},{7,1},{8,10},{9,11},{10,... | collective-permute-start | bytes 393224 | tf_op jit(solution)/shard_map/ppermute | solution.py:297

commit v4 on v0

--- a/solution.py
+++ b/solution.py
@@ -1,10 +1,367 @@
+import functools
+
 import jax
 import jax.numpy as jnp
 from jax import lax
+from jax.experimental import pallas as pl
+from jax.experimental.pallas import tpu as pltpu
 from jax.sharding import PartitionSpec as P
 
-
-def project(grid_blocks, tables, atom_ids, block_ids, atom_total):
+CORES = 2
+LANES = 128
+CHIPS = 4
+PARTNERS = 4
+PIECES = 4
+GROUP = 16
+HALVES = 2
+GATHER_BYTES = 10_000_000
+PROJECT_BYTES = 30_000_000
+F32 = jnp.float32
+BF16 = jnp.bfloat16
+VMEM_SPEC = pl.BlockSpec(memory_space=pltpu.VMEM)
+SMEM_SPEC = pl.BlockSpec(memory_space=pltpu.SMEM)
+PARAMS = pltpu.CompilerParams(vmem_limit_bytes=40 * 1024 * 1024)
+
+
+def dot(a, b, contract=((1,), (0,))):
+    return lax.dot_general(a, b, (contract, ((), ())), preferred_element_type=F32)
+
+
+def two_terms(x):
+    high = x.astype(BF16)
+    return high, (x - high.astype(F32)).astype(BF16)
+
+
+def after(x, *others):
+    return lax.optimization_barrier((x, *others))[0]
+
+
+def iota(shape, axis):
+    return lax.broadcasted_iota(jnp.int32, shape, axis)
+
+
+def slab_index(place_ref, turned, slab):
+    core = place_ref[0] if slab == 0 else CORES - 1 - place_ref[0]
+    return jnp.bitwise_xor(place_ref[2], turned) * CORES + core
+
+
+def owner(turned_chip, turned_column):
+    return (turned_chip & 1) | (turned_column & 2), (turned_chip & 2) | (turned_column & 1)
+
+
+def pieces_of(half_index):
+    return range(half_index * PIECES // HALVES, (half_index + 1) * PIECES // HALVES)
+
+
+def slot_ids(ids_ref, place_ref, slab, turned_chip, turned_column, kind):
+    slot_rows = ids_ref.shape[1] // 2
+    share = slot_rows // PARTNERS
+    index = slab_index(place_ref, turned_chip, slab)
+    first = kind * slot_rows + jnp.bitwise_xor(place_ref[1], turned_column) * share
+    return [ids_ref[index, pl.ds(first + i, 1), :] for i in range(share)]
+
+
+def atom_hits(ids_ref, place_ref, slab, pieces):
+    lane = iota((LANES, LANES), 1)
+    for piece in pieces:
+        for atoms in slot_ids(ids_ref, place_ref, slab, piece & 2, piece & 1, 1):
+            yield (down(atoms) == lane).astype(BF16)
+
+
+def down(ids):
+    return jnp.transpose(jnp.broadcast_to(ids, (LANES, LANES)))
+
+
+def rows_kernel(psi_ref, out_ref):
+    def move(i, carry):
+        part = psi_ref[0:1, pl.ds(pl.multiple_of(i * 2048, 2048), 2048)]
+        out_ref[pl.ds(pl.multiple_of(i * 16, 16), 16), :] = part.reshape(16, LANES)
+        return carry
+
+    lax.fori_loop(0, out_ref.shape[0] // 16, move, 0, unroll=8)
+
+
+def to_rows(psi):
+    rows = psi.shape[1] // LANES
+    return pl.pallas_call(
+        rows_kernel,
+        in_specs=[VMEM_SPEC],
+        out_specs=VMEM_SPEC,
+        out_shape=jax.ShapeDtypeStruct((rows, LANES), BF16),
+        compiler_params=PARAMS,
+    )(psi)
+
+
+def gather_kernel(place_ref, ids_ref, rows_ref, out_refs):
+    half = LANES // 2
+    slab_rows = rows_ref.shape[0] // (CORES * CHIPS)
+    lane = iota((LANES, LANES), 1)
+    low = iota((half, LANES), 1) < half
+    for chip in range(CHIPS):
+        for slab in range(CORES):
+            index = slab_index(place_ref, chip, slab)
+            odds, hits, places = [], [], []
+            for column in range(PARTNERS):
+                partner, piece = owner(chip, column)
+                ids = slot_ids(ids_ref, place_ref, slab, chip, column, 0)
+                for i, row in enumerate(ids):
+                    blocks = down(row)
+                    wanted = jnp.right_shift(blocks, 1)
+                    odds.append(jnp.bitwise_and(blocks, 1) == 1)
+                    hits.append(
+                        jnp.concatenate([(wanted - t * LANES == lane).astype(BF16) for t in range(slab_rows // LANES)], axis=1)
+                    )
+                    places.append((out_refs[partner], ((slab * PIECES + piece) * len(ids) + i) * half))
+            first_row = pl.multiple_of(index * slab_rows, slab_rows)
+            picked = dot(jnp.concatenate(hits, axis=0), rows_ref[pl.ds(first_row, slab_rows), :])
+            for i, (odd, (out_ref, first)) in enumerate(zip(odds, places)):
+                straight = picked[i * LANES : (i + 1) * LANES]
+                turned = pltpu.roll(straight, half, 1)
+                lower = jnp.where(odd, turned, straight)[:half]
+                upper = jnp.where(odd, straight, turned)[half:]
+                out_ref[first : first + half, :] = jnp.where(low, lower, upper).astype(BF16)
+
+
+def gather(place, ids, rows):
+    slots = CORES * PIECES * ids.shape[1] // 2 * LANES // PARTNERS
+
+    def kernel(place_ref, ids_ref, rows_ref, *out_refs):
+        gather_kernel(place_ref, ids_ref, rows_ref, out_refs)
+
+    return pl.pallas_call(
+        kernel,
+        in_specs=[SMEM_SPEC] + [VMEM_SPEC] * 2,
+        out_specs=[VMEM_SPEC] * PARTNERS,
+        out_shape=[jax.ShapeDtypeStruct((slots // 2, LANES), BF16)] * PARTNERS,
+        cost_estimate=pl.CostEstimate(flops=0, bytes_accessed=GATHER_BYTES, transcendentals=0),
+        compiler_params=PARAMS,
+    )(place, ids, rows)
+
+
+def project_kernel(projectors, padded, half_index, place_ref, ids_ref, table_refs, packed_refs, before_refs, coef_ref, picks_of, highs, rests):
+    bands = len(packed_refs)
+    slots = table_refs[0].shape[0]
+    pair_count = projectors // 2
+    wide = 2 * bands * GROUP
+    low = iota((bands * GROUP, LANES), 1) < LANES // 2
+    source = iota((pair_count * wide, bands * padded), 0) // GROUP
+    target = iota((pair_count * wide, bands * padded), 1)
+    gather_lanes = (target == lax.rem(source, bands) * padded + source // bands).astype(BF16)
+    diagonal = lax.rem(iota((GROUP, wide), 0), GROUP) == lax.rem(iota((GROUP, wide), 1), GROUP)
+    none = jnp.zeros((bands * GROUP, LANES), BF16)
+    half = LANES // 2
+    left = iota((half, LANES), 1) < half
+    for band, packed_ref in enumerate(packed_refs):
+        for i in range(CORES * slots // LANES):
+            slab, block = divmod(i, slots // LANES)
+            first = ((slab * HALVES + half_index) * (slots // LANES) + block) * half
+            straight = packed_ref[first : first + half, :].astype(F32)
+            turned = pltpu.roll(straight, half, 1)
+            picks_of[band, i * LANES : i * LANES + half, :] = jnp.where(left, straight, turned).astype(BF16)
+            picks_of[band, i * LANES + half : (i + 1) * LANES, :] = jnp.where(left, turned, straight).astype(BF16)
+    total = before_refs[0][...] if before_refs else None
+    for slab, table_ref in enumerate(table_refs):
+        of_atom = jnp.concatenate(list(atom_hits(ids_ref, place_ref, slab, pieces_of(half_index))), axis=0)
+        for group in range(slots // GROUP):
+            rows = slice(group * GROUP, (group + 1) * GROUP)
+            picked = slice(slab * slots + group * GROUP, slab * slots + (group + 1) * GROUP)
+            picks = jnp.concatenate([picks_of[band, picked, :] for band in range(bands)], axis=0)
+            values = jnp.concatenate([jnp.where(low, picks, none), jnp.where(low, none, picks)], axis=0)
+            tables = jnp.concatenate([table_ref[rows, t * LANES : (t + 1) * LANES] for t in range(pair_count)], axis=0)
+            crossed = dot(tables, values, ((1,), (1,)))
+            for t in range(pair_count):
+                kept = jnp.where(diagonal, crossed[t * GROUP : (t + 1) * GROUP], 0.0)
+                highs[rows, t * wide : (t + 1) * wide], rests[rows, t * wide : (t + 1) * wide] = two_terms(kept)
+        slot_coef = dot(highs[...], gather_lanes) + dot(rests[...], gather_lanes)
+        high, rest = two_terms(slot_coef)
+        summed = dot(high, of_atom, ((0,), (0,))) + dot(rest, of_atom, ((0,), (0,)))
+        total = summed if total is None else total + summed
+    coef_ref[...] = total
+
+
+def project(place, ids, tables, picks, projectors, padded, half_index, before):
+    bands = len(picks)
+    slots = tables[0].shape[0]
+    width = projectors * bands * GROUP
+
+    def kernel(place_ref, ids_ref, own_ref, other_ref, *rest):
+        ends = [bands, bands + len(before)]
+        project_kernel(
+            projectors, padded, half_index, place_ref, ids_ref, (own_ref, other_ref),
+            rest[: ends[0]], rest[ends[0] : ends[1]], *rest[ends[1] :],
+        )
+
+    return pl.pallas_call(
+        kernel,
+        in_specs=[SMEM_SPEC] + [VMEM_SPEC] * (3 + bands + len(before)),
+        out_specs=VMEM_SPEC,
+        out_shape=jax.ShapeDtypeStruct((bands * padded, LANES), F32),
+        scratch_shapes=[pltpu.VMEM((bands, CORES * slots, LANES), BF16)] + [pltpu.VMEM((slots, width), BF16)] * 2,
+        cost_estimate=pl.CostEstimate(flops=0, bytes_accessed=PROJECT_BYTES, transcendentals=0),
+        compiler_params=PARAMS,
+    )(place, ids, *tables, *picks, *before)
+
+
+def apply_kernel(wanted, projectors, padded, place_ref, ids_ref, table_refs, count_ref, strength_ref, coef_refs, out_refs, wide_refs):
+    pair_count = projectors // 2
+    width = projectors * LANES // 2
+    atom_total = strength_ref.shape[2]
+    half = LANES // 2
+    low = iota((half, LANES), 1) < half
+    valid = (iota((projectors, atom_total), 0) < count_ref[...]).astype(F32)
+    spread = (iota((projectors, width), 0) == iota((projectors, width), 1) // half).astype(BF16)
+    for band, wide_ref in zip(wanted, wide_refs):
+        total = coef_refs[0][band * padded : band * padded + projectors, :]
+        for away in range(1, PARTNERS):
+            first = (band ^ away) * padded
+            total = total + coef_refs[away][first : first + projectors, :]
+        total = total * valid
+        coupled = strength_ref[:, 0, :] * total[0:1]
+        for q in range(1, projectors):
+            coupled = coupled + strength_ref[:, q, :] * total[q : q + 1]
+        scaled = (coupled * valid).astype(BF16)
+        wide_ref[...] = dot(scaled, spread, ((0,), (0,))).astype(BF16)
+    for slab in range(CORES):
+        for half_index in range(HALVES):
+            table_ref = table_refs[half_index * CORES + slab]
+            blocks = table_ref.shape[0] // LANES
+            for i, of_atom in enumerate(atom_hits(ids_ref, place_ref, slab, pieces_of(half_index))):
+                rows = slice(i * LANES, (i + 1) * LANES)
+                first = ((slab * HALVES + half_index) * blocks + i) * half
+                for wide_ref, out_ref in zip(wide_refs, out_refs):
+                    total = None
+                    for t in range(pair_count):
+                        tile = slice(t * LANES, (t + 1) * LANES)
+                        term = dot(of_atom, wide_ref[:, tile]) * table_ref[rows, tile].astype(F32)
+                        total = term if total is None else total + term
+                    total = total + pltpu.roll(total, half, 1)
+                    packed = jnp.where(low, total[:half], total[half:])
+                    out_ref[first : first + half, :] = packed.astype(BF16)
+
+
+def back_project(wanted, place, ids, tables, count, strength, coefs, projectors, padded):
+    slots = sum(table.shape[0] for table in tables)
+    atom_total = strength.shape[2]
+
+    def kernel(place_ref, ids_ref, count_ref, strength_ref, *rest):
+        ends = [len(tables), len(tables) + len(coefs), len(tables) + len(coefs) + len(wanted)]
+        apply_kernel(
+            wanted, projectors, padded, place_ref, ids_ref, rest[: ends[0]], count_ref, strength_ref,
+            rest[ends[0] : ends[1]], rest[ends[1] : ends[2]], rest[ends[2] :],
+        )
+
+    return pl.pallas_call(
+        kernel,
+        in_specs=[SMEM_SPEC] + [VMEM_SPEC] * (3 + len(tables) + len(coefs)),
+        out_specs=[VMEM_SPEC] * len(wanted),
+        out_shape=[jax.ShapeDtypeStruct((slots // 2, LANES), BF16)] * len(wanted),
+        scratch_shapes=[pltpu.VMEM((atom_total, projectors * LANES // 2), BF16)] * len(wanted),
+        compiler_params=PARAMS,
+    )(place, ids, count, strength, *tables, *coefs)
+
+
+def place_kernel(chips, wanted, place_ref, *refs):
+    ids_ref, value_refs, out_ref = refs[0], dict(zip(wanted, refs[1:])), refs[-1]
+    step = pl.program_id(0)
+    half = LANES // 2
+    rows = out_ref.shape[1] // LANES // CORES
+    low = iota((half, LANES), 1) < half
+    for number, chip in enumerate(chips):
+
+        @pl.when(step == number)
+        def _(chip=chip):
+            for slab in range(CORES):
+                place = place_ref[0] if slab == 0 else CORES - 1 - place_ref[0]
+                parts, wanted = [], []
+                for column in range(PARTNERS):
+                    partner, piece = owner(chip, column)
+                    ids = slot_ids(ids_ref, place_ref, slab, chip, column, 0)
+                    for i, blocks in enumerate(ids):
+                        wanted.append(jnp.right_shift(blocks, 1))
+                        odd = jnp.bitwise_and(down(blocks), 1) == 1
+                        first = ((slab * PIECES + piece) * len(ids) + i) * half
+                        value = value_refs[partner][first : first + half, :].astype(F32)
+                        turned = pltpu.roll(value, half, 1)
+                        odd_a, odd_b = odd[:half], odd[half:]
+                        part_a = jnp.where(odd_a, turned, value)
+                        part_b = jnp.where(odd_b, value, turned)
+                        parts.append(jnp.where(low != odd_a, part_a, 0.0).astype(BF16))
+                        parts.append(jnp.where(low != odd_b, part_b, 0.0).astype(BF16))
+                values = jnp.concatenate(parts, axis=0)
+                wanted = jnp.concatenate(wanted, axis=1)
+                start = place * rows * LANES
+                for t in range(rows // LANES):
+                    hits = (iota((LANES, wanted.shape[1]), 0) + t * LANES == wanted).astype(BF16)
+                    total = dot(hits, values).astype(BF16)
+                    for i in range(LANES // 16):
+                        at = pl.multiple_of(start + t * LANES * LANES + i * 2048, 2048)
+                        out_ref[0:1, pl.ds(at, 2048)] = total[i * 16 : (i + 1) * 16].reshape(1, 2048)
+
+
+def place_rows(chips, place, ids, values, points, before):
+    share = points // CHIPS
+    wanted = tuple(values)
+    small = (ids, *values.values())
+    apart = chips[1] ^ chips[0]
+    return pl.pallas_call(
+        functools.partial(place_kernel, chips, wanted),
+        grid_spec=pltpu.PrefetchScalarGridSpec(
+            num_scalar_prefetch=1,
+            grid=(len(chips),),
+            in_specs=[pl.BlockSpec(x.shape, lambda i, place, rank=x.ndim: (0,) * rank) for x in small]
+            + [pl.BlockSpec(memory_space=pl.ANY)] * len(before),
+            out_specs=pl.BlockSpec((1, share), lambda i, place: (0, jnp.bitwise_xor(place[2], chips[0] + i * apart))),
+        ),
+        out_shape=jax.ShapeDtypeStruct((1, points), BF16),
+        input_output_aliases={1 + len(small): 0} if before else {},
+        compiler_params=PARAMS,
+    )(place, *small, *before)
+
+
+def body(columns, slabs, psi, beta, pair_atom, pair_block, proj_count, strength):
+    atom_total, projectors = strength.shape[:2]
+    padded = -(-projectors // 8) * 8
+    position = lax.axis_index("slab").astype(jnp.int32)
+    place = jnp.stack([lax.rem(position, CORES), lax.axis_index("band").astype(jnp.int32), position // CORES])
+
+    def exchange(x, chip=0, column=0, core=0):
+        turned = chip * CORES + core
+        if column == 0:
+            return lax.ppermute(x, "slab", [(i, i ^ turned) for i in range(slabs)])
+        if turned == 0:
+            return lax.ppermute(x, "band", [(i, i ^ column) for i in range(columns)])
+        pairs = [(i, i ^ (column * slabs + turned)) for i in range(columns * slabs)]
+        return lax.ppermute(x, ("band", "slab"), pairs)
+
+    def partners(parts):
+        return [parts[0]] + [exchange(parts[i], chip=i & 1, column=i & 2) for i in range(1, PARTNERS)]
+
+    ids = jnp.concatenate([pair_block, pair_atom], axis=0).reshape(1, -1, LANES)
+    ids = lax.all_to_all(jnp.broadcast_to(ids, (slabs, *ids.shape[1:])), "slab", 0, 0, tiled=True)
+    rows = to_rows(psi)
+    beside = exchange(beta[0], column=1)
+    above = exchange(beta[0], chip=2)
+    corner = exchange(above, column=1)
+    picks = gather(place, ids, rows)
+    shape = (projectors, padded)
+    first = jnp.concatenate([after(table, picks[0]) for table in (beta[0], beside)], axis=0)
+    picks = partners(picks)
+    first = (first, exchange(first, core=1))
+    coef = project(place, ids, first, picks, *shape, 0, ())
+    second = jnp.concatenate([after(table, *picks[1:]) for table in (above, corner)], axis=0)
+    second = (second, exchange(second, core=1))
+    coef = project(place, ids, second, picks, *shape, 1, (coef,))
+    coefs = partners([coef] * PARTNERS)
+    count, strength = proj_count.reshape(1, atom_total), strength.transpose(1, 2, 0)
+    given = (place, ids, first + second, count, strength, coefs, *shape)
+    outer = back_project((3, 1), *given)
+    inner = back_project((2, 0), *given)
+    results = partners([inner[1], outer[1], inner[0], outer[0]])
+    applied = place_rows((1, 3), place, ids, {1: results[1], 3: results[3]}, psi.shape[1], ())
+    return place_rows((0, 2), place, ids, {0: results[0], 2: results[2]}, psi.shape[1], (applied,))
+
+
+def plain_project(grid_blocks, tables, atom_ids, block_ids, atom_total):
     picked = jnp.take(grid_blocks, block_ids, axis=1)
     products = jnp.einsum("bkg,kpg->kpb", picked, tables, preferred_element_type=jnp.float32)
     slot_total = products.shape[0]
@@ -21,7 +378,7 @@
     return (coupled * proj_valid[:, :, None]).astype(jnp.bfloat16)
 
 
-def back_project(scaled, tables, atom_ids, block_ids, block_total):
+def plain_back_project(scaled, tables, atom_ids, block_ids, block_total):
     padded = jnp.concatenate([scaled, jnp.zeros((1,) + scaled.shape[1:], jnp.bfloat16)], axis=0)
     picked = jnp.take(padded, atom_ids, axis=0)
     products = jnp.einsum("kpg,kpb->kbg", tables, picked, preferred_element_type=jnp.float32)
@@ -30,7 +387,7 @@
     return summed.transpose(1, 0, 2).reshape(band_rows, -1).astype(jnp.bfloat16)
 
 
-def body(psi, beta, pair_atom, pair_block, proj_count, strength):
+def plain_body(psi, beta, pair_atom, pair_block, proj_count, strength):
     atom_total = strength.shape[0]
     proj_total = strength.shape[1]
     block_size = beta.shape[2] // proj_total
@@ -46,10 +403,10 @@
     tables = slab_tables.reshape(slot_count, proj_total, block_size)
     atom_ids = pair_atom.reshape(slot_count)
     block_ids = pair_block.reshape(slot_count)
-    coef_part = project(grid_blocks, tables, atom_ids, block_ids, atom_total)
+    coef_part = plain_project(grid_blocks, tables, atom_ids, block_ids, atom_total)
     coef_total = lax.psum(coef_part, "slab")
     scaled = apply_strength(coef_total, strength, proj_valid)
-    slab_applied = back_project(scaled, tables, atom_ids, block_ids, block_local)
+    slab_applied = plain_back_project(scaled, tables, atom_ids, block_ids, block_local)
     return lax.all_to_all(slab_applied, "slab", split_axis=0, concat_axis=1, tiled=True)
 
 
@@ -62,6 +419,17 @@
         P(),
         P(),
     )
+    columns, slabs = mesh.shape["band"], mesh.shape["slab"]
+
+    def chosen(*args):
+        if (columns, slabs) == (PARTNERS, CORES * CHIPS) and args[1].shape[1] % LANES == 0:
+            return body(columns, slabs, *args)
+        return plain_body(*args)
+
     return jax.shard_map(
-        body, mesh=mesh, in_specs=placed, out_specs=P(("band", "slab"), None), check_vma=False
+        chosen,
+        mesh=mesh,
+        in_specs=placed,
+        out_specs=P(("band", "slab"), None),
+        check_vma=False,
     )

time: 269 us -> 60.7 us (0.23)
  other arithmetic: 68.5 us -> 0.79 us
  waiting for transfers between devices: 80.5 us -> 17.4 us
  local copies, waits for them, and re-layouts: 52.5 us -> 2.34 us
  blocking collectives: 31.6 us -> 0 us
  Pallas kernels: 0 us -> 18.5 us
  starting transfers between devices: 6.58 us -> 21.3 us
  matrix products: 13.9 us -> 0 us
  between operations: 13.6 us -> 0.16 us
    psum x1 -> x0, waiting for transfers between devices: 50 us -> none  [body(): coef_total = lax.psum(coef_part, 'slab')]
    scatter-add x1 -> x0, other arithmetic: 49.8 us -> none  [back_project(): summed = jax.ops.segment_sum(products, block_ids, num_segments=block_total)]
    all_to_all x1 -> x0, blocking collectives: 31.6 us -> none  [body(): lax.all_to_all(slab_applied, 'slab', split_axis=0, concat_axis=1, tiled=T...]
    all_gather x1 -> x0, waiting for transfers between devices: 30.4 us -> none  [body(): slab_tables = lax.all_gather(beta, 'band', axis=1, tiled=True)]
    pallas_call x0 -> x8, Pallas kernels: none -> 18.5 us  [the longest x2 5.53 us: place_rows(): pl.pallas_call(functools.partial(place_kernel, chips, wanted), grid_spec=...]
    ppermute x0 -> x14, starting transfers between devices: none -> 17.9 us  [the longest x6 7.44 us: exchange(): return lax.ppermute(x, 'slab', [(i, i ^ turned) for i in range(slabs)])]
    dot_general x4 -> x0, matrix products: 13.9 us -> none  [the longest x1 4.12 us: apply_strength(): jnp.einsum('apq,aqb->apb', strength, masked, precision=lax.Precision.HIGH...]
    unnamed x19 -> x10, local copies, waits for them, and re-layouts: 15.3 us -> 1.65 us
  transfers between devices with their start and end apart: 3 -> 15, of which waited for: 2 -> 10; matrix products, arithmetic and copies ran while one was open for 2% -> 3% of each run, Pallas kernels for 0% -> 18%
where the time goes in v4:
time: 60.7 us; the launch traced here: 60.4 us
  starting transfers between devices  21.3 us (35%)
  Pallas kernels  18.5 us (30%)
  waiting for transfers between devices  17.4 us (29%)
  local copies, waits for them, and re-layouts  2.34 us (4%)
  other arithmetic  0.79 us (1%)
    ppermute x6, starting transfers between devices, exchange(): return lax.ppermute(x, 'slab', [(i, i ^ turned) for i in range(slabs)])  7.44 us
    all_to_all x1, waiting for transfers between devices, body(): lax.all_to_all(jnp.broadcast_to(ids, (slabs, *ids.shape[1:])), 'slab', 0,...  5.75 us
    ppermute x5, starting transfers between devices, exchange(): return lax.ppermute(x, 'band', [(i, i ^ column) for i in range(columns)])  5.71 us
    pallas_call x2, Pallas kernels, place_rows(): pl.pallas_call(functools.partial(place_kernel, chips, wanted), grid_spec=...  5.53 us
    pallas_call x2, Pallas kernels, project(): pl.pallas_call(kernel, in_specs=[SMEM_SPEC] + [VMEM_SPEC] * (3 + bands +...  5.51 us
    ppermute x3, waiting for transfers between devices, exchange(): return lax.ppermute(x, ('band', 'slab'), pairs)  5.17 us
    ppermute x3, starting transfers between devices, exchange(): return lax.ppermute(x, ('band', 'slab'), pairs)  4.8 us
    pallas_call x2, Pallas kernels, back_project(): pl.pallas_call(kernel, in_specs=[SMEM_SPEC] + [VMEM_SPEC] * (3 + len(tabl...  4.77 us
  transfers between devices with their start and end apart: 15, of which 10 were waited for; matrix products, arithmetic and copies ran while one was open for 3% of the time, Pallas kernels for 18%

profile of v4, /device:TPU:0, one launch (start us, length us, event | category | flops | bytes accessed | tf_op | source)
XLA Modules:
  0.0 60.4 jit_solution(7452176663828555215)
XLA Ops:
  0.0 4.0 %collective-permute-start.2 = (bf16[128,1152]{1,0:T(8,128)(2,1)}, bf16[128,1152]{1,0:T(8,128)(2,1)S(1)}, u32[]{:S(2)}, u32[]{:S(2)}) collective-permute-start(bf16[128,1152]{1,0:T(8,128)(2,1)} %bitcast.10), channel_id=1, source_target_pairs={{0,4},{1,5},{2,6},{3,7},{4,0},{5,1},{6,2},{7,3},{8,12},{9,13},{10,... | collective-permute-start | bytes 884744 | tf_op jit(solution)/shard_map/ppermute | solution.py:330
  4.0 1.5 %collective-permute-start = (bf16[128,1152]{1,0:T(8,128)(2,1)}, bf16[128,1152]{1,0:T(8,128)(2,1)S(1)}, u32[]{:S(2)}, u32[]{:S(2)}) collective-permute-start(bf16[128,1152]{1,0:T(8,128)(2,1)} %bitcast.11), channel_id=1, source_target_pairs={{0,8},{8,0},{16,24},{24,16},{1,9},{9,1},{17,25},{25,17},{2,10},{10... | collective-permute-start | bytes 884744 | tf_op jit(solution)/shard_map/ppermute | solution.py:332
  5.5 0.7 %pad_add_fusion = s32[2,512]{1,0:T(2,128)S(1)} fusion(s32[1,512]{1,0:T(1,128)} %param.8, s32[1,512]{1,0:T(1,128)} %param.9), kind=kLoop, calls=%fused_computation.4 | loop fusion | flops 1024 | bytes 8192 | tf_op jit(solution)/shard_map/concatenate | solution.py:339
  6.2 0.6 %broadcast_in_dim.8 = s32[8,8,128]{2,1,0:T(8,128)} broadcast(s32[8,128]{1,0:T(8,128)S(1)} %broadcast_in_dim.7), dimensions={1,2} | broadcast | bytes 36864 | tf_op jit(solution)/shard_map/broadcast_in_dim | solution.py:340
  6.9 3.3 %all-to-all-start = ((s32[8,8,128]{2,1,0:T(8,128)}), s32[8,8,128]{2,1,0:T(8,128)S(1)}, u32[]{:S(2)}, u32[]{:S(2)}) async-start(s32[8,8,128]{2,1,0:T(8,128)} %broadcast_in_dim.8), calls=%async_computation | async-start | bytes 65536 | tf_op jit(solution)/shard_map/all_to_all | solution.py:340
  10.2 0.0 copy-start
  10.2 1.6 %copy-done = bf16[1,524288]{1,0:T(2,128)(2,1)S(1)} copy-done((bf16[1,524288]{1,0:T(2,128)(2,1)S(1)}, bf16[1,524288]{1,0:T(2,128)(2,1)}, u32[]{:S(2)}) %copy-start) | copy-done | bytes 1048600
  11.8 0.6 %shard_map.64.rows_ref = bf16[4096,128]{1,0:T(8,128)(2,1)S(1)} custom-call(bf16[1,524288]{1,0:T(2,128)(2,1)S(1)} %copy-done), custom_call_target="tpu_custom_call" | custom-call | tf_op jit(solution)/shard_map/pallas_call | solution.py:86
  12.5 0.1 pad_add_fusion.1.place_ref
  12.6 5.8 %all-to-all-done.ids_ref.refs_0_ = s32[8,8,128]{2,1,0:T(8,128)S(1)} async-done(((s32[8,8,128]{2,1,0:T(8,128)}), s32[8,8,128]{2,1,0:T(8,128)S(1)}, u32[]{:S(2)}, u32[]{:S(2)}) %all-to-all-start) | async-done | bytes 32800 | tf_op jit(solution)/shard_map/all_to_all | solution.py:340
  18.3 2.1 %shard_map.65 = (bf16[512,128]{1,0:T(8,128)(2,1)S(1)}, bf16[512,128]{1,0:T(8,128)(2,1)S(1)}, bf16[512,128]{1,0:T(8,128)(2,1)S(1)}, bf16[512,128]{1,0:T(8,128)(2,1)S(1)}) custom-call(s32[3]{0:T(128)S(1)} %pad_add_fusion.1.place_ref, s32[8,8,128]{2,1,0:T(8,128)S(1)} %all-to-all-done.ids_ref.refs_0_, bf16[4096,128]{1,0:T(8,128)(2,1)S(1)} %shard_map.64.rows_ref), custom_call_target="tpu_custom_call" | custom-call | bytes 10000000 | tf_op jit(solution)/shard_map/pallas_call | solution.py:131
  20.4 0.8 %collective-permute-start.3 = (bf16[512,128]{1,0:T(8,128)(2,1)S(1)}, bf16[512,128]{1,0:T(8,128)(2,1)S(1)}, u32[]{:S(2)}, u32[]{:S(2)}) collective-permute-start(bf16[512,128]{1,0:T(8,128)(2,1)S(1)} %get-tuple-element.20), channel_id=1, source_target_pairs={{0,2},{1,3},{2,0},{3,1},{4,6},{5,7},{6,4},{7,5},{8,10},{9,11},{10,... | collective-permute-start | bytes 393224 | tf_op jit(solution)/shard_map/ppermute | solution.py:330
  21.1 1.5 %collective-permute-start.4 = (bf16[512,128]{1,0:T(8,128)(2,1)S(1)}, bf16[512,128]{1,0:T(8,128)(2,1)S(1)}, u32[]{:S(2)}, u32[]{:S(2)}) collective-permute-start(bf16[512,128]{1,0:T(8,128)(2,1)S(1)} %get-tuple-element.21), channel_id=1, source_target_pairs={{0,16},{8,24},{16,0},{24,8},{1,17},{9,25},{17,1},{25,9},{2,18},{10... | collective-permute-start | bytes 393224 | tf_op jit(solution)/shard_map/ppermute | solution.py:332
  22.7 1.3 %collective-permute-start.5 = (bf16[512,128]{1,0:T(8,128)(2,1)S(1)}, bf16[512,128]{1,0:T(8,128)(2,1)S(1)}, u32[]{:S(2)}, u32[]{:S(2)}) collective-permute-start(bf16[512,128]{1,0:T(8,128)(2,1)S(1)} %get-tuple-element.22), channel_id=1, source_target_pairs={{0,18},{1,19},{2,16},{3,17},{4,22},{5,23},{6,20},{7,21},{8,26},{9,... | collective-permute-start | bytes 393224 | tf_op jit(solution)/shard_map/ppermute | solution.py:334
  23.9 0.0 copy-done.3
  24.0 0.0 collective-permute-done
  24.0 0.0 collective-permute-done.2
  24.0 1.6 %collective-permute-start.6 = (bf16[128,1152]{1,0:T(8,128)(2,1)S(1)}, bf16[128,1152]{1,0:T(8,128)(2,1)S(1)}, u32[]{:S(2)}, u32[]{:S(2)}) collective-permute-start(bf16[128,1152]{1,0:T(8,128)(2,1)S(1)} %collective-permute-done.2), channel_id=1, source_target_pairs={{0,8},{8,0},{16,24},{24,16},{1,9},{9,1},{17,25},{25,17},{2,10},{10... | collective-permute-start | bytes 884744 | tf_op jit(solution)/shard_map/ppermute | solution.py:332
  25.6 1.2 %collective-permute-done.3.rest_1_ = bf16[512,128]{1,0:T(8,128)(2,1)S(1)} collective-permute-done((bf16[512,128]{1,0:T(8,128)(2,1)S(1)}, bf16[512,128]{1,0:T(8,128)(2,1)S(1)}, u32[]{:S(2)}, u32[]{:S(2)}) %collective-permute-start.3) | collective-permute-done | bytes 131104 | tf_op jit(solution)/shard_map/ppermute | solution.py:330
  26.8 1.3 %collective-permute-done.4.rest_2_ = bf16[512,128]{1,0:T(8,128)(2,1)S(1)} collective-permute-done((bf16[512,128]{1,0:T(8,128)(2,1)S(1)}, bf16[512,128]{1,0:T(8,128)(2,1)S(1)}, u32[]{:S(2)}, u32[]{:S(2)}) %collective-permute-start.4) | collective-permute-done | bytes 131104 | tf_op jit(solution)/shard_map/ppermute | solution.py:332
  28.1 1.4 %collective-permute-done.5.rest_3_ = bf16[512,128]{1,0:T(8,128)(2,1)S(1)} collective-permute-done((bf16[512,128]{1,0:T(8,128)(2,1)S(1)}, bf16[512,128]{1,0:T(8,128)(2,1)S(1)}, u32[]{:S(2)}, u32[]{:S(2)}) %collective-permute-start.5) | collective-permute-done | bytes 131104 | tf_op jit(solution)/shard_map/ppermute | solution.py:334
  29.6 0.0 collective-permute-start.1
  29.6 0.0 copy-start.1
  29.6 0.0 copy-start.2
  29.6 2.4 %collective-permute-done.6 = bf16[128,1152]{1,0:T(8,128)(2,1)S(1)} collective-permute-done((bf16[128,1152]{1,0:T(8,128)(2,1)S(1)}, bf16[128,1152]{1,0:T(8,128)(2,1)S(1)}, u32[]{:S(2)}, u32[]{:S(2)}) %collective-permute-start.6) | collective-permute-done | bytes 294944 | tf_op jit(solution)/shard_map/ppermute | solution.py:332
  32.1 0.1 collective-permute-start.7
  32.2 0.0 collective-permute-done.1.other_ref.rest_1_
  32.2 2.8 %shard_map.66.rest_4_ = f32[96,128]{1,0:T(8,128)S(1)} custom-call(s32[3]{0:T(128)S(1)} %pad_add_fusion.1.place_ref, s32[8,8,128]{2,1,0:T(8,128)S(1)} %all-to-all-done.ids_ref.refs_0_, bf16[256,1152]{1,0:T(8,128)(2,1)S(1)} %constant_dynamic-update-slice_fusion.own_ref.rest_0_, bf16[256,1152]{1,0:T(8,128)(2,1)S(1)} %collective-permute-done.1.other_ref.rest_1_, ...), custom_call_target="tpu_custom_call" | custom-call | bytes 30000000 | tf_op jit(solution)/shard_map/pallas_call | solution.py:194
  34.9 0.0 collective-permute-done.7.other_ref.rest_3_
  34.9 2.8 %shard_map.67.rest_4_ = f32[96,128]{1,0:T(8,128)S(1)} custom-call(s32[3]{0:T(128)S(1)} %pad_add_fusion.1.place_ref, s32[8,8,128]{2,1,0:T(8,128)S(1)} %all-to-all-done.ids_ref.refs_0_, bf16[256,1152]{1,0:T(8,128)(2,1)S(1)} %constant_dynamic-update-slice_fusion.2.own_ref.rest_2_, bf16[256,1152]{1,0:T(8,128)(2,1)S(1)} %collective-permute-done.7.other_ref.rest_3_, ...), custom_call_target="tpu_custom_call" | custom-call | bytes 30000000 | tf_op jit(solution)/shard_map/pallas_call | solution.py:194
  37.7 1.8 %collective-permute-start.10 = (f32[96,128]{1,0:T(8,128)S(1)}, f32[96,128]{1,0:T(8,128)S(1)}, u32[]{:S(2)}, u32[]{:S(2)}) collective-permute-start(f32[96,128]{1,0:T(8,128)S(1)} %shard_map.67.rest_4_), channel_id=1, source_target_pairs={{0,18},{1,19},{2,16},{3,17},{4,22},{5,23},{6,20},{7,21},{8,26},{9,... | collective-permute-start | bytes 147464 | tf_op jit(solution)/shard_map/ppermute | solution.py:334
  39.5 0.5 collective-permute-start.9
  40.0 1.3 %collective-permute-start.8 = (f32[96,128]{1,0:T(8,128)S(1)}, f32[96,128]{1,0:T(8,128)S(1)}, u32[]{:S(2)}, u32[]{:S(2)}) collective-permute-start(f32[96,128]{1,0:T(8,128)S(1)} %shard_map.67.rest_4_), channel_id=1, source_target_pairs={{0,2},{1,3},{2,0},{3,1},{4,6},{5,7},{6,4},{7,5},{8,10},{9,11},{10,... | collective-permute-start | bytes 147464 | tf_op jit(solution)/shard_map/ppermute | solution.py:330
  41.3 1.6 %collective-permute-done.10.rest_7_ = f32[96,128]{1,0:T(8,128)S(1)} collective-permute-done((f32[96,128]{1,0:T(8,128)S(1)}, f32[96,128]{1,0:T(8,128)S(1)}, u32[]{:S(2)}, u32[]{:S(2)}) %collective-permute-start.10) | collective-permute-done | bytes 49184 | tf_op jit(solution)/shard_map/ppermute | solution.py:334
  42.9 1.0 %collective-permute-done.9.rest_6_ = f32[96,128]{1,0:T(8,128)S(1)} collective-permute-done((f32[96,128]{1,0:T(8,128)S(1)}, f32[96,128]{1,0:T(8,128)S(1)}, u32[]{:S(2)}, u32[]{:S(2)}) %collective-permute-start.9) | collective-permute-done | bytes 49184 | tf_op jit(solution)/shard_map/ppermute | solution.py:332
  43.9 0.2 collective-permute-done.8.rest_5_
  44.1 0.0 copy-done.1
  44.1 0.0 copy-done.2
  44.1 2.4 %shard_map.69 = (bf16[512,128]{1,0:T(8,128)(2,1)S(1)}, bf16[512,128]{1,0:T(8,128)(2,1)S(1)}) custom-call(s32[3]{0:T(128)S(1)} %pad_add_fusion.1.place_ref, s32[8,8,128]{2,1,0:T(8,128)S(1)} %all-to-all-done.ids_ref.refs_0_, s32[1,128]{1,0:T(1,128)S(1)} %bitcast.8, f32[18,18,128]{2,1,0:T(8,128)S(1)} %bitcast.6, ...), custom_call_target="tpu_custom_call" | custom-call | tf_op jit(solution)/shard_map/pallas_call | solution.py:253
  46.5 1.3 %collective-permute-start.12 = (bf16[512,128]{1,0:T(8,128)(2,1)S(1)}, bf16[512,128]{1,0:T(8,128)(2,1)S(1)}, u32[]{:S(2)}, u32[]{:S(2)}) collective-permute-start(bf16[512,128]{1,0:T(8,128)(2,1)S(1)} %get-tuple-element.27), channel_id=1, source_target_pairs={{0,2},{1,3},{2,0},{3,1},{4,6},{5,7},{6,4},{7,5},{8,10},{9,11},{10,... | collective-permute-start | bytes 393224 | tf_op jit(solution)/shard_map/ppermute | solution.py:330
  47.8 1.7 %collective-permute-start.13 = (bf16[512,128]{1,0:T(8,128)(2,1)S(1)}, bf16[512,128]{1,0:T(8,128)(2,1)S(1)}, u32[]{:S(2)}, u32[]{:S(2)}) collective-permute-start(bf16[512,128]{1,0:T(8,128)(2,1)S(1)} %get-tuple-element.28), channel_id=1, source_target_pairs={{0,18},{1,19},{2,16},{3,17},{4,22},{5,23},{6,20},{7,21},{8,26},{9,... | collective-permute-start | bytes 393224 | tf_op jit(solution)/shard_map/ppermute | solution.py:334
  49.5 2.4 %shard_map.68 = (bf16[512,128]{1,0:T(8,128)(2,1)S(1)}, bf16[512,128]{1,0:T(8,128)(2,1)S(1)}) custom-call(s32[3]{0:T(128)S(1)} %pad_add_fusion.1.place_ref, s32[8,8,128]{2,1,0:T(8,128)S(1)} %all-to-all-done.ids_ref.refs_0_, s32[1,128]{1,0:T(1,128)S(1)} %bitcast.9, f32[18,18,128]{2,1,0:T(8,128)S(1)} %bitcast.7, ...), custom_call_target="tpu_custom_call" | custom-call | tf_op jit(solution)/shard_map/pallas_call | solution.py:253
  51.9 0.6 collective-permute-start.11
  52.5 0.3 collective-permute-done.12.refs_1_
  52.8 2.1 %collective-permute-done.13.refs_2_ = bf16[512,128]{1,0:T(8,128)(2,1)S(1)} collective-permute-done((bf16[512,128]{1,0:T(8,128)(2,1)S(1)}, bf16[512,128]{1,0:T(8,128)(2,1)S(1)}, u32[]{:S(2)}, u32[]{:S(2)}) %collective-permute-start.13) | collective-permute-done | bytes 131104 | tf_op jit(solution)/shard_map/ppermute | solution.py:334
  54.9 2.8 %shard_map.70.refs_3_ = bf16[1,524288]{1,0:T(2,128)(2,1)} custom-call(s32[3]{0:T(128)S(1)} %pad_add_fusion.1.place_ref, s32[8,8,128]{2,1,0:T(8,128)S(1)} %all-to-all-done.ids_ref.refs_0_, bf16[512,128]{1,0:T(8,128)(2,1)S(1)} %collective-permute-done.12.refs_1_, bf16[512,128]{1,0:T(8,128)(2,1)S(1)} %collective-permute-done.13.refs_2_), custom_call_target="tpu_custom_call" | custom-call | tf_op jit(solution)/shard_map/pallas_call | solution.py:306
  57.7 0.0 collective-permute-done.11.refs_2_
  57.7 2.8 %shard_map.71 = bf16[1,524288]{1,0:T(2,128)(2,1)} custom-call(s32[3]{0:T(128)S(1)} %pad_add_fusion.1.place_ref, s32[8,8,128]{2,1,0:T(8,128)S(1)} %all-to-all-done.ids_ref.refs_0_, bf16[512,128]{1,0:T(8,128)(2,1)S(1)} %get-tuple-element.25.refs_1_, bf16[512,128]{1,0:T(8,128)(2,1)S(1)} %collective-permute-done.11.refs_2_, ...), custom_call_target="tpu_custom_call", output_to_operand_aliasing={{}: (4, {})} | custom-call | tf_op jit(solution)/shard_map/pallas_call | solution.py:306
  (6 shorter events, 0.1 us)
Async XLA Ops:
  0.0 24.0 %collective-permute-start.2 = (bf16[128,1152]{1,0:T(8,128)(2,1)}, bf16[128,1152]{1,0:T(8,128)(2,1)S(1)}, u32[]{:S(2)}, u32[]{:S(2)}) collective-permute-start(bf16[128,1152]{1,0:T(8,128)(2,1)} %bitcast.10), channel_id=1, source_target_pairs={{0,4},{1,5},{2,6},{3,7},{4,0},{5,1},{6,2},{7,3},{8,12},{9,13},{10,... | collective-permute-start | bytes 884744 | tf_op jit(solution)/shard_map/ppermute | solution.py:330
  4.0 19.9 %collective-permute-start = (bf16[128,1152]{1,0:T(8,128)(2,1)}, bf16[128,1152]{1,0:T(8,128)(2,1)S(1)}, u32[]{:S(2)}, u32[]{:S(2)}) collective-permute-start(bf16[128,1152]{1,0:T(8,128)(2,1)} %bitcast.11), channel_id=1, source_target_pairs={{0,8},{8,0},{16,24},{24,16},{1,9},{9,1},{17,25},{25,17},{2,10},{10... | collective-permute-start | bytes 884744 | tf_op jit(solution)/shard_map/ppermute | solution.py:332
  6.9 11.4 %all-to-all-start = ((s32[8,8,128]{2,1,0:T(8,128)}), s32[8,8,128]{2,1,0:T(8,128)S(1)}, u32[]{:S(2)}, u32[]{:S(2)}) async-start(s32[8,8,128]{2,1,0:T(8,128)} %broadcast_in_dim.8), calls=%async_computation | async-start | bytes 65536 | tf_op jit(solution)/shard_map/all_to_all | solution.py:340
  10.2 1.6 %copy-start = (bf16[1,524288]{1,0:T(2,128)(2,1)S(1)}, bf16[1,524288]{1,0:T(2,128)(2,1)}, u32[]{:S(2)}) copy-start(bf16[1,524288]{1,0:T(2,128)(2,1)} %psi_ref.1) | copy-start | bytes 3145732
  11.8 12.1 %copy-start.3 = (bf16[1,128,1152]{2,1,0:T(8,128)(2,1)S(1)}, bf16[1,128,1152]{2,1,0:T(8,128)(2,1)}, u32[]{:S(2)}) copy-start(bf16[1,128,1152]{2,1,0:T(8,128)(2,1)} %param.7) | copy-start | bytes 884740
  20.4 6.4 %collective-permute-start.3 = (bf16[512,128]{1,0:T(8,128)(2,1)S(1)}, bf16[512,128]{1,0:T(8,128)(2,1)S(1)}, u32[]{:S(2)}, u32[]{:S(2)}) collective-permute-start(bf16[512,128]{1,0:T(8,128)(2,1)S(1)} %get-tuple-element.20), channel_id=1, source_target_pairs={{0,2},{1,3},{2,0},{3,1},{4,6},{5,7},{6,4},{7,5},{8,10},{9,11},{10,... | collective-permute-start | bytes 393224 | tf_op jit(solution)/shard_map/ppermute | solution.py:330
  21.1 7.0 %collective-permute-start.4 = (bf16[512,128]{1,0:T(8,128)(2,1)S(1)}, bf16[512,128]{1,0:T(8,128)(2,1)S(1)}, u32[]{:S(2)}, u32[]{:S(2)}) collective-permute-start(bf16[512,128]{1,0:T(8,128)(2,1)S(1)} %get-tuple-element.21), channel_id=1, source_target_pairs={{0,16},{8,24},{16,0},{24,8},{1,17},{9,25},{17,1},{25,9},{2,18},{10... | collective-permute-start | bytes 393224 | tf_op jit(solution)/shard_map/ppermute | solution.py:332
  22.7 6.9 %collective-permute-start.5 = (bf16[512,128]{1,0:T(8,128)(2,1)S(1)}, bf16[512,128]{1,0:T(8,128)(2,1)S(1)}, u32[]{:S(2)}, u32[]{:S(2)}) collective-permute-start(bf16[512,128]{1,0:T(8,128)(2,1)S(1)} %get-tuple-element.22), channel_id=1, source_target_pairs={{0,18},{1,19},{2,16},{3,17},{4,22},{5,23},{6,20},{7,21},{8,26},{9,... | collective-permute-start | bytes 393224 | tf_op jit(solution)/shard_map/ppermute | solution.py:334
  24.0 8.1 %collective-permute-start.6 = (bf16[128,1152]{1,0:T(8,128)(2,1)S(1)}, bf16[128,1152]{1,0:T(8,128)(2,1)S(1)}, u32[]{:S(2)}, u32[]{:S(2)}) collective-permute-start(bf16[128,1152]{1,0:T(8,128)(2,1)S(1)} %collective-permute-done.2), channel_id=1, source_target_pairs={{0,8},{8,0},{16,24},{24,16},{1,9},{9,1},{17,25},{25,17},{2,10},{10... | collective-permute-start | bytes 884744 | tf_op jit(solution)/shard_map/ppermute | solution.py:332
  29.6 2.6 %collective-permute-start.1 = (bf16[256,1152]{1,0:T(8,128)(2,1)S(1)}, bf16[256,1152]{1,0:T(8,128)(2,1)S(1)}, u32[]{:S(2)}, u32[]{:S(2)}) collective-permute-start(bf16[256,1152]{1,0:T(8,128)(2,1)S(1)} %constant_dynamic-update-slice_fusion.own_ref.rest_0_), channel_id=1, source_target_pairs={{0,1},{1,0},{2,3},{3,2},{4,5},{5,4},{6,7},{7,6},{8,9},{9,8},{10,11... | collective-permute-start | bytes 1769480 | tf_op jit(solution)/shard_map/ppermute | solution.py:330
  29.6 14.5 %copy-start.1 = (f32[128,18,18]{0,2,1:T(8,128)S(1)}, f32[128,18,18]{0,2,1:T(8,128)}, u32[]{:S(2)}) copy-start(f32[128,18,18]{0,2,1:T(8,128)} %param.11) | copy-start | bytes 497668
  29.6 14.5 %copy-start.2 = (s32[128]{0:T(128)S(1)}, s32[128]{0:T(128)}, u32[]{:S(2)}) copy-start(s32[128]{0:T(128)} %param.10) | copy-start | bytes 1540
  32.1 2.9 %collective-permute-start.7 = (bf16[256,1152]{1,0:T(8,128)(2,1)S(1)}, bf16[256,1152]{1,0:T(8,128)(2,1)S(1)}, u32[]{:S(2)}, u32[]{:S(2)}) collective-permute-start(bf16[256,1152]{1,0:T(8,128)(2,1)S(1)} %constant_dynamic-update-slice_fusion.2.own_ref.rest_2_), channel_id=1, source_target_pairs={{0,1},{1,0},{2,3},{3,2},{4,5},{5,4},{6,7},{7,6},{8,9},{9,8},{10,11... | collective-permute-start | bytes 1769480 | tf_op jit(solution)/shard_map/ppermute | solution.py:330
  37.7 5.2 %collective-permute-start.10 = (f32[96,128]{1,0:T(8,128)S(1)}, f32[96,128]{1,0:T(8,128)S(1)}, u32[]{:S(2)}, u32[]{:S(2)}) collective-permute-start(f32[96,128]{1,0:T(8,128)S(1)} %shard_map.67.rest_4_), channel_id=1, source_target_pairs={{0,18},{1,19},{2,16},{3,17},{4,22},{5,23},{6,20},{7,21},{8,26},{9,... | collective-permute-start | bytes 147464 | tf_op jit(solution)/shard_map/ppermute | solution.py:334
  39.5 4.4 %collective-permute-start.9 = (f32[96,128]{1,0:T(8,128)S(1)}, f32[96,128]{1,0:T(8,128)S(1)}, u32[]{:S(2)}, u32[]{:S(2)}) collective-permute-start(f32[96,128]{1,0:T(8,128)S(1)} %shard_map.67.rest_4_), channel_id=1, source_target_pairs={{0,16},{8,24},{16,0},{24,8},{1,17},{9,25},{17,1},{25,9},{2,18},{10... | collective-permute-start | bytes 147464 | tf_op jit(solution)/shard_map/ppermute | solution.py:332
  40.0 4.1 %collective-permute-start.8 = (f32[96,128]{1,0:T(8,128)S(1)}, f32[96,128]{1,0:T(8,128)S(1)}, u32[]{:S(2)}, u32[]{:S(2)}) collective-permute-start(f32[96,128]{1,0:T(8,128)S(1)} %shard_map.67.rest_4_), channel_id=1, source_target_pairs={{0,2},{1,3},{2,0},{3,1},{4,6},{5,7},{6,4},{7,5},{8,10},{9,11},{10,... | collective-permute-start | bytes 147464 | tf_op jit(solution)/shard_map/ppermute | solution.py:330
  46.5 6.3 %collective-permute-start.12 = (bf16[512,128]{1,0:T(8,128)(2,1)S(1)}, bf16[512,128]{1,0:T(8,128)(2,1)S(1)}, u32[]{:S(2)}, u32[]{:S(2)}) collective-permute-start(bf16[512,128]{1,0:T(8,128)(2,1)S(1)} %get-tuple-element.27), channel_id=1, source_target_pairs={{0,2},{1,3},{2,0},{3,1},{4,6},{5,7},{6,4},{7,5},{8,10},{9,11},{10,... | collective-permute-start | bytes 393224 | tf_op jit(solution)/shard_map/ppermute | solution.py:330
  47.8 7.1 %collective-permute-start.13 = (bf16[512,128]{1,0:T(8,128)(2,1)S(1)}, bf16[512,128]{1,0:T(8,128)(2,1)S(1)}, u32[]{:S(2)}, u32[]{:S(2)}) collective-permute-start(bf16[512,128]{1,0:T(8,128)(2,1)S(1)} %get-tuple-element.28), channel_id=1, source_target_pairs={{0,18},{1,19},{2,16},{3,17},{4,22},{5,23},{6,20},{7,21},{8,26},{9,... | collective-permute-start | bytes 393224 | tf_op jit(solution)/shard_map/ppermute | solution.py:334
  51.9 5.7 %collective-permute-start.11 = (bf16[512,128]{1,0:T(8,128)(2,1)S(1)}, bf16[512,128]{1,0:T(8,128)(2,1)S(1)}, u32[]{:S(2)}, u32[]{:S(2)}) collective-permute-start(bf16[512,128]{1,0:T(8,128)(2,1)S(1)} %get-tuple-element.26), channel_id=1, source_target_pairs={{0,16},{8,24},{16,0},{24,8},{1,17},{9,25},{17,1},{25,9},{2,18},{10... | collective-permute-start | bytes 393224 | tf_op jit(solution)/shard_map/ppermute | solution.py:332

commit v5 on v4

--- a/solution.py
+++ b/solution.py
@@ -53,18 +53,17 @@
     return range(half_index * PIECES // HALVES, (half_index + 1) * PIECES // HALVES)
 
 
-def slot_ids(ids_ref, place_ref, slab, turned_chip, turned_column, kind):
+def slot_ids(ids_ref, place_ref, turned_chip, turned_column, kind):
     slot_rows = ids_ref.shape[1] // 2
     share = slot_rows // PARTNERS
-    index = slab_index(place_ref, turned_chip, slab)
     first = kind * slot_rows + jnp.bitwise_xor(place_ref[1], turned_column) * share
-    return [ids_ref[index, pl.ds(first + i, 1), :] for i in range(share)]
-
-
-def atom_hits(ids_ref, place_ref, slab, pieces):
+    return [ids_ref[turned_chip, pl.ds(first + i, 1), :] for i in range(share)]
+
+
+def atom_hits(ids_ref, place_ref, pieces):
     lane = iota((LANES, LANES), 1)
     for piece in pieces:
-        for atoms in slot_ids(ids_ref, place_ref, slab, piece & 2, piece & 1, 1):
+        for atoms in slot_ids(ids_ref, place_ref, piece & 2, piece & 1, 1):
             yield (down(atoms) == lane).astype(BF16)
 
 
@@ -92,7 +91,7 @@
     )(psi)
 
 
-def gather_kernel(place_ref, ids_ref, rows_ref, out_refs):
+def gather_kernel(place_ref, ids_refs, rows_ref, out_refs):
     half = LANES // 2
     slab_rows = rows_ref.shape[0] // (CORES * CHIPS)
     lane = iota((LANES, LANES), 1)
@@ -103,7 +102,7 @@
             odds, hits, places = [], [], []
             for column in range(PARTNERS):
                 partner, piece = owner(chip, column)
-                ids = slot_ids(ids_ref, place_ref, slab, chip, column, 0)
+                ids = slot_ids(ids_refs[slab], place_ref, chip, column, 0)
                 for i, row in enumerate(ids):
                     blocks = down(row)
                     wanted = jnp.right_shift(blocks, 1)
@@ -123,22 +122,22 @@
 
 
 def gather(place, ids, rows):
-    slots = CORES * PIECES * ids.shape[1] // 2 * LANES // PARTNERS
-
-    def kernel(place_ref, ids_ref, rows_ref, *out_refs):
-        gather_kernel(place_ref, ids_ref, rows_ref, out_refs)
+    slots = CORES * PIECES * ids[0].shape[1] // 2 * LANES // PARTNERS
+
+    def kernel(place_ref, own_ids, other_ids, rows_ref, *out_refs):
+        gather_kernel(place_ref, (own_ids, other_ids), rows_ref, out_refs)
 
     return pl.pallas_call(
         kernel,
-        in_specs=[SMEM_SPEC] + [VMEM_SPEC] * 2,
+        in_specs=[SMEM_SPEC] + [VMEM_SPEC] * 3,
         out_specs=[VMEM_SPEC] * PARTNERS,
         out_shape=[jax.ShapeDtypeStruct((slots // 2, LANES), BF16)] * PARTNERS,
         cost_estimate=pl.CostEstimate(flops=0, bytes_accessed=GATHER_BYTES, transcendentals=0),
         compiler_params=PARAMS,
-    )(place, ids, rows)
-
-
-def project_kernel(projectors, padded, half_index, place_ref, ids_ref, table_refs, packed_refs, before_refs, coef_ref, picks_of, highs, rests):
+    )(place, *ids, rows)
+
+
+def project_kernel(projectors, padded, half_index, place_ref, ids_refs, table_refs, packed_refs, before_refs, coef_ref, picks_of, terms):
     bands = len(packed_refs)
     slots = table_refs[0].shape[0]
     pair_count = projectors // 2
@@ -159,24 +158,26 @@
             turned = pltpu.roll(straight, half, 1)
             picks_of[band, i * LANES : i * LANES + half, :] = jnp.where(left, straight, turned).astype(BF16)
             picks_of[band, i * LANES + half : (i + 1) * LANES, :] = jnp.where(left, turned, straight).astype(BF16)
-    total = before_refs[0][...] if before_refs else None
+    of_atom = []
     for slab, table_ref in enumerate(table_refs):
-        of_atom = jnp.concatenate(list(atom_hits(ids_ref, place_ref, slab, pieces_of(half_index))), axis=0)
+        of_atom += atom_hits(ids_refs[slab], place_ref, pieces_of(half_index))
         for group in range(slots // GROUP):
             rows = slice(group * GROUP, (group + 1) * GROUP)
-            picked = slice(slab * slots + group * GROUP, slab * slots + (group + 1) * GROUP)
-            picks = jnp.concatenate([picks_of[band, picked, :] for band in range(bands)], axis=0)
+            first = slab * slots + group * GROUP
+            high_rows, rest_rows = slice(first, first + GROUP), slice(CORES * slots + first, CORES * slots + first + GROUP)
+            picks = jnp.concatenate([picks_of[band, high_rows, :] for band in range(bands)], axis=0)
             values = jnp.concatenate([jnp.where(low, picks, none), jnp.where(low, none, picks)], axis=0)
             tables = jnp.concatenate([table_ref[rows, t * LANES : (t + 1) * LANES] for t in range(pair_count)], axis=0)
             crossed = dot(tables, values, ((1,), (1,)))
             for t in range(pair_count):
                 kept = jnp.where(diagonal, crossed[t * GROUP : (t + 1) * GROUP], 0.0)
-                highs[rows, t * wide : (t + 1) * wide], rests[rows, t * wide : (t + 1) * wide] = two_terms(kept)
-        slot_coef = dot(highs[...], gather_lanes) + dot(rests[...], gather_lanes)
-        high, rest = two_terms(slot_coef)
-        summed = dot(high, of_atom, ((0,), (0,))) + dot(rest, of_atom, ((0,), (0,)))
-        total = summed if total is None else total + summed
-    coef_ref[...] = total
+                lanes = slice(t * wide, (t + 1) * wide)
+                terms[high_rows, lanes], terms[rest_rows, lanes] = two_terms(kept)
+    slot_coef = dot(terms[...], gather_lanes)
+    high, rest = two_terms(slot_coef[: CORES * slots] + slot_coef[CORES * slots :])
+    of_atom = jnp.concatenate(of_atom, axis=0)
+    total = dot(high, of_atom, ((0,), (0,))) + dot(rest, of_atom, ((0,), (0,)))
+    coef_ref[...] = total + before_refs[0][...] if before_refs else total
 
 
 def project(place, ids, tables, picks, projectors, padded, half_index, before):
@@ -184,25 +185,25 @@
     slots = tables[0].shape[0]
     width = projectors * bands * GROUP
 
-    def kernel(place_ref, ids_ref, own_ref, other_ref, *rest):
+    def kernel(place_ref, own_ids, other_ids, own_ref, other_ref, *rest):
         ends = [bands, bands + len(before)]
         project_kernel(
-            projectors, padded, half_index, place_ref, ids_ref, (own_ref, other_ref),
+            projectors, padded, half_index, place_ref, (own_ids, other_ids), (own_ref, other_ref),
             rest[: ends[0]], rest[ends[0] : ends[1]], *rest[ends[1] :],
         )
 
     return pl.pallas_call(
         kernel,
-        in_specs=[SMEM_SPEC] + [VMEM_SPEC] * (3 + bands + len(before)),
+        in_specs=[SMEM_SPEC] + [VMEM_SPEC] * (4 + bands + len(before)),
         out_specs=VMEM_SPEC,
         out_shape=jax.ShapeDtypeStruct((bands * padded, LANES), F32),
-        scratch_shapes=[pltpu.VMEM((bands, CORES * slots, LANES), BF16)] + [pltpu.VMEM((slots, width), BF16)] * 2,
+        scratch_shapes=[pltpu.VMEM((bands, CORES * slots, LANES), BF16)] + [pltpu.VMEM((2 * CORES * slots, width), BF16)],
         cost_estimate=pl.CostEstimate(flops=0, bytes_accessed=PROJECT_BYTES, transcendentals=0),
         compiler_params=PARAMS,
-    )(place, ids, *tables, *picks, *before)
-
-
-def apply_kernel(wanted, projectors, padded, place_ref, ids_ref, table_refs, count_ref, strength_ref, coef_refs, out_refs, wide_refs):
+    )(place, *ids, *tables, *picks, *before)
+
+
+def apply_kernel(wanted, projectors, padded, place_ref, ids_refs, table_refs, count_ref, strength_ref, coef_refs, out_refs, wide_refs):
     pair_count = projectors // 2
     width = projectors * LANES // 2
     atom_total = strength_ref.shape[2]
@@ -225,7 +226,7 @@
         for half_index in range(HALVES):
             table_ref = table_refs[half_index * CORES + slab]
             blocks = table_ref.shape[0] // LANES
-            for i, of_atom in enumerate(atom_hits(ids_ref, place_ref, slab, pieces_of(half_index))):
+            for i, of_atom in enumerate(atom_hits(ids_refs[slab], place_ref, pieces_of(half_index))):
                 rows = slice(i * LANES, (i + 1) * LANES)
                 first = ((slab * HALVES + half_index) * blocks + i) * half
                 for wide_ref, out_ref in zip(wide_refs, out_refs):
@@ -243,25 +244,25 @@
     slots = sum(table.shape[0] for table in tables)
     atom_total = strength.shape[2]
 
-    def kernel(place_ref, ids_ref, count_ref, strength_ref, *rest):
+    def kernel(place_ref, own_ids, other_ids, count_ref, strength_ref, *rest):
         ends = [len(tables), len(tables) + len(coefs), len(tables) + len(coefs) + len(wanted)]
         apply_kernel(
-            wanted, projectors, padded, place_ref, ids_ref, rest[: ends[0]], count_ref, strength_ref,
+            wanted, projectors, padded, place_ref, (own_ids, other_ids), rest[: ends[0]], count_ref, strength_ref,
             rest[ends[0] : ends[1]], rest[ends[1] : ends[2]], rest[ends[2] :],
         )
 
     return pl.pallas_call(
         kernel,
-        in_specs=[SMEM_SPEC] + [VMEM_SPEC] * (3 + len(tables) + len(coefs)),
+        in_specs=[SMEM_SPEC] + [VMEM_SPEC] * (4 + len(tables) + len(coefs)),
         out_specs=[VMEM_SPEC] * len(wanted),
         out_shape=[jax.ShapeDtypeStruct((slots // 2, LANES), BF16)] * len(wanted),
         scratch_shapes=[pltpu.VMEM((atom_total, projectors * LANES // 2), BF16)] * len(wanted),
         compiler_params=PARAMS,
-    )(place, ids, count, strength, *tables, *coefs)
+    )(place, *ids, count, strength, *tables, *coefs)
 
 
 def place_kernel(chips, wanted, place_ref, *refs):
-    ids_ref, value_refs, out_ref = refs[0], dict(zip(wanted, refs[1:])), refs[-1]
+    ids_refs, value_refs, out_ref = refs[:CORES], dict(zip(wanted, refs[CORES:])), refs[-1]
     step = pl.program_id(0)
     half = LANES // 2
     rows = out_ref.shape[1] // LANES // CORES
@@ -275,7 +276,7 @@
                 parts, wanted = [], []
                 for column in range(PARTNERS):
                     partner, piece = owner(chip, column)
-                    ids = slot_ids(ids_ref, place_ref, slab, chip, column, 0)
+                    ids = slot_ids(ids_refs[slab], place_ref, chip, column, 0)
                     for i, blocks in enumerate(ids):
                         wanted.append(jnp.right_shift(blocks, 1))
                         odd = jnp.bitwise_and(down(blocks), 1) == 1
@@ -301,7 +302,7 @@
 def place_rows(chips, place, ids, values, points, before):
     share = points // CHIPS
     wanted = tuple(values)
-    small = (ids, *values.values())
+    small = (*ids, *values.values())
     apart = chips[1] ^ chips[0]
     return pl.pallas_call(
         functools.partial(place_kernel, chips, wanted),
@@ -337,7 +338,8 @@
         return [parts[0]] + [exchange(parts[i], chip=i & 1, column=i & 2) for i in range(1, PARTNERS)]
 
     ids = jnp.concatenate([pair_block, pair_atom], axis=0).reshape(1, -1, LANES)
-    ids = lax.all_to_all(jnp.broadcast_to(ids, (slabs, *ids.shape[1:])), "slab", 0, 0, tiled=True)
+    ids = jnp.concatenate([ids] + [exchange(ids, chip=chip) for chip in range(1, CHIPS)], axis=0)
+    ids = (ids, exchange(ids, core=1))
     rows = to_rows(psi)
     beside = exchange(beta[0], column=1)
     above = exchange(beta[0], chip=2)

time: 60.7 us -> 58.7 us (0.967)
  waiting for transfers between devices: 17.4 us -> 16.2 us
  Pallas kernels: 18.5 us -> 17.7 us
  starting transfers between devices: 21.3 us -> 22 us
  local copies, waits for them, and re-layouts: 2.34 us -> 1.73 us
    all_to_all x1 -> x0, waiting for transfers between devices: 5.75 us -> none  [body(): lax.all_to_all(jnp.broadcast_to(ids, (slabs, *ids.shape[1:])), 'slab', 0,...]
    ppermute x6 -> x10, starting transfers between devices: 7.44 us -> 12.5 us  [exchange(): return lax.ppermute(x, 'slab', [(i, i ^ turned) for i in range(slabs)])]
    ppermute x6 -> x10, waiting for transfers between devices: 1.69 us -> 5.98 us  [exchange(): return lax.ppermute(x, 'slab', [(i, i ^ turned) for i in range(slabs)])]
    all_to_all x1 -> x0, starting transfers between devices: 3.34 us -> none  [body(): lax.all_to_all(jnp.broadcast_to(ids, (slabs, *ids.shape[1:])), 'slab', 0,...]
    ppermute x3, waiting for transfers between devices: 5.17 us -> 7.82 us  [exchange(): return lax.ppermute(x, ('band', 'slab'), pairs)]
    ppermute x5, waiting for transfers between devices: 4.76 us -> 2.44 us  [exchange(): return lax.ppermute(x, 'band', [(i, i ^ column) for i in range(columns)])]
    ppermute x3, starting transfers between devices: 4.8 us -> 3.89 us  [exchange(): return lax.ppermute(x, ('band', 'slab'), pairs)]
    pallas_call x5, Pallas kernels: 12.3 us -> 11.5 us  [the longest x2 4.78 us: back_project(): pl.pallas_call(kernel, in_specs=[SMEM_SPEC] + [VMEM_SPEC] * (4 + len(tabl...]
  transfers between devices with their start and end apart: 15 -> 18, of which waited for: 10 -> 11; matrix products, arithmetic and copies ran while one was open for 3% -> 0% of each run, Pallas kernels for 18% -> 17%
where the time goes in v5:
time: 58.7 us; the launch traced here: 58.5 us
  starting transfers between devices  22 us (37%)
  Pallas kernels  17.7 us (30%)
  waiting for transfers between devices  16.2 us (28%)
  local copies, waits for them, and re-layouts  1.73 us (3%)
  other arithmetic  0.79 us (1%)
    ppermute x10, starting transfers between devices, exchange(): return lax.ppermute(x, 'slab', [(i, i ^ turned) for i in range(slabs)])  12.5 us
    ppermute x3, waiting for transfers between devices, exchange(): return lax.ppermute(x, ('band', 'slab'), pairs)  7.82 us
    ppermute x10, waiting for transfers between devices, exchange(): return lax.ppermute(x, 'slab', [(i, i ^ turned) for i in range(slabs)])  5.98 us
    ppermute x5, starting transfers between devices, exchange(): return lax.ppermute(x, 'band', [(i, i ^ column) for i in range(columns)])  5.58 us
    pallas_call x2, Pallas kernels, place_rows(): pl.pallas_call(functools.partial(place_kernel, chips, wanted), grid_spec=...  5.48 us
    pallas_call x2, Pallas kernels, back_project(): pl.pallas_call(kernel, in_specs=[SMEM_SPEC] + [VMEM_SPEC] * (4 + len(tabl...  4.78 us
    pallas_call x2, Pallas kernels, project(): pl.pallas_call(kernel, in_specs=[SMEM_SPEC] + [VMEM_SPEC] * (4 + bands +...  4.7 us
    ppermute x3, starting transfers between devices, exchange(): return lax.ppermute(x, ('band', 'slab'), pairs)  3.89 us
  transfers between devices with their start and end apart: 18, of which 11 were waited for; matrix products, arithmetic and copies ran while one was open for 0% of the time, Pallas kernels for 17%

profile of v5, /device:TPU:0, one launch (start us, length us, event | category | flops | bytes accessed | tf_op | source)
XLA Modules:
  0.0 58.5 jit_solution(12061288589753687233)
XLA Ops:
  0.0 0.7 %pad_add_fusion = s32[2,512]{1,0:T(2,128)S(1)} fusion(s32[1,512]{1,0:T(1,128)} %param.8, s32[1,512]{1,0:T(1,128)} %param.9), kind=kLoop, calls=%fused_computation.8 | loop fusion | flops 1024 | bytes 8192 | tf_op jit(solution)/shard_map/concatenate | solution.py:340
  0.7 5.1 %collective-permute-start.2 = (s32[1,8,128]{2,1,0:T(8,128)S(1)}, s32[1,8,128]{2,1,0:T(8,128)S(1)}, u32[]{:S(2)}, u32[]{:S(2)}) collective-permute-start(s32[1,8,128]{2,1,0:T(8,128)S(1)} %reshape.6), channel_id=1, source_target_pairs={{0,6},{1,7},{2,4},{3,5},{4,2},{5,3},{6,0},{7,1},{8,14},{9,15},{10,... | collective-permute-start | bytes 12296 | tf_op jit(solution)/shard_map/ppermute | solution.py:331
  5.8 0.0 collective-permute-start.1
  5.8 0.6 %collective-permute-start = (s32[1,8,128]{2,1,0:T(8,128)S(1)}, s32[1,8,128]{2,1,0:T(8,128)S(1)}, u32[]{:S(2)}, u32[]{:S(2)}) collective-permute-start(s32[1,8,128]{2,1,0:T(8,128)S(1)} %reshape.6), channel_id=1, source_target_pairs={{0,2},{1,3},{2,0},{3,1},{4,6},{5,7},{6,4},{7,5},{8,10},{9,11},{10,... | collective-permute-start | bytes 12296 | tf_op jit(solution)/shard_map/ppermute | solution.py:331
  6.5 2.3 %collective-permute-start.6 = (bf16[128,1152]{1,0:T(8,128)(2,1)}, bf16[128,1152]{1,0:T(8,128)(2,1)S(1)}, u32[]{:S(2)}, u32[]{:S(2)}) collective-permute-start(bf16[128,1152]{1,0:T(8,128)(2,1)} %bitcast.10), channel_id=1, source_target_pairs={{0,4},{1,5},{2,6},{3,7},{4,0},{5,1},{6,2},{7,3},{8,12},{9,13},{10,... | collective-permute-start | bytes 884744 | tf_op jit(solution)/shard_map/ppermute | solution.py:331
  8.8 1.5 %collective-permute-start.4 = (bf16[128,1152]{1,0:T(8,128)(2,1)}, bf16[128,1152]{1,0:T(8,128)(2,1)S(1)}, u32[]{:S(2)}, u32[]{:S(2)}) collective-permute-start(bf16[128,1152]{1,0:T(8,128)(2,1)} %bitcast.11), channel_id=1, source_target_pairs={{0,8},{8,0},{16,24},{24,16},{1,9},{9,1},{17,25},{25,17},{2,10},{10... | collective-permute-start | bytes 884744 | tf_op jit(solution)/shard_map/ppermute | solution.py:333
  10.2 0.0 collective-permute-done
  10.3 0.1 collective-permute-done.1
  10.4 0.0 collective-permute-done.2
  10.4 0.1 collective-permute-start.3
  10.4 0.1 pad_add_fusion.1.place_ref
  10.5 1.6 %copy-done = bf16[1,524288]{1,0:T(2,128)(2,1)S(1)} copy-done((bf16[1,524288]{1,0:T(2,128)(2,1)S(1)}, bf16[1,524288]{1,0:T(2,128)(2,1)}, u32[]{:S(2)}) %copy-start) | copy-done | bytes 1048600
  12.1 0.6 %shard_map.64.rows_ref = bf16[4096,128]{1,0:T(8,128)(2,1)S(1)} custom-call(bf16[1,524288]{1,0:T(2,128)(2,1)S(1)} %copy-done), custom_call_target="tpu_custom_call" | custom-call | tf_op jit(solution)/shard_map/pallas_call | solution.py:85
  12.8 0.0 collective-permute-done.3.other_ids.refs_1_
  12.8 2.1 %shard_map.65 = (bf16[512,128]{1,0:T(8,128)(2,1)S(1)}, bf16[512,128]{1,0:T(8,128)(2,1)S(1)}, bf16[512,128]{1,0:T(8,128)(2,1)S(1)}, bf16[512,128]{1,0:T(8,128)(2,1)S(1)}) custom-call(s32[3]{0:T(128)S(1)} %pad_add_fusion.1.place_ref, s32[4,8,128]{2,1,0:T(8,128)S(1)} %constant_dynamic-update-slice_fusion.own_ids.refs_0_, ...), custom_call_target="tpu_custom_call" | custom-call | bytes 10000000 | tf_op jit(solution)/shard_map/pallas_call | solution.py:130
  14.8 2.0 %collective-permute-start.7 = (bf16[512,128]{1,0:T(8,128)(2,1)S(1)}, bf16[512,128]{1,0:T(8,128)(2,1)S(1)}, u32[]{:S(2)}, u32[]{:S(2)}) collective-permute-start(bf16[512,128]{1,0:T(8,128)(2,1)S(1)} %get-tuple-element.20), channel_id=1, source_target_pairs={{0,2},{1,3},{2,0},{3,1},{4,6},{5,7},{6,4},{7,5},{8,10},{9,11},{10,... | collective-permute-start | bytes 393224 | tf_op jit(solution)/shard_map/ppermute | solution.py:331
  16.9 1.5 %collective-permute-start.8 = (bf16[512,128]{1,0:T(8,128)(2,1)S(1)}, bf16[512,128]{1,0:T(8,128)(2,1)S(1)}, u32[]{:S(2)}, u32[]{:S(2)}) collective-permute-start(bf16[512,128]{1,0:T(8,128)(2,1)S(1)} %get-tuple-element.21), channel_id=1, source_target_pairs={{0,16},{8,24},{16,0},{24,8},{1,17},{9,25},{17,1},{25,9},{2,18},{10... | collective-permute-start | bytes 393224 | tf_op jit(solution)/shard_map/ppermute | solution.py:333
  18.4 0.0 collective-permute-start.9
  18.4 0.0 collective-permute-done.4
  18.4 3.8 %collective-permute-done.6 = bf16[128,1152]{1,0:T(8,128)(2,1)S(1)} collective-permute-done((bf16[128,1152]{1,0:T(8,128)(2,1)}, bf16[128,1152]{1,0:T(8,128)(2,1)S(1)}, u32[]{:S(2)}, u32[]{:S(2)}) %collective-permute-start.6) | collective-permute-done | bytes 294944 | tf_op jit(solution)/shard_map/ppermute | solution.py:331
  22.2 1.5 %collective-permute-start.10 = (bf16[128,1152]{1,0:T(8,128)(2,1)S(1)}, bf16[128,1152]{1,0:T(8,128)(2,1)S(1)}, u32[]{:S(2)}, u32[]{:S(2)}) collective-permute-start(bf16[128,1152]{1,0:T(8,128)(2,1)S(1)} %collective-permute-done.6), channel_id=1, source_target_pairs={{0,8},{8,0},{16,24},{24,16},{1,9},{9,1},{17,25},{25,17},{2,10},{10... | collective-permute-start | bytes 884744 | tf_op jit(solution)/shard_map/ppermute | solution.py:333
  23.8 1.2 %collective-permute-done.7.rest_1_ = bf16[512,128]{1,0:T(8,128)(2,1)S(1)} collective-permute-done((bf16[512,128]{1,0:T(8,128)(2,1)S(1)}, bf16[512,128]{1,0:T(8,128)(2,1)S(1)}, u32[]{:S(2)}, u32[]{:S(2)}) %collective-permute-start.7) | collective-permute-done | bytes 131104 | tf_op jit(solution)/shard_map/ppermute | solution.py:331
  25.0 0.0 collective-permute-done.8.rest_2_
  25.0 3.7 %collective-permute-done.9.rest_3_ = bf16[512,128]{1,0:T(8,128)(2,1)S(1)} collective-permute-done((bf16[512,128]{1,0:T(8,128)(2,1)S(1)}, bf16[512,128]{1,0:T(8,128)(2,1)S(1)}, u32[]{:S(2)}, u32[]{:S(2)}) %collective-permute-start.9) | collective-permute-done | bytes 131104 | tf_op jit(solution)/shard_map/ppermute | solution.py:335
  28.7 0.1 collective-permute-start.5
  28.8 0.0 copy-start.1
  28.8 0.0 copy-start.2
  28.9 1.4 %collective-permute-done.10 = bf16[128,1152]{1,0:T(8,128)(2,1)S(1)} collective-permute-done((bf16[128,1152]{1,0:T(8,128)(2,1)S(1)}, bf16[128,1152]{1,0:T(8,128)(2,1)S(1)}, u32[]{:S(2)}, u32[]{:S(2)}) %collective-permute-start.10) | collective-permute-done | bytes 294944 | tf_op jit(solution)/shard_map/ppermute | solution.py:333
  30.3 0.1 collective-permute-start.11
  30.4 0.3 collective-permute-done.5.other_ref.rest_1_
  30.7 2.3 %shard_map.66.rest_4_ = f32[96,128]{1,0:T(8,128)S(1)} custom-call(s32[3]{0:T(128)S(1)} %pad_add_fusion.1.place_ref, s32[4,8,128]{2,1,0:T(8,128)S(1)} %constant_dynamic-update-slice_fusion.own_ids.refs_0_, s32[4,8,128]{2,1,0:T(8,128)S(1)} %collective-permute-done.3.other_ids.refs_1_, ...), custom_call_target="tpu_custom_call" | custom-call | bytes 30000000 | tf_op jit(solution)/shard_map/pallas_call | solution.py:195
  33.1 2.4 %shard_map.67.rest_4_ = f32[96,128]{1,0:T(8,128)S(1)} custom-call(s32[3]{0:T(128)S(1)} %pad_add_fusion.1.place_ref, s32[4,8,128]{2,1,0:T(8,128)S(1)} %constant_dynamic-update-slice_fusion.own_ids.refs_0_, s32[4,8,128]{2,1,0:T(8,128)S(1)} %collective-permute-done.3.other_ids.refs_1_, ...), custom_call_target="tpu_custom_call" | custom-call | bytes 30000000 | tf_op jit(solution)/shard_map/pallas_call | solution.py:195
  35.4 2.0 %collective-permute-start.14 = (f32[96,128]{1,0:T(8,128)S(1)}, f32[96,128]{1,0:T(8,128)S(1)}, u32[]{:S(2)}, u32[]{:S(2)}) collective-permute-start(f32[96,128]{1,0:T(8,128)S(1)} %shard_map.67.rest_4_), channel_id=1, source_target_pairs={{0,18},{1,19},{2,16},{3,17},{4,22},{5,23},{6,20},{7,21},{8,26},{9,... | collective-permute-start | bytes 147464 | tf_op jit(solution)/shard_map/ppermute | solution.py:335
  37.4 0.5 collective-permute-start.13
  37.9 1.1 %collective-permute-start.12 = (f32[96,128]{1,0:T(8,128)S(1)}, f32[96,128]{1,0:T(8,128)S(1)}, u32[]{:S(2)}, u32[]{:S(2)}) collective-permute-start(f32[96,128]{1,0:T(8,128)S(1)} %shard_map.67.rest_4_), channel_id=1, source_target_pairs={{0,2},{1,3},{2,0},{3,1},{4,6},{5,7},{6,4},{7,5},{8,10},{9,11},{10,... | collective-permute-start | bytes 147464 | tf_op jit(solution)/shard_map/ppermute | solution.py:331
  39.0 1.5 %collective-permute-done.14.rest_7_ = f32[96,128]{1,0:T(8,128)S(1)} collective-permute-done((f32[96,128]{1,0:T(8,128)S(1)}, f32[96,128]{1,0:T(8,128)S(1)}, u32[]{:S(2)}, u32[]{:S(2)}) %collective-permute-start.14) | collective-permute-done | bytes 49184 | tf_op jit(solution)/shard_map/ppermute | solution.py:335
  40.5 1.0 %collective-permute-done.13.rest_6_ = f32[96,128]{1,0:T(8,128)S(1)} collective-permute-done((f32[96,128]{1,0:T(8,128)S(1)}, f32[96,128]{1,0:T(8,128)S(1)}, u32[]{:S(2)}, u32[]{:S(2)}) %collective-permute-start.13) | collective-permute-done | bytes 49184 | tf_op jit(solution)/shard_map/ppermute | solution.py:333
  41.5 0.5 collective-permute-done.12.rest_5_
  42.0 2.4 %shard_map.69 = (bf16[512,128]{1,0:T(8,128)(2,1)S(1)}, bf16[512,128]{1,0:T(8,128)(2,1)S(1)}) custom-call(s32[3]{0:T(128)S(1)} %pad_add_fusion.1.place_ref, s32[4,8,128]{2,1,0:T(8,128)S(1)} %constant_dynamic-update-slice_fusion.own_ids.refs_0_, s32[4,8,128]{2,1,0:T(8,128)S(1)} %collective-permute-done.3.other_ids.refs_1_, s32[1,128]{1,0:T(1,128)S(1)} %bitcast.8, ...), custom_call_target="tpu_custom_call" | custom-call | tf_op jit(solution)/shard_map/pallas_call | solution.py:254
  44.4 1.1 %collective-permute-start.16 = (bf16[512,128]{1,0:T(8,128)(2,1)S(1)}, bf16[512,128]{1,0:T(8,128)(2,1)S(1)}, u32[]{:S(2)}, u32[]{:S(2)}) collective-permute-start(bf16[512,128]{1,0:T(8,128)(2,1)S(1)} %get-tuple-element.27), channel_id=1, source_target_pairs={{0,2},{1,3},{2,0},{3,1},{4,6},{5,7},{6,4},{7,5},{8,10},{9,11},{10,... | collective-permute-start | bytes 393224 | tf_op jit(solution)/shard_map/ppermute | solution.py:331
  45.5 1.9 %collective-permute-start.17 = (bf16[512,128]{1,0:T(8,128)(2,1)S(1)}, bf16[512,128]{1,0:T(8,128)(2,1)S(1)}, u32[]{:S(2)}, u32[]{:S(2)}) collective-permute-start(bf16[512,128]{1,0:T(8,128)(2,1)S(1)} %get-tuple-element.28), channel_id=1, source_target_pairs={{0,18},{1,19},{2,16},{3,17},{4,22},{5,23},{6,20},{7,21},{8,26},{9,... | collective-permute-start | bytes 393224 | tf_op jit(solution)/shard_map/ppermute | solution.py:335
  47.4 2.4 %shard_map.68 = (bf16[512,128]{1,0:T(8,128)(2,1)S(1)}, bf16[512,128]{1,0:T(8,128)(2,1)S(1)}) custom-call(s32[3]{0:T(128)S(1)} %pad_add_fusion.1.place_ref, s32[4,8,128]{2,1,0:T(8,128)S(1)} %constant_dynamic-update-slice_fusion.own_ids.refs_0_, s32[4,8,128]{2,1,0:T(8,128)S(1)} %collective-permute-done.3.other_ids.refs_1_, s32[1,128]{1,0:T(1,128)S(1)} %bitcast.9, ...), custom_call_target="tpu_custom_call" | custom-call | tf_op jit(solution)/shard_map/pallas_call | solution.py:254
  49.8 0.6 collective-permute-start.15
  50.4 0.1 collective-permute-done.16.refs_2_
  50.5 2.6 %collective-permute-done.17.refs_3_ = bf16[512,128]{1,0:T(8,128)(2,1)S(1)} collective-permute-done((bf16[512,128]{1,0:T(8,128)(2,1)S(1)}, bf16[512,128]{1,0:T(8,128)(2,1)S(1)}, u32[]{:S(2)}, u32[]{:S(2)}) %collective-permute-start.17) | collective-permute-done | bytes 131104 | tf_op jit(solution)/shard_map/ppermute | solution.py:335
  53.1 2.7 %shard_map.70.refs_4_ = bf16[1,524288]{1,0:T(2,128)(2,1)} custom-call(s32[3]{0:T(128)S(1)} %pad_add_fusion.1.place_ref, s32[4,8,128]{2,1,0:T(8,128)S(1)} %constant_dynamic-update-slice_fusion.own_ids.refs_0_, s32[4,8,128]{2,1,0:T(8,128)S(1)} %collective-permute-done.3.other_ids.refs_1_, bf16[512,128]{1,0:T(8,128)(2,1)S(1)} %collective-permute-done.16.refs_2_, ...), custom_call_target="tpu_custom_call" | custom-call | tf_op jit(solution)/shard_map/pallas_call | solution.py:307
  55.8 0.0 collective-permute-done.15.refs_3_
  55.8 2.7 %shard_map.71 = bf16[1,524288]{1,0:T(2,128)(2,1)} custom-call(s32[3]{0:T(128)S(1)} %pad_add_fusion.1.place_ref, s32[4,8,128]{2,1,0:T(8,128)S(1)} %constant_dynamic-update-slice_fusion.own_ids.refs_0_, s32[4,8,128]{2,1,0:T(8,128)S(1)} %collective-permute-done.3.other_ids.refs_1_, ...), custom_call_target="tpu_custom_call", output_to_operand_aliasing={{}: (5, {})} | custom-call | tf_op jit(solution)/shard_map/pallas_call | solution.py:307
  (15 shorter events, 0.1 us)
Async XLA Ops:
  0.7 9.6 %collective-permute-start.2 = (s32[1,8,128]{2,1,0:T(8,128)S(1)}, s32[1,8,128]{2,1,0:T(8,128)S(1)}, u32[]{:S(2)}, u32[]{:S(2)}) collective-permute-start(s32[1,8,128]{2,1,0:T(8,128)S(1)} %reshape.6), channel_id=1, source_target_pairs={{0,6},{1,7},{2,4},{3,5},{4,2},{5,3},{6,0},{7,1},{8,14},{9,15},{10,... | collective-permute-start | bytes 12296 | tf_op jit(solution)/shard_map/ppermute | solution.py:331
  5.8 4.5 %collective-permute-start.1 = (s32[1,8,128]{2,1,0:T(8,128)S(1)}, s32[1,8,128]{2,1,0:T(8,128)S(1)}, u32[]{:S(2)}, u32[]{:S(2)}) collective-permute-start(s32[1,8,128]{2,1,0:T(8,128)S(1)} %reshape.6), channel_id=1, source_target_pairs={{0,4},{1,5},{2,6},{3,7},{4,0},{5,1},{6,2},{7,3},{8,12},{9,13},{10,... | collective-permute-start | bytes 12296 | tf_op jit(solution)/shard_map/ppermute | solution.py:331
  5.8 4.4 %collective-permute-start = (s32[1,8,128]{2,1,0:T(8,128)S(1)}, s32[1,8,128]{2,1,0:T(8,128)S(1)}, u32[]{:S(2)}, u32[]{:S(2)}) collective-permute-start(s32[1,8,128]{2,1,0:T(8,128)S(1)} %reshape.6), channel_id=1, source_target_pairs={{0,2},{1,3},{2,0},{3,1},{4,6},{5,7},{6,4},{7,5},{8,10},{9,11},{10,... | collective-permute-start | bytes 12296 | tf_op jit(solution)/shard_map/ppermute | solution.py:331
  6.5 15.8 %collective-permute-start.6 = (bf16[128,1152]{1,0:T(8,128)(2,1)}, bf16[128,1152]{1,0:T(8,128)(2,1)S(1)}, u32[]{:S(2)}, u32[]{:S(2)}) collective-permute-start(bf16[128,1152]{1,0:T(8,128)(2,1)} %bitcast.10), channel_id=1, source_target_pairs={{0,4},{1,5},{2,6},{3,7},{4,0},{5,1},{6,2},{7,3},{8,12},{9,13},{10,... | collective-permute-start | bytes 884744 | tf_op jit(solution)/shard_map/ppermute | solution.py:331
  8.8 9.7 %collective-permute-start.4 = (bf16[128,1152]{1,0:T(8,128)(2,1)}, bf16[128,1152]{1,0:T(8,128)(2,1)S(1)}, u32[]{:S(2)}, u32[]{:S(2)}) collective-permute-start(bf16[128,1152]{1,0:T(8,128)(2,1)} %bitcast.11), channel_id=1, source_target_pairs={{0,8},{8,0},{16,24},{24,16},{1,9},{9,1},{17,25},{25,17},{2,10},{10... | collective-permute-start | bytes 884744 | tf_op jit(solution)/shard_map/ppermute | solution.py:333
  10.4 2.4 %collective-permute-start.3 = (s32[4,8,128]{2,1,0:T(8,128)S(1)}, s32[4,8,128]{2,1,0:T(8,128)S(1)}, u32[]{:S(2)}, u32[]{:S(2)}) collective-permute-start(s32[4,8,128]{2,1,0:T(8,128)S(1)} %constant_dynamic-update-slice_fusion.own_ids.refs_0_), channel_id=1, source_target_pairs={{0,1},{1,0},{2,3},{3,2},{4,5},{5,4},{6,7},{7,6},{8,9},{9,8},{10,11... | collective-permute-start | bytes 49160 | tf_op jit(solution)/shard_map/ppermute | solution.py:331
  10.5 1.6 %copy-start = (bf16[1,524288]{1,0:T(2,128)(2,1)S(1)}, bf16[1,524288]{1,0:T(2,128)(2,1)}, u32[]{:S(2)}) copy-start(bf16[1,524288]{1,0:T(2,128)(2,1)} %psi_ref.1) | copy-start | bytes 3145732
  12.1 6.3 %copy-start.3 = (bf16[1,128,1152]{2,1,0:T(8,128)(2,1)S(1)}, bf16[1,128,1152]{2,1,0:T(8,128)(2,1)}, u32[]{:S(2)}) copy-start(bf16[1,128,1152]{2,1,0:T(8,128)(2,1)} %param.7) | copy-start | bytes 884740
  14.8 10.1 %collective-permute-start.7 = (bf16[512,128]{1,0:T(8,128)(2,1)S(1)}, bf16[512,128]{1,0:T(8,128)(2,1)S(1)}, u32[]{:S(2)}, u32[]{:S(2)}) collective-permute-start(bf16[512,128]{1,0:T(8,128)(2,1)S(1)} %get-tuple-element.20), channel_id=1, source_target_pairs={{0,2},{1,3},{2,0},{3,1},{4,6},{5,7},{6,4},{7,5},{8,10},{9,11},{10,... | collective-permute-start | bytes 393224 | tf_op jit(solution)/shard_map/ppermute | solution.py:331
  16.9 8.1 %collective-permute-start.8 = (bf16[512,128]{1,0:T(8,128)(2,1)S(1)}, bf16[512,128]{1,0:T(8,128)(2,1)S(1)}, u32[]{:S(2)}, u32[]{:S(2)}) collective-permute-start(bf16[512,128]{1,0:T(8,128)(2,1)S(1)} %get-tuple-element.21), channel_id=1, source_target_pairs={{0,16},{8,24},{16,0},{24,8},{1,17},{9,25},{17,1},{25,9},{2,18},{10... | collective-permute-start | bytes 393224 | tf_op jit(solution)/shard_map/ppermute | solution.py:333
  18.4 10.3 %collective-permute-start.9 = (bf16[512,128]{1,0:T(8,128)(2,1)S(1)}, bf16[512,128]{1,0:T(8,128)(2,1)S(1)}, u32[]{:S(2)}, u32[]{:S(2)}) collective-permute-start(bf16[512,128]{1,0:T(8,128)(2,1)S(1)} %get-tuple-element.22), channel_id=1, source_target_pairs={{0,18},{1,19},{2,16},{3,17},{4,22},{5,23},{6,20},{7,21},{8,26},{9,... | collective-permute-start | bytes 393224 | tf_op jit(solution)/shard_map/ppermute | solution.py:335
  22.2 8.0 %collective-permute-start.10 = (bf16[128,1152]{1,0:T(8,128)(2,1)S(1)}, bf16[128,1152]{1,0:T(8,128)(2,1)S(1)}, u32[]{:S(2)}, u32[]{:S(2)}) collective-permute-start(bf16[128,1152]{1,0:T(8,128)(2,1)S(1)} %collective-permute-done.6), channel_id=1, source_target_pairs={{0,8},{8,0},{16,24},{24,16},{1,9},{9,1},{17,25},{25,17},{2,10},{10... | collective-permute-start | bytes 884744 | tf_op jit(solution)/shard_map/ppermute | solution.py:333
  28.7 2.0 %collective-permute-start.5 = (bf16[256,1152]{1,0:T(8,128)(2,1)S(1)}, bf16[256,1152]{1,0:T(8,128)(2,1)S(1)}, u32[]{:S(2)}, u32[]{:S(2)}) collective-permute-start(bf16[256,1152]{1,0:T(8,128)(2,1)S(1)} %constant_dynamic-update-slice_fusion.4.own_ref.rest_0_), channel_id=1, source_target_pairs={{0,1},{1,0},{2,3},{3,2},{4,5},{5,4},{6,7},{7,6},{8,9},{9,8},{10,11... | collective-permute-start | bytes 1769480 | tf_op jit(solution)/shard_map/ppermute | solution.py:331
  28.8 13.2 %copy-start.1 = (f32[128,18,18]{0,2,1:T(8,128)S(1)}, f32[128,18,18]{0,2,1:T(8,128)}, u32[]{:S(2)}) copy-start(f32[128,18,18]{0,2,1:T(8,128)} %param.11) | copy-start | bytes 497668
  28.8 13.2 %copy-start.2 = (s32[128]{0:T(128)S(1)}, s32[128]{0:T(128)}, u32[]{:S(2)}) copy-start(s32[128]{0:T(128)} %param.10) | copy-start | bytes 1540
  30.3 2.8 %collective-permute-start.11 = (bf16[256,1152]{1,0:T(8,128)(2,1)S(1)}, bf16[256,1152]{1,0:T(8,128)(2,1)S(1)}, u32[]{:S(2)}, u32[]{:S(2)}) collective-permute-start(bf16[256,1152]{1,0:T(8,128)(2,1)S(1)} %constant_dynamic-update-slice_fusion.6.own_ref.rest_2_), channel_id=1, source_target_pairs={{0,1},{1,0},{2,3},{3,2},{4,5},{5,4},{6,7},{7,6},{8,9},{9,8},{10,11... | collective-permute-start | bytes 1769480 | tf_op jit(solution)/shard_map/ppermute | solution.py:331
  35.4 5.1 %collective-permute-start.14 = (f32[96,128]{1,0:T(8,128)S(1)}, f32[96,128]{1,0:T(8,128)S(1)}, u32[]{:S(2)}, u32[]{:S(2)}) collective-permute-start(f32[96,128]{1,0:T(8,128)S(1)} %shard_map.67.rest_4_), channel_id=1, source_target_pairs={{0,18},{1,19},{2,16},{3,17},{4,22},{5,23},{6,20},{7,21},{8,26},{9,... | collective-permute-start | bytes 147464 | tf_op jit(solution)/shard_map/ppermute | solution.py:335
  37.4 4.1 %collective-permute-start.13 = (f32[96,128]{1,0:T(8,128)S(1)}, f32[96,128]{1,0:T(8,128)S(1)}, u32[]{:S(2)}, u32[]{:S(2)}) collective-permute-start(f32[96,128]{1,0:T(8,128)S(1)} %shard_map.67.rest_4_), channel_id=1, source_target_pairs={{0,16},{8,24},{16,0},{24,8},{1,17},{9,25},{17,1},{25,9},{2,18},{10... | collective-permute-start | bytes 147464 | tf_op jit(solution)/shard_map/ppermute | solution.py:333
  37.9 4.1 %collective-permute-start.12 = (f32[96,128]{1,0:T(8,128)S(1)}, f32[96,128]{1,0:T(8,128)S(1)}, u32[]{:S(2)}, u32[]{:S(2)}) collective-permute-start(f32[96,128]{1,0:T(8,128)S(1)} %shard_map.67.rest_4_), channel_id=1, source_target_pairs={{0,2},{1,3},{2,0},{3,1},{4,6},{5,7},{6,4},{7,5},{8,10},{9,11},{10,... | collective-permute-start | bytes 147464 | tf_op jit(solution)/shard_map/ppermute | solution.py:331
  44.4 6.1 %collective-permute-start.16 = (bf16[512,128]{1,0:T(8,128)(2,1)S(1)}, bf16[512,128]{1,0:T(8,128)(2,1)S(1)}, u32[]{:S(2)}, u32[]{:S(2)}) collective-permute-start(bf16[512,128]{1,0:T(8,128)(2,1)S(1)} %get-tuple-element.27), channel_id=1, source_target_pairs={{0,2},{1,3},{2,0},{3,1},{4,6},{5,7},{6,4},{7,5},{8,10},{9,11},{10,... | collective-permute-start | bytes 393224 | tf_op jit(solution)/shard_map/ppermute | solution.py:331
  45.5 7.5 %collective-permute-start.17 = (bf16[512,128]{1,0:T(8,128)(2,1)S(1)}, bf16[512,128]{1,0:T(8,128)(2,1)S(1)}, u32[]{:S(2)}, u32[]{:S(2)}) collective-permute-start(bf16[512,128]{1,0:T(8,128)(2,1)S(1)} %get-tuple-element.28), channel_id=1, source_target_pairs={{0,18},{1,19},{2,16},{3,17},{4,22},{5,23},{6,20},{7,21},{8,26},{9,... | collective-permute-start | bytes 393224 | tf_op jit(solution)/shard_map/ppermute | solution.py:335
  49.8 6.0 %collective-permute-start.15 = (bf16[512,128]{1,0:T(8,128)(2,1)S(1)}, bf16[512,128]{1,0:T(8,128)(2,1)S(1)}, u32[]{:S(2)}, u32[]{:S(2)}) collective-permute-start(bf16[512,128]{1,0:T(8,128)(2,1)S(1)} %get-tuple-element.26), channel_id=1, source_target_pairs={{0,16},{8,24},{16,0},{24,8},{1,17},{9,25},{17,1},{25,9},{2,18},{10... | collective-permute-start | bytes 393224 | tf_op jit(solution)/shard_map/ppermute | solution.py:333

commit v6 on v5

--- a/solution.py
+++ b/solution.py
@@ -19,7 +19,6 @@
 F32 = jnp.float32
 BF16 = jnp.bfloat16
 VMEM_SPEC = pl.BlockSpec(memory_space=pltpu.VMEM)
-SMEM_SPEC = pl.BlockSpec(memory_space=pltpu.SMEM)
 PARAMS = pltpu.CompilerParams(vmem_limit_bytes=40 * 1024 * 1024)
 
 
@@ -40,9 +39,14 @@
     return lax.broadcasted_iota(jnp.int32, shape, axis)
 
 
-def slab_index(place_ref, turned, slab):
-    core = place_ref[0] if slab == 0 else CORES - 1 - place_ref[0]
-    return jnp.bitwise_xor(place_ref[2], turned) * CORES + core
+def own_place():
+    position = lax.axis_index("slab")
+    return jnp.bitwise_and(position, CORES - 1), lax.axis_index("band"), jnp.right_shift(position, 1)
+
+
+def slab_index(place, turned, slab):
+    core = place[0] if slab == 0 else CORES - 1 - place[0]
+    return jnp.bitwise_xor(place[2], turned) * CORES + core
 
 
 def owner(turned_chip, turned_column):
@@ -53,17 +57,17 @@
     return range(half_index * PIECES // HALVES, (half_index + 1) * PIECES // HALVES)
 
 
-def slot_ids(ids_ref, place_ref, turned_chip, turned_column, kind):
+def slot_ids(ids_ref, place, turned_chip, turned_column, kind):
     slot_rows = ids_ref.shape[1] // 2
     share = slot_rows // PARTNERS
-    first = kind * slot_rows + jnp.bitwise_xor(place_ref[1], turned_column) * share
+    first = kind * slot_rows + jnp.bitwise_xor(place[1], turned_column) * share
     return [ids_ref[turned_chip, pl.ds(first + i, 1), :] for i in range(share)]
 
 
-def atom_hits(ids_ref, place_ref, pieces):
+def atom_hits(ids_ref, place, pieces):
     lane = iota((LANES, LANES), 1)
     for piece in pieces:
-        for atoms in slot_ids(ids_ref, place_ref, piece & 2, piece & 1, 1):
+        for atoms in slot_ids(ids_ref, place, piece & 2, piece & 1, 1):
             yield (down(atoms) == lane).astype(BF16)
 
 
@@ -91,18 +95,18 @@
     )(psi)
 
 
-def gather_kernel(place_ref, ids_refs, rows_ref, out_refs):
+def gather_kernel(ids_refs, rows_ref, out_refs):
     half = LANES // 2
     slab_rows = rows_ref.shape[0] // (CORES * CHIPS)
     lane = iota((LANES, LANES), 1)
     low = iota((half, LANES), 1) < half
     for chip in range(CHIPS):
         for slab in range(CORES):
-            index = slab_index(place_ref, chip, slab)
+            index = slab_index(own_place(), chip, slab)
             odds, hits, places = [], [], []
             for column in range(PARTNERS):
                 partner, piece = owner(chip, column)
-                ids = slot_ids(ids_refs[slab], place_ref, chip, column, 0)
+                ids = slot_ids(ids_refs[slab], own_place(), chip, column, 0)
                 for i, row in enumerate(ids):
                     blocks = down(row)
                     wanted = jnp.right_shift(blocks, 1)
@@ -121,23 +125,23 @@
                 out_ref[first : first + half, :] = jnp.where(low, lower, upper).astype(BF16)
 
 
-def gather(place, ids, rows):
+def gather(ids, rows):
     slots = CORES * PIECES * ids[0].shape[1] // 2 * LANES // PARTNERS
 
-    def kernel(place_ref, own_ids, other_ids, rows_ref, *out_refs):
-        gather_kernel(place_ref, (own_ids, other_ids), rows_ref, out_refs)
+    def kernel(own_ids, other_ids, rows_ref, *out_refs):
+        gather_kernel((own_ids, other_ids), rows_ref, out_refs)
 
     return pl.pallas_call(
         kernel,
-        in_specs=[SMEM_SPEC] + [VMEM_SPEC] * 3,
+        in_specs=[VMEM_SPEC] * 3,
         out_specs=[VMEM_SPEC] * PARTNERS,
         out_shape=[jax.ShapeDtypeStruct((slots // 2, LANES), BF16)] * PARTNERS,
         cost_estimate=pl.CostEstimate(flops=0, bytes_accessed=GATHER_BYTES, transcendentals=0),
         compiler_params=PARAMS,
-    )(place, *ids, rows)
-
-
-def project_kernel(projectors, padded, half_index, place_ref, ids_refs, table_refs, packed_refs, before_refs, coef_ref, picks_of, terms):
+    )(*ids, rows)
+
+
+def project_kernel(projectors, padded, half_index, ids_refs, table_refs, packed_refs, before_refs, coef_ref, picks_of, terms):
     bands = len(packed_refs)
     slots = table_refs[0].shape[0]
     pair_count = projectors // 2
@@ -160,7 +164,7 @@
             picks_of[band, i * LANES + half : (i + 1) * LANES, :] = jnp.where(left, turned, straight).astype(BF16)
     of_atom = []
     for slab, table_ref in enumerate(table_refs):
-        of_atom += atom_hits(ids_refs[slab], place_ref, pieces_of(half_index))
+        of_atom += atom_hits(ids_refs[slab], own_place(), pieces_of(half_index))
         for group in range(slots // GROUP):
             rows = slice(group * GROUP, (group + 1) * GROUP)
             first = slab * slots + group * GROUP
@@ -180,30 +184,30 @@
     coef_ref[...] = total + before_refs[0][...] if before_refs else total
 
 
-def project(place, ids, tables, picks, projectors, padded, half_index, before):
+def project(ids, tables, picks, projectors, padded, half_index, before):
     bands = len(picks)
     slots = tables[0].shape[0]
     width = projectors * bands * GROUP
 
-    def kernel(place_ref, own_ids, other_ids, own_ref, other_ref, *rest):
+    def kernel(own_ids, other_ids, own_ref, other_ref, *rest):
         ends = [bands, bands + len(before)]
         project_kernel(
-            projectors, padded, half_index, place_ref, (own_ids, other_ids), (own_ref, other_ref),
+            projectors, padded, half_index, (own_ids, other_ids), (own_ref, other_ref),
             rest[: ends[0]], rest[ends[0] : ends[1]], *rest[ends[1] :],
         )
 
     return pl.pallas_call(
         kernel,
-        in_specs=[SMEM_SPEC] + [VMEM_SPEC] * (4 + bands + len(before)),
+        in_specs=[VMEM_SPEC] * (4 + bands + len(before)),
         out_specs=VMEM_SPEC,
         out_shape=jax.ShapeDtypeStruct((bands * padded, LANES), F32),
         scratch_shapes=[pltpu.VMEM((bands, CORES * slots, LANES), BF16)] + [pltpu.VMEM((2 * CORES * slots, width), BF16)],
         cost_estimate=pl.CostEstimate(flops=0, bytes_accessed=PROJECT_BYTES, transcendentals=0),
         compiler_params=PARAMS,
-    )(place, *ids, *tables, *picks, *before)
-
-
-def apply_kernel(wanted, projectors, padded, place_ref, ids_refs, table_refs, count_ref, strength_ref, coef_refs, out_refs, wide_refs):
+    )(*ids, *tables, *picks, *before)
+
+
+def apply_kernel(wanted, projectors, padded, ids_refs, table_refs, count_ref, strength_ref, coef_refs, out_refs, wide_refs):
     pair_count = projectors // 2
     width = projectors * LANES // 2
     atom_total = strength_ref.shape[2]
@@ -226,7 +230,7 @@
         for half_index in range(HALVES):
             table_ref = table_refs[half_index * CORES + slab]
             blocks = table_ref.shape[0] // LANES
-            for i, of_atom in enumerate(atom_hits(ids_refs[slab], place_ref, pieces_of(half_index))):
+            for i, of_atom in enumerate(atom_hits(ids_refs[slab], own_place(), pieces_of(half_index))):
                 rows = slice(i * LANES, (i + 1) * LANES)
                 first = ((slab * HALVES + half_index) * blocks + i) * half
                 for wide_ref, out_ref in zip(wide_refs, out_refs):
@@ -240,28 +244,28 @@
                     out_ref[first : first + half, :] = packed.astype(BF16)
 
 
-def back_project(wanted, place, ids, tables, count, strength, coefs, projectors, padded):
+def back_project(wanted, ids, tables, count, strength, coefs, projectors, padded):
     slots = sum(table.shape[0] for table in tables)
     atom_total = strength.shape[2]
 
-    def kernel(place_ref, own_ids, other_ids, count_ref, strength_ref, *rest):
+    def kernel(own_ids, other_ids, count_ref, strength_ref, *rest):
         ends = [len(tables), len(tables) + len(coefs), len(tables) + len(coefs) + len(wanted)]
         apply_kernel(
-            wanted, projectors, padded, place_ref, (own_ids, other_ids), rest[: ends[0]], count_ref, strength_ref,
+            wanted, projectors, padded, (own_ids, other_ids), rest[: ends[0]], count_ref, strength_ref,
             rest[ends[0] : ends[1]], rest[ends[1] : ends[2]], rest[ends[2] :],
         )
 
     return pl.pallas_call(
         kernel,
-        in_specs=[SMEM_SPEC] + [VMEM_SPEC] * (4 + len(tables) + len(coefs)),
+        in_specs=[VMEM_SPEC] * (4 + len(tables) + len(coefs)),
         out_specs=[VMEM_SPEC] * len(wanted),
         out_shape=[jax.ShapeDtypeStruct((slots // 2, LANES), BF16)] * len(wanted),
         scratch_shapes=[pltpu.VMEM((atom_total, projectors * LANES // 2), BF16)] * len(wanted),
         compiler_params=PARAMS,
-    )(place, *ids, count, strength, *tables, *coefs)
-
-
-def place_kernel(chips, wanted, place_ref, *refs):
+    )(*ids, count, strength, *tables, *coefs)
+
+
+def place_kernel(chips, wanted, *refs):
     ids_refs, value_refs, out_ref = refs[:CORES], dict(zip(wanted, refs[CORES:])), refs[-1]
     step = pl.program_id(0)
     half = LANES // 2
@@ -272,11 +276,11 @@
         @pl.when(step == number)
         def _(chip=chip):
             for slab in range(CORES):
-                place = place_ref[0] if slab == 0 else CORES - 1 - place_ref[0]
+                place = own_place()[0] if slab == 0 else CORES - 1 - own_place()[0]
                 parts, wanted = [], []
                 for column in range(PARTNERS):
                     partner, piece = owner(chip, column)
-                    ids = slot_ids(ids_refs[slab], place_ref, chip, column, 0)
+                    ids = slot_ids(ids_refs[slab], own_place(), chip, column, 0)
                     for i, blocks in enumerate(ids):
                         wanted.append(jnp.right_shift(blocks, 1))
                         odd = jnp.bitwise_and(down(blocks), 1) == 1
@@ -299,31 +303,26 @@
                         out_ref[0:1, pl.ds(at, 2048)] = total[i * 16 : (i + 1) * 16].reshape(1, 2048)
 
 
-def place_rows(chips, place, ids, values, points, before):
+def place_rows(chips, ids, values, points, before):
     share = points // CHIPS
     wanted = tuple(values)
     small = (*ids, *values.values())
     apart = chips[1] ^ chips[0]
     return pl.pallas_call(
         functools.partial(place_kernel, chips, wanted),
-        grid_spec=pltpu.PrefetchScalarGridSpec(
-            num_scalar_prefetch=1,
-            grid=(len(chips),),
-            in_specs=[pl.BlockSpec(x.shape, lambda i, place, rank=x.ndim: (0,) * rank) for x in small]
-            + [pl.BlockSpec(memory_space=pl.ANY)] * len(before),
-            out_specs=pl.BlockSpec((1, share), lambda i, place: (0, jnp.bitwise_xor(place[2], chips[0] + i * apart))),
-        ),
+        grid=(len(chips),),
+        in_specs=[pl.BlockSpec(x.shape, lambda i, rank=x.ndim: (0,) * rank) for x in small]
+        + [pl.BlockSpec(memory_space=pl.ANY)] * len(before),
+        out_specs=pl.BlockSpec((1, share), lambda i: (0, jnp.bitwise_xor(own_place()[2], chips[0] + i * apart))),
         out_shape=jax.ShapeDtypeStruct((1, points), BF16),
-        input_output_aliases={1 + len(small): 0} if before else {},
+        input_output_aliases={len(small): 0} if before else {},
         compiler_params=PARAMS,
-    )(place, *small, *before)
+    )(*small, *before)
 
 
 def body(columns, slabs, psi, beta, pair_atom, pair_block, proj_count, strength):
     atom_total, projectors = strength.shape[:2]
     padded = -(-projectors // 8) * 8
-    position = lax.axis_index("slab").astype(jnp.int32)
-    place = jnp.stack([lax.rem(position, CORES), lax.axis_index("band").astype(jnp.int32), position // CORES])
 
     def exchange(x, chip=0, column=0, core=0):
         turned = chip * CORES + core
@@ -344,23 +343,23 @@
     beside = exchange(beta[0], column=1)
     above = exchange(beta[0], chip=2)
     corner = exchange(above, column=1)
-    picks = gather(place, ids, rows)
+    picks = gather(ids, rows)
     shape = (projectors, padded)
     first = jnp.concatenate([after(table, picks[0]) for table in (beta[0], beside)], axis=0)
     picks = partners(picks)
     first = (first, exchange(first, core=1))
-    coef = project(place, ids, first, picks, *shape, 0, ())
+    coef = project(ids, first, picks, *shape, 0, ())
     second = jnp.concatenate([after(table, *picks[1:]) for table in (above, corner)], axis=0)
     second = (second, exchange(second, core=1))
-    coef = project(place, ids, second, picks, *shape, 1, (coef,))
+    coef = project(ids, second, picks, *shape, 1, (coef,))
     coefs = partners([coef] * PARTNERS)
     count, strength = proj_count.reshape(1, atom_total), strength.transpose(1, 2, 0)
-    given = (place, ids, first + second, count, strength, coefs, *shape)
+    given = (ids, first + second, count, strength, coefs, *shape)
     outer = back_project((3, 1), *given)
     inner = back_project((2, 0), *given)
     results = partners([inner[1], outer[1], inner[0], outer[0]])
-    applied = place_rows((1, 3), place, ids, {1: results[1], 3: results[3]}, psi.shape[1], ())
-    return place_rows((0, 2), place, ids, {0: results[0], 2: results[2]}, psi.shape[1], (applied,))
+    applied = place_rows((1, 3), ids, {1: results[1], 3: results[3]}, psi.shape[1], ())
+    return place_rows((0, 2), ids, {0: results[0], 2: results[2]}, psi.shape[1], (applied,))
 
 
 def plain_project(grid_blocks, tables, atom_ids, block_ids, atom_total):

time: 58.7 us -> 56 us (0.954)
  Pallas kernels: 17.7 us -> 14 us
  waiting for transfers between devices: 16.2 us -> 17.3 us
    pallas_call x7, Pallas kernels: 17 us -> 13.3 us  [the longest x2 4.39 us: place_rows(): pl.pallas_call(functools.partial(place_kernel, chips, wanted), grid=(len(...]
    ppermute x10, waiting for transfers between devices: 5.98 us -> 6.85 us  [exchange(): return lax.ppermute(x, 'slab', [(i, i ^ turned) for i in range(slabs)])]
  transfers between devices with their start and end apart: 18 -> 18, of which waited for: 11 -> 11; matrix products, arithmetic and copies ran while one was open for 0% -> 0% of each run, Pallas kernels for 17% -> 14%
where the time goes in v6:
time: 56 us; the launch traced here: 55.8 us
  starting transfers between devices  22 us (39%)
  waiting for transfers between devices  17.3 us (31%)
  Pallas kernels  14 us (25%)
  local copies, waits for them, and re-layouts  1.73 us (3%)
  other arithmetic  0.71 us (1%)
    ppermute x10, starting transfers between devices, exchange(): return lax.ppermute(x, 'slab', [(i, i ^ turned) for i in range(slabs)])  12.2 us
    ppermute x3, waiting for transfers between devices, exchange(): return lax.ppermute(x, ('band', 'slab'), pairs)  7.9 us
    ppermute x10, waiting for transfers between devices, exchange(): return lax.ppermute(x, 'slab', [(i, i ^ turned) for i in range(slabs)])  6.85 us
    ppermute x5, starting transfers between devices, exchange(): return lax.ppermute(x, 'band', [(i, i ^ column) for i in range(columns)])  5.57 us
    pallas_call x2, Pallas kernels, place_rows(): pl.pallas_call(functools.partial(place_kernel, chips, wanted), grid=(len(...  4.39 us
    ppermute x3, starting transfers between devices, exchange(): return lax.ppermute(x, ('band', 'slab'), pairs)  4.19 us
    pallas_call x2, Pallas kernels, back_project(): pl.pallas_call(kernel, in_specs=[VMEM_SPEC] * (4 + len(tables) + len(coef...  3.8 us
    pallas_call x2, Pallas kernels, project(): pl.pallas_call(kernel, in_specs=[VMEM_SPEC] * (4 + bands + len(before)),...  3.62 us
  transfers between devices with their start and end apart: 18, of which 11 were waited for; matrix products, arithmetic and copies ran while one was open for 0% of the time, Pallas kernels for 14%

profile of v6, /device:TPU:0, one launch (start us, length us, event | category | flops | bytes accessed | tf_op | source)
XLA Modules:
  0.0 55.8 jit_solution(7236025371604589485)
XLA Ops:
  0.0 0.7 %pad_add_fusion = s32[2,512]{1,0:T(2,128)S(1)} fusion(s32[1,512]{1,0:T(1,128)} %param.8, s32[1,512]{1,0:T(1,128)} %param.9), kind=kLoop, calls=%fused_computation.8 | loop fusion | flops 1024 | bytes 8192 | tf_op jit(solution)/shard_map/concatenate | solution.py:339
  0.7 5.1 %collective-permute-start.2 = (s32[1,8,128]{2,1,0:T(8,128)S(1)}, s32[1,8,128]{2,1,0:T(8,128)S(1)}, u32[]{:S(2)}, u32[]{:S(2)}) collective-permute-start(s32[1,8,128]{2,1,0:T(8,128)S(1)} %reshape.6), channel_id=1, source_target_pairs={{0,6},{1,7},{2,4},{3,5},{4,2},{5,3},{6,0},{7,1},{8,14},{9,15},{10,... | collective-permute-start | bytes 12296 | tf_op jit(solution)/shard_map/ppermute | solution.py:330
  5.8 0.0 collective-permute-start.1
  5.8 0.6 %collective-permute-start = (s32[1,8,128]{2,1,0:T(8,128)S(1)}, s32[1,8,128]{2,1,0:T(8,128)S(1)}, u32[]{:S(2)}, u32[]{:S(2)}) collective-permute-start(s32[1,8,128]{2,1,0:T(8,128)S(1)} %reshape.6), channel_id=1, source_target_pairs={{0,2},{1,3},{2,0},{3,1},{4,6},{5,7},{6,4},{7,5},{8,10},{9,11},{10,... | collective-permute-start | bytes 12296 | tf_op jit(solution)/shard_map/ppermute | solution.py:330
  6.5 2.3 %collective-permute-start.6 = (bf16[128,1152]{1,0:T(8,128)(2,1)}, bf16[128,1152]{1,0:T(8,128)(2,1)S(1)}, u32[]{:S(2)}, u32[]{:S(2)}) collective-permute-start(bf16[128,1152]{1,0:T(8,128)(2,1)} %bitcast.7), channel_id=1, source_target_pairs={{0,4},{1,5},{2,6},{3,7},{4,0},{5,1},{6,2},{7,3},{8,12},{9,13},{10,... | collective-permute-start | bytes 884744 | tf_op jit(solution)/shard_map/ppermute | solution.py:330
  8.8 1.5 %collective-permute-start.4 = (bf16[128,1152]{1,0:T(8,128)(2,1)}, bf16[128,1152]{1,0:T(8,128)(2,1)S(1)}, u32[]{:S(2)}, u32[]{:S(2)}) collective-permute-start(bf16[128,1152]{1,0:T(8,128)(2,1)} %bitcast.8), channel_id=1, source_target_pairs={{0,8},{8,0},{16,24},{24,16},{1,9},{9,1},{17,25},{25,17},{2,10},{10... | collective-permute-start | bytes 884744 | tf_op jit(solution)/shard_map/ppermute | solution.py:332
  10.2 0.0 collective-permute-done
  10.3 0.1 collective-permute-done.1
  10.4 0.0 collective-permute-done.2
  10.4 0.1 collective-permute-start.3
  10.4 0.0 copy-start
  10.4 1.6 %copy-done = bf16[1,524288]{1,0:T(2,128)(2,1)S(1)} copy-done((bf16[1,524288]{1,0:T(2,128)(2,1)S(1)}, bf16[1,524288]{1,0:T(2,128)(2,1)}, u32[]{:S(2)}) %copy-start) | copy-done | bytes 1048600
  12.0 0.6 %shard_map.64.rows_ref = bf16[4096,128]{1,0:T(8,128)(2,1)S(1)} custom-call(bf16[1,524288]{1,0:T(2,128)(2,1)S(1)} %copy-done), custom_call_target="tpu_custom_call" | custom-call | tf_op jit(solution)/shard_map/pallas_call | solution.py:89
  12.7 0.0 collective-permute-done.3.other_ids.refs_1_
  12.7 1.5 %shard_map.65 = (bf16[512,128]{1,0:T(8,128)(2,1)S(1)}, bf16[512,128]{1,0:T(8,128)(2,1)S(1)}, bf16[512,128]{1,0:T(8,128)(2,1)S(1)}, bf16[512,128]{1,0:T(8,128)(2,1)S(1)}) custom-call(s32[4,8,128]{2,1,0:T(8,128)S(1)} %constant_dynamic-update-slice_fusion.own_ids.refs_0_, s32[4,8,128]{2,1,0:T(8,128)S(1)} %collective-permute-done.3.other_ids.refs_1_, ...), custom_call_target="tpu_custom_call" | custom-call | bytes 10000000 | tf_op jit(solution)/shard_map/pallas_call | solution.py:134
  14.2 2.0 %collective-permute-start.7 = (bf16[512,128]{1,0:T(8,128)(2,1)S(1)}, bf16[512,128]{1,0:T(8,128)(2,1)S(1)}, u32[]{:S(2)}, u32[]{:S(2)}) collective-permute-start(bf16[512,128]{1,0:T(8,128)(2,1)S(1)} %get-tuple-element.20), channel_id=1, source_target_pairs={{0,2},{1,3},{2,0},{3,1},{4,6},{5,7},{6,4},{7,5},{8,10},{9,11},{10,... | collective-permute-start | bytes 393224 | tf_op jit(solution)/shard_map/ppermute | solution.py:330
  16.3 1.5 %collective-permute-start.8 = (bf16[512,128]{1,0:T(8,128)(2,1)S(1)}, bf16[512,128]{1,0:T(8,128)(2,1)S(1)}, u32[]{:S(2)}, u32[]{:S(2)}) collective-permute-start(bf16[512,128]{1,0:T(8,128)(2,1)S(1)} %get-tuple-element.21), channel_id=1, source_target_pairs={{0,16},{8,24},{16,0},{24,8},{1,17},{9,25},{17,1},{25,9},{2,18},{10... | collective-permute-start | bytes 393224 | tf_op jit(solution)/shard_map/ppermute | solution.py:332
  17.8 0.0 collective-permute-start.9
  17.8 0.0 collective-permute-done.4
  17.8 4.4 %collective-permute-done.6 = bf16[128,1152]{1,0:T(8,128)(2,1)S(1)} collective-permute-done((bf16[128,1152]{1,0:T(8,128)(2,1)}, bf16[128,1152]{1,0:T(8,128)(2,1)S(1)}, u32[]{:S(2)}, u32[]{:S(2)}) %collective-permute-start.6) | collective-permute-done | bytes 294944 | tf_op jit(solution)/shard_map/ppermute | solution.py:330
  22.2 1.5 %collective-permute-start.10 = (bf16[128,1152]{1,0:T(8,128)(2,1)S(1)}, bf16[128,1152]{1,0:T(8,128)(2,1)S(1)}, u32[]{:S(2)}, u32[]{:S(2)}) collective-permute-start(bf16[128,1152]{1,0:T(8,128)(2,1)S(1)} %collective-permute-done.6), channel_id=1, source_target_pairs={{0,8},{8,0},{16,24},{24,16},{1,9},{9,1},{17,25},{25,17},{2,10},{10... | collective-permute-start | bytes 884744 | tf_op jit(solution)/shard_map/ppermute | solution.py:332
  23.8 1.2 %collective-permute-done.7.rest_1_ = bf16[512,128]{1,0:T(8,128)(2,1)S(1)} collective-permute-done((bf16[512,128]{1,0:T(8,128)(2,1)S(1)}, bf16[512,128]{1,0:T(8,128)(2,1)S(1)}, u32[]{:S(2)}, u32[]{:S(2)}) %collective-permute-start.7) | collective-permute-done | bytes 131104 | tf_op jit(solution)/shard_map/ppermute | solution.py:330
  25.0 3.7 %collective-permute-done.9.rest_3_ = bf16[512,128]{1,0:T(8,128)(2,1)S(1)} collective-permute-done((bf16[512,128]{1,0:T(8,128)(2,1)S(1)}, bf16[512,128]{1,0:T(8,128)(2,1)S(1)}, u32[]{:S(2)}, u32[]{:S(2)}) %collective-permute-start.9) | collective-permute-done | bytes 131104 | tf_op jit(solution)/shard_map/ppermute | solution.py:334
  28.7 0.1 collective-permute-start.5
  28.8 0.0 copy-start.1
  28.8 0.0 copy-start.2
  28.9 1.4 %collective-permute-done.10 = bf16[128,1152]{1,0:T(8,128)(2,1)S(1)} collective-permute-done((bf16[128,1152]{1,0:T(8,128)(2,1)S(1)}, bf16[128,1152]{1,0:T(8,128)(2,1)S(1)}, u32[]{:S(2)}, u32[]{:S(2)}) %collective-permute-start.10) | collective-permute-done | bytes 294944 | tf_op jit(solution)/shard_map/ppermute | solution.py:332
  30.3 0.1 collective-permute-start.11
  30.4 0.3 collective-permute-done.5.other_ref.rest_1_
  30.7 1.8 %shard_map.66.rest_4_ = f32[96,128]{1,0:T(8,128)S(1)} custom-call(s32[4,8,128]{2,1,0:T(8,128)S(1)} %constant_dynamic-update-slice_fusion.own_ids.refs_0_, s32[4,8,128]{2,1,0:T(8,128)S(1)} %collective-permute-done.3.other_ids.refs_1_, bf16[256,1152]{1,0:T(8,128)(2,1)S(1)} %constant_dynamic-update-slice_fusion.4.own_ref.rest_0_, ...), custom_call_target="tpu_custom_call" | custom-call | bytes 30000000 | tf_op jit(solution)/shard_map/pallas_call | solution.py:199
  32.5 0.0 collective-permute-done.11.other_ref.rest_3_
  32.5 1.8 %shard_map.67.rest_4_ = f32[96,128]{1,0:T(8,128)S(1)} custom-call(s32[4,8,128]{2,1,0:T(8,128)S(1)} %constant_dynamic-update-slice_fusion.own_ids.refs_0_, s32[4,8,128]{2,1,0:T(8,128)S(1)} %collective-permute-done.3.other_ids.refs_1_, bf16[256,1152]{1,0:T(8,128)(2,1)S(1)} %constant_dynamic-update-slice_fusion.6.own_ref.rest_2_, ...), custom_call_target="tpu_custom_call" | custom-call | bytes 30000000 | tf_op jit(solution)/shard_map/pallas_call | solution.py:199
  34.4 2.1 %collective-permute-start.14 = (f32[96,128]{1,0:T(8,128)S(1)}, f32[96,128]{1,0:T(8,128)S(1)}, u32[]{:S(2)}, u32[]{:S(2)}) collective-permute-start(f32[96,128]{1,0:T(8,128)S(1)} %shard_map.67.rest_4_), channel_id=1, source_target_pairs={{0,18},{1,19},{2,16},{3,17},{4,22},{5,23},{6,20},{7,21},{8,26},{9,... | collective-permute-start | bytes 147464 | tf_op jit(solution)/shard_map/ppermute | solution.py:334
  36.5 0.5 collective-permute-start.13
  37.0 0.9 %collective-permute-start.12 = (f32[96,128]{1,0:T(8,128)S(1)}, f32[96,128]{1,0:T(8,128)S(1)}, u32[]{:S(2)}, u32[]{:S(2)}) collective-permute-start(f32[96,128]{1,0:T(8,128)S(1)} %shard_map.67.rest_4_), channel_id=1, source_target_pairs={{0,2},{1,3},{2,0},{3,1},{4,6},{5,7},{6,4},{7,5},{8,10},{9,11},{10,... | collective-permute-start | bytes 147464 | tf_op jit(solution)/shard_map/ppermute | solution.py:330
  37.9 1.5 %collective-permute-done.14.rest_7_ = f32[96,128]{1,0:T(8,128)S(1)} collective-permute-done((f32[96,128]{1,0:T(8,128)S(1)}, f32[96,128]{1,0:T(8,128)S(1)}, u32[]{:S(2)}, u32[]{:S(2)}) %collective-permute-start.14) | collective-permute-done | bytes 49184 | tf_op jit(solution)/shard_map/ppermute | solution.py:334
  39.4 1.1 %collective-permute-done.13.rest_6_ = f32[96,128]{1,0:T(8,128)S(1)} collective-permute-done((f32[96,128]{1,0:T(8,128)S(1)}, f32[96,128]{1,0:T(8,128)S(1)}, u32[]{:S(2)}, u32[]{:S(2)}) %collective-permute-start.13) | collective-permute-done | bytes 49184 | tf_op jit(solution)/shard_map/ppermute | solution.py:332
  40.6 0.5 collective-permute-done.12.rest_5_
  41.1 1.9 %shard_map.69 = (bf16[512,128]{1,0:T(8,128)(2,1)S(1)}, bf16[512,128]{1,0:T(8,128)(2,1)S(1)}) custom-call(s32[4,8,128]{2,1,0:T(8,128)S(1)} %constant_dynamic-update-slice_fusion.own_ids.refs_0_, s32[4,8,128]{2,1,0:T(8,128)S(1)} %collective-permute-done.3.other_ids.refs_1_, s32[1,128]{1,0:T(1,128)S(1)} %bitcast.5, f32[18,18,128]{2,1,0:T(8,128)S(1)} %bitcast.3, ...), custom_call_target="tpu_custom_call" | custom-call | tf_op jit(solution)/shard_map/pallas_call | solution.py:258
  43.0 1.0 %collective-permute-start.16 = (bf16[512,128]{1,0:T(8,128)(2,1)S(1)}, bf16[512,128]{1,0:T(8,128)(2,1)S(1)}, u32[]{:S(2)}, u32[]{:S(2)}) collective-permute-start(bf16[512,128]{1,0:T(8,128)(2,1)S(1)} %get-tuple-element.27), channel_id=1, source_target_pairs={{0,2},{1,3},{2,0},{3,1},{4,6},{5,7},{6,4},{7,5},{8,10},{9,11},{10,... | collective-permute-start | bytes 393224 | tf_op jit(solution)/shard_map/ppermute | solution.py:330
  44.0 2.1 %collective-permute-start.17 = (bf16[512,128]{1,0:T(8,128)(2,1)S(1)}, bf16[512,128]{1,0:T(8,128)(2,1)S(1)}, u32[]{:S(2)}, u32[]{:S(2)}) collective-permute-start(bf16[512,128]{1,0:T(8,128)(2,1)S(1)} %get-tuple-element.28), channel_id=1, source_target_pairs={{0,18},{1,19},{2,16},{3,17},{4,22},{5,23},{6,20},{7,21},{8,26},{9,... | collective-permute-start | bytes 393224 | tf_op jit(solution)/shard_map/ppermute | solution.py:334
  46.0 1.9 %shard_map.68 = (bf16[512,128]{1,0:T(8,128)(2,1)S(1)}, bf16[512,128]{1,0:T(8,128)(2,1)S(1)}) custom-call(s32[4,8,128]{2,1,0:T(8,128)S(1)} %constant_dynamic-update-slice_fusion.own_ids.refs_0_, s32[4,8,128]{2,1,0:T(8,128)S(1)} %collective-permute-done.3.other_ids.refs_1_, s32[1,128]{1,0:T(1,128)S(1)} %bitcast.6, f32[18,18,128]{2,1,0:T(8,128)S(1)} %bitcast.4, ...), custom_call_target="tpu_custom_call" | custom-call | tf_op jit(solution)/shard_map/pallas_call | solution.py:258
  47.9 0.6 %collective-permute-start.15 = (bf16[512,128]{1,0:T(8,128)(2,1)S(1)}, bf16[512,128]{1,0:T(8,128)(2,1)S(1)}, u32[]{:S(2)}, u32[]{:S(2)}) collective-permute-start(bf16[512,128]{1,0:T(8,128)(2,1)S(1)} %get-tuple-element.26), channel_id=1, source_target_pairs={{0,16},{8,24},{16,0},{24,8},{1,17},{9,25},{17,1},{25,9},{2,18},{10... | collective-permute-start | bytes 393224 | tf_op jit(solution)/shard_map/ppermute | solution.py:332
  48.5 0.3 collective-permute-done.16.refs_2_
  48.8 2.6 %collective-permute-done.17.refs_3_ = bf16[512,128]{1,0:T(8,128)(2,1)S(1)} collective-permute-done((bf16[512,128]{1,0:T(8,128)(2,1)S(1)}, bf16[512,128]{1,0:T(8,128)(2,1)S(1)}, u32[]{:S(2)}, u32[]{:S(2)}) %collective-permute-start.17) | collective-permute-done | bytes 131104 | tf_op jit(solution)/shard_map/ppermute | solution.py:334
  51.4 2.2 %shard_map.70.refs_4_ = bf16[1,524288]{1,0:T(2,128)(2,1)} custom-call(s32[4,8,128]{2,1,0:T(8,128)S(1)} %constant_dynamic-update-slice_fusion.own_ids.refs_0_, s32[4,8,128]{2,1,0:T(8,128)S(1)} %collective-permute-done.3.other_ids.refs_1_, bf16[512,128]{1,0:T(8,128)(2,1)S(1)} %collective-permute-done.16.refs_2_, ...), custom_call_target="tpu_custom_call" | custom-call | tf_op jit(solution)/shard_map/pallas_call | solution.py:311
  53.6 0.0 collective-permute-done.15.refs_3_
  53.6 2.2 %shard_map.71 = bf16[1,524288]{1,0:T(2,128)(2,1)} custom-call(s32[4,8,128]{2,1,0:T(8,128)S(1)} %constant_dynamic-update-slice_fusion.own_ids.refs_0_, s32[4,8,128]{2,1,0:T(8,128)S(1)} %collective-permute-done.3.other_ids.refs_1_, bf16[512,128]{1,0:T(8,128)(2,1)S(1)} %get-tuple-element.25.refs_2_, ...), custom_call_target="tpu_custom_call", output_to_operand_aliasing={{}: (4, {})} | custom-call | tf_op jit(solution)/shard_map/pallas_call | solution.py:311
  (14 shorter events, 0.1 us)
Async XLA Ops:
  0.7 9.6 %collective-permute-start.2 = (s32[1,8,128]{2,1,0:T(8,128)S(1)}, s32[1,8,128]{2,1,0:T(8,128)S(1)}, u32[]{:S(2)}, u32[]{:S(2)}) collective-permute-start(s32[1,8,128]{2,1,0:T(8,128)S(1)} %reshape.6), channel_id=1, source_target_pairs={{0,6},{1,7},{2,4},{3,5},{4,2},{5,3},{6,0},{7,1},{8,14},{9,15},{10,... | collective-permute-start | bytes 12296 | tf_op jit(solution)/shard_map/ppermute | solution.py:330
  5.8 4.5 %collective-permute-start.1 = (s32[1,8,128]{2,1,0:T(8,128)S(1)}, s32[1,8,128]{2,1,0:T(8,128)S(1)}, u32[]{:S(2)}, u32[]{:S(2)}) collective-permute-start(s32[1,8,128]{2,1,0:T(8,128)S(1)} %reshape.6), channel_id=1, source_target_pairs={{0,4},{1,5},{2,6},{3,7},{4,0},{5,1},{6,2},{7,3},{8,12},{9,13},{10,... | collective-permute-start | bytes 12296 | tf_op jit(solution)/shard_map/ppermute | solution.py:330
  5.8 4.4 %collective-permute-start = (s32[1,8,128]{2,1,0:T(8,128)S(1)}, s32[1,8,128]{2,1,0:T(8,128)S(1)}, u32[]{:S(2)}, u32[]{:S(2)}) collective-permute-start(s32[1,8,128]{2,1,0:T(8,128)S(1)} %reshape.6), channel_id=1, source_target_pairs={{0,2},{1,3},{2,0},{3,1},{4,6},{5,7},{6,4},{7,5},{8,10},{9,11},{10,... | collective-permute-start | bytes 12296 | tf_op jit(solution)/shard_map/ppermute | solution.py:330
  6.5 15.8 %collective-permute-start.6 = (bf16[128,1152]{1,0:T(8,128)(2,1)}, bf16[128,1152]{1,0:T(8,128)(2,1)S(1)}, u32[]{:S(2)}, u32[]{:S(2)}) collective-permute-start(bf16[128,1152]{1,0:T(8,128)(2,1)} %bitcast.7), channel_id=1, source_target_pairs={{0,4},{1,5},{2,6},{3,7},{4,0},{5,1},{6,2},{7,3},{8,12},{9,13},{10,... | collective-permute-start | bytes 884744 | tf_op jit(solution)/shard_map/ppermute | solution.py:330
  8.8 9.1 %collective-permute-start.4 = (bf16[128,1152]{1,0:T(8,128)(2,1)}, bf16[128,1152]{1,0:T(8,128)(2,1)S(1)}, u32[]{:S(2)}, u32[]{:S(2)}) collective-permute-start(bf16[128,1152]{1,0:T(8,128)(2,1)} %bitcast.8), channel_id=1, source_target_pairs={{0,8},{8,0},{16,24},{24,16},{1,9},{9,1},{17,25},{25,17},{2,10},{10... | collective-permute-start | bytes 884744 | tf_op jit(solution)/shard_map/ppermute | solution.py:332
  10.4 2.3 %collective-permute-start.3 = (s32[4,8,128]{2,1,0:T(8,128)S(1)}, s32[4,8,128]{2,1,0:T(8,128)S(1)}, u32[]{:S(2)}, u32[]{:S(2)}) collective-permute-start(s32[4,8,128]{2,1,0:T(8,128)S(1)} %constant_dynamic-update-slice_fusion.own_ids.refs_0_), channel_id=1, source_target_pairs={{0,1},{1,0},{2,3},{3,2},{4,5},{5,4},{6,7},{7,6},{8,9},{9,8},{10,11... | collective-permute-start | bytes 49160 | tf_op jit(solution)/shard_map/ppermute | solution.py:330
  10.4 1.6 %copy-start = (bf16[1,524288]{1,0:T(2,128)(2,1)S(1)}, bf16[1,524288]{1,0:T(2,128)(2,1)}, u32[]{:S(2)}) copy-start(bf16[1,524288]{1,0:T(2,128)(2,1)} %psi_ref.1) | copy-start | bytes 3145732
  12.0 5.8 %copy-start.3 = (bf16[1,128,1152]{2,1,0:T(8,128)(2,1)S(1)}, bf16[1,128,1152]{2,1,0:T(8,128)(2,1)}, u32[]{:S(2)}) copy-start(bf16[1,128,1152]{2,1,0:T(8,128)(2,1)} %param.7) | copy-start | bytes 884740
  14.2 10.7 %collective-permute-start.7 = (bf16[512,128]{1,0:T(8,128)(2,1)S(1)}, bf16[512,128]{1,0:T(8,128)(2,1)S(1)}, u32[]{:S(2)}, u32[]{:S(2)}) collective-permute-start(bf16[512,128]{1,0:T(8,128)(2,1)S(1)} %get-tuple-element.20), channel_id=1, source_target_pairs={{0,2},{1,3},{2,0},{3,1},{4,6},{5,7},{6,4},{7,5},{8,10},{9,11},{10,... | collective-permute-start | bytes 393224 | tf_op jit(solution)/shard_map/ppermute | solution.py:330
  16.3 8.7 %collective-permute-start.8 = (bf16[512,128]{1,0:T(8,128)(2,1)S(1)}, bf16[512,128]{1,0:T(8,128)(2,1)S(1)}, u32[]{:S(2)}, u32[]{:S(2)}) collective-permute-start(bf16[512,128]{1,0:T(8,128)(2,1)S(1)} %get-tuple-element.21), channel_id=1, source_target_pairs={{0,16},{8,24},{16,0},{24,8},{1,17},{9,25},{17,1},{25,9},{2,18},{10... | collective-permute-start | bytes 393224 | tf_op jit(solution)/shard_map/ppermute | solution.py:332
  17.8 10.9 %collective-permute-start.9 = (bf16[512,128]{1,0:T(8,128)(2,1)S(1)}, bf16[512,128]{1,0:T(8,128)(2,1)S(1)}, u32[]{:S(2)}, u32[]{:S(2)}) collective-permute-start(bf16[512,128]{1,0:T(8,128)(2,1)S(1)} %get-tuple-element.22), channel_id=1, source_target_pairs={{0,18},{1,19},{2,16},{3,17},{4,22},{5,23},{6,20},{7,21},{8,26},{9,... | collective-permute-start | bytes 393224 | tf_op jit(solution)/shard_map/ppermute | solution.py:334
  22.2 8.0 %collective-permute-start.10 = (bf16[128,1152]{1,0:T(8,128)(2,1)S(1)}, bf16[128,1152]{1,0:T(8,128)(2,1)S(1)}, u32[]{:S(2)}, u32[]{:S(2)}) collective-permute-start(bf16[128,1152]{1,0:T(8,128)(2,1)S(1)} %collective-permute-done.6), channel_id=1, source_target_pairs={{0,8},{8,0},{16,24},{24,16},{1,9},{9,1},{17,25},{25,17},{2,10},{10... | collective-permute-start | bytes 884744 | tf_op jit(solution)/shard_map/ppermute | solution.py:332
  28.7 2.0 %collective-permute-start.5 = (bf16[256,1152]{1,0:T(8,128)(2,1)S(1)}, bf16[256,1152]{1,0:T(8,128)(2,1)S(1)}, u32[]{:S(2)}, u32[]{:S(2)}) collective-permute-start(bf16[256,1152]{1,0:T(8,128)(2,1)S(1)} %constant_dynamic-update-slice_fusion.4.own_ref.rest_0_), channel_id=1, source_target_pairs={{0,1},{1,0},{2,3},{3,2},{4,5},{5,4},{6,7},{7,6},{8,9},{9,8},{10,11... | collective-permute-start | bytes 1769480 | tf_op jit(solution)/shard_map/ppermute | solution.py:330
  28.8 12.2 %copy-start.1 = (f32[128,18,18]{0,2,1:T(8,128)S(1)}, f32[128,18,18]{0,2,1:T(8,128)}, u32[]{:S(2)}) copy-start(f32[128,18,18]{0,2,1:T(8,128)} %param.11) | copy-start | bytes 497668
  28.8 12.2 %copy-start.2 = (s32[128]{0:T(128)S(1)}, s32[128]{0:T(128)}, u32[]{:S(2)}) copy-start(s32[128]{0:T(128)} %param.10) | copy-start | bytes 1540
  30.3 2.2 %collective-permute-start.11 = (bf16[256,1152]{1,0:T(8,128)(2,1)S(1)}, bf16[256,1152]{1,0:T(8,128)(2,1)S(1)}, u32[]{:S(2)}, u32[]{:S(2)}) collective-permute-start(bf16[256,1152]{1,0:T(8,128)(2,1)S(1)} %constant_dynamic-update-slice_fusion.6.own_ref.rest_2_), channel_id=1, source_target_pairs={{0,1},{1,0},{2,3},{3,2},{4,5},{5,4},{6,7},{7,6},{8,9},{9,8},{10,11... | collective-permute-start | bytes 1769480 | tf_op jit(solution)/shard_map/ppermute | solution.py:330
  34.4 5.1 %collective-permute-start.14 = (f32[96,128]{1,0:T(8,128)S(1)}, f32[96,128]{1,0:T(8,128)S(1)}, u32[]{:S(2)}, u32[]{:S(2)}) collective-permute-start(f32[96,128]{1,0:T(8,128)S(1)} %shard_map.67.rest_4_), channel_id=1, source_target_pairs={{0,18},{1,19},{2,16},{3,17},{4,22},{5,23},{6,20},{7,21},{8,26},{9,... | collective-permute-start | bytes 147464 | tf_op jit(solution)/shard_map/ppermute | solution.py:334
  36.5 4.1 %collective-permute-start.13 = (f32[96,128]{1,0:T(8,128)S(1)}, f32[96,128]{1,0:T(8,128)S(1)}, u32[]{:S(2)}, u32[]{:S(2)}) collective-permute-start(f32[96,128]{1,0:T(8,128)S(1)} %shard_map.67.rest_4_), channel_id=1, source_target_pairs={{0,16},{8,24},{16,0},{24,8},{1,17},{9,25},{17,1},{25,9},{2,18},{10... | collective-permute-start | bytes 147464 | tf_op jit(solution)/shard_map/ppermute | solution.py:332
  37.0 4.1 %collective-permute-start.12 = (f32[96,128]{1,0:T(8,128)S(1)}, f32[96,128]{1,0:T(8,128)S(1)}, u32[]{:S(2)}, u32[]{:S(2)}) collective-permute-start(f32[96,128]{1,0:T(8,128)S(1)} %shard_map.67.rest_4_), channel_id=1, source_target_pairs={{0,2},{1,3},{2,0},{3,1},{4,6},{5,7},{6,4},{7,5},{8,10},{9,11},{10,... | collective-permute-start | bytes 147464 | tf_op jit(solution)/shard_map/ppermute | solution.py:330
  43.0 5.8 %collective-permute-start.16 = (bf16[512,128]{1,0:T(8,128)(2,1)S(1)}, bf16[512,128]{1,0:T(8,128)(2,1)S(1)}, u32[]{:S(2)}, u32[]{:S(2)}) collective-permute-start(bf16[512,128]{1,0:T(8,128)(2,1)S(1)} %get-tuple-element.27), channel_id=1, source_target_pairs={{0,2},{1,3},{2,0},{3,1},{4,6},{5,7},{6,4},{7,5},{8,10},{9,11},{10,... | collective-permute-start | bytes 393224 | tf_op jit(solution)/shard_map/ppermute | solution.py:330
  44.0 7.5 %collective-permute-start.17 = (bf16[512,128]{1,0:T(8,128)(2,1)S(1)}, bf16[512,128]{1,0:T(8,128)(2,1)S(1)}, u32[]{:S(2)}, u32[]{:S(2)}) collective-permute-start(bf16[512,128]{1,0:T(8,128)(2,1)S(1)} %get-tuple-element.28), channel_id=1, source_target_pairs={{0,18},{1,19},{2,16},{3,17},{4,22},{5,23},{6,20},{7,21},{8,26},{9,... | collective-permute-start | bytes 393224 | tf_op jit(solution)/shard_map/ppermute | solution.py:334
  47.9 5.7 %collective-permute-start.15 = (bf16[512,128]{1,0:T(8,128)(2,1)S(1)}, bf16[512,128]{1,0:T(8,128)(2,1)S(1)}, u32[]{:S(2)}, u32[]{:S(2)}) collective-permute-start(bf16[512,128]{1,0:T(8,128)(2,1)S(1)} %get-tuple-element.26), channel_id=1, source_target_pairs={{0,16},{8,24},{16,0},{24,8},{1,17},{9,25},{17,1},{25,9},{2,18},{10... | collective-permute-start | bytes 393224 | tf_op jit(solution)/shard_map/ppermute | solution.py:332

commit v7 on v6

--- a/solution.py
+++ b/solution.py
@@ -355,11 +355,13 @@
     coefs = partners([coef] * PARTNERS)
     count, strength = proj_count.reshape(1, atom_total), strength.transpose(1, 2, 0)
     given = (ids, first + second, count, strength, coefs, *shape)
-    outer = back_project((3, 1), *given)
-    inner = back_project((2, 0), *given)
-    results = partners([inner[1], outer[1], inner[0], outer[0]])
-    applied = place_rows((1, 3), ids, {1: results[1], 3: results[3]}, psi.shape[1], ())
-    return place_rows((0, 2), ids, {0: results[0], 2: results[2]}, psi.shape[1], (applied,))
+    results = [None] * PARTNERS
+    for wanted in ((2, 3), (1,), (0,)):
+        for partner, result in zip(wanted, back_project(wanted, *given)):
+            results[partner] = result
+    results = partners(results)
+    applied = place_rows((0, 2), ids, {0: results[0], 2: results[2]}, psi.shape[1], ())
+    return place_rows((1, 3), ids, {1: results[1], 3: results[3]}, psi.shape[1], (applied,))
 
 
 def plain_project(grid_blocks, tables, atom_ids, block_ids, atom_total):

time: 56 us -> 54.6 us (0.975)
  waiting for transfers between devices: 17.3 us -> 15.3 us
    ppermute x3, waiting for transfers between devices: 7.9 us -> 5.27 us  [exchange(): return lax.ppermute(x, ('band', 'slab'), pairs)]
    ppermute x3, starting transfers between devices: 4.19 us -> 3.01 us  [exchange(): return lax.ppermute(x, ('band', 'slab'), pairs)]
    ppermute x5, starting transfers between devices: 5.57 us -> 6.59 us  [exchange(): return lax.ppermute(x, 'band', [(i, i ^ column) for i in range(columns)])]
    ppermute x5, waiting for transfers between devices: 2.54 us -> 3.37 us  [exchange(): return lax.ppermute(x, 'band', [(i, i ^ column) for i in range(columns)])]
    pallas_call x2 -> x3, Pallas kernels: 3.8 us -> 4.32 us  [back_project(): pl.pallas_call(kernel, in_specs=[VMEM_SPEC] * (4 + len(tables) + len(coef...]
  transfers between devices with their start and end apart: 18 -> 18, of which waited for: 11 -> 11; matrix products, arithmetic and copies ran while one was open for 0% -> 0% of each run, Pallas kernels for 14% -> 16%
where the time goes in v7:
time: 54.6 us; the launch traced here: 54.4 us
  starting transfers between devices  22 us (40%)
  waiting for transfers between devices  15.3 us (28%)
  Pallas kernels  14.5 us (27%)
  local copies, waits for them, and re-layouts  1.73 us (3%)
  other arithmetic  0.71 us (1%)
    ppermute x10, starting transfers between devices, exchange(): return lax.ppermute(x, 'slab', [(i, i ^ turned) for i in range(slabs)])  12.4 us
    ppermute x10, waiting for transfers between devices, exchange(): return lax.ppermute(x, 'slab', [(i, i ^ turned) for i in range(slabs)])  6.68 us
    ppermute x5, starting transfers between devices, exchange(): return lax.ppermute(x, 'band', [(i, i ^ column) for i in range(columns)])  6.59 us
    ppermute x3, waiting for transfers between devices, exchange(): return lax.ppermute(x, ('band', 'slab'), pairs)  5.27 us
    pallas_call x2, Pallas kernels, place_rows(): pl.pallas_call(functools.partial(place_kernel, chips, wanted), grid=(len(...  4.39 us
    pallas_call x3, Pallas kernels, back_project(): pl.pallas_call(kernel, in_specs=[VMEM_SPEC] * (4 + len(tables) + len(coef...  4.32 us
    pallas_call x2, Pallas kernels, project(): pl.pallas_call(kernel, in_specs=[VMEM_SPEC] * (4 + bands + len(before)),...  3.62 us
    ppermute x5, waiting for transfers between devices, exchange(): return lax.ppermute(x, 'band', [(i, i ^ column) for i in range(columns)])  3.37 us
  transfers between devices with their start and end apart: 18, of which 11 were waited for; matrix products, arithmetic and copies ran while one was open for 0% of the time, Pallas kernels for 16%

profile of v7, /device:TPU:0, one launch (start us, length us, event | category | flops | bytes accessed | tf_op | source)
XLA Modules:
  0.0 54.4 jit_solution(11109771398018515)
XLA Ops:
  0.0 0.7 %pad_add_fusion = s32[2,512]{1,0:T(2,128)S(1)} fusion(s32[1,512]{1,0:T(1,128)} %param.8, s32[1,512]{1,0:T(1,128)} %param.9), kind=kLoop, calls=%fused_computation.8 | loop fusion | flops 1024 | bytes 8192 | tf_op jit(solution)/shard_map/concatenate | solution.py:339
  0.7 5.1 %collective-permute-start.2 = (s32[1,8,128]{2,1,0:T(8,128)S(1)}, s32[1,8,128]{2,1,0:T(8,128)S(1)}, u32[]{:S(2)}, u32[]{:S(2)}) collective-permute-start(s32[1,8,128]{2,1,0:T(8,128)S(1)} %reshape.6), channel_id=1, source_target_pairs={{0,6},{1,7},{2,4},{3,5},{4,2},{5,3},{6,0},{7,1},{8,14},{9,15},{10,... | collective-permute-start | bytes 12296 | tf_op jit(solution)/shard_map/ppermute | solution.py:330
  5.8 0.0 collective-permute-start.1
  5.8 0.6 %collective-permute-start = (s32[1,8,128]{2,1,0:T(8,128)S(1)}, s32[1,8,128]{2,1,0:T(8,128)S(1)}, u32[]{:S(2)}, u32[]{:S(2)}) collective-permute-start(s32[1,8,128]{2,1,0:T(8,128)S(1)} %reshape.6), channel_id=1, source_target_pairs={{0,2},{1,3},{2,0},{3,1},{4,6},{5,7},{6,4},{7,5},{8,10},{9,11},{10,... | collective-permute-start | bytes 12296 | tf_op jit(solution)/shard_map/ppermute | solution.py:330
  6.5 2.3 %collective-permute-start.6 = (bf16[128,1152]{1,0:T(8,128)(2,1)}, bf16[128,1152]{1,0:T(8,128)(2,1)S(1)}, u32[]{:S(2)}, u32[]{:S(2)}) collective-permute-start(bf16[128,1152]{1,0:T(8,128)(2,1)} %bitcast.9), channel_id=1, source_target_pairs={{0,4},{1,5},{2,6},{3,7},{4,0},{5,1},{6,2},{7,3},{8,12},{9,13},{10,... | collective-permute-start | bytes 884744 | tf_op jit(solution)/shard_map/ppermute | solution.py:330
  8.8 1.5 %collective-permute-start.4 = (bf16[128,1152]{1,0:T(8,128)(2,1)}, bf16[128,1152]{1,0:T(8,128)(2,1)S(1)}, u32[]{:S(2)}, u32[]{:S(2)}) collective-permute-start(bf16[128,1152]{1,0:T(8,128)(2,1)} %bitcast.10), channel_id=1, source_target_pairs={{0,8},{8,0},{16,24},{24,16},{1,9},{9,1},{17,25},{25,17},{2,10},{10... | collective-permute-start | bytes 884744 | tf_op jit(solution)/shard_map/ppermute | solution.py:332
  10.2 0.0 collective-permute-done
  10.3 0.1 collective-permute-done.1
  10.4 0.0 collective-permute-done.2
  10.4 0.1 collective-permute-start.3
  10.4 0.0 copy-start
  10.4 1.6 %copy-done = bf16[1,524288]{1,0:T(2,128)(2,1)S(1)} copy-done((bf16[1,524288]{1,0:T(2,128)(2,1)S(1)}, bf16[1,524288]{1,0:T(2,128)(2,1)}, u32[]{:S(2)}) %copy-start) | copy-done | bytes 1048600
  12.0 0.6 %shard_map.64.rows_ref = bf16[4096,128]{1,0:T(8,128)(2,1)S(1)} custom-call(bf16[1,524288]{1,0:T(2,128)(2,1)S(1)} %copy-done), custom_call_target="tpu_custom_call" | custom-call | tf_op jit(solution)/shard_map/pallas_call | solution.py:89
  12.7 1.5 %shard_map.65 = (bf16[512,128]{1,0:T(8,128)(2,1)S(1)}, bf16[512,128]{1,0:T(8,128)(2,1)S(1)}, bf16[512,128]{1,0:T(8,128)(2,1)S(1)}, bf16[512,128]{1,0:T(8,128)(2,1)S(1)}) custom-call(s32[4,8,128]{2,1,0:T(8,128)S(1)} %constant_dynamic-update-slice_fusion.own_ids.refs_0_, s32[4,8,128]{2,1,0:T(8,128)S(1)} %collective-permute-done.3.other_ids.refs_1_, ...), custom_call_target="tpu_custom_call" | custom-call | bytes 10000000 | tf_op jit(solution)/shard_map/pallas_call | solution.py:134
  14.2 2.0 %collective-permute-start.7 = (bf16[512,128]{1,0:T(8,128)(2,1)S(1)}, bf16[512,128]{1,0:T(8,128)(2,1)S(1)}, u32[]{:S(2)}, u32[]{:S(2)}) collective-permute-start(bf16[512,128]{1,0:T(8,128)(2,1)S(1)} %get-tuple-element.18), channel_id=1, source_target_pairs={{0,2},{1,3},{2,0},{3,1},{4,6},{5,7},{6,4},{7,5},{8,10},{9,11},{10,... | collective-permute-start | bytes 393224 | tf_op jit(solution)/shard_map/ppermute | solution.py:330
  16.3 1.5 %collective-permute-start.8 = (bf16[512,128]{1,0:T(8,128)(2,1)S(1)}, bf16[512,128]{1,0:T(8,128)(2,1)S(1)}, u32[]{:S(2)}, u32[]{:S(2)}) collective-permute-start(bf16[512,128]{1,0:T(8,128)(2,1)S(1)} %get-tuple-element.19), channel_id=1, source_target_pairs={{0,16},{8,24},{16,0},{24,8},{1,17},{9,25},{17,1},{25,9},{2,18},{10... | collective-permute-start | bytes 393224 | tf_op jit(solution)/shard_map/ppermute | solution.py:332
  17.8 0.0 collective-permute-start.9
  17.8 0.0 collective-permute-done.4
  17.8 4.4 %collective-permute-done.6 = bf16[128,1152]{1,0:T(8,128)(2,1)S(1)} collective-permute-done((bf16[128,1152]{1,0:T(8,128)(2,1)}, bf16[128,1152]{1,0:T(8,128)(2,1)S(1)}, u32[]{:S(2)}, u32[]{:S(2)}) %collective-permute-start.6) | collective-permute-done | bytes 294944 | tf_op jit(solution)/shard_map/ppermute | solution.py:330
  22.2 1.5 %collective-permute-start.10 = (bf16[128,1152]{1,0:T(8,128)(2,1)S(1)}, bf16[128,1152]{1,0:T(8,128)(2,1)S(1)}, u32[]{:S(2)}, u32[]{:S(2)}) collective-permute-start(bf16[128,1152]{1,0:T(8,128)(2,1)S(1)} %collective-permute-done.6), channel_id=1, source_target_pairs={{0,8},{8,0},{16,24},{24,16},{1,9},{9,1},{17,25},{25,17},{2,10},{10... | collective-permute-start | bytes 884744 | tf_op jit(solution)/shard_map/ppermute | solution.py:332
  23.8 1.2 %collective-permute-done.7.rest_1_ = bf16[512,128]{1,0:T(8,128)(2,1)S(1)} collective-permute-done((bf16[512,128]{1,0:T(8,128)(2,1)S(1)}, bf16[512,128]{1,0:T(8,128)(2,1)S(1)}, u32[]{:S(2)}, u32[]{:S(2)}) %collective-permute-start.7) | collective-permute-done | bytes 131104 | tf_op jit(solution)/shard_map/ppermute | solution.py:330
  25.0 0.0 collective-permute-done.8.rest_2_
  25.0 3.7 %collective-permute-done.9.rest_3_ = bf16[512,128]{1,0:T(8,128)(2,1)S(1)} collective-permute-done((bf16[512,128]{1,0:T(8,128)(2,1)S(1)}, bf16[512,128]{1,0:T(8,128)(2,1)S(1)}, u32[]{:S(2)}, u32[]{:S(2)}) %collective-permute-start.9) | collective-permute-done | bytes 131104 | tf_op jit(solution)/shard_map/ppermute | solution.py:334
  28.7 0.1 collective-permute-start.5
  28.8 0.0 copy-start.1
  28.8 0.0 copy-start.2
  28.9 1.4 %collective-permute-done.10 = bf16[128,1152]{1,0:T(8,128)(2,1)S(1)} collective-permute-done((bf16[128,1152]{1,0:T(8,128)(2,1)S(1)}, bf16[128,1152]{1,0:T(8,128)(2,1)S(1)}, u32[]{:S(2)}, u32[]{:S(2)}) %collective-permute-start.10) | collective-permute-done | bytes 294944 | tf_op jit(solution)/shard_map/ppermute | solution.py:332
  30.3 0.1 collective-permute-start.11
  30.4 0.3 collective-permute-done.5.other_ref.rest_1_
  30.7 1.8 %shard_map.66.rest_4_ = f32[96,128]{1,0:T(8,128)S(1)} custom-call(s32[4,8,128]{2,1,0:T(8,128)S(1)} %constant_dynamic-update-slice_fusion.own_ids.refs_0_, s32[4,8,128]{2,1,0:T(8,128)S(1)} %collective-permute-done.3.other_ids.refs_1_, bf16[256,1152]{1,0:T(8,128)(2,1)S(1)} %constant_dynamic-update-slice_fusion.4.own_ref.rest_0_, ...), custom_call_target="tpu_custom_call" | custom-call | bytes 30000000 | tf_op jit(solution)/shard_map/pallas_call | solution.py:199
  32.5 1.8 %shard_map.67.rest_4_ = f32[96,128]{1,0:T(8,128)S(1)} custom-call(s32[4,8,128]{2,1,0:T(8,128)S(1)} %constant_dynamic-update-slice_fusion.own_ids.refs_0_, s32[4,8,128]{2,1,0:T(8,128)S(1)} %collective-permute-done.3.other_ids.refs_1_, bf16[256,1152]{1,0:T(8,128)(2,1)S(1)} %constant_dynamic-update-slice_fusion.6.own_ref.rest_2_, ...), custom_call_target="tpu_custom_call" | custom-call | bytes 30000000 | tf_op jit(solution)/shard_map/pallas_call | solution.py:199
  34.4 2.1 %collective-permute-start.14 = (f32[96,128]{1,0:T(8,128)S(1)}, f32[96,128]{1,0:T(8,128)S(1)}, u32[]{:S(2)}, u32[]{:S(2)}) collective-permute-start(f32[96,128]{1,0:T(8,128)S(1)} %shard_map.67.rest_4_), channel_id=1, source_target_pairs={{0,18},{1,19},{2,16},{3,17},{4,22},{5,23},{6,20},{7,21},{8,26},{9,... | collective-permute-start | bytes 147464 | tf_op jit(solution)/shard_map/ppermute | solution.py:334
  36.5 0.5 collective-permute-start.13
  37.0 0.9 %collective-permute-start.12 = (f32[96,128]{1,0:T(8,128)S(1)}, f32[96,128]{1,0:T(8,128)S(1)}, u32[]{:S(2)}, u32[]{:S(2)}) collective-permute-start(f32[96,128]{1,0:T(8,128)S(1)} %shard_map.67.rest_4_), channel_id=1, source_target_pairs={{0,2},{1,3},{2,0},{3,1},{4,6},{5,7},{6,4},{7,5},{8,10},{9,11},{10,... | collective-permute-start | bytes 147464 | tf_op jit(solution)/shard_map/ppermute | solution.py:330
  37.9 1.5 %collective-permute-done.14.rest_7_ = f32[96,128]{1,0:T(8,128)S(1)} collective-permute-done((f32[96,128]{1,0:T(8,128)S(1)}, f32[96,128]{1,0:T(8,128)S(1)}, u32[]{:S(2)}, u32[]{:S(2)}) %collective-permute-start.14) | collective-permute-done | bytes 49184 | tf_op jit(solution)/shard_map/ppermute | solution.py:334
  39.4 1.1 %collective-permute-done.13.rest_6_ = f32[96,128]{1,0:T(8,128)S(1)} collective-permute-done((f32[96,128]{1,0:T(8,128)S(1)}, f32[96,128]{1,0:T(8,128)S(1)}, u32[]{:S(2)}, u32[]{:S(2)}) %collective-permute-start.13) | collective-permute-done | bytes 49184 | tf_op jit(solution)/shard_map/ppermute | solution.py:332
  40.6 0.5 collective-permute-done.12.rest_5_
  41.1 1.9 %shard_map.69 = (bf16[512,128]{1,0:T(8,128)(2,1)S(1)}, bf16[512,128]{1,0:T(8,128)(2,1)S(1)}) custom-call(s32[4,8,128]{2,1,0:T(8,128)S(1)} %constant_dynamic-update-slice_fusion.own_ids.refs_0_, s32[4,8,128]{2,1,0:T(8,128)S(1)} %collective-permute-done.3.other_ids.refs_1_, s32[1,128]{1,0:T(1,128)S(1)} %bitcast.6, f32[18,18,128]{2,1,0:T(8,128)S(1)} %bitcast.3, ...), custom_call_target="tpu_custom_call" | custom-call | tf_op jit(solution)/shard_map/pallas_call | solution.py:258
  43.0 1.6 %collective-permute-start.17 = (bf16[512,128]{1,0:T(8,128)(2,1)S(1)}, bf16[512,128]{1,0:T(8,128)(2,1)S(1)}, u32[]{:S(2)}, u32[]{:S(2)}) collective-permute-start(bf16[512,128]{1,0:T(8,128)(2,1)S(1)} %get-tuple-element.24), channel_id=1, source_target_pairs={{0,16},{8,24},{16,0},{24,8},{1,17},{9,25},{17,1},{25,9},{2,18},{10... | collective-permute-start | bytes 393224 | tf_op jit(solution)/shard_map/ppermute | solution.py:332
  44.6 0.9 %collective-permute-start.16 = (bf16[512,128]{1,0:T(8,128)(2,1)S(1)}, bf16[512,128]{1,0:T(8,128)(2,1)S(1)}, u32[]{:S(2)}, u32[]{:S(2)}) collective-permute-start(bf16[512,128]{1,0:T(8,128)(2,1)S(1)} %get-tuple-element.23), channel_id=1, source_target_pairs={{0,18},{1,19},{2,16},{3,17},{4,22},{5,23},{6,20},{7,21},{8,26},{9,... | collective-permute-start | bytes 393224 | tf_op jit(solution)/shard_map/ppermute | solution.py:334
  45.4 1.2 %shard_map.68 = bf16[512,128]{1,0:T(8,128)(2,1)S(1)} custom-call(s32[4,8,128]{2,1,0:T(8,128)S(1)} %constant_dynamic-update-slice_fusion.own_ids.refs_0_, s32[4,8,128]{2,1,0:T(8,128)S(1)} %collective-permute-done.3.other_ids.refs_1_, s32[1,128]{1,0:T(1,128)S(1)} %bitcast.7, f32[18,18,128]{2,1,0:T(8,128)S(1)} %bitcast.4, ...), custom_call_target="tpu_custom_call" | custom-call | tf_op jit(solution)/shard_map/pallas_call | solution.py:258
  46.7 1.2 %collective-permute-start.15 = (bf16[512,128]{1,0:T(8,128)(2,1)S(1)}, bf16[512,128]{1,0:T(8,128)(2,1)S(1)}, u32[]{:S(2)}, u32[]{:S(2)}) collective-permute-start(bf16[512,128]{1,0:T(8,128)(2,1)S(1)} %shard_map.68), channel_id=1, source_target_pairs={{0,2},{1,3},{2,0},{3,1},{4,6},{5,7},{6,4},{7,5},{8,10},{9,11},{10,... | collective-permute-start | bytes 393224 | tf_op jit(solution)/shard_map/ppermute | solution.py:330
  47.8 1.2 %shard_map.70.refs_2_ = bf16[512,128]{1,0:T(8,128)(2,1)S(1)} custom-call(s32[4,8,128]{2,1,0:T(8,128)S(1)} %constant_dynamic-update-slice_fusion.own_ids.refs_0_, s32[4,8,128]{2,1,0:T(8,128)S(1)} %collective-permute-done.3.other_ids.refs_1_, s32[1,128]{1,0:T(1,128)S(1)} %bitcast.8, f32[18,18,128]{2,1,0:T(8,128)S(1)} %bitcast.5, ...), custom_call_target="tpu_custom_call" | custom-call | tf_op jit(solution)/shard_map/pallas_call | solution.py:258
  49.0 0.8 %collective-permute-done.17.refs_3_ = bf16[512,128]{1,0:T(8,128)(2,1)S(1)} collective-permute-done((bf16[512,128]{1,0:T(8,128)(2,1)S(1)}, bf16[512,128]{1,0:T(8,128)(2,1)S(1)}, u32[]{:S(2)}, u32[]{:S(2)}) %collective-permute-start.17) | collective-permute-done | bytes 131104 | tf_op jit(solution)/shard_map/ppermute | solution.py:332
  49.9 2.2 %shard_map.71.refs_4_ = bf16[1,524288]{1,0:T(2,128)(2,1)} custom-call(s32[4,8,128]{2,1,0:T(8,128)S(1)} %constant_dynamic-update-slice_fusion.own_ids.refs_0_, s32[4,8,128]{2,1,0:T(8,128)S(1)} %collective-permute-done.3.other_ids.refs_1_, bf16[512,128]{1,0:T(8,128)(2,1)S(1)} %shard_map.70.refs_2_, bf16[512,128]{1,0:T(8,128)(2,1)S(1)} %collective-permute-done.17.refs_3_), custom_call_target="tpu_custom_call" | custom-call | tf_op jit(solution)/shard_map/pallas_call | solution.py:311
  52.1 0.0 collective-permute-done.16.refs_3_
  52.1 0.1 collective-permute-done.15.refs_2_
  52.2 2.2 %shard_map.72 = bf16[1,524288]{1,0:T(2,128)(2,1)} custom-call(s32[4,8,128]{2,1,0:T(8,128)S(1)} %constant_dynamic-update-slice_fusion.own_ids.refs_0_, s32[4,8,128]{2,1,0:T(8,128)S(1)} %collective-permute-done.3.other_ids.refs_1_, bf16[512,128]{1,0:T(8,128)(2,1)S(1)} %collective-permute-done.15.refs_2_, ...), custom_call_target="tpu_custom_call", output_to_operand_aliasing={{}: (4, {})} | custom-call | tf_op jit(solution)/shard_map/pallas_call | solution.py:311
  (15 shorter events, 0.1 us)
Async XLA Ops:
  0.7 9.6 %collective-permute-start.2 = (s32[1,8,128]{2,1,0:T(8,128)S(1)}, s32[1,8,128]{2,1,0:T(8,128)S(1)}, u32[]{:S(2)}, u32[]{:S(2)}) collective-permute-start(s32[1,8,128]{2,1,0:T(8,128)S(1)} %reshape.6), channel_id=1, source_target_pairs={{0,6},{1,7},{2,4},{3,5},{4,2},{5,3},{6,0},{7,1},{8,14},{9,15},{10,... | collective-permute-start | bytes 12296 | tf_op jit(solution)/shard_map/ppermute | solution.py:330
  5.8 4.5 %collective-permute-start.1 = (s32[1,8,128]{2,1,0:T(8,128)S(1)}, s32[1,8,128]{2,1,0:T(8,128)S(1)}, u32[]{:S(2)}, u32[]{:S(2)}) collective-permute-start(s32[1,8,128]{2,1,0:T(8,128)S(1)} %reshape.6), channel_id=1, source_target_pairs={{0,4},{1,5},{2,6},{3,7},{4,0},{5,1},{6,2},{7,3},{8,12},{9,13},{10,... | collective-permute-start | bytes 12296 | tf_op jit(solution)/shard_map/ppermute | solution.py:330
  5.8 4.4 %collective-permute-start = (s32[1,8,128]{2,1,0:T(8,128)S(1)}, s32[1,8,128]{2,1,0:T(8,128)S(1)}, u32[]{:S(2)}, u32[]{:S(2)}) collective-permute-start(s32[1,8,128]{2,1,0:T(8,128)S(1)} %reshape.6), channel_id=1, source_target_pairs={{0,2},{1,3},{2,0},{3,1},{4,6},{5,7},{6,4},{7,5},{8,10},{9,11},{10,... | collective-permute-start | bytes 12296 | tf_op jit(solution)/shard_map/ppermute | solution.py:330
  6.5 15.8 %collective-permute-start.6 = (bf16[128,1152]{1,0:T(8,128)(2,1)}, bf16[128,1152]{1,0:T(8,128)(2,1)S(1)}, u32[]{:S(2)}, u32[]{:S(2)}) collective-permute-start(bf16[128,1152]{1,0:T(8,128)(2,1)} %bitcast.9), channel_id=1, source_target_pairs={{0,4},{1,5},{2,6},{3,7},{4,0},{5,1},{6,2},{7,3},{8,12},{9,13},{10,... | collective-permute-start | bytes 884744 | tf_op jit(solution)/shard_map/ppermute | solution.py:330
  8.8 9.1 %collective-permute-start.4 = (bf16[128,1152]{1,0:T(8,128)(2,1)}, bf16[128,1152]{1,0:T(8,128)(2,1)S(1)}, u32[]{:S(2)}, u32[]{:S(2)}) collective-permute-start(bf16[128,1152]{1,0:T(8,128)(2,1)} %bitcast.10), channel_id=1, source_target_pairs={{0,8},{8,0},{16,24},{24,16},{1,9},{9,1},{17,25},{25,17},{2,10},{10... | collective-permute-start | bytes 884744 | tf_op jit(solution)/shard_map/ppermute | solution.py:332
  10.4 2.3 %collective-permute-start.3 = (s32[4,8,128]{2,1,0:T(8,128)S(1)}, s32[4,8,128]{2,1,0:T(8,128)S(1)}, u32[]{:S(2)}, u32[]{:S(2)}) collective-permute-start(s32[4,8,128]{2,1,0:T(8,128)S(1)} %constant_dynamic-update-slice_fusion.own_ids.refs_0_), channel_id=1, source_target_pairs={{0,1},{1,0},{2,3},{3,2},{4,5},{5,4},{6,7},{7,6},{8,9},{9,8},{10,11... | collective-permute-start | bytes 49160 | tf_op jit(solution)/shard_map/ppermute | solution.py:330
  10.4 1.6 %copy-start = (bf16[1,524288]{1,0:T(2,128)(2,1)S(1)}, bf16[1,524288]{1,0:T(2,128)(2,1)}, u32[]{:S(2)}) copy-start(bf16[1,524288]{1,0:T(2,128)(2,1)} %psi_ref.1) | copy-start | bytes 3145732
  12.0 5.8 %copy-start.3 = (bf16[1,128,1152]{2,1,0:T(8,128)(2,1)S(1)}, bf16[1,128,1152]{2,1,0:T(8,128)(2,1)}, u32[]{:S(2)}) copy-start(bf16[1,128,1152]{2,1,0:T(8,128)(2,1)} %param.7) | copy-start | bytes 884740
  14.2 10.7 %collective-permute-start.7 = (bf16[512,128]{1,0:T(8,128)(2,1)S(1)}, bf16[512,128]{1,0:T(8,128)(2,1)S(1)}, u32[]{:S(2)}, u32[]{:S(2)}) collective-permute-start(bf16[512,128]{1,0:T(8,128)(2,1)S(1)} %get-tuple-element.18), channel_id=1, source_target_pairs={{0,2},{1,3},{2,0},{3,1},{4,6},{5,7},{6,4},{7,5},{8,10},{9,11},{10,... | collective-permute-start | bytes 393224 | tf_op jit(solution)/shard_map/ppermute | solution.py:330
  16.3 8.7 %collective-permute-start.8 = (bf16[512,128]{1,0:T(8,128)(2,1)S(1)}, bf16[512,128]{1,0:T(8,128)(2,1)S(1)}, u32[]{:S(2)}, u32[]{:S(2)}) collective-permute-start(bf16[512,128]{1,0:T(8,128)(2,1)S(1)} %get-tuple-element.19), channel_id=1, source_target_pairs={{0,16},{8,24},{16,0},{24,8},{1,17},{9,25},{17,1},{25,9},{2,18},{10... | collective-permute-start | bytes 393224 | tf_op jit(solution)/shard_map/ppermute | solution.py:332
  17.8 10.9 %collective-permute-start.9 = (bf16[512,128]{1,0:T(8,128)(2,1)S(1)}, bf16[512,128]{1,0:T(8,128)(2,1)S(1)}, u32[]{:S(2)}, u32[]{:S(2)}) collective-permute-start(bf16[512,128]{1,0:T(8,128)(2,1)S(1)} %get-tuple-element.20), channel_id=1, source_target_pairs={{0,18},{1,19},{2,16},{3,17},{4,22},{5,23},{6,20},{7,21},{8,26},{9,... | collective-permute-start | bytes 393224 | tf_op jit(solution)/shard_map/ppermute | solution.py:334
  22.2 8.0 %collective-permute-start.10 = (bf16[128,1152]{1,0:T(8,128)(2,1)S(1)}, bf16[128,1152]{1,0:T(8,128)(2,1)S(1)}, u32[]{:S(2)}, u32[]{:S(2)}) collective-permute-start(bf16[128,1152]{1,0:T(8,128)(2,1)S(1)} %collective-permute-done.6), channel_id=1, source_target_pairs={{0,8},{8,0},{16,24},{24,16},{1,9},{9,1},{17,25},{25,17},{2,10},{10... | collective-permute-start | bytes 884744 | tf_op jit(solution)/shard_map/ppermute | solution.py:332
  28.7 2.0 %collective-permute-start.5 = (bf16[256,1152]{1,0:T(8,128)(2,1)S(1)}, bf16[256,1152]{1,0:T(8,128)(2,1)S(1)}, u32[]{:S(2)}, u32[]{:S(2)}) collective-permute-start(bf16[256,1152]{1,0:T(8,128)(2,1)S(1)} %constant_dynamic-update-slice_fusion.4.own_ref.rest_0_), channel_id=1, source_target_pairs={{0,1},{1,0},{2,3},{3,2},{4,5},{5,4},{6,7},{7,6},{8,9},{9,8},{10,11... | collective-permute-start | bytes 1769480 | tf_op jit(solution)/shard_map/ppermute | solution.py:330
  28.8 12.2 %copy-start.1 = (f32[128,18,18]{0,2,1:T(8,128)S(1)}, f32[128,18,18]{0,2,1:T(8,128)}, u32[]{:S(2)}) copy-start(f32[128,18,18]{0,2,1:T(8,128)} %param.11) | copy-start | bytes 497668
  28.8 12.2 %copy-start.2 = (s32[128]{0:T(128)S(1)}, s32[128]{0:T(128)}, u32[]{:S(2)}) copy-start(s32[128]{0:T(128)} %param.10) | copy-start | bytes 1540
  30.3 2.2 %collective-permute-start.11 = (bf16[256,1152]{1,0:T(8,128)(2,1)S(1)}, bf16[256,1152]{1,0:T(8,128)(2,1)S(1)}, u32[]{:S(2)}, u32[]{:S(2)}) collective-permute-start(bf16[256,1152]{1,0:T(8,128)(2,1)S(1)} %constant_dynamic-update-slice_fusion.6.own_ref.rest_2_), channel_id=1, source_target_pairs={{0,1},{1,0},{2,3},{3,2},{4,5},{5,4},{6,7},{7,6},{8,9},{9,8},{10,11... | collective-permute-start | bytes 1769480 | tf_op jit(solution)/shard_map/ppermute | solution.py:330
  34.4 5.1 %collective-permute-start.14 = (f32[96,128]{1,0:T(8,128)S(1)}, f32[96,128]{1,0:T(8,128)S(1)}, u32[]{:S(2)}, u32[]{:S(2)}) collective-permute-start(f32[96,128]{1,0:T(8,128)S(1)} %shard_map.67.rest_4_), channel_id=1, source_target_pairs={{0,18},{1,19},{2,16},{3,17},{4,22},{5,23},{6,20},{7,21},{8,26},{9,... | collective-permute-start | bytes 147464 | tf_op jit(solution)/shard_map/ppermute | solution.py:334
  36.5 4.1 %collective-permute-start.13 = (f32[96,128]{1,0:T(8,128)S(1)}, f32[96,128]{1,0:T(8,128)S(1)}, u32[]{:S(2)}, u32[]{:S(2)}) collective-permute-start(f32[96,128]{1,0:T(8,128)S(1)} %shard_map.67.rest_4_), channel_id=1, source_target_pairs={{0,16},{8,24},{16,0},{24,8},{1,17},{9,25},{17,1},{25,9},{2,18},{10... | collective-permute-start | bytes 147464 | tf_op jit(solution)/shard_map/ppermute | solution.py:332
  37.0 4.1 %collective-permute-start.12 = (f32[96,128]{1,0:T(8,128)S(1)}, f32[96,128]{1,0:T(8,128)S(1)}, u32[]{:S(2)}, u32[]{:S(2)}) collective-permute-start(f32[96,128]{1,0:T(8,128)S(1)} %shard_map.67.rest_4_), channel_id=1, source_target_pairs={{0,2},{1,3},{2,0},{3,1},{4,6},{5,7},{6,4},{7,5},{8,10},{9,11},{10,... | collective-permute-start | bytes 147464 | tf_op jit(solution)/shard_map/ppermute | solution.py:330
  43.0 6.9 %collective-permute-start.17 = (bf16[512,128]{1,0:T(8,128)(2,1)S(1)}, bf16[512,128]{1,0:T(8,128)(2,1)S(1)}, u32[]{:S(2)}, u32[]{:S(2)}) collective-permute-start(bf16[512,128]{1,0:T(8,128)(2,1)S(1)} %get-tuple-element.24), channel_id=1, source_target_pairs={{0,16},{8,24},{16,0},{24,8},{1,17},{9,25},{17,1},{25,9},{2,18},{10... | collective-permute-start | bytes 393224 | tf_op jit(solution)/shard_map/ppermute | solution.py:332
  44.6 7.5 %collective-permute-start.16 = (bf16[512,128]{1,0:T(8,128)(2,1)S(1)}, bf16[512,128]{1,0:T(8,128)(2,1)S(1)}, u32[]{:S(2)}, u32[]{:S(2)}) collective-permute-start(bf16[512,128]{1,0:T(8,128)(2,1)S(1)} %get-tuple-element.23), channel_id=1, source_target_pairs={{0,18},{1,19},{2,16},{3,17},{4,22},{5,23},{6,20},{7,21},{8,26},{9,... | collective-permute-start | bytes 393224 | tf_op jit(solution)/shard_map/ppermute | solution.py:334
  46.7 5.5 %collective-permute-start.15 = (bf16[512,128]{1,0:T(8,128)(2,1)S(1)}, bf16[512,128]{1,0:T(8,128)(2,1)S(1)}, u32[]{:S(2)}, u32[]{:S(2)}) collective-permute-start(bf16[512,128]{1,0:T(8,128)(2,1)S(1)} %shard_map.68), channel_id=1, source_target_pairs={{0,2},{1,3},{2,0},{3,1},{4,6},{5,7},{6,4},{7,5},{8,10},{9,11},{10,... | collective-permute-start | bytes 393224 | tf_op jit(solution)/shard_map/ppermute | solution.py:330

commit v8 on v7

--- a/solution.py
+++ b/solution.py
@@ -141,15 +141,14 @@
     )(*ids, rows)
 
 
-def project_kernel(projectors, padded, half_index, ids_refs, table_refs, packed_refs, before_refs, coef_ref, picks_of, terms):
+def project_kernel(projectors, half_index, ids_refs, table_refs, packed_refs, before_refs, coef_ref, picks_of, terms):
     bands = len(packed_refs)
     slots = table_refs[0].shape[0]
     pair_count = projectors // 2
     wide = 2 * bands * GROUP
     low = iota((bands * GROUP, LANES), 1) < LANES // 2
-    source = iota((pair_count * wide, bands * padded), 0) // GROUP
-    target = iota((pair_count * wide, bands * padded), 1)
-    gather_lanes = (target == lax.rem(source, bands) * padded + source // bands).astype(BF16)
+    folded = (pair_count * wide, bands * projectors)
+    gather_lanes = (iota(folded, 0) // GROUP == iota(folded, 1)).astype(BF16)
     diagonal = lax.rem(iota((GROUP, wide), 0), GROUP) == lax.rem(iota((GROUP, wide), 1), GROUP)
     none = jnp.zeros((bands * GROUP, LANES), BF16)
     half = LANES // 2
@@ -184,7 +183,7 @@
     coef_ref[...] = total + before_refs[0][...] if before_refs else total
 
 
-def project(ids, tables, picks, projectors, padded, half_index, before):
+def project(ids, tables, picks, projectors, half_index, before):
     bands = len(picks)
     slots = tables[0].shape[0]
     width = projectors * bands * GROUP
@@ -192,7 +191,7 @@
     def kernel(own_ids, other_ids, own_ref, other_ref, *rest):
         ends = [bands, bands + len(before)]
         project_kernel(
-            projectors, padded, half_index, (own_ids, other_ids), (own_ref, other_ref),
+            projectors, half_index, (own_ids, other_ids), (own_ref, other_ref),
             rest[: ends[0]], rest[ends[0] : ends[1]], *rest[ends[1] :],
         )
 
@@ -200,14 +199,14 @@
         kernel,
         in_specs=[VMEM_SPEC] * (4 + bands + len(before)),
         out_specs=VMEM_SPEC,
-        out_shape=jax.ShapeDtypeStruct((bands * padded, LANES), F32),
+        out_shape=jax.ShapeDtypeStruct((bands * projectors, LANES), F32),
         scratch_shapes=[pltpu.VMEM((bands, CORES * slots, LANES), BF16)] + [pltpu.VMEM((2 * CORES * slots, width), BF16)],
         cost_estimate=pl.CostEstimate(flops=0, bytes_accessed=PROJECT_BYTES, transcendentals=0),
         compiler_params=PARAMS,
     )(*ids, *tables, *picks, *before)
 
 
-def apply_kernel(wanted, projectors, padded, ids_refs, table_refs, count_ref, strength_ref, coef_refs, out_refs, wide_refs):
+def apply_kernel(wanted, projectors, ids_refs, table_refs, count_ref, strength_ref, coef_refs, out_refs, wide_refs):
     pair_count = projectors // 2
     width = projectors * LANES // 2
     atom_total = strength_ref.shape[2]
@@ -216,14 +215,11 @@
     valid = (iota((projectors, atom_total), 0) < count_ref[...]).astype(F32)
     spread = (iota((projectors, width), 0) == iota((projectors, width), 1) // half).astype(BF16)
     for band, wide_ref in zip(wanted, wide_refs):
-        total = coef_refs[0][band * padded : band * padded + projectors, :]
-        for away in range(1, PARTNERS):
-            first = (band ^ away) * padded
-            total = total + coef_refs[away][first : first + projectors, :]
-        total = total * valid
-        coupled = strength_ref[:, 0, :] * total[0:1]
-        for q in range(1, projectors):
-            coupled = coupled + strength_ref[:, q, :] * total[q : q + 1]
+        coupled = jnp.zeros((projectors, atom_total), F32)
+        for q in range(projectors):
+            rows = [coef_refs[away][q * PARTNERS + (band ^ away)][None] for away in range(PARTNERS)]
+            total = (rows[0] + rows[1] + rows[2] + rows[3]) * valid[q : q + 1]
+            coupled = coupled + strength_ref[:, q, :] * total
         scaled = (coupled * valid).astype(BF16)
         wide_ref[...] = dot(scaled, spread, ((0,), (0,))).astype(BF16)
     for slab in range(CORES):
@@ -244,14 +240,14 @@
                     out_ref[first : first + half, :] = packed.astype(BF16)
 
 
-def back_project(wanted, ids, tables, count, strength, coefs, projectors, padded):
+def back_project(wanted, ids, tables, count, strength, coefs, projectors):
     slots = sum(table.shape[0] for table in tables)
     atom_total = strength.shape[2]
 
     def kernel(own_ids, other_ids, count_ref, strength_ref, *rest):
         ends = [len(tables), len(tables) + len(coefs), len(tables) + len(coefs) + len(wanted)]
         apply_kernel(
-            wanted, projectors, padded, (own_ids, other_ids), rest[: ends[0]], count_ref, strength_ref,
+            wanted, projectors, (own_ids, other_ids), rest[: ends[0]], count_ref, strength_ref,
             rest[ends[0] : ends[1]], rest[ends[1] : ends[2]], rest[ends[2] :],
         )
 
@@ -265,56 +261,63 @@
     )(*ids, count, strength, *tables, *coefs)
 
 
-def place_kernel(chips, wanted, *refs):
-    ids_refs, value_refs, out_ref = refs[:CORES], dict(zip(wanted, refs[CORES:])), refs[-1]
-    step = pl.program_id(0)
+def place_kernel(chips, wanted, ids_refs, value_refs, out_ref, stages, sems):
+    value_refs = dict(zip(wanted, value_refs))
+    core, _, own_chip = place = own_place()
     half = LANES // 2
-    rows = out_ref.shape[1] // LANES // CORES
+    points = stages[0].shape[1]
     low = iota((half, LANES), 1) < half
-    for number, chip in enumerate(chips):
-
-        @pl.when(step == number)
-        def _(chip=chip):
-            for slab in range(CORES):
-                place = own_place()[0] if slab == 0 else CORES - 1 - own_place()[0]
-                parts, wanted = [], []
-                for column in range(PARTNERS):
-                    partner, piece = owner(chip, column)
-                    ids = slot_ids(ids_refs[slab], own_place(), chip, column, 0)
-                    for i, blocks in enumerate(ids):
-                        wanted.append(jnp.right_shift(blocks, 1))
-                        odd = jnp.bitwise_and(down(blocks), 1) == 1
-                        first = ((slab * PIECES + piece) * len(ids) + i) * half
-                        value = value_refs[partner][first : first + half, :].astype(F32)
-                        turned = pltpu.roll(value, half, 1)
-                        odd_a, odd_b = odd[:half], odd[half:]
-                        part_a = jnp.where(odd_a, turned, value)
-                        part_b = jnp.where(odd_b, value, turned)
-                        parts.append(jnp.where(low != odd_a, part_a, 0.0).astype(BF16))
-                        parts.append(jnp.where(low != odd_b, part_b, 0.0).astype(BF16))
-                values = jnp.concatenate(parts, axis=0)
-                wanted = jnp.concatenate(wanted, axis=1)
-                start = place * rows * LANES
-                for t in range(rows // LANES):
-                    hits = (iota((LANES, wanted.shape[1]), 0) + t * LANES == wanted).astype(BF16)
-                    total = dot(hits, values).astype(BF16)
-                    for i in range(LANES // 16):
-                        at = pl.multiple_of(start + t * LANES * LANES + i * 2048, 2048)
-                        out_ref[0:1, pl.ds(at, 2048)] = total[i * 16 : (i + 1) * 16].reshape(1, 2048)
+    copies = []
+    for chip in chips:
+        for slab in range(CORES):
+            parts, block_rows = [], []
+            for column in range(PARTNERS):
+                partner, piece = owner(chip, column)
+                ids = slot_ids(ids_refs[slab], place, chip, column, 0)
+                for i, blocks in enumerate(ids):
+                    block_rows.append(jnp.right_shift(blocks, 1))
+                    odd = jnp.bitwise_and(down(blocks), 1) == 1
+                    first = ((slab * PIECES + piece) * len(ids) + i) * half
+                    value = value_refs[partner][first : first + half, :].astype(F32)
+                    turned = pltpu.roll(value, half, 1)
+                    odd_a, odd_b = odd[:half], odd[half:]
+                    part_a = jnp.where(odd_a, turned, value)
+                    part_b = jnp.where(odd_b, value, turned)
+                    parts.append(jnp.where(low != odd_a, part_a, 0.0).astype(BF16))
+                    parts.append(jnp.where(low != odd_b, part_b, 0.0).astype(BF16))
+            values = jnp.concatenate(parts, axis=0)
+            block_row = jnp.concatenate(block_rows, axis=1)
+            stage = stages[len(copies)]
+            for t in range(points // LANES // LANES):
+                hits = (iota((LANES, block_row.shape[1]), 0) + t * LANES == block_row).astype(BF16)
+                total = dot(hits, values).astype(BF16)
+                for i in range(LANES // 16):
+                    at = t * LANES * LANES + i * 2048
+                    stage[0:1, at : at + 2048] = total[i * 16 : (i + 1) * 16].reshape(1, 2048)
+            index = jnp.bitwise_xor(own_chip, chip) * CORES + jnp.bitwise_xor(core, slab)
+            there = out_ref.at[:, pl.ds(pl.multiple_of(index * points, points), points)]
+            copies.append(pltpu.make_async_copy(stage, there, sems.at[len(copies)]))
+            copies[-1].start()
+    for copy in copies:
+        copy.wait()
 
 
 def place_rows(chips, ids, values, points, before):
-    share = points // CHIPS
     wanted = tuple(values)
     small = (*ids, *values.values())
-    apart = chips[1] ^ chips[0]
+    slabs = CORES * len(chips)
+
+    def kernel(*refs):
+        first_out = len(small) + len(before)
+        stages = refs[first_out + 1 : first_out + 1 + slabs]
+        place_kernel(chips, wanted, refs[:CORES], refs[CORES : len(small)], refs[first_out], stages, refs[-1])
+
     return pl.pallas_call(
-        functools.partial(place_kernel, chips, wanted),
-        grid=(len(chips),),
-        in_specs=[pl.BlockSpec(x.shape, lambda i, rank=x.ndim: (0,) * rank) for x in small]
-        + [pl.BlockSpec(memory_space=pl.ANY)] * len(before),
-        out_specs=pl.BlockSpec((1, share), lambda i: (0, jnp.bitwise_xor(own_place()[2], chips[0] + i * apart))),
+        kernel,
+        in_specs=[VMEM_SPEC] * len(small) + [pl.BlockSpec(memory_space=pl.ANY)] * len(before),
+        out_specs=pl.BlockSpec(memory_space=pl.ANY),
         out_shape=jax.ShapeDtypeStruct((1, points), BF16),
+        scratch_shapes=[pltpu.VMEM((1, points // (CORES * CHIPS)), BF16)] * slabs + [pltpu.SemaphoreType.DMA((slabs,))],
         input_output_aliases={len(small): 0} if before else {},
         compiler_params=PARAMS,
     )(*small, *before)
@@ -322,7 +325,6 @@
 
 def body(columns, slabs, psi, beta, pair_atom, pair_block, proj_count, strength):
     atom_total, projectors = strength.shape[:2]
-    padded = -(-projectors // 8) * 8
 
     def exchange(x, chip=0, column=0, core=0):
         turned = chip * CORES + core
@@ -344,17 +346,16 @@
     above = exchange(beta[0], chip=2)
     corner = exchange(above, column=1)
     picks = gather(ids, rows)
-    shape = (projectors, padded)
     first = jnp.concatenate([after(table, picks[0]) for table in (beta[0], beside)], axis=0)
     picks = partners(picks)
     first = (first, exchange(first, core=1))
-    coef = project(ids, first, picks, *shape, 0, ())
+    coef = project(ids, first, picks, projectors, 0, ())
     second = jnp.concatenate([after(table, *picks[1:]) for table in (above, corner)], axis=0)
     second = (second, exchange(second, core=1))
-    coef = project(ids, second, picks, *shape, 1, (coef,))
+    coef = project(ids, second, picks, projectors, 1, (coef,))
     coefs = partners([coef] * PARTNERS)
     count, strength = proj_count.reshape(1, atom_total), strength.transpose(1, 2, 0)
-    given = (ids, first + second, count, strength, coefs, *shape)
+    given = (ids, first + second, count, strength, coefs, projectors)
     results = [None] * PARTNERS
     for wanted in ((2, 3), (1,), (0,)):
         for partner, result in zip(wanted, back_project(wanted, *given)):

time: 54.6 us -> 53.9 us (0.987)
  Pallas kernels: 14.5 us -> 13.6 us
    pallas_call x2, Pallas kernels: 4.39 us -> 3.55 us  [place_rows(): pl.pallas_call(kernel, in_specs=[VMEM_SPEC] * len(small) + [pl.BlockSpec(...]
  transfers between devices with their start and end apart: 18 -> 18, of which waited for: 11 -> 11; matrix products, arithmetic and copies ran while one was open for 0% -> 0% of each run, Pallas kernels for 16% -> 15%
where the time goes in v8:
time: 53.9 us; the launch traced here: 53.7 us
  starting transfers between devices  22 us (41%)
  waiting for transfers between devices  15.5 us (29%)
  Pallas kernels  13.6 us (25%)
  local copies, waits for them, and re-layouts  1.73 us (3%)
  other arithmetic  0.71 us (1%)
    ppermute x10, starting transfers between devices, exchange(): return lax.ppermute(x, 'slab', [(i, i ^ turned) for i in range(slabs)])  12.4 us
    ppermute x10, waiting for transfers between devices, exchange(): return lax.ppermute(x, 'slab', [(i, i ^ turned) for i in range(slabs)])  7.02 us
    ppermute x5, starting transfers between devices, exchange(): return lax.ppermute(x, 'band', [(i, i ^ column) for i in range(columns)])  6.6 us
    ppermute x3, waiting for transfers between devices, exchange(): return lax.ppermute(x, ('band', 'slab'), pairs)  5.13 us
    pallas_call x3, Pallas kernels, back_project(): pl.pallas_call(kernel, in_specs=[VMEM_SPEC] * (4 + len(tables) + len(coef...  4.39 us
    pallas_call x2, Pallas kernels, place_rows(): pl.pallas_call(kernel, in_specs=[VMEM_SPEC] * len(small) + [pl.BlockSpec(...  3.55 us
    pallas_call x2, Pallas kernels, project(): pl.pallas_call(kernel, in_specs=[VMEM_SPEC] * (4 + bands + len(before)),...  3.53 us
    ppermute x5, waiting for transfers between devices, exchange(): return lax.ppermute(x, 'band', [(i, i ^ column) for i in range(columns)])  3.33 us
  transfers between devices with their start and end apart: 18, of which 11 were waited for; matrix products, arithmetic and copies ran while one was open for 0% of the time, Pallas kernels for 15%

profile of v8, /device:TPU:0, one launch (start us, length us, event | category | flops | bytes accessed | tf_op | source)
XLA Modules:
  0.0 53.7 jit_solution(11350273059528005319)
XLA Ops:
  0.0 0.7 %pad_add_fusion = s32[2,512]{1,0:T(2,128)S(1)} fusion(s32[1,512]{1,0:T(1,128)} %param.8, s32[1,512]{1,0:T(1,128)} %param.9), kind=kLoop, calls=%fused_computation.8 | loop fusion | flops 1024 | bytes 8192 | tf_op jit(solution)/shard_map/concatenate | solution.py:341
  0.7 5.1 %collective-permute-start.2 = (s32[1,8,128]{2,1,0:T(8,128)S(1)}, s32[1,8,128]{2,1,0:T(8,128)S(1)}, u32[]{:S(2)}, u32[]{:S(2)}) collective-permute-start(s32[1,8,128]{2,1,0:T(8,128)S(1)} %reshape.6), channel_id=1, source_target_pairs={{0,6},{1,7},{2,4},{3,5},{4,2},{5,3},{6,0},{7,1},{8,14},{9,15},{10,... | collective-permute-start | bytes 12296 | tf_op jit(solution)/shard_map/ppermute | solution.py:332
  5.8 0.0 collective-permute-start.1
  5.8 0.6 %collective-permute-start = (s32[1,8,128]{2,1,0:T(8,128)S(1)}, s32[1,8,128]{2,1,0:T(8,128)S(1)}, u32[]{:S(2)}, u32[]{:S(2)}) collective-permute-start(s32[1,8,128]{2,1,0:T(8,128)S(1)} %reshape.6), channel_id=1, source_target_pairs={{0,2},{1,3},{2,0},{3,1},{4,6},{5,7},{6,4},{7,5},{8,10},{9,11},{10,... | collective-permute-start | bytes 12296 | tf_op jit(solution)/shard_map/ppermute | solution.py:332
  6.5 2.3 %collective-permute-start.6 = (bf16[128,1152]{1,0:T(8,128)(2,1)}, bf16[128,1152]{1,0:T(8,128)(2,1)S(1)}, u32[]{:S(2)}, u32[]{:S(2)}) collective-permute-start(bf16[128,1152]{1,0:T(8,128)(2,1)} %bitcast.9), channel_id=1, source_target_pairs={{0,4},{1,5},{2,6},{3,7},{4,0},{5,1},{6,2},{7,3},{8,12},{9,13},{10,... | collective-permute-start | bytes 884744 | tf_op jit(solution)/shard_map/ppermute | solution.py:332
  8.8 1.5 %collective-permute-start.4 = (bf16[128,1152]{1,0:T(8,128)(2,1)}, bf16[128,1152]{1,0:T(8,128)(2,1)S(1)}, u32[]{:S(2)}, u32[]{:S(2)}) collective-permute-start(bf16[128,1152]{1,0:T(8,128)(2,1)} %bitcast.10), channel_id=1, source_target_pairs={{0,8},{8,0},{16,24},{24,16},{1,9},{9,1},{17,25},{25,17},{2,10},{10... | collective-permute-start | bytes 884744 | tf_op jit(solution)/shard_map/ppermute | solution.py:334
  10.2 0.0 collective-permute-done
  10.3 0.1 collective-permute-done.1
  10.4 0.0 collective-permute-done.2
  10.4 0.1 collective-permute-start.3
  10.4 0.0 copy-start
  10.4 1.6 %copy-done = bf16[1,524288]{1,0:T(2,128)(2,1)S(1)} copy-done((bf16[1,524288]{1,0:T(2,128)(2,1)S(1)}, bf16[1,524288]{1,0:T(2,128)(2,1)}, u32[]{:S(2)}) %copy-start) | copy-done | bytes 1048600
  12.0 0.6 %shard_map.64.rows_ref = bf16[4096,128]{1,0:T(8,128)(2,1)S(1)} custom-call(bf16[1,524288]{1,0:T(2,128)(2,1)S(1)} %copy-done), custom_call_target="tpu_custom_call" | custom-call | tf_op jit(solution)/shard_map/pallas_call | solution.py:89
  12.7 0.0 collective-permute-done.3.other_ids.refs_1_
  12.7 1.5 %shard_map.65 = (bf16[512,128]{1,0:T(8,128)(2,1)S(1)}, bf16[512,128]{1,0:T(8,128)(2,1)S(1)}, bf16[512,128]{1,0:T(8,128)(2,1)S(1)}, bf16[512,128]{1,0:T(8,128)(2,1)S(1)}) custom-call(s32[4,8,128]{2,1,0:T(8,128)S(1)} %constant_dynamic-update-slice_fusion.own_ids.refs_0_, s32[4,8,128]{2,1,0:T(8,128)S(1)} %collective-permute-done.3.other_ids.refs_1_, ...), custom_call_target="tpu_custom_call" | custom-call | bytes 10000000 | tf_op jit(solution)/shard_map/pallas_call | solution.py:134
  14.2 2.0 %collective-permute-start.7 = (bf16[512,128]{1,0:T(8,128)(2,1)S(1)}, bf16[512,128]{1,0:T(8,128)(2,1)S(1)}, u32[]{:S(2)}, u32[]{:S(2)}) collective-permute-start(bf16[512,128]{1,0:T(8,128)(2,1)S(1)} %get-tuple-element.18), channel_id=1, source_target_pairs={{0,2},{1,3},{2,0},{3,1},{4,6},{5,7},{6,4},{7,5},{8,10},{9,11},{10,... | collective-permute-start | bytes 393224 | tf_op jit(solution)/shard_map/ppermute | solution.py:332
  16.3 1.5 %collective-permute-start.8 = (bf16[512,128]{1,0:T(8,128)(2,1)S(1)}, bf16[512,128]{1,0:T(8,128)(2,1)S(1)}, u32[]{:S(2)}, u32[]{:S(2)}) collective-permute-start(bf16[512,128]{1,0:T(8,128)(2,1)S(1)} %get-tuple-element.19), channel_id=1, source_target_pairs={{0,16},{8,24},{16,0},{24,8},{1,17},{9,25},{17,1},{25,9},{2,18},{10... | collective-permute-start | bytes 393224 | tf_op jit(solution)/shard_map/ppermute | solution.py:334
  17.8 0.0 collective-permute-start.9
  17.8 0.0 collective-permute-done.4
  17.8 4.4 %collective-permute-done.6 = bf16[128,1152]{1,0:T(8,128)(2,1)S(1)} collective-permute-done((bf16[128,1152]{1,0:T(8,128)(2,1)}, bf16[128,1152]{1,0:T(8,128)(2,1)S(1)}, u32[]{:S(2)}, u32[]{:S(2)}) %collective-permute-start.6) | collective-permute-done | bytes 294944 | tf_op jit(solution)/shard_map/ppermute | solution.py:332
  22.2 1.5 %collective-permute-start.10 = (bf16[128,1152]{1,0:T(8,128)(2,1)S(1)}, bf16[128,1152]{1,0:T(8,128)(2,1)S(1)}, u32[]{:S(2)}, u32[]{:S(2)}) collective-permute-start(bf16[128,1152]{1,0:T(8,128)(2,1)S(1)} %collective-permute-done.6), channel_id=1, source_target_pairs={{0,8},{8,0},{16,24},{24,16},{1,9},{9,1},{17,25},{25,17},{2,10},{10... | collective-permute-start | bytes 884744 | tf_op jit(solution)/shard_map/ppermute | solution.py:334
  23.8 1.2 %collective-permute-done.7.rest_1_ = bf16[512,128]{1,0:T(8,128)(2,1)S(1)} collective-permute-done((bf16[512,128]{1,0:T(8,128)(2,1)S(1)}, bf16[512,128]{1,0:T(8,128)(2,1)S(1)}, u32[]{:S(2)}, u32[]{:S(2)}) %collective-permute-start.7) | collective-permute-done | bytes 131104 | tf_op jit(solution)/shard_map/ppermute | solution.py:332
  25.0 0.0 collective-permute-done.8.rest_2_
  25.0 3.7 %collective-permute-done.9.rest_3_ = bf16[512,128]{1,0:T(8,128)(2,1)S(1)} collective-permute-done((bf16[512,128]{1,0:T(8,128)(2,1)S(1)}, bf16[512,128]{1,0:T(8,128)(2,1)S(1)}, u32[]{:S(2)}, u32[]{:S(2)}) %collective-permute-start.9) | collective-permute-done | bytes 131104 | tf_op jit(solution)/shard_map/ppermute | solution.py:336
  28.7 0.1 collective-permute-start.5
  28.8 0.0 copy-start.1
  28.8 0.0 copy-start.2
  28.9 1.4 %collective-permute-done.10 = bf16[128,1152]{1,0:T(8,128)(2,1)S(1)} collective-permute-done((bf16[128,1152]{1,0:T(8,128)(2,1)S(1)}, bf16[128,1152]{1,0:T(8,128)(2,1)S(1)}, u32[]{:S(2)}, u32[]{:S(2)}) %collective-permute-start.10) | collective-permute-done | bytes 294944 | tf_op jit(solution)/shard_map/ppermute | solution.py:334
  30.3 0.1 collective-permute-start.11
  30.4 0.3 collective-permute-done.5.other_ref.rest_1_
  30.7 1.8 %shard_map.66.rest_4_ = f32[72,128]{1,0:T(8,128)S(1)} custom-call(s32[4,8,128]{2,1,0:T(8,128)S(1)} %constant_dynamic-update-slice_fusion.own_ids.refs_0_, s32[4,8,128]{2,1,0:T(8,128)S(1)} %collective-permute-done.3.other_ids.refs_1_, bf16[256,1152]{1,0:T(8,128)(2,1)S(1)} %constant_dynamic-update-slice_fusion.4.own_ref.rest_0_, ...), custom_call_target="tpu_custom_call" | custom-call | bytes 30000000 | tf_op jit(solution)/shard_map/pallas_call | solution.py:198
  32.5 1.8 %shard_map.67.rest_4_ = f32[72,128]{1,0:T(8,128)S(1)} custom-call(s32[4,8,128]{2,1,0:T(8,128)S(1)} %constant_dynamic-update-slice_fusion.own_ids.refs_0_, s32[4,8,128]{2,1,0:T(8,128)S(1)} %collective-permute-done.3.other_ids.refs_1_, bf16[256,1152]{1,0:T(8,128)(2,1)S(1)} %constant_dynamic-update-slice_fusion.6.own_ref.rest_2_, ...), custom_call_target="tpu_custom_call" | custom-call | bytes 30000000 | tf_op jit(solution)/shard_map/pallas_call | solution.py:198
  34.3 2.2 %collective-permute-start.14 = (f32[72,128]{1,0:T(8,128)S(1)}, f32[72,128]{1,0:T(8,128)S(1)}, u32[]{:S(2)}, u32[]{:S(2)}) collective-permute-start(f32[72,128]{1,0:T(8,128)S(1)} %shard_map.67.rest_4_), channel_id=1, source_target_pairs={{0,18},{1,19},{2,16},{3,17},{4,22},{5,23},{6,20},{7,21},{8,26},{9,... | collective-permute-start | bytes 110600 | tf_op jit(solution)/shard_map/ppermute | solution.py:336
  36.4 0.5 collective-permute-start.13
  36.9 0.9 %collective-permute-start.12 = (f32[72,128]{1,0:T(8,128)S(1)}, f32[72,128]{1,0:T(8,128)S(1)}, u32[]{:S(2)}, u32[]{:S(2)}) collective-permute-start(f32[72,128]{1,0:T(8,128)S(1)} %shard_map.67.rest_4_), channel_id=1, source_target_pairs={{0,2},{1,3},{2,0},{3,1},{4,6},{5,7},{6,4},{7,5},{8,10},{9,11},{10,... | collective-permute-start | bytes 110600 | tf_op jit(solution)/shard_map/ppermute | solution.py:332
  37.8 1.4 %collective-permute-done.14.rest_7_ = f32[72,128]{1,0:T(8,128)S(1)} collective-permute-done((f32[72,128]{1,0:T(8,128)S(1)}, f32[72,128]{1,0:T(8,128)S(1)}, u32[]{:S(2)}, u32[]{:S(2)}) %collective-permute-start.14) | collective-permute-done | bytes 36896 | tf_op jit(solution)/shard_map/ppermute | solution.py:336
  39.2 1.2 %collective-permute-done.13.rest_6_ = f32[72,128]{1,0:T(8,128)S(1)} collective-permute-done((f32[72,128]{1,0:T(8,128)S(1)}, f32[72,128]{1,0:T(8,128)S(1)}, u32[]{:S(2)}, u32[]{:S(2)}) %collective-permute-start.13) | collective-permute-done | bytes 36896 | tf_op jit(solution)/shard_map/ppermute | solution.py:334
  40.4 0.5 collective-permute-done.12.rest_5_
  40.9 1.9 %shard_map.69 = (bf16[512,128]{1,0:T(8,128)(2,1)S(1)}, bf16[512,128]{1,0:T(8,128)(2,1)S(1)}) custom-call(s32[4,8,128]{2,1,0:T(8,128)S(1)} %constant_dynamic-update-slice_fusion.own_ids.refs_0_, s32[4,8,128]{2,1,0:T(8,128)S(1)} %collective-permute-done.3.other_ids.refs_1_, s32[1,128]{1,0:T(1,128)S(1)} %bitcast.6, f32[18,18,128]{2,1,0:T(8,128)S(1)} %bitcast.3, ...), custom_call_target="tpu_custom_call" | custom-call | tf_op jit(solution)/shard_map/pallas_call | solution.py:254
  42.8 1.6 %collective-permute-start.17 = (bf16[512,128]{1,0:T(8,128)(2,1)S(1)}, bf16[512,128]{1,0:T(8,128)(2,1)S(1)}, u32[]{:S(2)}, u32[]{:S(2)}) collective-permute-start(bf16[512,128]{1,0:T(8,128)(2,1)S(1)} %get-tuple-element.24), channel_id=1, source_target_pairs={{0,16},{8,24},{16,0},{24,8},{1,17},{9,25},{17,1},{25,9},{2,18},{10... | collective-permute-start | bytes 393224 | tf_op jit(solution)/shard_map/ppermute | solution.py:334
  44.4 0.8 %collective-permute-start.16 = (bf16[512,128]{1,0:T(8,128)(2,1)S(1)}, bf16[512,128]{1,0:T(8,128)(2,1)S(1)}, u32[]{:S(2)}, u32[]{:S(2)}) collective-permute-start(bf16[512,128]{1,0:T(8,128)(2,1)S(1)} %get-tuple-element.23), channel_id=1, source_target_pairs={{0,18},{1,19},{2,16},{3,17},{4,22},{5,23},{6,20},{7,21},{8,26},{9,... | collective-permute-start | bytes 393224 | tf_op jit(solution)/shard_map/ppermute | solution.py:336
  45.3 1.2 %shard_map.68 = bf16[512,128]{1,0:T(8,128)(2,1)S(1)} custom-call(s32[4,8,128]{2,1,0:T(8,128)S(1)} %constant_dynamic-update-slice_fusion.own_ids.refs_0_, s32[4,8,128]{2,1,0:T(8,128)S(1)} %collective-permute-done.3.other_ids.refs_1_, s32[1,128]{1,0:T(1,128)S(1)} %bitcast.7, f32[18,18,128]{2,1,0:T(8,128)S(1)} %bitcast.4, ...), custom_call_target="tpu_custom_call" | custom-call | tf_op jit(solution)/shard_map/pallas_call | solution.py:254
  46.5 1.2 %collective-permute-start.15 = (bf16[512,128]{1,0:T(8,128)(2,1)S(1)}, bf16[512,128]{1,0:T(8,128)(2,1)S(1)}, u32[]{:S(2)}, u32[]{:S(2)}) collective-permute-start(bf16[512,128]{1,0:T(8,128)(2,1)S(1)} %shard_map.68), channel_id=1, source_target_pairs={{0,2},{1,3},{2,0},{3,1},{4,6},{5,7},{6,4},{7,5},{8,10},{9,11},{10,... | collective-permute-start | bytes 393224 | tf_op jit(solution)/shard_map/ppermute | solution.py:332
  47.7 1.2 %shard_map.70.refs_2_ = bf16[512,128]{1,0:T(8,128)(2,1)S(1)} custom-call(s32[4,8,128]{2,1,0:T(8,128)S(1)} %constant_dynamic-update-slice_fusion.own_ids.refs_0_, s32[4,8,128]{2,1,0:T(8,128)S(1)} %collective-permute-done.3.other_ids.refs_1_, s32[1,128]{1,0:T(1,128)S(1)} %bitcast.8, f32[18,18,128]{2,1,0:T(8,128)S(1)} %bitcast.5, ...), custom_call_target="tpu_custom_call" | custom-call | tf_op jit(solution)/shard_map/pallas_call | solution.py:254
  48.9 0.7 %collective-permute-done.17.refs_3_ = bf16[512,128]{1,0:T(8,128)(2,1)S(1)} collective-permute-done((bf16[512,128]{1,0:T(8,128)(2,1)S(1)}, bf16[512,128]{1,0:T(8,128)(2,1)S(1)}, u32[]{:S(2)}, u32[]{:S(2)}) %collective-permute-start.17) | collective-permute-done | bytes 131104 | tf_op jit(solution)/shard_map/ppermute | solution.py:334
  49.6 1.8 %shard_map.71.refs_4_ = bf16[1,524288]{1,0:T(2,128)(2,1)} custom-call(s32[4,8,128]{2,1,0:T(8,128)S(1)} %constant_dynamic-update-slice_fusion.own_ids.refs_0_, s32[4,8,128]{2,1,0:T(8,128)S(1)} %collective-permute-done.3.other_ids.refs_1_, bf16[512,128]{1,0:T(8,128)(2,1)S(1)} %shard_map.70.refs_2_, bf16[512,128]{1,0:T(8,128)(2,1)S(1)} %collective-permute-done.17.refs_3_), custom_call_target="tpu_custom_call" | custom-call | tf_op jit(solution)/shard_map/pallas_call | solution.py:315
  51.4 0.5 collective-permute-done.15.refs_2_
  51.9 1.8 %shard_map.72 = bf16[1,524288]{1,0:T(2,128)(2,1)} custom-call(s32[4,8,128]{2,1,0:T(8,128)S(1)} %constant_dynamic-update-slice_fusion.own_ids.refs_0_, s32[4,8,128]{2,1,0:T(8,128)S(1)} %collective-permute-done.3.other_ids.refs_1_, bf16[512,128]{1,0:T(8,128)(2,1)S(1)} %collective-permute-done.15.refs_2_, ...), custom_call_target="tpu_custom_call", output_to_operand_aliasing={{}: (4, {})} | custom-call | tf_op jit(solution)/shard_map/pallas_call | solution.py:315
  (15 shorter events, 0.1 us)
Async XLA Ops:
  0.7 9.6 %collective-permute-start.2 = (s32[1,8,128]{2,1,0:T(8,128)S(1)}, s32[1,8,128]{2,1,0:T(8,128)S(1)}, u32[]{:S(2)}, u32[]{:S(2)}) collective-permute-start(s32[1,8,128]{2,1,0:T(8,128)S(1)} %reshape.6), channel_id=1, source_target_pairs={{0,6},{1,7},{2,4},{3,5},{4,2},{5,3},{6,0},{7,1},{8,14},{9,15},{10,... | collective-permute-start | bytes 12296 | tf_op jit(solution)/shard_map/ppermute | solution.py:332
  5.8 4.5 %collective-permute-start.1 = (s32[1,8,128]{2,1,0:T(8,128)S(1)}, s32[1,8,128]{2,1,0:T(8,128)S(1)}, u32[]{:S(2)}, u32[]{:S(2)}) collective-permute-start(s32[1,8,128]{2,1,0:T(8,128)S(1)} %reshape.6), channel_id=1, source_target_pairs={{0,4},{1,5},{2,6},{3,7},{4,0},{5,1},{6,2},{7,3},{8,12},{9,13},{10,... | collective-permute-start | bytes 12296 | tf_op jit(solution)/shard_map/ppermute | solution.py:332
  5.8 4.4 %collective-permute-start = (s32[1,8,128]{2,1,0:T(8,128)S(1)}, s32[1,8,128]{2,1,0:T(8,128)S(1)}, u32[]{:S(2)}, u32[]{:S(2)}) collective-permute-start(s32[1,8,128]{2,1,0:T(8,128)S(1)} %reshape.6), channel_id=1, source_target_pairs={{0,2},{1,3},{2,0},{3,1},{4,6},{5,7},{6,4},{7,5},{8,10},{9,11},{10,... | collective-permute-start | bytes 12296 | tf_op jit(solution)/shard_map/ppermute | solution.py:332
  6.5 15.8 %collective-permute-start.6 = (bf16[128,1152]{1,0:T(8,128)(2,1)}, bf16[128,1152]{1,0:T(8,128)(2,1)S(1)}, u32[]{:S(2)}, u32[]{:S(2)}) collective-permute-start(bf16[128,1152]{1,0:T(8,128)(2,1)} %bitcast.9), channel_id=1, source_target_pairs={{0,4},{1,5},{2,6},{3,7},{4,0},{5,1},{6,2},{7,3},{8,12},{9,13},{10,... | collective-permute-start | bytes 884744 | tf_op jit(solution)/shard_map/ppermute | solution.py:332
  8.8 9.1 %collective-permute-start.4 = (bf16[128,1152]{1,0:T(8,128)(2,1)}, bf16[128,1152]{1,0:T(8,128)(2,1)S(1)}, u32[]{:S(2)}, u32[]{:S(2)}) collective-permute-start(bf16[128,1152]{1,0:T(8,128)(2,1)} %bitcast.10), channel_id=1, source_target_pairs={{0,8},{8,0},{16,24},{24,16},{1,9},{9,1},{17,25},{25,17},{2,10},{10... | collective-permute-start | bytes 884744 | tf_op jit(solution)/shard_map/ppermute | solution.py:334
  10.4 2.3 %collective-permute-start.3 = (s32[4,8,128]{2,1,0:T(8,128)S(1)}, s32[4,8,128]{2,1,0:T(8,128)S(1)}, u32[]{:S(2)}, u32[]{:S(2)}) collective-permute-start(s32[4,8,128]{2,1,0:T(8,128)S(1)} %constant_dynamic-update-slice_fusion.own_ids.refs_0_), channel_id=1, source_target_pairs={{0,1},{1,0},{2,3},{3,2},{4,5},{5,4},{6,7},{7,6},{8,9},{9,8},{10,11... | collective-permute-start | bytes 49160 | tf_op jit(solution)/shard_map/ppermute | solution.py:332
  10.4 1.6 %copy-start = (bf16[1,524288]{1,0:T(2,128)(2,1)S(1)}, bf16[1,524288]{1,0:T(2,128)(2,1)}, u32[]{:S(2)}) copy-start(bf16[1,524288]{1,0:T(2,128)(2,1)} %psi_ref.1) | copy-start | bytes 3145732
  12.0 5.8 %copy-start.3 = (bf16[1,128,1152]{2,1,0:T(8,128)(2,1)S(1)}, bf16[1,128,1152]{2,1,0:T(8,128)(2,1)}, u32[]{:S(2)}) copy-start(bf16[1,128,1152]{2,1,0:T(8,128)(2,1)} %param.7) | copy-start | bytes 884740
  14.2 10.7 %collective-permute-start.7 = (bf16[512,128]{1,0:T(8,128)(2,1)S(1)}, bf16[512,128]{1,0:T(8,128)(2,1)S(1)}, u32[]{:S(2)}, u32[]{:S(2)}) collective-permute-start(bf16[512,128]{1,0:T(8,128)(2,1)S(1)} %get-tuple-element.18), channel_id=1, source_target_pairs={{0,2},{1,3},{2,0},{3,1},{4,6},{5,7},{6,4},{7,5},{8,10},{9,11},{10,... | collective-permute-start | bytes 393224 | tf_op jit(solution)/shard_map/ppermute | solution.py:332
  16.3 8.7 %collective-permute-start.8 = (bf16[512,128]{1,0:T(8,128)(2,1)S(1)}, bf16[512,128]{1,0:T(8,128)(2,1)S(1)}, u32[]{:S(2)}, u32[]{:S(2)}) collective-permute-start(bf16[512,128]{1,0:T(8,128)(2,1)S(1)} %get-tuple-element.19), channel_id=1, source_target_pairs={{0,16},{8,24},{16,0},{24,8},{1,17},{9,25},{17,1},{25,9},{2,18},{10... | collective-permute-start | bytes 393224 | tf_op jit(solution)/shard_map/ppermute | solution.py:334
  17.8 10.9 %collective-permute-start.9 = (bf16[512,128]{1,0:T(8,128)(2,1)S(1)}, bf16[512,128]{1,0:T(8,128)(2,1)S(1)}, u32[]{:S(2)}, u32[]{:S(2)}) collective-permute-start(bf16[512,128]{1,0:T(8,128)(2,1)S(1)} %get-tuple-element.20), channel_id=1, source_target_pairs={{0,18},{1,19},{2,16},{3,17},{4,22},{5,23},{6,20},{7,21},{8,26},{9,... | collective-permute-start | bytes 393224 | tf_op jit(solution)/shard_map/ppermute | solution.py:336
  22.2 8.0 %collective-permute-start.10 = (bf16[128,1152]{1,0:T(8,128)(2,1)S(1)}, bf16[128,1152]{1,0:T(8,128)(2,1)S(1)}, u32[]{:S(2)}, u32[]{:S(2)}) collective-permute-start(bf16[128,1152]{1,0:T(8,128)(2,1)S(1)} %collective-permute-done.6), channel_id=1, source_target_pairs={{0,8},{8,0},{16,24},{24,16},{1,9},{9,1},{17,25},{25,17},{2,10},{10... | collective-permute-start | bytes 884744 | tf_op jit(solution)/shard_map/ppermute | solution.py:334
  28.7 2.0 %collective-permute-start.5 = (bf16[256,1152]{1,0:T(8,128)(2,1)S(1)}, bf16[256,1152]{1,0:T(8,128)(2,1)S(1)}, u32[]{:S(2)}, u32[]{:S(2)}) collective-permute-start(bf16[256,1152]{1,0:T(8,128)(2,1)S(1)} %constant_dynamic-update-slice_fusion.4.own_ref.rest_0_), channel_id=1, source_target_pairs={{0,1},{1,0},{2,3},{3,2},{4,5},{5,4},{6,7},{7,6},{8,9},{9,8},{10,11... | collective-permute-start | bytes 1769480 | tf_op jit(solution)/shard_map/ppermute | solution.py:332
  28.8 12.1 %copy-start.1 = (f32[128,18,18]{0,2,1:T(8,128)S(1)}, f32[128,18,18]{0,2,1:T(8,128)}, u32[]{:S(2)}) copy-start(f32[128,18,18]{0,2,1:T(8,128)} %param.11) | copy-start | bytes 497668
  28.8 12.1 %copy-start.2 = (s32[128]{0:T(128)S(1)}, s32[128]{0:T(128)}, u32[]{:S(2)}) copy-start(s32[128]{0:T(128)} %param.10) | copy-start | bytes 1540
  30.3 2.2 %collective-permute-start.11 = (bf16[256,1152]{1,0:T(8,128)(2,1)S(1)}, bf16[256,1152]{1,0:T(8,128)(2,1)S(1)}, u32[]{:S(2)}, u32[]{:S(2)}) collective-permute-start(bf16[256,1152]{1,0:T(8,128)(2,1)S(1)} %constant_dynamic-update-slice_fusion.6.own_ref.rest_2_), channel_id=1, source_target_pairs={{0,1},{1,0},{2,3},{3,2},{4,5},{5,4},{6,7},{7,6},{8,9},{9,8},{10,11... | collective-permute-start | bytes 1769480 | tf_op jit(solution)/shard_map/ppermute | solution.py:332
  34.3 4.9 %collective-permute-start.14 = (f32[72,128]{1,0:T(8,128)S(1)}, f32[72,128]{1,0:T(8,128)S(1)}, u32[]{:S(2)}, u32[]{:S(2)}) collective-permute-start(f32[72,128]{1,0:T(8,128)S(1)} %shard_map.67.rest_4_), channel_id=1, source_target_pairs={{0,18},{1,19},{2,16},{3,17},{4,22},{5,23},{6,20},{7,21},{8,26},{9,... | collective-permute-start | bytes 110600 | tf_op jit(solution)/shard_map/ppermute | solution.py:336
  36.4 4.0 %collective-permute-start.13 = (f32[72,128]{1,0:T(8,128)S(1)}, f32[72,128]{1,0:T(8,128)S(1)}, u32[]{:S(2)}, u32[]{:S(2)}) collective-permute-start(f32[72,128]{1,0:T(8,128)S(1)} %shard_map.67.rest_4_), channel_id=1, source_target_pairs={{0,16},{8,24},{16,0},{24,8},{1,17},{9,25},{17,1},{25,9},{2,18},{10... | collective-permute-start | bytes 110600 | tf_op jit(solution)/shard_map/ppermute | solution.py:334
  36.9 4.0 %collective-permute-start.12 = (f32[72,128]{1,0:T(8,128)S(1)}, f32[72,128]{1,0:T(8,128)S(1)}, u32[]{:S(2)}, u32[]{:S(2)}) collective-permute-start(f32[72,128]{1,0:T(8,128)S(1)} %shard_map.67.rest_4_), channel_id=1, source_target_pairs={{0,2},{1,3},{2,0},{3,1},{4,6},{5,7},{6,4},{7,5},{8,10},{9,11},{10,... | collective-permute-start | bytes 110600 | tf_op jit(solution)/shard_map/ppermute | solution.py:332
  42.8 6.8 %collective-permute-start.17 = (bf16[512,128]{1,0:T(8,128)(2,1)S(1)}, bf16[512,128]{1,0:T(8,128)(2,1)S(1)}, u32[]{:S(2)}, u32[]{:S(2)}) collective-permute-start(bf16[512,128]{1,0:T(8,128)(2,1)S(1)} %get-tuple-element.24), channel_id=1, source_target_pairs={{0,16},{8,24},{16,0},{24,8},{1,17},{9,25},{17,1},{25,9},{2,18},{10... | collective-permute-start | bytes 393224 | tf_op jit(solution)/shard_map/ppermute | solution.py:334
  44.4 7.0 %collective-permute-start.16 = (bf16[512,128]{1,0:T(8,128)(2,1)S(1)}, bf16[512,128]{1,0:T(8,128)(2,1)S(1)}, u32[]{:S(2)}, u32[]{:S(2)}) collective-permute-start(bf16[512,128]{1,0:T(8,128)(2,1)S(1)} %get-tuple-element.23), channel_id=1, source_target_pairs={{0,18},{1,19},{2,16},{3,17},{4,22},{5,23},{6,20},{7,21},{8,26},{9,... | collective-permute-start | bytes 393224 | tf_op jit(solution)/shard_map/ppermute | solution.py:336
  46.5 5.4 %collective-permute-start.15 = (bf16[512,128]{1,0:T(8,128)(2,1)S(1)}, bf16[512,128]{1,0:T(8,128)(2,1)S(1)}, u32[]{:S(2)}, u32[]{:S(2)}) collective-permute-start(bf16[512,128]{1,0:T(8,128)(2,1)S(1)} %shard_map.68), channel_id=1, source_target_pairs={{0,2},{1,3},{2,0},{3,1},{4,6},{5,7},{6,4},{7,5},{8,10},{9,11},{10,... | collective-permute-start | bytes 393224 | tf_op jit(solution)/shard_map/ppermute | solution.py:332

commit v9 on v8

--- a/solution.py
+++ b/solution.py
@@ -24,6 +24,11 @@
 
 def dot(a, b, contract=((1,), (0,))):
     return lax.dot_general(a, b, (contract, ((), ())), preferred_element_type=F32)
+
+
+def same(number, wanted):
+    near = number.astype(F32).astype(BF16) == wanted.astype(F32).astype(BF16)
+    return jnp.where(near, jnp.ones((), BF16), jnp.zeros((), BF16))
 
 
 def two_terms(x):
@@ -288,8 +293,9 @@
             values = jnp.concatenate(parts, axis=0)
             block_row = jnp.concatenate(block_rows, axis=1)
             stage = stages[len(copies)]
+            number = iota((LANES, block_row.shape[1]), 0)
             for t in range(points // LANES // LANES):
-                hits = (iota((LANES, block_row.shape[1]), 0) + t * LANES == block_row).astype(BF16)
+                hits = same(number, block_row - t * LANES)
                 total = dot(hits, values).astype(BF16)
                 for i in range(LANES // 16):
                     at = t * LANES * LANES + i * 2048

time: 53.9 us -> 53.9 us (level)
  no operation moved by 1% of the time
where the time goes in v9:
time: 53.9 us; the launch traced here: 53.7 us
  starting transfers between devices  22 us (41%)
  waiting for transfers between devices  15.5 us (29%)
  Pallas kernels  13.6 us (25%)
  local copies, waits for them, and re-layouts  1.73 us (3%)
  other arithmetic  0.71 us (1%)
    ppermute x10, starting transfers between devices, exchange(): return lax.ppermute(x, 'slab', [(i, i ^ turned) for i in range(slabs)])  12.4 us
    ppermute x10, waiting for transfers between devices, exchange(): return lax.ppermute(x, 'slab', [(i, i ^ turned) for i in range(slabs)])  7.05 us
    ppermute x5, starting transfers between devices, exchange(): return lax.ppermute(x, 'band', [(i, i ^ column) for i in range(columns)])  6.6 us
    ppermute x3, waiting for transfers between devices, exchange(): return lax.ppermute(x, ('band', 'slab'), pairs)  5.13 us
    pallas_call x3, Pallas kernels, back_project(): pl.pallas_call(kernel, in_specs=[VMEM_SPEC] * (4 + len(tables) + len(coef...  4.39 us
    pallas_call x2, Pallas kernels, project(): pl.pallas_call(kernel, in_specs=[VMEM_SPEC] * (4 + bands + len(before)),...  3.53 us
    pallas_call x2, Pallas kernels, place_rows(): pl.pallas_call(kernel, in_specs=[VMEM_SPEC] * len(small) + [pl.BlockSpec(...  3.49 us
    ppermute x5, waiting for transfers between devices, exchange(): return lax.ppermute(x, 'band', [(i, i ^ column) for i in range(columns)])  3.33 us
  transfers between devices with their start and end apart: 18, of which 11 were waited for; matrix products, arithmetic and copies ran while one was open for 0% of the time, Pallas kernels for 15%

profile of v9, /device:TPU:0, one launch (start us, length us, event | category | flops | bytes accessed | tf_op | source)
XLA Modules:
  0.0 53.7 jit_solution(3326825620164400330)
XLA Ops:
  0.0 0.7 %pad_add_fusion = s32[2,512]{1,0:T(2,128)S(1)} fusion(s32[1,512]{1,0:T(1,128)} %param.8, s32[1,512]{1,0:T(1,128)} %param.9), kind=kLoop, calls=%fused_computation.8 | loop fusion | flops 1024 | bytes 8192 | tf_op jit(solution)/shard_map/concatenate | solution.py:347
  0.7 5.1 %collective-permute-start.2 = (s32[1,8,128]{2,1,0:T(8,128)S(1)}, s32[1,8,128]{2,1,0:T(8,128)S(1)}, u32[]{:S(2)}, u32[]{:S(2)}) collective-permute-start(s32[1,8,128]{2,1,0:T(8,128)S(1)} %reshape.6), channel_id=1, source_target_pairs={{0,6},{1,7},{2,4},{3,5},{4,2},{5,3},{6,0},{7,1},{8,14},{9,15},{10,... | collective-permute-start | bytes 12296 | tf_op jit(solution)/shard_map/ppermute | solution.py:338
  5.8 0.6 %collective-permute-start = (s32[1,8,128]{2,1,0:T(8,128)S(1)}, s32[1,8,128]{2,1,0:T(8,128)S(1)}, u32[]{:S(2)}, u32[]{:S(2)}) collective-permute-start(s32[1,8,128]{2,1,0:T(8,128)S(1)} %reshape.6), channel_id=1, source_target_pairs={{0,2},{1,3},{2,0},{3,1},{4,6},{5,7},{6,4},{7,5},{8,10},{9,11},{10,... | collective-permute-start | bytes 12296 | tf_op jit(solution)/shard_map/ppermute | solution.py:338
  6.5 2.3 %collective-permute-start.6 = (bf16[128,1152]{1,0:T(8,128)(2,1)}, bf16[128,1152]{1,0:T(8,128)(2,1)S(1)}, u32[]{:S(2)}, u32[]{:S(2)}) collective-permute-start(bf16[128,1152]{1,0:T(8,128)(2,1)} %bitcast.9), channel_id=1, source_target_pairs={{0,4},{1,5},{2,6},{3,7},{4,0},{5,1},{6,2},{7,3},{8,12},{9,13},{10,... | collective-permute-start | bytes 884744 | tf_op jit(solution)/shard_map/ppermute | solution.py:338
  8.8 1.5 %collective-permute-start.4 = (bf16[128,1152]{1,0:T(8,128)(2,1)}, bf16[128,1152]{1,0:T(8,128)(2,1)S(1)}, u32[]{:S(2)}, u32[]{:S(2)}) collective-permute-start(bf16[128,1152]{1,0:T(8,128)(2,1)} %bitcast.10), channel_id=1, source_target_pairs={{0,8},{8,0},{16,24},{24,16},{1,9},{9,1},{17,25},{25,17},{2,10},{10... | collective-permute-start | bytes 884744 | tf_op jit(solution)/shard_map/ppermute | solution.py:340
  10.2 0.0 collective-permute-done
  10.3 0.1 collective-permute-done.1
  10.4 0.0 collective-permute-done.2
  10.4 0.1 collective-permute-start.3
  10.4 0.0 copy-start
  10.4 1.6 %copy-done = bf16[1,524288]{1,0:T(2,128)(2,1)S(1)} copy-done((bf16[1,524288]{1,0:T(2,128)(2,1)S(1)}, bf16[1,524288]{1,0:T(2,128)(2,1)}, u32[]{:S(2)}) %copy-start) | copy-done | bytes 1048600
  12.0 0.6 %shard_map.64.rows_ref = bf16[4096,128]{1,0:T(8,128)(2,1)S(1)} custom-call(bf16[1,524288]{1,0:T(2,128)(2,1)S(1)} %copy-done), custom_call_target="tpu_custom_call" | custom-call | tf_op jit(solution)/shard_map/pallas_call | solution.py:94
  12.7 0.0 collective-permute-done.3.other_ids.refs_1_
  12.7 1.5 %shard_map.65 = (bf16[512,128]{1,0:T(8,128)(2,1)S(1)}, bf16[512,128]{1,0:T(8,128)(2,1)S(1)}, bf16[512,128]{1,0:T(8,128)(2,1)S(1)}, bf16[512,128]{1,0:T(8,128)(2,1)S(1)}) custom-call(s32[4,8,128]{2,1,0:T(8,128)S(1)} %constant_dynamic-update-slice_fusion.own_ids.refs_0_, s32[4,8,128]{2,1,0:T(8,128)S(1)} %collective-permute-done.3.other_ids.refs_1_, ...), custom_call_target="tpu_custom_call" | custom-call | bytes 10000000 | tf_op jit(solution)/shard_map/pallas_call | solution.py:139
  14.2 2.0 %collective-permute-start.7 = (bf16[512,128]{1,0:T(8,128)(2,1)S(1)}, bf16[512,128]{1,0:T(8,128)(2,1)S(1)}, u32[]{:S(2)}, u32[]{:S(2)}) collective-permute-start(bf16[512,128]{1,0:T(8,128)(2,1)S(1)} %get-tuple-element.18), channel_id=1, source_target_pairs={{0,2},{1,3},{2,0},{3,1},{4,6},{5,7},{6,4},{7,5},{8,10},{9,11},{10,... | collective-permute-start | bytes 393224 | tf_op jit(solution)/shard_map/ppermute | solution.py:338
  16.3 1.5 %collective-permute-start.8 = (bf16[512,128]{1,0:T(8,128)(2,1)S(1)}, bf16[512,128]{1,0:T(8,128)(2,1)S(1)}, u32[]{:S(2)}, u32[]{:S(2)}) collective-permute-start(bf16[512,128]{1,0:T(8,128)(2,1)S(1)} %get-tuple-element.19), channel_id=1, source_target_pairs={{0,16},{8,24},{16,0},{24,8},{1,17},{9,25},{17,1},{25,9},{2,18},{10... | collective-permute-start | bytes 393224 | tf_op jit(solution)/shard_map/ppermute | solution.py:340
  17.8 0.0 collective-permute-start.9
  17.8 0.0 collective-permute-done.4
  17.8 4.4 %collective-permute-done.6 = bf16[128,1152]{1,0:T(8,128)(2,1)S(1)} collective-permute-done((bf16[128,1152]{1,0:T(8,128)(2,1)}, bf16[128,1152]{1,0:T(8,128)(2,1)S(1)}, u32[]{:S(2)}, u32[]{:S(2)}) %collective-permute-start.6) | collective-permute-done | bytes 294944 | tf_op jit(solution)/shard_map/ppermute | solution.py:338
  22.2 1.5 %collective-permute-start.10 = (bf16[128,1152]{1,0:T(8,128)(2,1)S(1)}, bf16[128,1152]{1,0:T(8,128)(2,1)S(1)}, u32[]{:S(2)}, u32[]{:S(2)}) collective-permute-start(bf16[128,1152]{1,0:T(8,128)(2,1)S(1)} %collective-permute-done.6), channel_id=1, source_target_pairs={{0,8},{8,0},{16,24},{24,16},{1,9},{9,1},{17,25},{25,17},{2,10},{10... | collective-permute-start | bytes 884744 | tf_op jit(solution)/shard_map/ppermute | solution.py:340
  23.8 1.2 %collective-permute-done.7.rest_1_ = bf16[512,128]{1,0:T(8,128)(2,1)S(1)} collective-permute-done((bf16[512,128]{1,0:T(8,128)(2,1)S(1)}, bf16[512,128]{1,0:T(8,128)(2,1)S(1)}, u32[]{:S(2)}, u32[]{:S(2)}) %collective-permute-start.7) | collective-permute-done | bytes 131104 | tf_op jit(solution)/shard_map/ppermute | solution.py:338
  25.0 0.0 collective-permute-done.8.rest_2_
  25.0 3.7 %collective-permute-done.9.rest_3_ = bf16[512,128]{1,0:T(8,128)(2,1)S(1)} collective-permute-done((bf16[512,128]{1,0:T(8,128)(2,1)S(1)}, bf16[512,128]{1,0:T(8,128)(2,1)S(1)}, u32[]{:S(2)}, u32[]{:S(2)}) %collective-permute-start.9) | collective-permute-done | bytes 131104 | tf_op jit(solution)/shard_map/ppermute | solution.py:342
  28.7 0.1 collective-permute-start.5
  28.8 0.0 copy-start.1
  28.8 0.0 copy-start.2
  28.9 1.4 %collective-permute-done.10 = bf16[128,1152]{1,0:T(8,128)(2,1)S(1)} collective-permute-done((bf16[128,1152]{1,0:T(8,128)(2,1)S(1)}, bf16[128,1152]{1,0:T(8,128)(2,1)S(1)}, u32[]{:S(2)}, u32[]{:S(2)}) %collective-permute-start.10) | collective-permute-done | bytes 294944 | tf_op jit(solution)/shard_map/ppermute | solution.py:340
  30.3 0.1 collective-permute-start.11
  30.4 0.3 collective-permute-done.5.other_ref.rest_1_
  30.7 1.8 %shard_map.66.rest_4_ = f32[72,128]{1,0:T(8,128)S(1)} custom-call(s32[4,8,128]{2,1,0:T(8,128)S(1)} %constant_dynamic-update-slice_fusion.own_ids.refs_0_, s32[4,8,128]{2,1,0:T(8,128)S(1)} %collective-permute-done.3.other_ids.refs_1_, bf16[256,1152]{1,0:T(8,128)(2,1)S(1)} %constant_dynamic-update-slice_fusion.4.own_ref.rest_0_, ...), custom_call_target="tpu_custom_call" | custom-call | bytes 30000000 | tf_op jit(solution)/shard_map/pallas_call | solution.py:203
  32.5 0.0 collective-permute-done.11.other_ref.rest_3_
  32.5 1.8 %shard_map.67.rest_4_ = f32[72,128]{1,0:T(8,128)S(1)} custom-call(s32[4,8,128]{2,1,0:T(8,128)S(1)} %constant_dynamic-update-slice_fusion.own_ids.refs_0_, s32[4,8,128]{2,1,0:T(8,128)S(1)} %collective-permute-done.3.other_ids.refs_1_, bf16[256,1152]{1,0:T(8,128)(2,1)S(1)} %constant_dynamic-update-slice_fusion.6.own_ref.rest_2_, ...), custom_call_target="tpu_custom_call" | custom-call | bytes 30000000 | tf_op jit(solution)/shard_map/pallas_call | solution.py:203
  34.3 2.2 %collective-permute-start.14 = (f32[72,128]{1,0:T(8,128)S(1)}, f32[72,128]{1,0:T(8,128)S(1)}, u32[]{:S(2)}, u32[]{:S(2)}) collective-permute-start(f32[72,128]{1,0:T(8,128)S(1)} %shard_map.67.rest_4_), channel_id=1, source_target_pairs={{0,18},{1,19},{2,16},{3,17},{4,22},{5,23},{6,20},{7,21},{8,26},{9,... | collective-permute-start | bytes 110600 | tf_op jit(solution)/shard_map/ppermute | solution.py:342
  36.4 0.5 collective-permute-start.13
  36.9 0.9 %collective-permute-start.12 = (f32[72,128]{1,0:T(8,128)S(1)}, f32[72,128]{1,0:T(8,128)S(1)}, u32[]{:S(2)}, u32[]{:S(2)}) collective-permute-start(f32[72,128]{1,0:T(8,128)S(1)} %shard_map.67.rest_4_), channel_id=1, source_target_pairs={{0,2},{1,3},{2,0},{3,1},{4,6},{5,7},{6,4},{7,5},{8,10},{9,11},{10,... | collective-permute-start | bytes 110600 | tf_op jit(solution)/shard_map/ppermute | solution.py:338
  37.8 1.4 %collective-permute-done.14.rest_7_ = f32[72,128]{1,0:T(8,128)S(1)} collective-permute-done((f32[72,128]{1,0:T(8,128)S(1)}, f32[72,128]{1,0:T(8,128)S(1)}, u32[]{:S(2)}, u32[]{:S(2)}) %collective-permute-start.14) | collective-permute-done | bytes 36896 | tf_op jit(solution)/shard_map/ppermute | solution.py:342
  39.2 1.2 %collective-permute-done.13.rest_6_ = f32[72,128]{1,0:T(8,128)S(1)} collective-permute-done((f32[72,128]{1,0:T(8,128)S(1)}, f32[72,128]{1,0:T(8,128)S(1)}, u32[]{:S(2)}, u32[]{:S(2)}) %collective-permute-start.13) | collective-permute-done | bytes 36896 | tf_op jit(solution)/shard_map/ppermute | solution.py:340
  40.4 0.5 collective-permute-done.12.rest_5_
  40.9 1.9 %shard_map.69 = (bf16[512,128]{1,0:T(8,128)(2,1)S(1)}, bf16[512,128]{1,0:T(8,128)(2,1)S(1)}) custom-call(s32[4,8,128]{2,1,0:T(8,128)S(1)} %constant_dynamic-update-slice_fusion.own_ids.refs_0_, s32[4,8,128]{2,1,0:T(8,128)S(1)} %collective-permute-done.3.other_ids.refs_1_, s32[1,128]{1,0:T(1,128)S(1)} %bitcast.6, f32[18,18,128]{2,1,0:T(8,128)S(1)} %bitcast.3, ...), custom_call_target="tpu_custom_call" | custom-call | tf_op jit(solution)/shard_map/pallas_call | solution.py:259
  42.8 1.6 %collective-permute-start.17 = (bf16[512,128]{1,0:T(8,128)(2,1)S(1)}, bf16[512,128]{1,0:T(8,128)(2,1)S(1)}, u32[]{:S(2)}, u32[]{:S(2)}) collective-permute-start(bf16[512,128]{1,0:T(8,128)(2,1)S(1)} %get-tuple-element.24), channel_id=1, source_target_pairs={{0,16},{8,24},{16,0},{24,8},{1,17},{9,25},{17,1},{25,9},{2,18},{10... | collective-permute-start | bytes 393224 | tf_op jit(solution)/shard_map/ppermute | solution.py:340
  44.4 0.8 %collective-permute-start.16 = (bf16[512,128]{1,0:T(8,128)(2,1)S(1)}, bf16[512,128]{1,0:T(8,128)(2,1)S(1)}, u32[]{:S(2)}, u32[]{:S(2)}) collective-permute-start(bf16[512,128]{1,0:T(8,128)(2,1)S(1)} %get-tuple-element.23), channel_id=1, source_target_pairs={{0,18},{1,19},{2,16},{3,17},{4,22},{5,23},{6,20},{7,21},{8,26},{9,... | collective-permute-start | bytes 393224 | tf_op jit(solution)/shard_map/ppermute | solution.py:342
  45.3 1.2 %shard_map.68 = bf16[512,128]{1,0:T(8,128)(2,1)S(1)} custom-call(s32[4,8,128]{2,1,0:T(8,128)S(1)} %constant_dynamic-update-slice_fusion.own_ids.refs_0_, s32[4,8,128]{2,1,0:T(8,128)S(1)} %collective-permute-done.3.other_ids.refs_1_, s32[1,128]{1,0:T(1,128)S(1)} %bitcast.7, f32[18,18,128]{2,1,0:T(8,128)S(1)} %bitcast.4, ...), custom_call_target="tpu_custom_call" | custom-call | tf_op jit(solution)/shard_map/pallas_call | solution.py:259
  46.5 1.2 %collective-permute-start.15 = (bf16[512,128]{1,0:T(8,128)(2,1)S(1)}, bf16[512,128]{1,0:T(8,128)(2,1)S(1)}, u32[]{:S(2)}, u32[]{:S(2)}) collective-permute-start(bf16[512,128]{1,0:T(8,128)(2,1)S(1)} %shard_map.68), channel_id=1, source_target_pairs={{0,2},{1,3},{2,0},{3,1},{4,6},{5,7},{6,4},{7,5},{8,10},{9,11},{10,... | collective-permute-start | bytes 393224 | tf_op jit(solution)/shard_map/ppermute | solution.py:338
  47.7 1.2 %shard_map.70.refs_2_ = bf16[512,128]{1,0:T(8,128)(2,1)S(1)} custom-call(s32[4,8,128]{2,1,0:T(8,128)S(1)} %constant_dynamic-update-slice_fusion.own_ids.refs_0_, s32[4,8,128]{2,1,0:T(8,128)S(1)} %collective-permute-done.3.other_ids.refs_1_, s32[1,128]{1,0:T(1,128)S(1)} %bitcast.8, f32[18,18,128]{2,1,0:T(8,128)S(1)} %bitcast.5, ...), custom_call_target="tpu_custom_call" | custom-call | tf_op jit(solution)/shard_map/pallas_call | solution.py:259
  48.9 0.7 %collective-permute-done.17.refs_3_ = bf16[512,128]{1,0:T(8,128)(2,1)S(1)} collective-permute-done((bf16[512,128]{1,0:T(8,128)(2,1)S(1)}, bf16[512,128]{1,0:T(8,128)(2,1)S(1)}, u32[]{:S(2)}, u32[]{:S(2)}) %collective-permute-start.17) | collective-permute-done | bytes 131104 | tf_op jit(solution)/shard_map/ppermute | solution.py:340
  49.6 1.7 %shard_map.71.refs_4_ = bf16[1,524288]{1,0:T(2,128)(2,1)} custom-call(s32[4,8,128]{2,1,0:T(8,128)S(1)} %constant_dynamic-update-slice_fusion.own_ids.refs_0_, s32[4,8,128]{2,1,0:T(8,128)S(1)} %collective-permute-done.3.other_ids.refs_1_, bf16[512,128]{1,0:T(8,128)(2,1)S(1)} %shard_map.70.refs_2_, bf16[512,128]{1,0:T(8,128)(2,1)S(1)} %collective-permute-done.17.refs_3_), custom_call_target="tpu_custom_call" | custom-call | tf_op jit(solution)/shard_map/pallas_call | solution.py:321
  51.4 0.5 collective-permute-done.15.refs_2_
  51.9 1.8 %shard_map.72 = bf16[1,524288]{1,0:T(2,128)(2,1)} custom-call(s32[4,8,128]{2,1,0:T(8,128)S(1)} %constant_dynamic-update-slice_fusion.own_ids.refs_0_, s32[4,8,128]{2,1,0:T(8,128)S(1)} %collective-permute-done.3.other_ids.refs_1_, bf16[512,128]{1,0:T(8,128)(2,1)S(1)} %collective-permute-done.15.refs_2_, ...), custom_call_target="tpu_custom_call", output_to_operand_aliasing={{}: (4, {})} | custom-call | tf_op jit(solution)/shard_map/pallas_call | solution.py:321
  (15 shorter events, 0.1 us)
Async XLA Ops:
  0.7 9.6 %collective-permute-start.2 = (s32[1,8,128]{2,1,0:T(8,128)S(1)}, s32[1,8,128]{2,1,0:T(8,128)S(1)}, u32[]{:S(2)}, u32[]{:S(2)}) collective-permute-start(s32[1,8,128]{2,1,0:T(8,128)S(1)} %reshape.6), channel_id=1, source_target_pairs={{0,6},{1,7},{2,4},{3,5},{4,2},{5,3},{6,0},{7,1},{8,14},{9,15},{10,... | collective-permute-start | bytes 12296 | tf_op jit(solution)/shard_map/ppermute | solution.py:338
  5.8 4.5 %collective-permute-start.1 = (s32[1,8,128]{2,1,0:T(8,128)S(1)}, s32[1,8,128]{2,1,0:T(8,128)S(1)}, u32[]{:S(2)}, u32[]{:S(2)}) collective-permute-start(s32[1,8,128]{2,1,0:T(8,128)S(1)} %reshape.6), channel_id=1, source_target_pairs={{0,4},{1,5},{2,6},{3,7},{4,0},{5,1},{6,2},{7,3},{8,12},{9,13},{10,... | collective-permute-start | bytes 12296 | tf_op jit(solution)/shard_map/ppermute | solution.py:338
  5.8 4.4 %collective-permute-start = (s32[1,8,128]{2,1,0:T(8,128)S(1)}, s32[1,8,128]{2,1,0:T(8,128)S(1)}, u32[]{:S(2)}, u32[]{:S(2)}) collective-permute-start(s32[1,8,128]{2,1,0:T(8,128)S(1)} %reshape.6), channel_id=1, source_target_pairs={{0,2},{1,3},{2,0},{3,1},{4,6},{5,7},{6,4},{7,5},{8,10},{9,11},{10,... | collective-permute-start | bytes 12296 | tf_op jit(solution)/shard_map/ppermute | solution.py:338
  6.5 15.8 %collective-permute-start.6 = (bf16[128,1152]{1,0:T(8,128)(2,1)}, bf16[128,1152]{1,0:T(8,128)(2,1)S(1)}, u32[]{:S(2)}, u32[]{:S(2)}) collective-permute-start(bf16[128,1152]{1,0:T(8,128)(2,1)} %bitcast.9), channel_id=1, source_target_pairs={{0,4},{1,5},{2,6},{3,7},{4,0},{5,1},{6,2},{7,3},{8,12},{9,13},{10,... | collective-permute-start | bytes 884744 | tf_op jit(solution)/shard_map/ppermute | solution.py:338
  8.8 9.1 %collective-permute-start.4 = (bf16[128,1152]{1,0:T(8,128)(2,1)}, bf16[128,1152]{1,0:T(8,128)(2,1)S(1)}, u32[]{:S(2)}, u32[]{:S(2)}) collective-permute-start(bf16[128,1152]{1,0:T(8,128)(2,1)} %bitcast.10), channel_id=1, source_target_pairs={{0,8},{8,0},{16,24},{24,16},{1,9},{9,1},{17,25},{25,17},{2,10},{10... | collective-permute-start | bytes 884744 | tf_op jit(solution)/shard_map/ppermute | solution.py:340
  10.4 2.3 %collective-permute-start.3 = (s32[4,8,128]{2,1,0:T(8,128)S(1)}, s32[4,8,128]{2,1,0:T(8,128)S(1)}, u32[]{:S(2)}, u32[]{:S(2)}) collective-permute-start(s32[4,8,128]{2,1,0:T(8,128)S(1)} %constant_dynamic-update-slice_fusion.own_ids.refs_0_), channel_id=1, source_target_pairs={{0,1},{1,0},{2,3},{3,2},{4,5},{5,4},{6,7},{7,6},{8,9},{9,8},{10,11... | collective-permute-start | bytes 49160 | tf_op jit(solution)/shard_map/ppermute | solution.py:338
  10.4 1.6 %copy-start = (bf16[1,524288]{1,0:T(2,128)(2,1)S(1)}, bf16[1,524288]{1,0:T(2,128)(2,1)}, u32[]{:S(2)}) copy-start(bf16[1,524288]{1,0:T(2,128)(2,1)} %psi_ref.1) | copy-start | bytes 3145732
  12.0 5.8 %copy-start.3 = (bf16[1,128,1152]{2,1,0:T(8,128)(2,1)S(1)}, bf16[1,128,1152]{2,1,0:T(8,128)(2,1)}, u32[]{:S(2)}) copy-start(bf16[1,128,1152]{2,1,0:T(8,128)(2,1)} %param.7) | copy-start | bytes 884740
  14.2 10.7 %collective-permute-start.7 = (bf16[512,128]{1,0:T(8,128)(2,1)S(1)}, bf16[512,128]{1,0:T(8,128)(2,1)S(1)}, u32[]{:S(2)}, u32[]{:S(2)}) collective-permute-start(bf16[512,128]{1,0:T(8,128)(2,1)S(1)} %get-tuple-element.18), channel_id=1, source_target_pairs={{0,2},{1,3},{2,0},{3,1},{4,6},{5,7},{6,4},{7,5},{8,10},{9,11},{10,... | collective-permute-start | bytes 393224 | tf_op jit(solution)/shard_map/ppermute | solution.py:338
  16.3 8.7 %collective-permute-start.8 = (bf16[512,128]{1,0:T(8,128)(2,1)S(1)}, bf16[512,128]{1,0:T(8,128)(2,1)S(1)}, u32[]{:S(2)}, u32[]{:S(2)}) collective-permute-start(bf16[512,128]{1,0:T(8,128)(2,1)S(1)} %get-tuple-element.19), channel_id=1, source_target_pairs={{0,16},{8,24},{16,0},{24,8},{1,17},{9,25},{17,1},{25,9},{2,18},{10... | collective-permute-start | bytes 393224 | tf_op jit(solution)/shard_map/ppermute | solution.py:340
  17.8 10.9 %collective-permute-start.9 = (bf16[512,128]{1,0:T(8,128)(2,1)S(1)}, bf16[512,128]{1,0:T(8,128)(2,1)S(1)}, u32[]{:S(2)}, u32[]{:S(2)}) collective-permute-start(bf16[512,128]{1,0:T(8,128)(2,1)S(1)} %get-tuple-element.20), channel_id=1, source_target_pairs={{0,18},{1,19},{2,16},{3,17},{4,22},{5,23},{6,20},{7,21},{8,26},{9,... | collective-permute-start | bytes 393224 | tf_op jit(solution)/shard_map/ppermute | solution.py:342
  22.2 8.0 %collective-permute-start.10 = (bf16[128,1152]{1,0:T(8,128)(2,1)S(1)}, bf16[128,1152]{1,0:T(8,128)(2,1)S(1)}, u32[]{:S(2)}, u32[]{:S(2)}) collective-permute-start(bf16[128,1152]{1,0:T(8,128)(2,1)S(1)} %collective-permute-done.6), channel_id=1, source_target_pairs={{0,8},{8,0},{16,24},{24,16},{1,9},{9,1},{17,25},{25,17},{2,10},{10... | collective-permute-start | bytes 884744 | tf_op jit(solution)/shard_map/ppermute | solution.py:340
  28.7 2.0 %collective-permute-start.5 = (bf16[256,1152]{1,0:T(8,128)(2,1)S(1)}, bf16[256,1152]{1,0:T(8,128)(2,1)S(1)}, u32[]{:S(2)}, u32[]{:S(2)}) collective-permute-start(bf16[256,1152]{1,0:T(8,128)(2,1)S(1)} %constant_dynamic-update-slice_fusion.4.own_ref.rest_0_), channel_id=1, source_target_pairs={{0,1},{1,0},{2,3},{3,2},{4,5},{5,4},{6,7},{7,6},{8,9},{9,8},{10,11... | collective-permute-start | bytes 1769480 | tf_op jit(solution)/shard_map/ppermute | solution.py:338
  28.8 12.1 %copy-start.1 = (f32[128,18,18]{0,2,1:T(8,128)S(1)}, f32[128,18,18]{0,2,1:T(8,128)}, u32[]{:S(2)}) copy-start(f32[128,18,18]{0,2,1:T(8,128)} %param.11) | copy-start | bytes 497668
  28.8 12.1 %copy-start.2 = (s32[128]{0:T(128)S(1)}, s32[128]{0:T(128)}, u32[]{:S(2)}) copy-start(s32[128]{0:T(128)} %param.10) | copy-start | bytes 1540
  30.3 2.2 %collective-permute-start.11 = (bf16[256,1152]{1,0:T(8,128)(2,1)S(1)}, bf16[256,1152]{1,0:T(8,128)(2,1)S(1)}, u32[]{:S(2)}, u32[]{:S(2)}) collective-permute-start(bf16[256,1152]{1,0:T(8,128)(2,1)S(1)} %constant_dynamic-update-slice_fusion.6.own_ref.rest_2_), channel_id=1, source_target_pairs={{0,1},{1,0},{2,3},{3,2},{4,5},{5,4},{6,7},{7,6},{8,9},{9,8},{10,11... | collective-permute-start | bytes 1769480 | tf_op jit(solution)/shard_map/ppermute | solution.py:338
  34.3 4.9 %collective-permute-start.14 = (f32[72,128]{1,0:T(8,128)S(1)}, f32[72,128]{1,0:T(8,128)S(1)}, u32[]{:S(2)}, u32[]{:S(2)}) collective-permute-start(f32[72,128]{1,0:T(8,128)S(1)} %shard_map.67.rest_4_), channel_id=1, source_target_pairs={{0,18},{1,19},{2,16},{3,17},{4,22},{5,23},{6,20},{7,21},{8,26},{9,... | collective-permute-start | bytes 110600 | tf_op jit(solution)/shard_map/ppermute | solution.py:342
  36.4 4.0 %collective-permute-start.13 = (f32[72,128]{1,0:T(8,128)S(1)}, f32[72,128]{1,0:T(8,128)S(1)}, u32[]{:S(2)}, u32[]{:S(2)}) collective-permute-start(f32[72,128]{1,0:T(8,128)S(1)} %shard_map.67.rest_4_), channel_id=1, source_target_pairs={{0,16},{8,24},{16,0},{24,8},{1,17},{9,25},{17,1},{25,9},{2,18},{10... | collective-permute-start | bytes 110600 | tf_op jit(solution)/shard_map/ppermute | solution.py:340
  36.9 4.0 %collective-permute-start.12 = (f32[72,128]{1,0:T(8,128)S(1)}, f32[72,128]{1,0:T(8,128)S(1)}, u32[]{:S(2)}, u32[]{:S(2)}) collective-permute-start(f32[72,128]{1,0:T(8,128)S(1)} %shard_map.67.rest_4_), channel_id=1, source_target_pairs={{0,2},{1,3},{2,0},{3,1},{4,6},{5,7},{6,4},{7,5},{8,10},{9,11},{10,... | collective-permute-start | bytes 110600 | tf_op jit(solution)/shard_map/ppermute | solution.py:338
  42.8 6.8 %collective-permute-start.17 = (bf16[512,128]{1,0:T(8,128)(2,1)S(1)}, bf16[512,128]{1,0:T(8,128)(2,1)S(1)}, u32[]{:S(2)}, u32[]{:S(2)}) collective-permute-start(bf16[512,128]{1,0:T(8,128)(2,1)S(1)} %get-tuple-element.24), channel_id=1, source_target_pairs={{0,16},{8,24},{16,0},{24,8},{1,17},{9,25},{17,1},{25,9},{2,18},{10... | collective-permute-start | bytes 393224 | tf_op jit(solution)/shard_map/ppermute | solution.py:340
  44.4 7.0 %collective-permute-start.16 = (bf16[512,128]{1,0:T(8,128)(2,1)S(1)}, bf16[512,128]{1,0:T(8,128)(2,1)S(1)}, u32[]{:S(2)}, u32[]{:S(2)}) collective-permute-start(bf16[512,128]{1,0:T(8,128)(2,1)S(1)} %get-tuple-element.23), channel_id=1, source_target_pairs={{0,18},{1,19},{2,16},{3,17},{4,22},{5,23},{6,20},{7,21},{8,26},{9,... | collective-permute-start | bytes 393224 | tf_op jit(solution)/shard_map/ppermute | solution.py:342
  46.5 5.4 %collective-permute-start.15 = (bf16[512,128]{1,0:T(8,128)(2,1)S(1)}, bf16[512,128]{1,0:T(8,128)(2,1)S(1)}, u32[]{:S(2)}, u32[]{:S(2)}) collective-permute-start(bf16[512,128]{1,0:T(8,128)(2,1)S(1)} %shard_map.68), channel_id=1, source_target_pairs={{0,2},{1,3},{2,0},{3,1},{4,6},{5,7},{6,4},{7,5},{8,10},{9,11},{10,... | collective-permute-start | bytes 393224 | tf_op jit(solution)/shard_map/ppermute | solution.py:338
